TPU v7x, 32 devices: a whole 2x2x4 slice. The times are simulated.
32 devices in a mesh: rows: 16 (over z, x, core), heads: 2 (over y).
Axes of the slice: x: 2, y: 2, z: 4, core: 2. Of those that a mesh axis runs over, the one named last changes fastest.
Arguments:
- tokens: bfloat16 [49152, 1152], P(('rows', 'heads')), may hold values from -6 to 6
- condition: bfloat16 [128, 1152], P('rows'), may hold values from -6 to 6
- segment_ids: int32 [48, 1024], P('rows'), may hold values from 0 to 3, never falling along the last dimension, each value on 1 to 512 neighbouring positions
- tile_mask: int32 [48, 8, 8], P('rows'), may hold values 0 or 1
- image_index: int32 [48, 4], P('rows'), may hold values from 0 to 7
- w_ada: float32 [1152, 6912], P(None, 'heads'), may hold values from -0.1875 to 0.1875
- b_ada: float32 [6912], P('heads'), may hold values from -3 to 3
- w_query: float32 [1152, 1152], P('rows', 'heads'), may hold values from -0.1875 to 0.1875
- w_key: float32 [1152, 1152], P('rows', 'heads'), may hold values from -0.1875 to 0.1875
- w_value: float32 [1152, 1152], P('rows', 'heads'), may hold values from -0.1875 to 0.1875
- b_query: float32 [1152], P('heads'), may hold values from -3 to 3
- b_value: float32 [1152], P('heads'), may hold values from -3 to 3
- w_out: float32 [1152, 1152], P('rows', 'heads'), may hold values from -1.5 to 1.5
- b_out: float32 [1152], replicated, may hold values from -3 to 3
- w_up: float32 [1152, 4608], P('rows', 'heads'), may hold values from -0.1875 to 0.1875
- b_up: float32 [4608], P('heads'), may hold values from -3 to 3
- w_down: float32 [1152, 4608], P('rows', 'heads'), may hold values from -0.1875 to 0.1875
- b_down: float32 [1152], replicated, may hold values from -3 to 3
- cotangent: bfloat16 [49152, 1152], P(('rows', 'heads')), may hold values from -6 to 6
Outputs:
- output: bfloat16 [49152, 1152], P(('rows', 'heads'))
- grad_tokens: float32 [49152, 1152], P(('rows', 'heads'))
- grad_condition: float32 [128, 1152], P('rows')
- grad_w_ada: float32 [1152, 6912], P(None, 'heads')
- grad_b_ada: float32 [6912], P('heads')
- grad_w_query: float32 [1152, 1152], P('rows', 'heads')
- grad_w_key: float32 [1152, 1152], P('rows', 'heads')
- grad_w_value: float32 [1152, 1152], P('rows', 'heads')
- grad_b_query: float32 [1152], P('heads')
- grad_b_value: float32 [1152], P('heads')
- grad_w_out: float32 [1152, 1152], P('rows', 'heads')
- grad_b_out: float32 [1152], P('heads')
- grad_w_up: float32 [1152, 4608], P('rows', 'heads')
- grad_b_up: float32 [4608], P('heads')
- grad_w_down: float32 [1152, 4608], P('rows', 'heads')
- grad_b_down: float32 [1152], P('heads')
All inputs are finite; a program needn't handle non-finite values. No bound on the sum of `tile_mask` on one device may be relied on, other than what follows from the above.
Results may differ from a plain program's by a relative error of at most 0.014.
The roundings to bfloat16 on the way count: a program that leaves them out, or rounds other values in their place, can miss the bound.
Values may be sent and summed in bfloat16 or wider, within the bound.
No kernel may reach another device: no remote copies, remote signals or barrier semaphores. Data moves between devices by JAX's collectives and lax.ppermute only.
A program may use at most 576 MiB of HBM per device.

v0:
```python
from functools import partial

import jax
import jax.numpy as jnp
from jax import lax
from jax.sharding import PartitionSpec as P

HEAD_DIM = 72
TILE = 128


EPSILON = 1e-06
MASKED_SCORE = -1e30
PRECISE = lax.Precision.HIGHEST


def layer_norm(values):
    centred = values - jnp.mean(values, axis=-1, keepdims=True)
    inverse = lax.rsqrt(jnp.mean(centred * centred, axis=-1, keepdims=True) + EPSILON)
    return (centred * inverse, inverse)


def norm_back(normed, inverse, grad):
    return inverse * (
        grad
        - jnp.mean(grad, axis=-1, keepdims=True)
        - normed * jnp.mean(grad * normed, axis=-1, keepdims=True)
    )


def contract_last(left, right):
    return lax.dot_general(
        left, right, (((1,), (1,)), ((), ())), preferred_element_type=jnp.float32
    )


def contract_first(left, right):
    return lax.dot_general(
        left, right, (((0,), (0,)), ((), ())), preferred_element_type=jnp.float32
    )


def body(
    tokens,
    condition,
    segment_ids,
    tile_mask,
    image_index,
    w_ada,
    b_ada,
    w_query,
    w_key,
    w_value,
    b_query,
    b_value,
    w_out,
    b_out,
    w_up,
    b_up,
    w_down,
    b_down,
    cotangent,
):
    scaling = HEAD_DIM ** (-0.5)
    own_rows = tokens.shape[0]
    seq_count = segment_ids.shape[0]
    length = segment_ids.shape[1]
    group_rows = seq_count * length
    own_start = lax.axis_index("heads") * own_rows
    img_count = condition.shape[0]
    slot_count = image_index.shape[1]
    local_heads = w_query.shape[1] // HEAD_DIM
    block_rows = min(512, length)
    tile_count = length // TILE
    bfloat = jnp.bfloat16
    own_segments = lax.dynamic_slice_in_dim(segment_ids.reshape(group_rows), own_start, own_rows)
    own_seqs = (own_start + jnp.arange(own_rows, dtype=jnp.int32)) // length
    seq_match = own_seqs[:, None] == jnp.arange(seq_count, dtype=jnp.int32)[None, :]
    slot_match = own_segments[:, None] == jnp.arange(slot_count, dtype=jnp.int32)[None, :]
    own_image = jnp.sum(
        jnp.where(seq_match[:, :, None] & slot_match[:, None, :], image_index[None, :, :], 0),
        axis=(1, 2),
    )
    image_onehot = (own_image[:, None] == jnp.arange(img_count, dtype=jnp.int32)[None, :]).astype(
        jnp.float32
    )
    cond_full = condition.astype(jnp.float32)
    silu_cond = jax.nn.silu(cond_full)
    mod_cols = jnp.dot(silu_cond, w_ada, precision=PRECISE) + b_ada
    mod_full, up_bias_all = (
        lax.all_gather(mod_cols, "heads", axis=1, tiled=True),
        lax.all_gather(b_up.reshape(1, -1), "heads", axis=1, tiled=True),
    )
    per_token = jnp.dot(image_onehot, mod_full, precision=PRECISE)
    shift_one, scale_one, gate_one, shift_two, scale_two, gate_two = jnp.split(per_token, 6, axis=1)

    def gather_weights():
        return (
            lax.all_gather(w_query.astype(bfloat), "rows", axis=0, tiled=True),
            lax.all_gather(w_key.astype(bfloat), "rows", axis=0, tiled=True),
            lax.all_gather(w_value.astype(bfloat), "rows", axis=0, tiled=True),
            lax.all_gather(w_out.astype(bfloat), "rows", axis=0, tiled=True),
            lax.all_gather(w_up.astype(bfloat), "rows", axis=0, tiled=True),
            lax.all_gather(w_down.astype(bfloat), "rows", axis=0, tiled=True),
        )

    def spread_first(values):
        return lax.all_gather(values, "heads", axis=0, tiled=True)

    query_full, key_full, value_full, out_full, up_full, down_full = gather_weights()
    token_full = tokens.astype(jnp.float32)
    normed_one, inverse_one = layer_norm(token_full)
    hidden_own_one = (normed_one * (1.0 + scale_one) + shift_one).astype(bfloat)
    hidden_one = spread_first(hidden_own_one)
    head_shape = (group_rows, local_heads, HEAD_DIM)
    query_heads = (
        (jnp.dot(hidden_one, query_full, preferred_element_type=jnp.float32) + b_query)
        .astype(bfloat)
        .reshape(head_shape)
    )
    key_heads = (
        jnp.dot(hidden_one, key_full, preferred_element_type=jnp.float32)
        .astype(bfloat)
        .reshape(head_shape)
    )
    value_heads = (
        (jnp.dot(hidden_one, value_full, preferred_element_type=jnp.float32) + b_value)
        .astype(bfloat)
        .reshape(head_shape)
    )
    tile_of = jnp.arange(length, dtype=jnp.int32) // TILE

    def scores_for(seq_index, block_start):
        seq_start = seq_index * length
        block_query = query_heads[seq_start + block_start : seq_start + block_start + block_rows]
        seq_keys = key_heads[seq_start : seq_start + length]
        block_tiles = tile_mask[seq_index][block_start // TILE : (block_start + block_rows) // TILE]
        expanded = jnp.broadcast_to(
            block_tiles[:, None, :, None], (block_rows // TILE, TILE, tile_count, TILE)
        ).reshape(block_rows, length)
        seg_row = segment_ids[seq_index]
        same_image = seg_row[block_start : block_start + block_rows][:, None] == seg_row[None, :]
        diagonal = tile_of[block_start : block_start + block_rows][:, None] == tile_of[None, :]
        allowed = same_image & ((expanded > 0) | diagonal)
        raw = (
            jnp.einsum("qhd,khd->hqk", block_query, seq_keys, preferred_element_type=jnp.float32)
            * scaling
        )
        return (jnp.where(allowed[None], raw, MASKED_SCORE), block_query, seq_keys)

    attended_parts = []
    log_totals = []
    for seq_index in range(seq_count):
        seq_values = value_heads[seq_index * length : (seq_index + 1) * length]
        for block_start in range(0, length, block_rows):
            scores, block_query, seq_keys = scores_for(seq_index, block_start)
            top_score = jnp.max(scores, axis=-1, keepdims=True)
            log_total = top_score + jnp.log(
                jnp.sum(jnp.exp(scores - top_score), axis=-1, keepdims=True)
            )
            probs_low = jnp.exp(scores - log_total).astype(bfloat)
            attended_parts.append(
                jnp.einsum(
                    "hqk,khd->qhd", probs_low, seq_values, preferred_element_type=jnp.float32
                )
            )
            log_totals.append(log_total)
    attended = (
        jnp.concatenate(attended_parts, axis=0)
        .reshape(group_rows, local_heads * HEAD_DIM)
        .astype(bfloat)
    )
    branch_one = (
        lax.psum_scatter(
            contract_last(attended, out_full), "heads", scatter_dimension=0, tiled=True
        )
        + b_out
    )
    middle = token_full + gate_one * branch_one
    normed_two, inverse_two = layer_norm(middle)
    hidden_own_two = (normed_two * (1.0 + scale_two) + shift_two).astype(bfloat)
    up_all, down_all = (
        lax.all_gather(up_full, "heads", axis=1, tiled=True),
        lax.all_gather(down_full, "heads", axis=1, tiled=True),
    )
    pre_act = jnp.dot(hidden_own_two, up_all, preferred_element_type=jnp.float32) + up_bias_all[0]
    activated = jax.nn.gelu(pre_act, approximate=True).astype(bfloat)
    branch_two = contract_last(activated, down_all) + b_down
    output = (middle + gate_two * branch_two).astype(bfloat)
    query_back, key_back, value_back, out_back, up_back, down_back = gather_weights()
    hidden_one_back = spread_first(hidden_own_one)
    grad_out = cotangent.astype(jnp.float32)
    grad_branch_two = (grad_out * gate_two).astype(bfloat)
    grad_gate_two = grad_out * branch_two
    grad_down_all = contract_first(grad_branch_two, activated)
    grad_act = jnp.dot(grad_branch_two, down_all, preferred_element_type=jnp.float32)
    _, gelu_back = jax.vjp(partial(jax.nn.gelu, approximate=True), pre_act)
    grad_pre = gelu_back(grad_act)[0].astype(bfloat)
    grad_up_all = contract_first(hidden_own_two, grad_pre)
    grad_bias_all = jnp.sum(grad_pre, axis=0, dtype=jnp.float32).reshape(1, -1)
    grad_hidden_two = contract_last(grad_pre, up_all)
    grad_w_up, grad_w_down, grad_bias_cols = (
        lax.psum_scatter(grad_up_all, "heads", scatter_dimension=1, tiled=True),
        lax.psum_scatter(grad_down_all, "heads", scatter_dimension=1, tiled=True),
        lax.psum_scatter(grad_bias_all, "heads", scatter_dimension=1, tiled=True),
    )
    grad_b_up = grad_bias_cols[0]
    grad_scale_two = grad_hidden_two * normed_two
    grad_middle = grad_out + norm_back(normed_two, inverse_two, grad_hidden_two * (1.0 + scale_two))
    grad_branch_one = (grad_middle * gate_one).astype(bfloat)
    grad_gate_one = grad_middle * branch_one
    grad_one_full = lax.all_gather(grad_branch_one, "heads", axis=0, tiled=True)
    grad_w_out = contract_first(grad_one_full, attended)
    grad_attended = (
        jnp.dot(grad_one_full, out_back, preferred_element_type=jnp.float32)
        .astype(bfloat)
        .reshape(head_shape)
    )
    grad_query_parts = []
    grad_key_parts = []
    grad_value_parts = []
    block_number = 0
    for seq_index in range(seq_count):
        seq_start = seq_index * length
        seq_values = value_heads[seq_start : seq_start + length]
        key_total = jnp.zeros((length, local_heads, HEAD_DIM), jnp.float32)
        value_total = jnp.zeros((length, local_heads, HEAD_DIM), jnp.float32)
        for block_start in range(0, length, block_rows):
            scores, block_query, seq_keys = scores_for(seq_index, block_start)
            probs = jnp.exp(scores - log_totals[block_number])
            block_number += 1
            grad_block = grad_attended[
                seq_start + block_start : seq_start + block_start + block_rows
            ]
            grad_probs = jnp.einsum(
                "qhd,khd->hqk", grad_block, seq_values, preferred_element_type=jnp.float32
            )
            centre = jnp.sum(probs * grad_probs, axis=-1, keepdims=True)
            grad_scores = (probs * (grad_probs - centre)).astype(bfloat)
            grad_query_parts.append(
                (
                    jnp.einsum(
                        "hqk,khd->qhd", grad_scores, seq_keys, preferred_element_type=jnp.float32
                    )
                    * scaling
                ).astype(bfloat)
            )
            key_total = (
                key_total
                + jnp.einsum(
                    "hqk,qhd->khd", grad_scores, block_query, preferred_element_type=jnp.float32
                )
                * scaling
            )
            value_total = value_total + jnp.einsum(
                "hqk,qhd->khd", probs.astype(bfloat), grad_block, preferred_element_type=jnp.float32
            )
        grad_key_parts.append(key_total.astype(bfloat))
        grad_value_parts.append(value_total.astype(bfloat))
    flat_shape = (group_rows, local_heads * HEAD_DIM)
    grad_queries = jnp.concatenate(grad_query_parts, axis=0).reshape(flat_shape)
    grad_keys = jnp.concatenate(grad_key_parts, axis=0).reshape(flat_shape)
    grad_values = jnp.concatenate(grad_value_parts, axis=0).reshape(flat_shape)
    grad_w_query = contract_first(hidden_one_back, grad_queries)
    grad_w_key = contract_first(hidden_one_back, grad_keys)
    grad_w_value = contract_first(hidden_one_back, grad_values)
    grad_b_query = jnp.sum(grad_queries, axis=0, dtype=jnp.float32)
    grad_b_value = jnp.sum(grad_values, axis=0, dtype=jnp.float32)
    total = contract_last(grad_queries, query_back)
    total = total + contract_last(grad_keys, key_back)
    grad_hidden_one = lax.psum_scatter(
        total + contract_last(grad_values, value_back), "heads", scatter_dimension=0, tiled=True
    )
    grad_scale_one = grad_hidden_one * normed_one
    grad_tokens = grad_middle + norm_back(
        normed_one, inverse_one, grad_hidden_one * (1.0 + scale_one)
    )
    grad_mod_tokens = jnp.concatenate(
        [
            grad_hidden_one,
            grad_scale_one,
            grad_gate_one,
            grad_hidden_two,
            grad_scale_two,
            grad_gate_two,
        ],
        axis=1,
    )
    grad_mod_images = lax.dot_general(
        image_onehot,
        grad_mod_tokens,
        (((0,), (0,)), ((), ())),
        precision=PRECISE,
        preferred_element_type=jnp.float32,
    )
    bias_parts = jnp.stack(
        [
            jnp.sum(grad_branch_one, axis=0, dtype=jnp.float32),
            jnp.sum(grad_branch_two, axis=0, dtype=jnp.float32),
        ],
        axis=0,
    )
    grad_mod_cols, bias_cols = (
        lax.psum_scatter(grad_mod_images, "heads", scatter_dimension=1, tiled=True),
        lax.psum_scatter(bias_parts, "heads", scatter_dimension=1, tiled=True),
    )
    grad_w_ada = lax.dot_general(
        silu_cond,
        grad_mod_cols,
        (((0,), (0,)), ((), ())),
        precision=PRECISE,
        preferred_element_type=jnp.float32,
    )
    grad_b_ada = jnp.sum(grad_mod_cols, axis=0)
    grad_silu = lax.dot_general(
        grad_mod_cols,
        w_ada,
        (((1,), (1,)), ((), ())),
        precision=PRECISE,
        preferred_element_type=jnp.float32,
    )
    grad_silu = lax.psum(grad_silu, "heads")
    _, silu_back = jax.vjp(jax.nn.silu, cond_full)
    grad_condition = silu_back(grad_silu)[0]
    grad_w_ada, grad_b_ada, grad_b_query, grad_b_value, grad_b_up, bias_cols = lax.psum(
        (grad_w_ada, grad_b_ada, grad_b_query, grad_b_value, grad_b_up, bias_cols), "rows"
    )
    grad_w_query, grad_w_key, grad_w_value, grad_w_out, grad_w_up, grad_w_down = (
        lax.psum_scatter(grad_w_query, "rows", scatter_dimension=0, tiled=True),
        lax.psum_scatter(grad_w_key, "rows", scatter_dimension=0, tiled=True),
        lax.psum_scatter(grad_w_value, "rows", scatter_dimension=0, tiled=True),
        lax.psum_scatter(grad_w_out, "rows", scatter_dimension=0, tiled=True),
        lax.psum_scatter(grad_w_up, "rows", scatter_dimension=0, tiled=True),
        lax.psum_scatter(grad_w_down, "rows", scatter_dimension=0, tiled=True),
    )
    return (
        output,
        grad_tokens,
        grad_condition,
        grad_w_ada,
        grad_b_ada,
        grad_w_query,
        grad_w_key,
        grad_w_value,
        grad_b_query,
        grad_b_value,
        grad_w_out,
        bias_cols[0],
        grad_w_up,
        grad_b_up,
        grad_w_down,
        bias_cols[1],
    )


def solution(mesh):
    placed = (
        P(("rows", "heads"), None),
        P("rows", None),
        P("rows", None),
        P("rows", None, None),
        P("rows", None),
        P(None, "heads"),
        P("heads"),
        P("rows", "heads"),
        P("rows", "heads"),
        P("rows", "heads"),
        P("heads"),
        P("heads"),
        P("rows", "heads"),
        P(),
        P("rows", "heads"),
        P("heads"),
        P("rows", "heads"),
        P(),
        P(("rows", "heads"), None),
    )
    return jax.shard_map(
        body,
        mesh=mesh,
        in_specs=placed,
        out_specs=(
            P(("rows", "heads"), None),
            P(("rows", "heads"), None),
            P("rows", None),
            P(None, "heads"),
            P("heads"),
            P("rows", "heads"),
            P("rows", "heads"),
            P("rows", "heads"),
            P("heads"),
            P("heads"),
            P("rows", "heads"),
            P("heads"),
            P("rows", "heads"),
            P("heads"),
            P("rows", "heads"),
            P("heads"),
        ),
        check_vma=False,
    )
```

profile of v0, /device:TPU:9, one launch (start us, length us, event | category | flops | bytes accessed | tf_op | source)
XLA Modules:
  0.0 2944.9 jit_solution(13988093790023210941)
XLA Ops:
  12.3 11.4 convolution_add_fusion.1
  28.5 21.7 fusion.81
  69.8 81.0 %all-gather.13.cloned.1.call-done = bf16[3072,1152]{1,0:T(8,128)(2,1)} async-done(((bf16[1536,1152]{1,0:T(8,128)(2,1)}), bf16[3072,1152]{1,0:T(8,128)(2,1)}) %all-gather.13.cloned.1.call-update) | async-done | bytes 7077904 | tf_op jit(solution)/shard_map/all_gather | solution.py:108
  150.8 8.2 convolution_convert_fusion.1
  159.4 32.9 %all-gather.17.cloned.1.call-done = bf16[1152,576]{1,0:T(8,128)(2,1)} async-done(((bf16[72,576]{1,0:T(8,128)(2,1)}), bf16[1152,576]{1,0:T(8,128)(2,1)}) %all-gather.17.cloned.1.call-update) | async-done | bytes 1327120 | tf_op jit(solution)/shard_map/all_gather | solution.py:99
  192.3 8.2 add_convert_fusion.1
  259.0 8.4 add_convert_fusion.2
  269.2 8.4 fusion.57
  277.7 8.8 fusion.59
  294.7 9.2 fusion.63
  309.6 8.7 fusion.67
  318.4 11.3 fusion.130
  332.8 57.7 %all-gather.27.cloned.1.call-done = bf16[1152,2304]{1,0:T(8,128)(2,1)} async-done(((bf16[72,2304]{1,0:T(8,128)(2,1)}), bf16[1152,2304]{1,0:T(8,128)(2,1)}) %all-gather.27.cloned.1.call-update) | async-done | bytes 5308432 | tf_op jit(solution)/shard_map/all_gather | solution.py:104
  397.3 155.6 %reduce-scatter.26.cloned.1.call-done = f32[1536,1152]{1,0:T(8,128)} async-done(((f32[3072,1152]{1,0:T(8,128)}), f32[1536,1152]{1,0:T(8,128)}) %reduce-scatter.26.cloned.1.call-update) | async-done | bytes 7077904 | tf_op jit(solution)/shard_map/reduce_scatter | solution.py:174
  563.7 14.5 convert_reduce_fusion.2
  578.2 107.3 %all-gather.25.cloned.1.call-done = bf16[1152,4608]{1,0:T(8,128)(2,1)} async-done(((bf16[1152,2304]{1,0:T(8,128)(2,1)}), bf16[1152,4608]{1,0:T(8,128)(2,1)}) %all-gather.25.cloned.1.call-update) | async-done | bytes 10616848 | tf_op jit(solution)/shard_map/all_gather | solution.py:183
  685.5 33.7 %multiply_convert_fusion = (bf16[1536,4608]{1,0:T(8,128)(2,1)}, f32[1536,4608]{1,0:T(8,128)}) fusion(f32[4608]{0:T(1024)} %reshape.693, bf16[1536,1152]{1,0:T(8,128)(2,1)} %get-tuple-element.37, bf16[1152,4608]{1,0:T(8,128)(2,1)} %all-gather.25.cloned.1.call-done), kind=kOutput, calls=%fused_computation.10 | convolution fusion | flops 16378232832 | bytes 56641536 | tf_op jit(solution)/shard_map/dot_general | solution.py:186
  719.1 98.7 %all-gather.29.cloned.1.call-done = bf16[1152,4608]{1,0:T(8,128)(2,1)} async-done(((bf16[1152,2304]{1,0:T(8,128)(2,1)}), bf16[1152,4608]{1,0:T(8,128)(2,1)}) %all-gather.29.cloned.1.call-update) | async-done | bytes 10616848 | tf_op jit(solution)/shard_map/all_gather | solution.py:184
  817.8 40.6 %convert_reduce_fusion = (f32[4608]{0:T(1024)}, bf16[1536,4608]{1,0:T(8,128)(2,1)}) fusion(f32[1536,4608]{1,0:T(8,128)} %get-tuple-element.101, f32[4608]{0:T(1024)} %reshape.693, bf16[1536,1152]{1,0:T(8,128)(2,1)S(1)} %copy-done.69, bf16[1152,4608]{1,0:T(8,128)(2,1)} %all-gather.29.cloned.1.call-done), kind=kOutput, calls=%fused_computation.9 | convolution fusion | flops 16470241280 | bytes 56659968 | tf_op jit(solution)/shard_map/dot_general | solution.py:196
  858.4 27.8 fusion.119
  887.4 33.6 %convert_reduce_fusion.3 = (f32[1152]{0:T(1024)}, bf16[1536,1152]{1,0:T(8,128)(2,1)}, f32[1536,1152]{1,0:T(8,128)}, bf16[1536,1152]{1,0:T(8,128)(2,1)}, f32[1536,1152]{1,0:T(8,128)}) fusion(f32[1536,6912]{1,0:T(8,128)} %fusion.81, f32[1536]{0:T(1024)} %broadcast_multiply_fusion.2, f32[1536,1152]{1,0:T(8,128)} %copy-done.9, ...), kind=kOutput, calls=%fused_computation.82 | convolution fusion | flops 16339303424 | bytes 84968448 | tf_op jit(solution)/shard_map/dot_general | solution.py:32
  921.2 89.2 %all-gather.31.cloned.1.call-done = bf16[3072,1152]{1,0:T(8,128)(2,1)} async-done(((bf16[1536,1152]{1,0:T(8,128)(2,1)}), bf16[3072,1152]{1,0:T(8,128)(2,1)}) %all-gather.31.cloned.1.call-update) | async-done | bytes 7077904 | tf_op jit(solution)/shard_map/all_gather | solution.py:212
  1010.4 8.2 convolution_convert_fusion
  1019.9 9.7 fusion.116
  1029.7 12.7 multiply_reduce_fusion.5
  1042.4 12.6 multiply_reduce_fusion.4
  1055.0 29.3 multiply_convert_fusion.5
  1093.9 9.6 fusion.113
  1103.5 13.3 multiply_reduce_fusion.3
  1116.8 8.2 fusion.110
  1125.0 12.7 multiply_reduce_fusion.1
  1137.8 12.6 multiply_reduce_fusion
  1150.4 9.5 fusion.46
  1159.9 15.4 multiply_reduce_fusion.2
  1175.3 10.6 fusion.45
  1205.1 29.4 multiply_convert_fusion.3
  1249.2 29.1 multiply_convert_fusion.1
  1295.1 8.8 fusion.131
  1303.9 8.8 fusion.135
  1312.8 15.4 add_add_fusion
  1328.2 161.5 %reduce-scatter.28.cloned.1.call-done = f32[1536,1152]{1,0:T(8,128)} async-done(((f32[3072,1152]{1,0:T(8,128)}), f32[1536,1152]{1,0:T(8,128)}) %reduce-scatter.28.cloned.1.call-update) | async-done | bytes 7077904 | tf_op jit(solution)/shard_map/reduce_scatter | solution.py:271
  1500.7 12.5 fusion.31
  1513.1 8.6 multiply_dynamic-update-slice_fusion.1
  1539.8 20.0 fusion.80
  1559.8 22.9 fusion.142
  1584.7 22.6 fusion.141
  1612.4 11.8 fusion.140
  1624.3 10.4 fusion.139
  1635.0 11.6 fusion.137
  1646.7 10.5 fusion.138
  1657.6 16.4 fusion.89
  1674.0 145.9 %reduce-scatter.36.cloned.1.call-done = f32[1152,2304]{1,0:T(8,128)} async-done(((f32[1152,4608]{1,0:T(8,128)}), f32[1152,2304]{1,0:T(8,128)}) %reduce-scatter.36.cloned.1.call-update) | async-done | bytes 10616848 | tf_op jit(solution)/shard_map/reduce_scatter | solution.py:204
  1820.0 239.2 %reduce-scatter.32.cloned.1.call-done = f32[1152,2304]{1,0:T(8,128)} async-done(((f32[1152,4608]{1,0:T(8,128)}), f32[1152,2304]{1,0:T(8,128)}) %reduce-scatter.32.cloned.1.call-update) | async-done | bytes 10616848 | tf_op jit(solution)/shard_map/reduce_scatter | solution.py:203
  2059.3 17.4 reduce-scatter.40.cloned.1.call-done
  2078.4 35.2 %reduce-scatter.42.cloned.1.call-done = f32[2304,1]{1,0:T(8,128)} async-done(((f32[4608,1]{1,0:T(8,128)}), f32[2304,1]{1,0:T(8,128)}) %reduce-scatter.42.cloned.1.call-update) | async-done | bytes 9232
  2117.5 49.9 %all-reduce.4 = (f32[3456]{0:T(1024)}, f32[576]{0:T(1024)}, f32[576]{0:T(1024)}, f32[2,576]{1,0:T(2,128)S(1)}, f32[2304]{0:T(1024)}) all-reduce(f32[3456]{0:T(1024)S(1)} %reduce_sum.268, f32[576]{0:T(1024)S(1)} %reduce_sum.270, f32[576]{0:T(1024)} %reduce_sum.272, ...), channel_id=1, replica_groups=mesh['rows'=16,'heads'=2] {'rows'}, use_global_device_ids=true, to_apply=%region_33.34 | all-reduce | flops 8064 | bytes 64512 | tf_op jit(solution)/shard_map/psum | solution.py:325
  2167.5 16.8 fusion.136
  2191.0 59.1 %reduce-scatter.48.cloned.1.call-done = f32[72,576]{1,0:T(8,128)} async-done(((f32[1152,576]{1,0:T(8,128)}), f32[72,576]{1,0:T(8,128)}) %reduce-scatter.48.cloned.1.call-update) | async-done | bytes 165904
  2250.1 68.7 %reduce-scatter.44.cloned.1.call-done = f32[72,576]{1,0:T(8,128)} async-done(((f32[1152,576]{1,0:T(8,128)}), f32[72,576]{1,0:T(8,128)}) %reduce-scatter.44.cloned.1.call-update) | async-done | bytes 165904
  2318.8 68.9 %reduce-scatter.46.cloned.1.call-done = f32[72,576]{1,0:T(8,128)} async-done(((f32[1152,576]{1,0:T(8,128)}), f32[72,576]{1,0:T(8,128)}) %reduce-scatter.46.cloned.1.call-update) | async-done | bytes 165904
  2387.6 289.5 %all-reduce.7.cloned.1.call-done = f32[1152,3456]{1,0:T(8,128)} async-done(((f32[1152,3456]{1,0:T(8,128)}), f32[1152,3456]{1,0:T(8,128)}) %all-reduce.7.cloned.1.call-update) | async-done | bytes 15925264 | tf_op jit(solution)/shard_map/psum | solution.py:325
  2677.2 124.9 %reduce-scatter.38.cloned.1.call-done = f32[72,2304]{1,0:T(8,128)} async-done(((f32[1152,2304]{1,0:T(8,128)}), f32[72,2304]{1,0:T(8,128)}) %reduce-scatter.38.cloned.1.call-update) | async-done | bytes 663568 | tf_op jit(solution)/shard_map/reduce_scatter | solution.py:334
  2802.1 124.5 %reduce-scatter.34.cloned.1.call-done = f32[72,2304]{1,0:T(8,128)} async-done(((f32[1152,2304]{1,0:T(8,128)}), f32[72,2304]{1,0:T(8,128)}) %reduce-scatter.34.cloned.1.call-update) | async-done | bytes 663568 | tf_op jit(solution)/shard_map/reduce_scatter | solution.py:333
  2926.6 11.1 copy.82
  (441 shorter events, 236.0 us)
Async XLA Ops:
  7.2 62.6 %all-gather.19.cloned.1.call-start = ((), (), s32[]{:S(2)}) async-start(), calls=%async_computation.16 | async-start | bytes 1566720 | tf_op jit(solution)/shard_map/all_gather | solution.py:100
  8.8 142.0 %all-gather.13.cloned.1.call-start = ((), (), s32[]{:S(2)}) async-start(), calls=%async_computation.13 | async-start | bytes 10616832 | tf_op jit(solution)/shard_map/all_gather | solution.py:108
  12.3 16.1 copy-start.118
  28.4 21.7 copy-start.82
  28.5 21.7 copy-start.6
  59.4 132.9 %all-gather.17.cloned.1.call-start = ((), (), s32[]{:S(2)}) async-start(), calls=%async_computation.15 | async-start | bytes 1566720 | tf_op jit(solution)/shard_map/all_gather | solution.py:99
  60.2 198.8 %all-gather.15.cloned.1.call-start = ((), (), s32[]{:S(2)}) async-start(), calls=%async_computation.14 | async-start | bytes 1566720 | tf_op jit(solution)/shard_map/all_gather | solution.py:101
  60.9 257.5 %all-gather.21.cloned.1.call-start = ((), (), s32[]{:S(2)}) async-start(), calls=%async_computation.17 | async-start | bytes 1566720 | tf_op jit(solution)/shard_map/all_gather | solution.py:102
  61.7 271.1 %all-gather.23.cloned.1.call-start = ((), (), s32[]{:S(2)}) async-start(), calls=%async_computation.19 | async-start | bytes 5640192 | tf_op jit(solution)/shard_map/all_gather | solution.py:103
  62.5 328.0 %all-gather.27.cloned.1.call-start = ((), (), s32[]{:S(2)}) async-start(), calls=%async_computation.21 | async-start | bytes 5640192 | tf_op jit(solution)/shard_map/all_gather | solution.py:104
  63.3 489.6 %reduce-scatter.26.cloned.1.call-start = ((), (), s32[]{:S(2)}) async-start(), calls=%async_computation.18 | async-start | bytes 21233664 | tf_op jit(solution)/shard_map/reduce_scatter | solution.py:174
  159.0 33.4 %copy-start.121 = (f32[576]{0:T(1024)S(1)}, f32[576]{0:T(1024)}, u32[]{:S(2)}) copy-start(f32[576]{0:T(1024)} %param.29) | copy-start | bytes 6916
  159.3 51.6 %copy-start.16 = (bf16[1024,576]{0,1:T(8,128)(2,1)}, bf16[1024,576]{0,1:T(8,128)(2,1)S(1)}, u32[]{:S(2)}) copy-start(bf16[1024,576]{0,1:T(8,128)(2,1)S(1)} %get-tuple-element.52) | copy-start | bytes 3538948
  159.4 71.4 %copy-start.18 = (bf16[1024,576]{0,1:T(8,128)(2,1)}, bf16[1024,576]{0,1:T(8,128)(2,1)S(1)}, u32[]{:S(2)}) copy-start(bf16[1024,576]{0,1:T(8,128)(2,1)S(1)} %get-tuple-element.53) | copy-start | bytes 3538948
  159.4 90.3 %copy-start.20 = (bf16[1024,576]{0,1:T(8,128)(2,1)}, bf16[1024,576]{0,1:T(8,128)(2,1)S(1)}, u32[]{:S(2)}) copy-start(bf16[1024,576]{0,1:T(8,128)(2,1)S(1)} %get-tuple-element.54) | copy-start | bytes 3538948
  201.0 20.0 copy-start.55
  201.0 29.8 %copy-start.61 = (bf16[512,576]{0,1:T(8,128)(2,1)}, bf16[512,576]{0,1:T(8,128)(2,1)S(1)}, u32[]{:S(2)}) copy-start(bf16[512,576]{0,1:T(8,128)(2,1)S(1)} %get-tuple-element.49) | copy-start | bytes 1769476
  201.0 39.6 %copy-start.57 = (bf16[512,576]{0,1:T(8,128)(2,1)}, bf16[512,576]{0,1:T(8,128)(2,1)S(1)}, u32[]{:S(2)}) copy-start(bf16[512,576]{0,1:T(8,128)(2,1)S(1)} %get-tuple-element.50) | copy-start | bytes 1769476
  201.0 48.7 %copy-start.63 = (bf16[512,576]{0,1:T(8,128)(2,1)}, bf16[512,576]{0,1:T(8,128)(2,1)S(1)}, u32[]{:S(2)}) copy-start(bf16[512,576]{0,1:T(8,128)(2,1)S(1)} %get-tuple-element.51) | copy-start | bytes 1769476
  211.0 93.0 %copy-start.90 = (f32[8,512]{1,0:T(8,128)}, f32[8,512]{1,0:T(8,128)S(1)}, u32[]{:S(2)}) copy-start(f32[8,512]{1,0:T(8,128)S(1)} %log_add_fusion.1) | copy-start | bytes 49156
  258.9 18.7 copy-start.98
  269.2 19.1 slice-start.4
  269.2 19.1 slice-start.5
  269.2 19.1 slice-start.6
  288.4 15.6 slice-start
  329.7 223.3 %copy-start.7 = (bf16[1536,1152]{1,0:T(8,128)(2,1)S(1)}, bf16[1536,1152]{1,0:T(8,128)(2,1)}, u32[]{:S(2)}) copy-start(bf16[1536,1152]{1,0:T(8,128)(2,1)} %param.19) | copy-start | bytes 10616836
  329.7 223.3 %copy-start.111 = (f32[1152]{0:T(1024)S(1)}, f32[1152]{0:T(1024)}, u32[]{:S(2)}) copy-start(f32[1152]{0:T(1024)} %param.32) | copy-start | bytes 13828
  329.7 355.7 %all-gather.25.cloned.1.call-start = ((), (), s32[]{:S(2)}) async-start(), calls=%async_computation.20 | async-start | bytes 15925248 | tf_op jit(solution)/shard_map/all_gather | solution.py:183
  332.8 485.0 %all-gather.29.cloned.1.call-start = ((), (), s32[]{:S(2)}) async-start(), calls=%async_computation.22 | async-start | bytes 15925248 | tf_op jit(solution)/shard_map/all_gather | solution.py:184
  390.5 619.9 %all-gather.31.cloned.1.call-start = ((), (), s32[]{:S(2)}) async-start(), calls=%async_computation.23 | async-start | bytes 10616832 | tf_op jit(solution)/shard_map/all_gather | solution.py:212
  559.0 328.4 %copy-start.102 = (f32[1536]{0:T(1024)}, f32[1536]{0:T(1024)S(1)}, u32[]{:S(2)}) copy-start(f32[1536]{0:T(1024)S(1)} %broadcast_multiply_fusion.4) | copy-start | bytes 18436
  563.7 323.7 %copy-start.107 = (f32[1536]{0:T(1024)}, f32[1536]{0:T(1024)S(1)}, u32[]{:S(2)}) copy-start(f32[1536]{0:T(1024)S(1)} %add_rsqrt_fusion) | copy-start | bytes 18436
  685.5 132.4 %copy-start.69 = (bf16[1536,1152]{1,0:T(8,128)(2,1)S(1)}, bf16[1536,1152]{1,0:T(8,128)(2,1)}, u32[]{:S(2)}) copy-start(bf16[1536,1152]{1,0:T(8,128)(2,1)} %get-tuple-element.31) | copy-start | bytes 10616836
  858.4 29.0 copy-start.25
  921.0 568.8 %reduce-scatter.28.cloned.1.call-start = ((), (), s32[]{:S(2)}) async-start(), calls=%async_computation.24 | async-start | bytes 21233664 | tf_op jit(solution)/shard_map/reduce_scatter | solution.py:271
  1019.9 22.4 copy-start.73
  1055.0 29.3 copy-start.64
  1159.9 26.0 slice-start.8
  1159.9 26.0 slice-start.9
  1159.9 26.0 slice-start.10
  1205.1 29.4 copy-start.62
  1249.2 29.1 copy-start.60
  1294.0 18.7 copy-start.22
  1328.2 161.6 %copy-start.8 = (bf16[1536,1152]{1,0:T(8,128)(2,1)S(1)}, bf16[1536,1152]{1,0:T(8,128)(2,1)}, u32[]{:S(2)}) copy-start(bf16[1536,1152]{1,0:T(8,128)(2,1)} %param.19) | copy-start | bytes 10616836
  1328.2 161.6 %copy-start.86 = (f32[1536]{0:T(1024)S(1)}, f32[1536]{0:T(1024)}, u32[]{:S(2)}) copy-start(f32[1536]{0:T(1024)} %copy-done.85) | copy-start | bytes 18436
  1328.2 161.6 %copy-start.105 = (f32[1536]{0:T(1024)S(1)}, f32[1536]{0:T(1024)}, u32[]{:S(2)}) copy-start(f32[1536]{0:T(1024)} %copy-done.104) | copy-start | bytes 18436
  1328.2 329.4 %reduce-scatter.30.cloned.1.call-start = ((), (), s32[]{:S(2)}) async-start(), calls=%async_computation.25 | async-start | bytes 331776 | tf_op jit(solution)/shard_map/reduce_scatter | solution.py:304
  1496.9 31.4 %slice-start.12 = ((s8[7077888]{0:T(1024)(128)(4,1)}), s8[4194304]{0:T(1024)(128)(4,1)S(1)}, s32[]{:S(2)}) async-start(s8[7077888]{0:T(1024)(128)(4,1)} %bitcast.242), calls=%async_computation.49 | async-start | bytes 8388608
  1500.7 27.6 slice-start.13
  1539.8 20.1 copy-start.70
  1559.8 260.2 %reduce-scatter.36.cloned.1.call-start = ((), (), s32[]{:S(2)}) async-start(), calls=%async_computation.29 | async-start | bytes 31850496 | tf_op jit(solution)/shard_map/reduce_scatter | solution.py:204
  1582.7 476.5 %reduce-scatter.32.cloned.1.call-start = ((), (), s32[]{:S(2)}) async-start(), calls=%async_computation.27 | async-start | bytes 31850496 | tf_op jit(solution)/shard_map/reduce_scatter | solution.py:203
  1607.3 469.4 %reduce-scatter.40.cloned.1.call-start = ((), (), s32[]{:S(2)}) async-start(), calls=%async_computation.31 | async-start | bytes 884736
  1609.1 504.5 %reduce-scatter.42.cloned.1.call-start = ((), (), s32[]{:S(2)}) async-start(), calls=%async_computation.32 | async-start | bytes 3538944
  1612.2 578.8 %reduce-scatter.50.cloned.1.call-start = ((), (), s32[]{:S(2)}) async-start(), calls=%async_computation.36 | async-start | bytes 3133440
  1624.2 625.9 %reduce-scatter.48.cloned.1.call-start = ((), (), s32[]{:S(2)}) async-start(), calls=%async_computation.35 | async-start | bytes 3133440
  1634.7 684.1 %reduce-scatter.44.cloned.1.call-start = ((), (), s32[]{:S(2)}) async-start(), calls=%async_computation.33 | async-start | bytes 3133440
  1646.7 741.0 %reduce-scatter.46.cloned.1.call-start = ((), (), s32[]{:S(2)}) async-start(), calls=%async_computation.34 | async-start | bytes 3133440
  1657.3 1019.9 %all-reduce.7.cloned.1.call-start = ((), (), s32[]{:S(2)}) async-start(), calls=%async_computation.26 | async-start | bytes 31850496 | tf_op jit(solution)/shard_map/psum | solution.py:325
  1674.0 1128.1 %reduce-scatter.38.cloned.1.call-start = ((), (), s32[]{:S(2)}) async-start(), calls=%async_computation.30 | async-start | bytes 11280384 | tf_op jit(solution)/shard_map/reduce_scatter | solution.py:334
  1820.0 295.3 %copy-start.115 = (f32[8,72]{1,0:T(8,128)S(1)}, f32[8,72]{1,0:T(8,128)}, u32[]{:S(2)}) copy-start(f32[8,72]{1,0:T(8,128)} %get-tuple-element.32) | copy-start | bytes 6916
  1820.0 296.0 %copy-start.67 = (bf16[3072,8,72]{0,2,1:T(8,128)(2,1)S(1)}, bf16[3072,8,72]{0,2,1:T(8,128)(2,1)}, u32[]{:S(2)}) copy-start(bf16[3072,8,72]{0,2,1:T(8,128)(2,1)} %copy-done.66) | copy-start | bytes 10616836
  1820.0 1106.6 %reduce-scatter.34.cloned.1.call-start = ((), (), s32[]{:S(2)}) async-start(), calls=%async_computation.28 | async-start | bytes 11280384 | tf_op jit(solution)/shard_map/reduce_scatter | solution.py:333
  2167.5 22.9 copy-start.84
  (101 other events, 690.6 us)
Sparse Core Ops, SparseCore 0:
  10.7 39.9 all-gather.18
  59.6 91.1 all-gather.12
  153.5 38.7 all-gather.16
  194.9 38.1 all-gather.14
  235.7 38.2 all-gather.20
  276.6 56.1 all-gather.22
  335.5 54.9 all-gather.26
  393.4 159.5 reduce-scatter.25
  554.5 130.8 all-gather.24
  686.9 130.9 all-gather.28
  921.1 89.2 all-gather.30
  1328.3 161.4 reduce-scatter.27
  1559.9 11.1 reduce-scatter.29
  1582.9 237.0 reduce-scatter.35
  1822.2 237.0 reduce-scatter.31
  2061.4 15.2 reduce-scatter.39
  2078.9 34.6 reduce-scatter.41
  2118.0 63.2 reduce-scatter.49
  2185.8 64.2 reduce-scatter.47
  2254.4 64.2 reduce-scatter.43
  2323.3 64.3 reduce-scatter.45
  2392.1 285.0 all-reduce.6
  2681.8 120.2 reduce-scatter.37
  2806.6 119.9 reduce-scatter.33
where the time goes:
time: 2960 us; the launch traced here: 2940 us
  waiting for transfers between devices  1960 us (66%)
  matrix products  638 us (22%)
  other arithmetic  204 us (7%)
  blocking collectives  63.4 us (2%)
  local copies, waits for them, and re-layouts  60.6 us (2%)
    psum x1, waiting for transfers between devices, body(): lax.psum((grad_w_ada, grad_b_ada, grad_b_query, grad_b_value, grad_b_up,...  290 us
    unnamed x30, waiting for transfers between devices  250 us
    reduce_scatter x1, waiting for transfers between devices, body(): lax.psum_scatter(grad_up_all, 'heads', scatter_dimension=1, tiled=True)  239 us
    reduce_scatter x1, waiting for transfers between devices, body(): lax.psum_scatter(total + contract_last(grad_values, value_back), 'heads',...  162 us
    reduce_scatter x1, waiting for transfers between devices, body(): lax.psum_scatter(contract_last(attended, out_full), 'heads', scatter_dime...  156 us
    reduce_scatter x1, waiting for transfers between devices, body(): lax.psum_scatter(grad_down_all, 'heads', scatter_dimension=1, tiled=True)  146 us
    reduce_scatter x1, waiting for transfers between devices, body(): lax.psum_scatter(grad_w_down, 'rows', scatter_dimension=0, tiled=True)  125 us
    reduce_scatter x1, waiting for transfers between devices, body(): lax.psum_scatter(grad_w_up, 'rows', scatter_dimension=0, tiled=True)  124 us
  transfers between devices with their start and end apart: 24, of which 19 were waited for; matrix products, arithmetic and copies ran while one was open for 13% of the time, Pallas kernels for 0%

commit v1 on v0

--- a/solution.py
+++ b/solution.py
@@ -3,6 +3,8 @@
 import jax
 import jax.numpy as jnp
 from jax import lax
+from jax.experimental import pallas as pl
+from jax.experimental.pallas import tpu as pltpu
 from jax.sharding import PartitionSpec as P
 
 HEAD_DIM = 72
@@ -40,7 +42,7 @@
     )
 
 
-def body(
+def general_body(
     tokens,
     condition,
     segment_ids,
@@ -353,7 +355,830 @@
     )
 
 
+LOG2E = 1.4426950408889634
+GELU_SLOPE = 0.7978845608028654
+GELU_CUBE = 0.044715
+BF = jnp.bfloat16
+F32 = jnp.float32
+MIB = 2**20
+
+
+def rows_by_columns(left, right):
+    return jnp.dot(left, right, preferred_element_type=F32)
+
+
+def shape(dims, dtype):
+    return jax.ShapeDtypeStruct(dims, dtype)
+
+
+def params(mib=56):
+    return pltpu.CompilerParams(vmem_limit_bytes=mib * MIB)
+
+
+def cost(flops, bytes_accessed, transcendentals=0):
+    return pl.CostEstimate(
+        flops=int(flops), bytes_accessed=int(bytes_accessed), transcendentals=int(transcendentals)
+    )
+
+
+def three_parts(values):
+    high = lax.reduce_precision(values, 8, 7)
+    rest = values - high
+    middle = lax.reduce_precision(rest, 8, 7)
+    return jnp.concatenate([high, middle, rest - middle], axis=-2).astype(BF)
+
+
+def norm_kernel(side, tok_ref, hot_ref, parts_ref, perm_ref, h_ref, ht_ref):
+    width = tok_ref.shape[1]
+    normed, _ = layer_norm(tok_ref[...].astype(F32))
+    mod = rows_by_columns(hot_ref[...], parts_ref[0, :, : 2 * width])
+    hidden = (normed * (1.0 + mod[:, width:]) + mod[:, :width]).astype(BF)
+    h_ref[...] = hidden
+    ht_ref[...] = contract_last(perm_ref[...], hidden).astype(BF)
+
+
+def first_norm(side, tokens, hot, parts, perm, block):
+    rows, width = tokens.shape
+    return pl.pallas_call(
+        norm_kernel,
+        grid_spec=pltpu.PrefetchScalarGridSpec(
+            num_scalar_prefetch=1,
+            grid=(rows // block,),
+            in_specs=[
+                pl.BlockSpec((block, width), lambda i, y: ((i + y[0]) % 3, 0)),
+                pl.BlockSpec((block, hot.shape[1]), lambda i, y: (i, 0)),
+                pl.BlockSpec((1,) + parts.shape[1:], lambda i, y: (0, 0, 0)),
+                pl.BlockSpec(perm.shape, lambda i, y: (0, 0)),
+            ],
+            out_specs=[
+                pl.BlockSpec((block, width), lambda i, y: (i, 0)),
+                pl.BlockSpec((width, block), lambda i, y: (0, i)),
+            ],
+        ),
+        out_shape=[shape((rows, width), BF), shape((width, rows), BF)],
+        compiler_params=params(),
+        cost_estimate=cost(2 * rows * width * (width + 512), rows * width * 6),
+    )(side, tokens, hot, parts, perm)
+
+
+def project_kernel(side, h_ref, w_ref, bias_ref, out_ref):
+    width = out_ref.shape[2]
+    out_ref[0] = (rows_by_columns(h_ref[...], w_ref[0, :, :width]) + bias_ref[0]).astype(BF)
+
+
+def project(side, hidden, weights, bias, block):
+    rows, width = hidden.shape
+    cols = bias.shape[2]
+    pick = lambda a, y: a + y[0] - 2 * a * y[0]
+    return pl.pallas_call(
+        project_kernel,
+        grid_spec=pltpu.PrefetchScalarGridSpec(
+            num_scalar_prefetch=1,
+            grid=(2, rows // block),
+            in_specs=[
+                pl.BlockSpec((block, width), lambda a, i, y: (i, 0)),
+                pl.BlockSpec((1,) + weights.shape[1:], lambda a, i, y: (pick(a, y), 0, 0)),
+                pl.BlockSpec((1, 1, cols), lambda a, i, y: (pick(a, y), 0, 0)),
+            ],
+            out_specs=pl.BlockSpec((1, block, cols), lambda a, i, y: (a, i, 0)),
+        ),
+        out_shape=shape((2, rows, cols), BF),
+        compiler_params=params(),
+        cost_estimate=cost(4 * rows * width * cols, 4 * rows * cols + 4 * width * cols),
+    )(side, hidden, weights, bias)
+
+
+def attend_kernel(heads, block, q_ref, kv_ref, code_ref, seg_ref, o_ref, keys, values, bias):
+    i = pl.program_id(1)
+    width = heads * HEAD_DIM
+
+    @pl.when(i == 0)
+    def _():
+        for h in range(heads):
+            at = h * HEAD_DIM
+            keys[h] = kv_ref[0, :, width + at : width + at + HEAD_DIM]
+            values[h] = kv_ref[0, :, 2 * width + at : 2 * width + at + HEAD_DIM]
+
+    for t in range(block // TILE):
+        code = code_ref[pl.ds(i * (block // TILE) + t, 1), :]
+        seg = seg_ref[pl.ds(i * block + t * TILE, TILE), :]
+        bias[t * TILE : (t + 1) * TILE, :] = jnp.where(code == seg, 0.0, MASKED_SCORE)
+    parts = []
+    for h in range(heads):
+        query = q_ref[0, :, h * HEAD_DIM : (h + 1) * HEAD_DIM]
+        scores = contract_last(query, keys[h]) * (HEAD_DIM**-0.5 * LOG2E) + bias[...]
+        powers = jnp.exp2(scores - jnp.max(scores, axis=1, keepdims=True))
+        probs = powers * (1.0 / jnp.sum(powers, axis=1, keepdims=True))
+        parts.append(rows_by_columns(probs.astype(BF), values[h]).astype(BF))
+    o_ref[0] = jnp.concatenate(parts, axis=1)
+
+
+def attend(qkv, code, seg, block):
+    groups, _, cols = qkv.shape
+    length = code.shape[1]
+    heads = cols // (3 * HEAD_DIM)
+    width = heads * HEAD_DIM
+    return pl.pallas_call(
+        partial(attend_kernel, heads, block),
+        grid=(groups, length // block),
+        in_specs=[
+            pl.BlockSpec((1, block, cols), lambda a, i: (a, i, 0)),
+            pl.BlockSpec((1, length, cols), lambda a, i: (a, 0, 0)),
+            pl.BlockSpec(code.shape, lambda a, i: (0, 0)),
+            pl.BlockSpec(seg.shape, lambda a, i: (0, 0)),
+        ],
+        out_specs=pl.BlockSpec((1, block, width), lambda a, i: (a, i, 0)),
+        out_shape=shape((groups, length, width), BF),
+        scratch_shapes=[
+            pltpu.VMEM((heads, length, HEAD_DIM), BF),
+            pltpu.VMEM((heads, length, HEAD_DIM), BF),
+            pltpu.VMEM((block, length), F32),
+        ],
+        compiler_params=params(),
+        cost_estimate=cost(
+            groups * 16 * length * length * width,
+            groups * length * cols * 4,
+            groups * heads * length * length,
+        ),
+    )(qkv, qkv, code, seg)
+
+
+def attend_back_kernel(
+    heads, block, qkv_ref, do_ref, code_ref, seg_ref, out_ref, keys, values, turned, dk, dv, bias
+):
+    i = pl.program_id(1)
+    width = heads * HEAD_DIM
+    scaling = HEAD_DIM**-0.5
+
+    @pl.when(i == 0)
+    def _():
+        for h in range(heads):
+            at = h * HEAD_DIM
+            key = qkv_ref[0, :, width + at : width + at + HEAD_DIM]
+            keys[h] = key
+            turned[h] = key.astype(F32).T.astype(BF)
+            values[h] = qkv_ref[0, :, 2 * width + at : 2 * width + at + HEAD_DIM]
+        dk[...] = jnp.zeros_like(dk)
+        dv[...] = jnp.zeros_like(dv)
+
+    for t in range(block // TILE):
+        tile = i * (block // TILE) + t
+        seg = seg_ref[pl.ds(tile, 1), :]
+        code = code_ref[pl.ds(tile, 1)].reshape(code_ref.shape[1:])
+        bias[:, t * TILE : (t + 1) * TILE] = jnp.where(code == seg, 0.0, MASKED_SCORE)
+    rows = pl.ds(pl.multiple_of(i * block, block), block)
+    parts = []
+    for h in range(heads):
+        query = qkv_ref[0, rows, h * HEAD_DIM : (h + 1) * HEAD_DIM]
+        grad = do_ref[0, rows, h * HEAD_DIM : (h + 1) * HEAD_DIM]
+        scores = contract_last(keys[h], query) * (scaling * LOG2E) + bias[...]
+        powers = jnp.exp2(scores - jnp.max(scores, axis=0, keepdims=True))
+        probs = powers * (1.0 / jnp.sum(powers, axis=0, keepdims=True))
+        grad_probs = contract_last(values[h], grad)
+        centre = jnp.sum(probs * grad_probs, axis=0, keepdims=True)
+        grad_scores = (probs * (grad_probs - centre)).astype(BF)
+        dv[h] += rows_by_columns(probs.astype(BF), grad)
+        dk[h] += rows_by_columns(grad_scores, query)
+        parts.append((rows_by_columns(turned[h], grad_scores) * scaling).T.astype(BF))
+    out_ref[0, rows, :width] = jnp.concatenate(parts, axis=1)
+
+    @pl.when(i == pl.num_programs(1) - 1)
+    def _():
+        out_ref[0, :, width:] = jnp.concatenate(
+            [(dk[h] * scaling).astype(BF) for h in range(heads)]
+            + [dv[h].astype(BF) for h in range(heads)],
+            axis=1,
+        )
+
+
+def attend_back(qkv, grad, code, seg, block):
+    groups, _, cols = qkv.shape
+    length = code.shape[1]
+    heads = cols // (3 * HEAD_DIM)
+    width = heads * HEAD_DIM
+    return pl.pallas_call(
+        partial(attend_back_kernel, heads, block),
+        grid=(groups, length // block),
+        in_specs=[
+            pl.BlockSpec((1, length, cols), lambda a, i: (a, 0, 0)),
+            pl.BlockSpec((1, length, width), lambda a, i: (a, 0, 0)),
+            pl.BlockSpec(code.shape, lambda a, i: (0, 0, 0)),
+            pl.BlockSpec(seg.shape, lambda a, i: (0, 0)),
+        ],
+        out_specs=pl.BlockSpec((1, length, cols), lambda a, i: (a, 0, 0)),
+        out_shape=shape((groups, length, cols), BF),
+        scratch_shapes=[
+            pltpu.VMEM((heads, length, HEAD_DIM), BF),
+            pltpu.VMEM((heads, length, HEAD_DIM), BF),
+            pltpu.VMEM((heads, HEAD_DIM, length), BF),
+            pltpu.VMEM((heads, length, HEAD_DIM), F32),
+            pltpu.VMEM((heads, length, HEAD_DIM), F32),
+            pltpu.VMEM((length, block), F32),
+        ],
+        compiler_params=params(58),
+        cost_estimate=cost(
+            groups * 32 * length * length * width,
+            groups * length * cols * 8,
+            groups * heads * length * length,
+        ),
+    )(qkv, grad, code, seg)
+
+
+def middle_kernel(
+    side, tok_ref, dy_ref, full_ref, half_ref, w_own, w_other, b_ref, hot_ref, parts_ref, perm_ref,
+    branch_ref, h_ref, g_ref, ht_ref, gt_ref, gb_ref,
+):
+    i = pl.program_id(0)
+    width = tok_ref.shape[1]
+    att = jnp.where(i < 2, full_ref[...], half_ref[...])
+    branch = contract_last(att[0], w_own[0]) + contract_last(att[1], w_other[0]) + b_ref[...]
+    branch_ref[...] = branch
+    hot = hot_ref[...]
+    gate = rows_by_columns(hot, parts_ref[0, :, 2 * width :])
+    mod = rows_by_columns(hot, parts_ref[1])
+    normed, _ = layer_norm(tok_ref[...].astype(F32) + gate * branch)
+    hidden = (normed * (1.0 + mod[:, width : 2 * width]) + mod[:, :width]).astype(BF)
+    grad = (dy_ref[...].astype(F32) * mod[:, 2 * width :]).astype(BF)
+    h_ref[...] = hidden
+    g_ref[...] = grad
+    ht_ref[...] = contract_last(perm_ref[...], hidden).astype(BF)
+    gt_ref[...] = contract_last(perm_ref[...], grad).astype(BF)
+    total = jnp.sum(grad.astype(F32), axis=0, keepdims=True)
+
+    @pl.when(i == 0)
+    def _():
+        gb_ref[...] = total
+
+    @pl.when(i != 0)
+    def _():
+        gb_ref[...] += total
+
+
+def middle_part(side, tokens, cotangent, full, half, w_out, b_out, hot, parts, perm, block):
+    rows, width = tokens.shape
+    cols = full.shape[2]
+    spec = lambda dims: pl.BlockSpec(dims, lambda i, y: (0,) * len(dims))
+    placed = pl.BlockSpec((block, width), lambda i, y: ((i + y[0]) % 3, 0))
+    plain = pl.BlockSpec((block, width), lambda i, y: (i, 0))
+    turned = pl.BlockSpec((width, block), lambda i, y: (0, i))
+    return pl.pallas_call(
+        middle_kernel,
+        grid_spec=pltpu.PrefetchScalarGridSpec(
+            num_scalar_prefetch=1,
+            grid=(rows // block,),
+            in_specs=[
+                placed,
+                placed,
+                pl.BlockSpec((2, block, cols), lambda i, y: (0, jnp.minimum(i, 1), 0)),
+                spec((2, block, cols)),
+                pl.BlockSpec((1, width, cols), lambda i, y: (y[0], 0, 0)),
+                pl.BlockSpec((1, width, cols), lambda i, y: (1 - y[0], 0, 0)),
+                spec((1, width)),
+                pl.BlockSpec((block, hot.shape[1]), lambda i, y: (i, 0)),
+                spec(parts.shape),
+                spec(perm.shape),
+            ],
+            out_specs=[plain, plain, plain, turned, turned, spec((1, width))],
+        ),
+        out_shape=[
+            shape((rows, width), F32),
+            shape((rows, width), BF),
+            shape((rows, width), BF),
+            shape((width, rows), BF),
+            shape((width, rows), BF),
+            shape((1, width), F32),
+        ],
+        compiler_params=params(),
+        cost_estimate=cost(2 * rows * width * (3 * width + 1024), rows * width * 22),
+    )(side, tokens, cotangent, full, half, w_out, w_out, b_out, hot, parts, perm)
+
+
+def feed_kernel(
+    chunk, pick, h_ref, g_ref, ht_ref, gt_ref, up_ref, down_ref, bias_ref,
+    branch_ref, back_ref, mine_ref, theirs_ref, gb_ref, act, pre,
+):
+    j = pl.program_id(0)
+    rows = h_ref.shape[0]
+    half = ht_ref.shape[0] // 2
+    up = up_ref[0]
+    down = down_ref[0]
+    total = jnp.zeros(gb_ref.shape, F32)
+    for start in range(0, rows, chunk):
+        at = slice(start, start + chunk)
+        u = rows_by_columns(h_ref[at], up) + bias_ref[0]
+        grad = rows_by_columns(g_ref[at], down)
+        cube = GELU_CUBE * u * u
+        bent = jnp.tanh(GELU_SLOPE * (u + cube * u))
+        part = 0.5 * (1.0 + bent)
+        slope = part + 0.5 * u * (1.0 - bent * bent) * (GELU_SLOPE * (1.0 + 3.0 * cube))
+        low = (u * part).astype(BF)
+        back = (grad * slope).astype(BF)
+        act[at] = low
+        pre[at] = back
+        total += jnp.sum(back.astype(F32), axis=0, keepdims=True)
+        branch_part = contract_last(low, down)
+        back_part = contract_last(back, up)
+
+        @pl.when(j == 0)
+        def _():
+            branch_ref[at] = branch_part
+            back_ref[at] = back_part
+
+        @pl.when(j != 0)
+        def _():
+            branch_ref[at] += branch_part
+            back_ref[at] += back_part
+
+    gb_ref[...] = total
+    mine_ref[0] = rows_by_columns(ht_ref[:half], pre[...])
+    theirs_ref[0] = rows_by_columns(ht_ref[half:], pre[...]).astype(BF)
+    mine_ref[1] = rows_by_columns(gt_ref[:half], act[...])
+    theirs_ref[1] = rows_by_columns(gt_ref[half:], act[...]).astype(BF)
+
+
+def feed(pick, hidden, grad, hidden_turned, grad_turned, up, down, bias, chunk, cols):
+    rows, width = hidden.shape
+    units = up.shape[2]
+    half = width // 2
+    whole = lambda dims: pl.BlockSpec(dims, lambda j, y: (0, 0), pipeline_mode=pl.Buffered(1))
+    columns = pl.BlockSpec((1, width, cols), lambda j, y: (y[0], 0, j))
+    return pl.pallas_call(
+        partial(feed_kernel, chunk),
+        grid_spec=pltpu.PrefetchScalarGridSpec(
+            num_scalar_prefetch=1,
+            grid=(units // cols,),
+            in_specs=[
+                whole((rows, width)),
+                whole((rows, width)),
+                whole((width, rows)),
+                whole((width, rows)),
+                columns,
+                columns,
+                pl.BlockSpec((1, 1, cols), lambda j, y: (y[0], 0, j)),
+            ],
+            out_specs=[
+                whole((rows, width)),
+                whole((rows, width)),
+                pl.BlockSpec((2, half, cols), lambda j, y: (0, 0, j)),
+                pl.BlockSpec((2, half, cols), lambda j, y: (0, 0, j)),
+                pl.BlockSpec((1, cols), lambda j, y: (0, j)),
+            ],
+            scratch_shapes=[pltpu.VMEM((rows, cols), BF), pltpu.VMEM((rows, cols), BF)],
+        ),
+        out_shape=[
+            shape((rows, width), F32),
+            shape((rows, width), F32),
+            shape((2, half, units), F32),
+            shape((2, half, units), BF),
+            shape((1, units), F32),
+        ],
+        compiler_params=params(60),
+        cost_estimate=cost(
+            12 * rows * width * units, rows * width * 16 + width * units * 10, rows * units
+        ),
+    )(pick, hidden, grad, hidden_turned, grad_turned, up, down, bias)
+
+
+def image_sums(hot_turned, values):
+    high = values.astype(BF)
+    low = (values - high.astype(F32)).astype(BF)
+    return rows_by_columns(hot_turned, high) + rows_by_columns(hot_turned, low)
+
+
+def add_up(ref, value):
+    @pl.when(pl.program_id(0) == 0)
+    def _():
+        ref[...] = value
+
+    @pl.when(pl.program_id(0) != 0)
+    def _():
+        ref[...] += value
+
+
+def back_two_kernel(
+    side, tok_ref, dy_ref, branch_ref, two_a, two_b, b_ref, back_a, back_b, w_own, w_other, hot_ref,
+    turn_ref, parts_ref, perm_ref, out_ref, middle_ref, gt_ref, att_ref, sums_ref, gb_ref,
+):
+    width = tok_ref.shape[1]
+    hot = hot_ref[...]
+    turn = turn_ref[...]
+    gate = rows_by_columns(hot, parts_ref[0, :, 2 * width :])
+    mod = rows_by_columns(hot, parts_ref[1])
+    branch = branch_ref[...]
+    middle = tok_ref[...].astype(F32) + gate * branch
+    branch_two = two_a[...] + two_b[...] + b_ref[...]
+    grad_hidden = back_a[...] + back_b[...]
+    dy = dy_ref[...].astype(F32)
+    out_ref[...] = (middle + mod[:, 2 * width :] * branch_two).astype(BF)
+    normed, inverse = layer_norm(middle)
+    grad_middle = dy + norm_back(normed, inverse, grad_hidden * (1.0 + mod[:, width : 2 * width]))
+    middle_ref[...] = grad_middle
+    grad = (grad_middle * gate).astype(BF)
+    gt_ref[...] = contract_last(perm_ref[...], grad).astype(BF)
+    att_ref[0] = rows_by_columns(grad, w_own[0]).astype(BF)
+    att_ref[1] = rows_by_columns(grad, w_other[0]).astype(BF)
+    sums = [
+        image_sums(turn, grad_middle * branch),
+        image_sums(turn, grad_hidden),
+        image_sums(turn, grad_hidden * normed),
+        image_sums(turn, dy * branch_two),
+    ]
+    add_up(sums_ref, jnp.stack(sums, axis=0))
+    add_up(gb_ref, jnp.sum(grad.astype(F32), axis=0, keepdims=True))
+
+
+def back_two(
+    side, tokens, cotangent, branch, two_a, two_b, b_down, back_a, back_b, w_out, hot, turn, parts, perm,
+    block, images,
+):
+    rows, width = tokens.shape
+    cols = w_out.shape[2]
+    per = rows // 3 // block
+    spec = lambda dims: pl.BlockSpec(dims, lambda i, y: (0,) * len(dims))
+    placed = pl.BlockSpec(
+        (block, width), lambda i, y: (((i // per + y[0]) % 3) * per + i % per, 0)
+    )
+    plain = pl.BlockSpec((block, width), lambda i, y: (i, 0))
+    return pl.pallas_call(
+        back_two_kernel,
+        grid_spec=pltpu.PrefetchScalarGridSpec(
+            num_scalar_prefetch=1,
+            grid=(rows // block,),
+            in_specs=[
+                placed,
+                placed,
+                plain,
+                plain,
+                plain,
+                spec((1, width)),
+                plain,
+                plain,
+                pl.BlockSpec((1, width, cols), lambda i, y: (y[0], 0, 0)),
+                pl.BlockSpec((1, width, cols), lambda i, y: (1 - y[0], 0, 0)),
+                pl.BlockSpec((block, hot.shape[1]), lambda i, y: (i, 0)),
+                pl.BlockSpec((images, block), lambda i, y: (0, i)),
+                spec(parts.shape),
+                spec(perm.shape),
+            ],
+            out_specs=[
+                placed,
+                plain,
+                pl.BlockSpec((width, block), lambda i, y: (0, i)),
+                pl.BlockSpec((2, block, cols), lambda i, y: (0, i, 0)),
+                spec((4, images, width)),
+                spec((1, width)),
+            ],
+        ),
+        out_shape=[
+            shape((rows, width), BF),
+            shape((rows, width), F32),
+            shape((width, rows), BF),
+            shape((2, rows, cols), BF),
+            shape((4, images, width), F32),
+            shape((1, width), F32),
+        ],
+        compiler_params=params(),
+        cost_estimate=cost(2 * rows * width * (3 * width + 1024), rows * width * 34),
+    )(side, tokens, cotangent, branch, two_a, two_b, b_down, back_a, back_b, w_out, w_out, hot, turn, parts, perm)
+
+
+def outer_kernel(ht_ref, full_ref, half_ref, mine_ref, theirs_ref, sums_ref):
+    length = full_ref.shape[1]
+    side = mine_ref.shape[1]
+    full = full_ref[0]
+    rest = half_ref[0]
+
+    def product(start):
+        at = slice(start, start + side)
+        return rows_by_columns(ht_ref[at, :length], full) + rows_by_columns(
+            ht_ref[at, length:], rest
+        )
+
+    mine_ref[0] = product(0)
+    theirs_ref[0] = product(side).astype(BF)
+    sums_ref[0] = jnp.sum(full.astype(F32), axis=0, keepdims=True) + jnp.sum(
+        rest.astype(F32), axis=0, keepdims=True
+    )
+
+
+def outer(turned, full, half):
+    width, rows = turned.shape
+    _, length, cols = full.shape
+    side = width // 2
+    block = pl.BlockSpec((1, side, cols), lambda a: (a, 0, 0))
+    return pl.pallas_call(
+        outer_kernel,
+        grid=(2,),
+        in_specs=[
+            pl.BlockSpec((width, rows), lambda a: (0, 0)),
+            pl.BlockSpec((1, length, cols), lambda a: (a, 0, 0)),
+            pl.BlockSpec((1, half.shape[1], cols), lambda a: (a, 0, 0)),
+        ],
+        out_specs=[block, block, pl.BlockSpec((1, 1, cols), lambda a: (a, 0, 0))],
+        out_shape=[
+            shape((2, side, cols), F32),
+            shape((2, side, cols), BF),
+            shape((2, 1, cols), F32),
+        ],
+        compiler_params=params(60),
+        cost_estimate=cost(4 * rows * width * cols, rows * width * 2 + rows * cols * 4),
+    )(turned, full, half)
+
+
+def back_one_kernel(
+    side, full_ref, half_ref, w_own, w_other, tok_ref, middle_ref, hot_ref, turn_ref, parts_ref,
+    out_ref, sums_ref,
+):
+    i = pl.program_id(0)
+    width = tok_ref.shape[1]
+    cols = full_ref.shape[2]
+    scale = rows_by_columns(hot_ref[...], parts_ref[0, :, width : 2 * width])
+    grads = jnp.where(i < 2 * pl.num_programs(0) // 3, full_ref[...], half_ref[...])
+    grad_hidden = contract_last(grads[0], w_own[0, :, :cols]) + contract_last(
+        grads[1], w_other[0, :, :cols]
+    )
+    normed, inverse = layer_norm(tok_ref[...].astype(F32))
+    out_ref[...] = middle_ref[...] + norm_back(normed, inverse, grad_hidden * (1.0 + scale))
+    turn = turn_ref[...]
+    sums = [image_sums(turn, grad_hidden), image_sums(turn, grad_hidden * normed)]
+    add_up(sums_ref, jnp.stack(sums, axis=0))
+
+
+def back_one(side, full, half, weights, tokens, middle, hot, turn, parts, block, images):
+    rows, width = tokens.shape
+    cols = full.shape[2]
+    per = rows // 3 // block
+    spec = lambda dims: pl.BlockSpec(dims, lambda i, y: (0,) * len(dims))
+    once = pl.Buffered(1)
+    placed = pl.BlockSpec(
+        (block, width), lambda i, y: (((i // per + y[0]) % 3) * per + i % per, 0)
+    )
+    return pl.pallas_call(
+        back_one_kernel,
+        grid_spec=pltpu.PrefetchScalarGridSpec(
+            num_scalar_prefetch=1,
+            grid=(rows // block,),
+            in_specs=[
+                pl.BlockSpec((2, block, cols), lambda i, y: (0, jnp.minimum(i, 2 * per - 1), 0)),
+                pl.BlockSpec((2, block, cols), lambda i, y: (0, jnp.maximum(i - 2 * per, 0), 0)),
+                pl.BlockSpec(
+                    (1,) + weights.shape[1:], lambda i, y: (y[0], 0, 0), pipeline_mode=once
+                ),
+                pl.BlockSpec(
+                    (1,) + weights.shape[1:], lambda i, y: (1 - y[0], 0, 0), pipeline_mode=once
+                ),
+                placed,
+                pl.BlockSpec((block, width), lambda i, y: (i, 0)),
+                pl.BlockSpec((block, hot.shape[1]), lambda i, y: (i, 0)),
+                pl.BlockSpec((images, block), lambda i, y: (0, i)),
+                spec(parts.shape),
+            ],
+            out_specs=[placed, spec((2, images, width))],
+        ),
+        out_shape=[shape((rows, width), F32), shape((2, images, width), F32)],
+        compiler_params=params(),
+        cost_estimate=cost(4 * rows * width * cols, rows * width * 10 + rows * cols * 4),
+    )(side, full, half, weights, weights, tokens, middle, hot, turn, parts)
+
+
+def fast_body(mesh):
+    ring = mesh.shape["rows"]
+    both = ("rows", "heads")
+
+    def moves(row_of, other_heads):
+        pairs = []
+        for r in range(ring):
+            for y in range(2):
+                pairs.append((2 * r + y, 2 * row_of(r) + (1 - y if other_heads else y)))
+        return pairs
+
+    to_core = moves(lambda r: r ^ 1, False)
+    to_heads = moves(lambda r: r, True)
+    to_x = moves(lambda r: r ^ 2, False)
+    to_corner = moves(lambda r: r ^ 2, True)
+    levels = ring // 4
+    to_level = [moves(lambda r, k=k: (r + 4 * k) % ring, False) for k in range(levels)]
+
+    def send(values, pairs):
+        return lax.ppermute(values, both, pairs)
+
+    def body(
+        tokens,
+        condition,
+        segment_ids,
+        tile_mask,
+        image_index,
+        w_ada,
+        b_ada,
+        w_query,
+        w_key,
+        w_value,
+        b_query,
+        b_value,
+        w_out,
+        b_out,
+        w_up,
+        b_up,
+        w_down,
+        b_down,
+        cotangent,
+    ):
+        y = lax.axis_index("heads")
+        r = lax.axis_index("rows")
+        rows, width = tokens.shape
+        length = segment_ids.shape[1]
+        third = rows // 3
+        images = condition.shape[0]
+        side = y.reshape(1)
+        units = w_up.shape[1]
+        cols = w_query.shape[1]
+
+        attention_shard = jnp.concatenate([w_query, w_key, w_value, w_out], axis=1).astype(BF)
+        gather = lambda v: lax.all_gather(v, ("heads", "rows"), axis=0, tiled=True).reshape(
+            2, width, v.shape[1]
+        )
+        attention_weights = gather(attention_shard)
+        up = gather(w_up.astype(BF))
+        down = gather(w_down.astype(BF))
+        all_conditions = lax.all_gather(condition, "rows", axis=0, tiled=True)
+
+        cond = condition.astype(F32)
+        mod_cols = jnp.dot(jax.nn.silu(cond), w_ada, precision=PRECISE) + b_ada
+        biases = jnp.concatenate([b_up, b_query, b_value])[None]
+        spread = lax.all_gather(jnp.concatenate([mod_cols, biases], axis=0)[None], "heads", axis=0, tiled=True)
+        parts = three_parts(spread[:, :images])
+        up_bias = spread[:, images:, :units]
+        qkv_bias = jnp.concatenate(
+            [
+                spread[:, images:, units : units + cols],
+                jnp.zeros((2, 1, cols), F32),
+                spread[:, images:, units + cols :],
+            ],
+            axis=2,
+        )
+
+        tile_of = jnp.arange(length, dtype=jnp.int32) // TILE
+        tiles = length // TILE
+
+        def pattern(seg, tiles_on):
+            on = (tiles_on > 0) | jnp.eye(tiles, dtype=bool)
+            code = jnp.where(jnp.repeat(on, TILE, axis=1), seg[None, :], -1)
+            return (code, seg[:, None]), (code[:, :, None], seg.reshape(tiles, TILE))
+
+        seg_full = lax.dynamic_index_in_dim(segment_ids, 2 * y, 0, keepdims=False)
+        tile_full = lax.dynamic_index_in_dim(tile_mask, 2 * y, 0, keepdims=False)
+        seg_half = jnp.where(y == 0, segment_ids[1], jnp.roll(segment_ids[1], -third))
+        shift = third // TILE
+        tile_half = jnp.where(
+            y == 0, tile_mask[1], jnp.roll(tile_mask[1], (-shift, -shift), axis=(0, 1))
+        )
+        full_on, full_back_on = pattern(seg_full, tile_full)
+        half_on, half_back_on = pattern(seg_half, tile_half)
+
+        def image_of(seg, index):
+            slots = jnp.arange(index.shape[0], dtype=jnp.int32)
+            return jnp.sum(jnp.where(seg[:, None] == slots[None, :], index[None, :], 0), axis=1)
+
+        own_image = jnp.concatenate(
+            [
+                image_of(seg_full, lax.dynamic_index_in_dim(image_index, 2 * y, 0, keepdims=False)),
+                image_of(seg_half[:third], image_index[1]),
+            ]
+        )
+        chosen = jnp.arange(images, dtype=jnp.int32)
+        hot = (own_image[:, None] == jnp.tile(chosen, 3)[None, :]).astype(BF)
+        turn = (chosen[:, None] == own_image[None, :]).astype(BF)
+
+        order = jnp.arange(ring, dtype=jnp.int32)
+        core_of, x_of, level_of = order // (ring // 2), (order // levels) % 2, order % levels
+        owner = ((r // 4 + level_of) % levels) * 4 + ((r // 2 % 2) ^ x_of) * 2 + ((r % 2) ^ core_of)
+        piece = width // ring
+        feature = (owner[:, None] * piece + jnp.arange(piece, dtype=jnp.int32)[None, :]).reshape(-1)
+        perm = (feature[:, None] == jnp.arange(width, dtype=jnp.int32)[None, :]).astype(BF)
+
+        hidden_one, hidden_one_turned = first_norm(side, tokens, hot, parts, perm, third)
+        qkv = project(side, hidden_one, attention_weights, qkv_bias, third)
+        qkv_got = send(qkv[1, 2 * third :], to_heads)
+        attended_full = attend(qkv, *full_on, third)
+        qkv_shared = jnp.concatenate([qkv[0, 2 * third :], qkv_got], axis=0)[None]
+        attended_shared = attend(qkv_shared, *half_on, third)
+        attended_got = send(attended_shared[0, third:], to_heads)
+        attended_half = jnp.stack([attended_shared[0, :third], attended_got])
+        w_out_all = attention_weights[:, :, 3 * cols :]
+        branch_one, hidden_two, grad_two, hidden_two_turned, grad_two_turned, grad_b_down = middle_part(
+            side, tokens, cotangent, attended_full, attended_half, w_out_all, b_out[None], hot, parts, perm, third
+        )
+
+        feed_args = (hidden_two, grad_two, hidden_two_turned, grad_two_turned, up, down, up_bias)
+        two_b, back_b, feed_mine_b, feed_theirs_b, grad_b_up_b = feed(1 - side, *feed_args, third, 768)
+        two_a, back_a, feed_mine_a, feed_theirs_a, grad_b_up_a = feed(side, *feed_args, third, 768)
+
+        def over_cores(mine, theirs):
+            return mine + send(theirs, to_core).astype(F32)
+
+        def over_plane(own_side, other_side):
+            count = own_side.shape[-2] // 2
+            near, far = own_side[..., :count, :], own_side[..., count:, :].astype(BF)
+            over, corner = other_side[..., :count, :].astype(BF), other_side[..., count:, :].astype(BF)
+            return (
+                near
+                + send(far, to_x).astype(F32)
+                + send(over, to_heads).astype(F32)
+                + send(corner, to_corner).astype(F32)
+            )
+
+        def over_levels(values):
+            total = values[..., :piece, :]
+            for k in range(1, levels):
+                part = values[..., k * piece : (k + 1) * piece, :].astype(BF)
+                total = total + send(part, to_level[k]).astype(F32)
+            return total
+
+        feed_b = over_cores(feed_mine_b, feed_theirs_b)
+        feed_a = over_cores(feed_mine_a, feed_theirs_a)
+        grad_w_up, grad_w_down = over_levels(over_plane(feed_a, feed_b))
+
+        output, grad_middle, grad_one_turned, grad_attended, sums_two, grad_b_out = back_two(
+            side, tokens, cotangent, branch_one, two_a, two_b, b_down[None], back_a, back_b, w_out_all, hot, turn, parts,
+            perm, third // 2, images,
+        )
+        grad_attended_got = send(grad_attended[1, 2 * third :], to_heads)
+        out_mine, out_theirs, _ = outer(grad_one_turned, attended_full, attended_half)
+        out_sum = over_cores(out_mine, out_theirs)
+        grad_w_out = over_levels(over_plane(out_sum[0], out_sum[1]))
+        grad_qkv_full = attend_back(qkv, grad_attended, *full_back_on, third)
+        shared_grad = jnp.concatenate([grad_attended[0, 2 * third :], grad_attended_got], axis=0)[None]
+        grad_qkv_shared = attend_back(qkv_shared, shared_grad, *half_back_on, third)
+        grad_qkv_got = send(grad_qkv_shared[0, third:], to_heads)
+        grad_qkv_half = jnp.stack([grad_qkv_shared[0, :third], grad_qkv_got])
+        qkv_mine, qkv_theirs, grad_qkv_bias = outer(hidden_one_turned, grad_qkv_full, grad_qkv_half)
+        qkv_sum = over_cores(qkv_mine, qkv_theirs)
+        grad_w_qkv = over_levels(over_plane(qkv_sum[0], qkv_sum[1]))
+        grad_tokens, sums_one = back_one(
+            side, grad_qkv_full, grad_qkv_half, attention_weights, tokens, grad_middle, hot, turn, parts,
+            third // 2, images,
+        )
+
+        sums = jnp.concatenate([sums_one, sums_two], axis=0).reshape(2, 3, images, width)
+        sums = sums.transpose(0, 2, 1, 3).reshape(2, images, 3 * width)
+        grad_b_qkv = grad_qkv_bias[:, 0]
+        narrow = jnp.concatenate([grad_b_out, grad_b_down], axis=0).reshape(2, 2, cols)
+
+        def packet(which, up_sum, qkv_sum):
+            first = jnp.concatenate([up_sum[0], qkv_sum[:cols], qkv_sum[2 * cols :]])
+            second = lax.dynamic_index_in_dim(narrow, which, 1, keepdims=False).reshape(-1)
+            second = jnp.concatenate([second, jnp.zeros((3 * width - 2 * cols,), F32)])
+            chunk = lax.dynamic_index_in_dim(sums, which, 0, keepdims=False)
+            return jnp.concatenate([chunk, first[None], second[None]], axis=0)
+
+        own_packet = packet(y, grad_b_up_a, grad_b_qkv[0]) + send(
+            packet(1 - y, grad_b_up_b, grad_b_qkv[1]), to_heads
+        )
+        packets = lax.all_gather(own_packet[None], "rows", axis=0, tiled=True)
+        grad_mod = packets[:, :images].reshape(ring * images, 3 * width)
+        bias_sums = jnp.sum(packets[:, images:], axis=0)
+        grad_w_ada = lax.dot_general(
+            jax.nn.silu(all_conditions.astype(F32)),
+            grad_mod,
+            (((0,), (0,)), ((), ())),
+            precision=PRECISE,
+            preferred_element_type=F32,
+        )
+        grad_b_ada = jnp.sum(grad_mod, axis=0)
+        grad_silu = lax.dot_general(
+            own_packet[:images],
+            w_ada,
+            (((1,), (1,)), ((), ())),
+            precision=PRECISE,
+            preferred_element_type=F32,
+        )
+        grad_silu = grad_silu + send(grad_silu, to_heads)
+        _, silu_back = jax.vjp(jax.nn.silu, cond)
+        grad_condition = silu_back(grad_silu)[0]
+        return (
+            output,
+            grad_tokens,
+            grad_condition,
+            grad_w_ada,
+            grad_b_ada,
+            grad_w_qkv[:, :cols],
+            grad_w_qkv[:, cols : 2 * cols],
+            grad_w_qkv[:, 2 * cols :],
+            bias_sums[0, units : units + cols],
+            bias_sums[0, units + cols :],
+            grad_w_out,
+            bias_sums[1, :cols],
+            grad_w_up,
+            bias_sums[0, :units],
+            grad_w_down,
+            bias_sums[1, cols : 2 * cols],
+        )
+
+    return body
+
+
 def solution(mesh):
+    body = fast_body(mesh) if mesh.shape["heads"] == 2 and mesh.shape["rows"] == 16 else general_body
     placed = (
         P(("rows", "heads"), None),
         P("rows", None),

time: 2960 us -> 1020 us (0.34)
  waiting for transfers between devices: 1960 us -> 251 us
  matrix products: 638 us -> 45.7 us
  Pallas kernels: 0 us -> 497 us
  other arithmetic: 204 us -> 83.7 us
  blocking collectives: 63.4 us -> 26.5 us
    reduce_scatter x7 -> x0, waiting for transfers between devices: 952 us -> none  [the longest x1 239 us: body(): lax.psum_scatter(grad_up_all, 'heads', scatter_dimension=1, tiled=True)]
    dot_general x59 -> x3, matrix products: 638 us -> 45.7 us  [the longest x1 17.3 us: body(): lax.dot_general(jax.nn.silu(all_conditions.astype(F32)), grad_mod, (((0,)...]
    pallas_call x0 -> x13, Pallas kernels: none -> 497 us  [the longest x2 139 us: attend_back(): pl.pallas_call(partial(attend_back_kernel, heads, block), grid=(groups, l...]
    all_gather x10 -> x4, waiting for transfers between devices: 470 us -> 34.8 us  [the longest x3 34.7 us: body(): lax.all_gather(v, ('heads', 'rows'), axis=0, tiled=True)]
    psum x1 -> x0, waiting for transfers between devices: 290 us -> none  [body(): lax.psum((grad_w_ada, grad_b_ada, grad_b_query, grad_b_value, grad_b_up,...]
    unnamed x30 -> x4, waiting for transfers between devices: 250 us -> 0.07 us
    ppermute x0 -> x28, waiting for transfers between devices: none -> 216 us  [send(): return lax.ppermute(values, both, pairs)]
    convert_element_type x10 -> x5, other arithmetic: 100 us -> 6.28 us  [the longest x1 2 us: body(): (feature[:, None] == jnp.arange(width, dtype=jnp.int32)[None, :]).astype(BF)]
  transfers between devices with their start and end apart: 24 -> 32, of which waited for: 19 -> 12; matrix products, arithmetic and copies ran while one was open for 13% -> 18% of each run, Pallas kernels for 0% -> 32%
where the time goes in v1:
time: 1020 us
  Pallas kernels  497 us (49%)
  waiting for transfers between devices  251 us (25%)
  other arithmetic  83.7 us (8%)
  local copies, waits for them, and re-layouts  66.1 us (6%)
  matrix products  45.7 us (4%)
  starting transfers between devices  30.3 us (3%)
  blocking collectives  26.5 us (3%)
  between operations  14.6 us (1%)
    ppermute x28, waiting for transfers between devices, send(): return lax.ppermute(values, both, pairs)  216 us
    pallas_call x2, Pallas kernels, attend_back(): pl.pallas_call(partial(attend_back_kernel, heads, block), grid=(groups, l...  139 us
    pallas_call x2, Pallas kernels, feed(): pl.pallas_call(partial(feed_kernel, chunk), grid_spec=pltpu.PrefetchScala...  136 us
    pallas_call x2, Pallas kernels, attend(): pl.pallas_call(partial(attend_kernel, heads, block), grid=(groups, length...  69.8 us
    another operation x11, other arithmetic  37.7 us
    all_gather x3, waiting for transfers between devices, body(): lax.all_gather(v, ('heads', 'rows'), axis=0, tiled=True)  34.7 us
    pallas_call x1, Pallas kernels, back_two(): pl.pallas_call(back_two_kernel, grid_spec=pltpu.PrefetchScalarGridSpec(nu...  32.5 us
    pallas_call x1, Pallas kernels, back_one(): pl.pallas_call(back_one_kernel, grid_spec=pltpu.PrefetchScalarGridSpec(nu...  30.4 us
  transfers between devices with their start and end apart: 32, of which 12 were waited for; matrix products, arithmetic and copies ran while one was open for 18% of the time, Pallas kernels for 32%

profile of v1, /device:TPU:9, one launch (start us, length us, event | category | flops | bytes accessed | tf_op | source)
XLA Modules:
  0.0 1015.3 jit_solution(14687157492033156016)
XLA Ops:
  12.1 1.9 convert_element_type.128
  18.9 11.4 %convolution_add_fusion = f32[8,3456]{1,0:T(8,128)S(1)} fusion(f32[1152,3456]{1,0:T(8,128)} %param.24, f32[3456]{0:T(1024)S(1)} %copy-done.13, bf16[8,1152]{1,0:T(8,128)(2,1)S(1)} %copy-done.3), kind=kOutput, calls=%fused_computation.9 | convolution fusion | flops 382279680 | bytes 16068096 | tf_op jit(solution)/shard_map/dot_general | solution.py:1006
  30.4 7.4 all-gather.2
  39.3 4.4 reshape.334
  43.8 5.2 reshape.333
  52.7 2.0 fusion.2.perm_ref
  54.7 11.4 %shard_map.306 = (bf16[1536,1152]{1,0:T(8,128)(2,1)}, bf16[1152,1536]{1,0:T(8,128)(2,1)}) custom-call(s32[1]{0:T(128)} %bitcast.side.pick, bf16[1536,1152]{1,0:T(8,128)(2,1)} %tok_ref.7, bf16[1536,24]{1,0:T(8,128)(2,1)} %compare_convert_fusion.hot_ref, bf16[2,24,3456]{2,1,0:T(8,128)(2,1)} %pad_maximum_fusion.2.parts_ref, bf16[1152,1152]{1,0:T(8,128)(2,1)} %fusion.2.perm_ref), custom_call_target="tpu_custom_call" | custom-call | flops 5888802816 | bytes 10616832 | tf_op jit(solution)/shard_map/pallas_call | solution.py:402
  66.1 34.7 %all-gather.9.cloned.1.call-done = bf16[2304,2304]{1,0:T(8,128)(2,1)} async-done(((bf16[72,2304]{1,0:T(8,128)(2,1)}), bf16[2304,2304]{1,0:T(8,128)(2,1)}) %all-gather.9.cloned.1.call-update) | async-done | bytes 10616848 | tf_op jit(solution)/shard_map/all_gather | solution.py:997
  100.8 21.2 %shard_map.307.q_ref.kv_ref.qkv_ref = bf16[2,1536,1728]{2,1,0:T(8,128)(2,1)} custom-call(s32[1]{0:T(128)} %bitcast.side.pick, bf16[1536,1152]{1,0:T(8,128)(2,1)} %get-tuple-element.47.h_ref, bf16[2,1152,2304]{2,1,0:T(8,128)(2,1)} %bitcast.119, f32[2,1,1728]{2,1,0:T(1,128)} %concatenate.91.bias_ref), custom_call_target="tpu_custom_call" | custom-call | flops 12230590464 | bytes 18579456 | tf_op jit(solution)/shard_map/pallas_call | solution.py:433
  122.0 3.5 slice_bitcast_fusion.3
  125.5 3.8 copy.55
  130.5 19.0 %all_gather.22 = bf16[128,1152]{1,0:T(8,128)(2,1)} all-gather(bf16[8,1152]{1,0:T(8,128)(2,1)S(1)} %copy-done.3), channel_id=1, replica_groups=mesh['rows'=16,'heads'=2] {'rows'}, dimensions={0}, use_global_device_ids=true | all-gather | bytes 313344 | tf_op jit(solution)/shard_map/all_gather | solution.py:1003
  151.0 2.6 broadcast_select_fusion.code_ref
  153.6 2.6 broadcast_select_fusion.1.code_ref
  156.8 33.3 %collective-permute-done = bf16[512,1728]{0,1:T(8,128)(2,1)} collective-permute-done((bf16[512,1728]{0,1:T(8,128)(2,1)}, bf16[512,1728]{0,1:T(8,128)(2,1)}, u32[]{:S(2)}, u32[]{:S(2)}) %collective-permute-start) | collective-permute-done | bytes 1769504 | tf_op jit(solution)/shard_map/ppermute | solution.py:963
  190.1 3.9 copy.56
  194.0 3.9 maximum_bitcast_fusion.q_ref.kv_ref.qkv_ref
  197.9 24.5 %shard_map.309 = bf16[1,1024,576]{2,1,0:T(8,128)(2,1)} custom-call(bf16[1,1024,1728]{2,1,0:T(8,128)(2,1)} %maximum_bitcast_fusion.q_ref.kv_ref.qkv_ref, bf16[1,1024,1728]{2,1,0:T(8,128)(2,1)} %maximum_bitcast_fusion.q_ref.kv_ref.qkv_ref, s32[8,1024]{1,0:T(8,128)} %bitcast_select_fusion.code_ref, s32[1024,1]{1,0:T(8,128)} %broadcast_select_fusion.2.seg_ref), custom_call_target="tpu_custom_call" | custom-call | flops 9663676416 | bytes 7077888 | tf_op jit(solution)/shard_map/pallas_call | solution.py:481
  222.3 1.4 fusion.61
  224.3 45.3 %shard_map.308.full_ref = bf16[2,1024,576]{2,1,0:T(8,128)(2,1)} custom-call(bf16[2,1536,1728]{2,1,0:T(8,128)(2,1)} %shard_map.307.q_ref.kv_ref.qkv_ref, bf16[2,1536,1728]{2,1,0:T(8,128)(2,1)} %shard_map.307.q_ref.kv_ref.qkv_ref, s32[8,1024]{1,0:T(8,128)} %bitcast_select_fusion.1.code_ref, s32[1024,1]{1,0:T(8,128)} %copy.54.seg_ref), custom_call_target="tpu_custom_call" | custom-call | flops 19327352832 | bytes 14155776 | tf_op jit(solution)/shard_map/pallas_call | solution.py:481
  269.6 5.0 slice.351.w_own.w_other
  276.2 28.6 %shard_map.310 = (f32[1536,1152]{1,0:T(8,128)}, bf16[1536,1152]{1,0:T(8,128)(2,1)}, bf16[1536,1152]{1,0:T(8,128)(2,1)}, bf16[1152,1536]{1,0:T(8,128)(2,1)}, bf16...) custom-call(s32[1]{0:T(128)} %bitcast.side.pick, bf16[1536,1152]{1,0:T(8,128)(2,1)} %tok_ref.7, bf16[1536,1152]{1,0:T(8,128)(2,1)} %dy_ref.3, ...), custom_call_target="tpu_custom_call" | custom-call | flops 15854469120 | bytes 38928384 | tf_op jit(solution)/shard_map/pallas_call | solution.py:624
  304.9 67.9 %shard_map.311 = (f32[1536,1152]{1,0:T(8,128)}, f32[1536,1152]{1,0:T(8,128)}, f32[2,576,2304]{2,1,0:T(8,128)}, bf16[2,576,2304]{2,1,0:T(8,128)(2,1)}, f32[1,2304]{1,0:T(1,128)}) custom-call(s32[1]{0:T(128)} %bitcast.side.pick, bf16[1536,1152]{1,0:T(8,128)(2,1)} %get-tuple-element.49.h_ref, bf16[1536,1152]{1,0:T(8,128)(2,1)} %get-tuple-element.50.g_ref, ...), custom_call_target="tpu_custom_call" | custom-call | flops 48922361856 | bytes 54853632 | tf_op jit(solution)/shard_map/pallas_call | solution.py:705
  372.8 68.4 %shard_map.312 = (f32[1536,1152]{1,0:T(8,128)}, f32[1536,1152]{1,0:T(8,128)}, f32[2,576,2304]{2,1,0:T(8,128)}, bf16[2,576,2304]{2,1,0:T(8,128)(2,1)}, f32[1,2304]{1,0:T(1,128)}) custom-call(s32[1]{0:T(128)S(6)} %sub.36.pick, bf16[1536,1152]{1,0:T(8,128)(2,1)} %get-tuple-element.49.h_ref, bf16[1536,1152]{1,0:T(8,128)(2,1)} %get-tuple-element.50.g_ref, ...), custom_call_target="tpu_custom_call" | custom-call | flops 48922361856 | bytes 54853632 | tf_op jit(solution)/shard_map/pallas_call | solution.py:705
  441.2 32.5 %shard_map.313 = (bf16[1536,1152]{1,0:T(8,128)(2,1)}, f32[1536,1152]{1,0:T(8,128)}, bf16[1152,1536]{1,0:T(8,128)(2,1)}, bf16[2,1536,576]{2,1,0:T(8,128)(2,1)}, f32[4,8,1152]{2,1,0:T(8,128)}, /*index=5*/f32[1,1152]{1,0:T(1,128)}) custom-call(s32[1]{0:T(128)} %bitcast.side.pick, bf16[1536,1152]{1,0:T(8,128)(2,1)} %tok_ref.7, bf16[1536,1152]{1,0:T(8,128)(2,1)} %dy_ref.3, ...), custom_call_target="tpu_custom_call" | custom-call | flops 15854469120 | bytes 60162048 | tf_op jit(solution)/shard_map/pallas_call | solution.py:802
  473.7 1.4 slice_bitcast_fusion.12
  478.1 1.6 collective-permute-start.22
  479.6 9.8 shard_map.318
  492.6 43.5 %shard_map.315 = bf16[1,1024,1728]{2,1,0:T(8,128)(2,1)} custom-call(bf16[1,1024,1728]{2,1,0:T(8,128)(2,1)} %maximum_bitcast_fusion.q_ref.kv_ref.qkv_ref, bf16[1,1024,576]{2,1,0:T(8,128)(2,1)} %maximum_bitcast_fusion.1.do_ref, s32[8,1024,1]{2,1,0:T(8,128)} %broadcast_select_fusion.code_ref, s32[8,128]{1,0:T(8,128)} %add_select_fusion.2.seg_ref), custom_call_target="tpu_custom_call" | custom-call | flops 19327352832 | bytes 14155776 | tf_op jit(solution)/shard_map/pallas_call | solution.py:559
  536.1 3.5 fusion.59
  539.6 3.8 copy.65
  544.7 3.8 fusion.54
  552.0 95.5 %shard_map.314.full_ref = bf16[2,1024,1728]{2,1,0:T(8,128)(2,1)} custom-call(bf16[2,1536,1728]{2,1,0:T(8,128)(2,1)} %shard_map.307.q_ref.kv_ref.qkv_ref, bf16[2,1536,576]{2,1,0:T(8,128)(2,1)} %get-tuple-element.58.do_ref, s32[8,1024,1]{2,1,0:T(8,128)} %broadcast_select_fusion.1.code_ref, s32[8,128]{1,0:T(8,128)} %bitcast.127), custom_call_target="tpu_custom_call" | custom-call | flops 38654705664 | bytes 28311552 | tf_op jit(solution)/shard_map/pallas_call | solution.py:559
  647.9 3.4 collective-permute-start.20
  651.4 1.4 fusion.52
  652.8 1.4 collective-permute-start.17
  655.5 3.7 copy.66
  659.2 3.7 pad_maximum_fusion.half_ref
  662.9 18.2 %shard_map.317 = (f32[2,576,1728]{2,1,0:T(8,128)}, bf16[2,576,1728]{2,1,0:T(8,128)(2,1)}, f32[2,1,1728]{2,1,0:T(1,128)}) custom-call(bf16[1152,1536]{1,0:T(8,128)(2,1)} %get-tuple-element.64.ht_ref, bf16[2,1024,1728]{2,1,0:T(8,128)(2,1)} %shard_map.314.full_ref, bf16[2,512,1728]{2,1,0:T(8,128)(2,1)} %pad_maximum_fusion.half_ref), custom_call_target="tpu_custom_call" | custom-call | flops 12230590464 | bytes 14155776 | tf_op jit(solution)/shard_map/pallas_call | solution.py:869
  682.0 30.4 %shard_map.316 = (f32[1536,1152]{1,0:T(8,128)}, f32[2,8,1152]{2,1,0:T(8,128)}) custom-call(s32[1]{0:T(128)} %bitcast.side.pick, bf16[2,1024,1728]{2,1,0:T(8,128)(2,1)} %shard_map.314.full_ref, bf16[2,512,1728]{2,1,0:T(8,128)(2,1)} %pad_maximum_fusion.half_ref, bf16[2,1152,2304]{2,1,0:T(8,128)(2,1)} %bitcast.121, bf16[2,1152,2304]{2,1,0:T(8,128)(2,1)} %bitcast.122, ...), custom_call_target="tpu_custom_call" | custom-call | flops 12230590464 | bytes 28311552 | tf_op jit(solution)/shard_map/pallas_call | solution.py:916
  716.1 4.9 collective-permute-done.4
  721.8 17.0 %fusion.23 = f32[8,1152]{1,0:T(8,128)S(1)} fusion(f32[1152,3456]{1,0:T(8,128)} %param.24, f32[10,3456]{1,0:T(8,128)} %maximum_add_fusion), kind=kOutput, calls=%fused_computation.71 | convolution fusion | flops 382205952 | bytes 16072704 | tf_op jit(solution)/shard_map/dot_general | solution.py:1148
  740.0 9.0 add_convert_fusion
  749.0 5.3 fusion.58
  756.1 8.9 fusion.57
  765.1 1.7 slice_bitcast_fusion.6
  767.6 10.7 %convert_add_fusion = f32[2,576,2304]{2,1,0:T(8,128)} fusion(f32[2,576,2304]{2,1,0:T(8,128)} %get-tuple-element.74, bf16[2,576,2304]{2,1,0:T(8,128)(2,1)} %collective-permute-done.20), kind=kLoop, calls=%fused_computation.1 | loop fusion | flops 5308416 | bytes 26542080 | tf_op jit(solution)/shard_map/add | solution.py:1077
  778.3 2.8 slice.470
  783.6 1.6 slice_reduce_fusion.1
  785.2 53.4 %collective-permute-done.7 = bf16[288,1728]{1,0:T(8,128)(2,1)} collective-permute-done((bf16[288,1728]{1,0:T(8,128)(2,1)}, bf16[288,1728]{1,0:T(8,128)(2,1)}, u32[]{:S(2)}, u32[]{:S(2)}) %collective-permute-start.7) | collective-permute-done | bytes 995360 | tf_op jit(solution)/shard_map/ppermute | solution.py:963
  841.2 2.3 slice_reduce_fusion
  843.5 17.3 %fusion.6 = f32[1152,3456]{1,0:T(8,128)} fusion(f32[16,10,3456]{2,1,0:T(8,128)} %all-gather.15.cloned.1.call-done, bf16[128,1152]{1,0:T(8,128)(2,1)S(1)} %copy-done.1), kind=kOutput, calls=%fused_computation.22 | convolution fusion | flops 6116032512 | bytes 17989632 | tf_op jit(solution)/shard_map/dot_general | solution.py:1140
  860.9 30.6 %collective-permute-done.8 = bf16[288,1728]{1,0:T(8,128)(2,1)} collective-permute-done((bf16[288,1728]{1,0:T(8,128)(2,1)}, bf16[288,1728]{1,0:T(8,128)(2,1)}, u32[]{:S(2)}, u32[]{:S(2)}) %collective-permute-start.8) | collective-permute-done | bytes 995360 | tf_op jit(solution)/shard_map/ppermute | solution.py:963
  891.5 27.0 %collective-permute-done.9 = bf16[288,1728]{1,0:T(8,128)(2,1)S(1)} collective-permute-done((bf16[288,1728]{1,0:T(8,128)(2,1)}, bf16[288,1728]{1,0:T(8,128)(2,1)S(1)}, u32[]{:S(2)}, u32[]{:S(2)}) %collective-permute-start.9) | collective-permute-done | bytes 995360 | tf_op jit(solution)/shard_map/ppermute | solution.py:963
  918.5 3.9 fusion.55
  925.3 1.5 collective-permute-start.12
  926.8 6.8 fusion.50
  933.8 3.4 collective-permute-start.26
  937.2 8.9 collective-permute-done.11
  946.1 31.2 %collective-permute-done.12 = bf16[72,1728]{1,0:T(8,128)(2,1)S(1)} collective-permute-done((bf16[72,1728]{1,0:T(8,128)(2,1)}, bf16[72,1728]{1,0:T(8,128)(2,1)S(1)}, u32[]{:S(2)}, u32[]{:S(2)}) %collective-permute-start.12) | collective-permute-done | bytes 248864 | tf_op jit(solution)/shard_map/ppermute | solution.py:963
  979.3 9.3 collective-permute-done.25
  988.7 14.2 %collective-permute-done.26 = bf16[2,72,2304]{2,1,0:T(8,128)(2,1)S(1)} collective-permute-done((bf16[2,72,2304]{2,1,0:T(8,128)(2,1)S(1)}, bf16[2,72,2304]{2,1,0:T(8,128)(2,1)S(1)}, u32[]{:S(2)}, u32[]{:S(2)}) %collective-permute-start.26) | collective-permute-done | bytes 663584 | tf_op jit(solution)/shard_map/ppermute | solution.py:963
  1002.9 2.9 collective-permute-done.27
  1005.8 1.6 fusion.10
  (196 shorter events, 53.2 us)
Async XLA Ops:
  7.2 6.9 copy-start.2
  7.2 7.9 copy-start.16
  7.2 8.7 copy-start.23
  7.2 8.7 copy-start.24
  7.2 8.7 copy-start.15
  7.2 11.1 %copy-start.19 = (f32[1152]{0:T(1024)S(1)}, f32[1152]{0:T(1024)}, u32[]{:S(2)}) copy-start(f32[1152]{0:T(1024)} %param.32) | copy-start | bytes 13828
  7.2 11.7 %copy-start.3 = (bf16[8,1152]{1,0:T(8,128)(2,1)S(1)}, bf16[8,1152]{1,0:T(8,128)(2,1)}, u32[]{:S(2)}) copy-start(bf16[8,1152]{1,0:T(8,128)(2,1)} %param.20) | copy-start | bytes 55300
  7.3 11.7 %copy-start.13 = (f32[3456]{0:T(1024)S(1)}, f32[3456]{0:T(1024)}, u32[]{:S(2)}) copy-start(f32[3456]{0:T(1024)} %param.25) | copy-start | bytes 41476
  7.3 93.5 %all-gather.9.cloned.1.call-start = ((), (), s32[]{:S(2)}) async-start(), calls=%async_computation | async-start | bytes 10948608 | tf_op jit(solution)/shard_map/all_gather | solution.py:997
  12.1 292.8 %all-gather.11.cloned.1.call-start = ((), (), s32[]{:S(2)}) async-start(), calls=%async_computation.1 | async-start | bytes 10948608 | tf_op jit(solution)/shard_map/all_gather | solution.py:997
  14.0 290.9 %all-gather.13.cloned.1.call-start = ((), (), s32[]{:S(2)}) async-start(), calls=%async_computation.2 | async-start | bytes 10948608 | tf_op jit(solution)/shard_map/all_gather | solution.py:997
  14.9 768.7 %all-gather.15.cloned.1.call-start = ((), (), s32[]{:S(2)}) async-start(), calls=%async_computation.3 | async-start | bytes 3760128 | tf_op jit(solution)/shard_map/all_gather | solution.py:1137
  15.2 15.2 %copy-start.9 = (s32[1,512]{1,0:T(1,128)}, s32[1,512]{1,0:T(1,128)S(1)}, u32[]{:S(2)}) copy-start(s32[1,512]{1,0:T(1,128)S(1)} %get-tuple-element.137) | copy-start | bytes 6148
  15.2 15.2 %copy-start.11 = (s32[1,512]{1,0:T(1,128)}, s32[1,512]{1,0:T(1,128)S(1)}, u32[]{:S(2)}) copy-start(s32[1,512]{1,0:T(1,128)S(1)} %get-tuple-element.138) | copy-start | bytes 6148
  15.2 0.6 copy-start.7
  15.2 138.3 %copy-start.6 = (s32[1,1024]{1,0:T(1,128)}, s32[1,1024]{1,0:T(1,128)S(1)}, u32[]{:S(2)}) copy-start(s32[1,1024]{1,0:T(1,128)S(1)} %get-tuple-element.142) | copy-start | bytes 12292
  18.9 19.6 %copy-start.20 = (f32[1152]{0:T(1024)S(1)}, f32[1152]{0:T(1024)}, u32[]{:S(2)}) copy-start(f32[1152]{0:T(1024)} %param.36) | copy-start | bytes 13828
  18.9 20.1 %copy-start.14 = (s32[3,8,8]{2,1,0:T(8,128)S(1)}, s32[3,8,8]{2,1,0:T(8,128)}, u32[]{:S(2)}) copy-start(s32[3,8,8]{2,1,0:T(8,128)} %param.22) | copy-start | bytes 2308
  18.9 30.9 %copy-start.25 = (s32[3,4]{1,0:T(4,128)S(1)}, s32[3,4]{1,0:T(4,128)}, u32[]{:S(2)}) copy-start(s32[3,4]{1,0:T(4,128)} %param.23) | copy-start | bytes 148
  129.3 24.3 %copy-start = (pred[8,1024,1]{2,1,0:T(8,128)(4,1)S(1)}, pred[8,1024,1]{2,1,0:T(8,128)(4,1)}, u32[]{:S(2)}) copy-start(pred[8,1024,1]{2,1,0:T(8,128)(4,1)} %reshape.333) | copy-start | bytes 24580
  129.3 60.8 %collective-permute-start = (bf16[512,1728]{0,1:T(8,128)(2,1)}, bf16[512,1728]{0,1:T(8,128)(2,1)}, u32[]{:S(2)}, u32[]{:S(2)}) collective-permute-start(bf16[512,1728]{0,1:T(8,128)(2,1)} %copy.55), channel_id=1, source_target_pairs={{0,1},{1,0},{2,3},{3,2},{4,5},{5,4},{6,7},{7,6},{8,9},{9,8},{10,11... | collective-permute-start | bytes 5308424 | tf_op jit(solution)/shard_map/ppermute | solution.py:963
  224.0 50.6 %collective-permute-start.1 = (bf16[512,576]{0,1:T(8,128)(2,1)S(1)}, bf16[512,576]{0,1:T(8,128)(2,1)S(1)}, u32[]{:S(2)}, u32[]{:S(2)}) collective-permute-start(bf16[512,576]{0,1:T(8,128)(2,1)S(1)} %copy.59), channel_id=1, source_target_pairs={{0,1},{1,0},{2,3},{3,2},{4,5},{5,4},{6,7},{7,6},{8,9},{9,8},{10,11... | collective-permute-start | bytes 1769480 | tf_op jit(solution)/shard_map/ppermute | solution.py:963
  473.7 3.7 copy-start.8
  473.7 3.7 copy-start.10
  473.7 3.7 copy-start.12
  476.2 13.8 %collective-permute-start.2 = (bf16[512,576]{0,1:T(8,128)(2,1)}, bf16[512,576]{0,1:T(8,128)(2,1)}, u32[]{:S(2)}, u32[]{:S(2)}) collective-permute-start(bf16[512,576]{0,1:T(8,128)(2,1)} %copy.62), channel_id=1, source_target_pairs={{0,1},{1,0},{2,3},{3,2},{4,5},{5,4},{6,7},{7,6},{8,9},{9,8},{10,11... | collective-permute-start | bytes 1769480 | tf_op jit(solution)/shard_map/ppermute | solution.py:963
  478.1 261.9 %collective-permute-start.22 = (bf16[2,576,2304]{2,1,0:T(8,128)(2,1)}, bf16[2,576,2304]{2,1,0:T(8,128)(2,1)}, u32[]{:S(2)}, u32[]{:S(2)}) collective-permute-start(bf16[2,576,2304]{2,1,0:T(8,128)(2,1)} %get-tuple-element.77), channel_id=1, source_target_pairs={{0,2},{1,3},{2,0},{3,1},{4,6},{5,7},{6,4},{7,5},{8,10},{9,11},{10,... | collective-permute-start | bytes 15925256 | tf_op jit(solution)/shard_map/ppermute | solution.py:963
  489.5 55.2 %collective-permute-start.13 = (bf16[2,576,576]{2,1,0:T(8,128)(2,1)}, bf16[2,576,576]{2,1,0:T(8,128)(2,1)S(1)}, u32[]{:S(2)}, u32[]{:S(2)}) collective-permute-start(bf16[2,576,576]{2,1,0:T(8,128)(2,1)} %get-tuple-element.73), channel_id=1, source_target_pairs={{0,2},{1,3},{2,0},{3,1},{4,6},{5,7},{6,4},{7,5},{8,10},{9,11},{10,... | collective-permute-start | bytes 3981320 | tf_op jit(solution)/shard_map/ppermute | solution.py:963
  543.4 111.7 %collective-permute-start.3 = (bf16[512,1728]{0,1:T(8,128)(2,1)}, bf16[512,1728]{0,1:T(8,128)(2,1)}, u32[]{:S(2)}, u32[]{:S(2)}) collective-permute-start(bf16[512,1728]{0,1:T(8,128)(2,1)} %copy.65), channel_id=1, source_target_pairs={{0,1},{1,0},{2,3},{3,2},{4,5},{5,4},{6,7},{7,6},{8,9},{9,8},{10,11... | collective-permute-start | bytes 5308424 | tf_op jit(solution)/shard_map/ppermute | solution.py:963
  549.3 98.6 %collective-permute-start.14 = (bf16[288,576]{1,0:T(8,128)(2,1)}, bf16[288,576]{1,0:T(8,128)(2,1)S(1)}, u32[]{:S(2)}, u32[]{:S(2)}) collective-permute-start(bf16[288,576]{1,0:T(8,128)(2,1)} %get-tuple-element.112), channel_id=1, source_target_pairs={{0,4},{1,5},{2,6},{3,7},{4,0},{5,1},{6,2},{7,3},{8,12},{9,13},{10,... | collective-permute-start | bytes 995336 | tf_op jit(solution)/shard_map/ppermute | solution.py:963
  550.6 100.7 %collective-permute-start.15 = (bf16[288,576]{1,0:T(8,128)(2,1)S(1)}, bf16[288,576]{1,0:T(8,128)(2,1)S(1)}, u32[]{:S(2)}, u32[]{:S(2)}) collective-permute-start(bf16[288,576]{1,0:T(8,128)(2,1)S(1)} %get-tuple-element.114), channel_id=1, source_target_pairs={{0,1},{1,0},{2,3},{3,2},{4,5},{5,4},{6,7},{7,6},{8,9},{9,8},{10,11... | collective-permute-start | bytes 995336 | tf_op jit(solution)/shard_map/ppermute | solution.py:963
  551.2 100.2 %collective-permute-start.16 = (bf16[288,576]{1,0:T(8,128)(2,1)S(1)}, bf16[288,576]{1,0:T(8,128)(2,1)}, u32[]{:S(2)}, u32[]{:S(2)}) collective-permute-start(bf16[288,576]{1,0:T(8,128)(2,1)S(1)} %get-tuple-element.113), channel_id=1, source_target_pairs={{0,5},{1,4},{2,7},{3,6},{4,1},{5,0},{6,3},{7,2},{8,13},{9,12},{10,... | collective-permute-start | bytes 995336 | tf_op jit(solution)/shard_map/ppermute | solution.py:963
  552.0 95.5 %copy-start.17 = (f32[1,2304]{1,0:T(1,128)S(1)}, f32[1,2304]{1,0:T(1,128)}, u32[]{:S(2)}) copy-start(f32[1,2304]{1,0:T(1,128)} %get-tuple-element.63) | copy-start | bytes 27652
  552.0 95.5 %copy-start.18 = (f32[1,2304]{1,0:T(1,128)S(1)}, f32[1,2304]{1,0:T(1,128)}, u32[]{:S(2)}) copy-start(f32[1,2304]{1,0:T(1,128)} %get-tuple-element.68) | copy-start | bytes 27652
  552.0 95.6 %copy-start.21 = (f32[1,1152]{1,0:T(1,128)S(1)}, f32[1,1152]{1,0:T(1,128)}, u32[]{:S(2)}) copy-start(f32[1,1152]{1,0:T(1,128)} %get-tuple-element.67) | copy-start | bytes 13828
  552.0 95.6 %copy-start.22 = (f32[1,1152]{1,0:T(1,128)S(1)}, f32[1,1152]{1,0:T(1,128)}, u32[]{:S(2)}) copy-start(f32[1,1152]{1,0:T(1,128)} %get-tuple-element.66) | copy-start | bytes 13828
  647.9 119.6 %collective-permute-start.20 = (bf16[2,576,2304]{2,1,0:T(8,128)(2,1)}, bf16[2,576,2304]{2,1,0:T(8,128)(2,1)}, u32[]{:S(2)}, u32[]{:S(2)}) collective-permute-start(bf16[2,576,2304]{2,1,0:T(8,128)(2,1)} %get-tuple-element.75), channel_id=1, source_target_pairs={{0,2},{1,3},{2,0},{3,1},{4,6},{5,7},{6,4},{7,5},{8,10},{9,11},{10,... | collective-permute-start | bytes 15925256 | tf_op jit(solution)/shard_map/ppermute | solution.py:963
  652.8 60.5 %collective-permute-start.17 = (bf16[72,576]{1,0:T(8,128)(2,1)S(1)}, bf16[72,576]{1,0:T(8,128)(2,1)S(1)}, u32[]{:S(2)}, u32[]{:S(2)}) collective-permute-start(bf16[72,576]{1,0:T(8,128)(2,1)S(1)} %get-tuple-element.130), channel_id=1, source_target_pairs={{0,8},{1,9},{2,10},{3,11},{4,12},{5,13},{6,14},{7,15},{8,16},{9,17... | collective-permute-start | bytes 248840 | tf_op jit(solution)/shard_map/ppermute | solution.py:963
  654.2 59.8 %collective-permute-start.18 = (bf16[72,576]{1,0:T(8,128)(2,1)S(1)}, bf16[72,576]{1,0:T(8,128)(2,1)S(1)}, u32[]{:S(2)}, u32[]{:S(2)}) collective-permute-start(bf16[72,576]{1,0:T(8,128)(2,1)S(1)} %get-tuple-element.132), channel_id=1, source_target_pairs={{0,16},{1,17},{2,18},{3,19},{4,20},{5,21},{6,22},{7,23},{8,24},{9,... | collective-permute-start | bytes 248840 | tf_op jit(solution)/shard_map/ppermute | solution.py:963
  655.2 60.1 %collective-permute-start.19 = (bf16[72,576]{1,0:T(8,128)(2,1)S(1)}, bf16[72,576]{1,0:T(8,128)(2,1)S(1)}, u32[]{:S(2)}, u32[]{:S(2)}) collective-permute-start(bf16[72,576]{1,0:T(8,128)(2,1)S(1)} %get-tuple-element.131), channel_id=1, source_target_pairs={{0,24},{1,25},{2,26},{3,27},{4,28},{5,29},{6,30},{7,31},{8,0},{9,1... | collective-permute-start | bytes 248840 | tf_op jit(solution)/shard_map/ppermute | solution.py:963
  682.0 30.4 %copy-start.5 = (f32[4,8,1152]{2,1,0:T(8,128)S(1)}, f32[4,8,1152]{2,1,0:T(8,128)}, u32[]{:S(2)}) copy-start(f32[4,8,1152]{2,1,0:T(8,128)} %get-tuple-element.62) | copy-start | bytes 442372
  713.4 42.8 %collective-permute-start.6 = (bf16[2,576,1728]{2,1,0:T(8,128)(2,1)}, bf16[2,576,1728]{2,1,0:T(8,128)(2,1)}, u32[]{:S(2)}, u32[]{:S(2)}) collective-permute-start(bf16[2,576,1728]{2,1,0:T(8,128)(2,1)} %get-tuple-element.70), channel_id=1, source_target_pairs={{0,2},{1,3},{2,0},{3,1},{4,6},{5,7},{6,4},{7,5},{8,10},{9,11},{10,... | collective-permute-start | bytes 11943944 | tf_op jit(solution)/shard_map/ppermute | solution.py:963
  714.0 7.0 collective-permute-start.4
  738.7 43.1 %collective-permute-start.5 = (f32[8,1152]{1,0:T(8,128)S(1)}, f32[8,1152]{1,0:T(8,128)S(1)}, u32[]{:S(2)}, u32[]{:S(2)}) collective-permute-start(f32[8,1152]{1,0:T(8,128)S(1)} %fusion.23), channel_id=1, source_target_pairs={{0,1},{1,0},{2,3},{3,2},{4,5},{5,4},{6,7},{7,6},{8,9},{9,8},{10,11... | collective-permute-start | bytes 110600 | tf_op jit(solution)/shard_map/ppermute | solution.py:963
  754.3 171.1 %collective-permute-start.23 = (bf16[2,288,2304]{2,1,0:T(8,128)(2,1)}, bf16[2,288,2304]{2,1,0:T(8,128)(2,1)}, u32[]{:S(2)}, u32[]{:S(2)}) collective-permute-start(bf16[2,288,2304]{2,1,0:T(8,128)(2,1)} %get-tuple-element.100), channel_id=1, source_target_pairs={{0,1},{1,0},{2,3},{3,2},{4,5},{5,4},{6,7},{7,6},{8,9},{9,8},{10,11... | collective-permute-start | bytes 7962632 | tf_op jit(solution)/shard_map/ppermute | solution.py:963
  754.9 171.9 %collective-permute-start.24 = (bf16[2,288,2304]{2,1,0:T(8,128)(2,1)}, bf16[2,288,2304]{2,1,0:T(8,128)(2,1)}, u32[]{:S(2)}, u32[]{:S(2)}) collective-permute-start(bf16[2,288,2304]{2,1,0:T(8,128)(2,1)} %get-tuple-element.101), channel_id=1, source_target_pairs={{0,5},{1,4},{2,7},{3,6},{4,1},{5,0},{6,3},{7,2},{8,13},{9,12},{10,... | collective-permute-start | bytes 7962632 | tf_op jit(solution)/shard_map/ppermute | solution.py:963
  766.8 71.8 %collective-permute-start.7 = (bf16[288,1728]{1,0:T(8,128)(2,1)}, bf16[288,1728]{1,0:T(8,128)(2,1)}, u32[]{:S(2)}, u32[]{:S(2)}) collective-permute-start(bf16[288,1728]{1,0:T(8,128)(2,1)} %get-tuple-element.102), channel_id=1, source_target_pairs={{0,4},{1,5},{2,6},{3,7},{4,0},{5,1},{6,2},{7,3},{8,12},{9,13},{10,... | collective-permute-start | bytes 2985992 | tf_op jit(solution)/shard_map/ppermute | solution.py:963
  778.3 3.5 copy-start.4
  778.3 65.2 %copy-start.1 = (bf16[128,1152]{1,0:T(8,128)(2,1)S(1)}, bf16[128,1152]{1,0:T(8,128)(2,1)}, u32[]{:S(2)}) copy-start(bf16[128,1152]{1,0:T(8,128)(2,1)} %all_gather.22) | copy-start | bytes 884740
  781.1 145.7 %collective-permute-start.21 = (bf16[2,288,2304]{2,1,0:T(8,128)(2,1)S(1)}, bf16[2,288,2304]{2,1,0:T(8,128)(2,1)}, u32[]{:S(2)}, u32[]{:S(2)}) collective-permute-start(bf16[2,288,2304]{2,1,0:T(8,128)(2,1)S(1)} %slice.470), channel_id=1, source_target_pairs={{0,4},{1,5},{2,6},{3,7},{4,0},{5,1},{6,2},{7,3},{8,12},{9,13},{10,... | collective-permute-start | bytes 7962632 | tf_op jit(solution)/shard_map/ppermute | solution.py:963
  782.5 109.0 %collective-permute-start.8 = (bf16[288,1728]{1,0:T(8,128)(2,1)}, bf16[288,1728]{1,0:T(8,128)(2,1)}, u32[]{:S(2)}, u32[]{:S(2)}) collective-permute-start(bf16[288,1728]{1,0:T(8,128)(2,1)} %get-tuple-element.104), channel_id=1, source_target_pairs={{0,1},{1,0},{2,3},{3,2},{4,5},{5,4},{6,7},{7,6},{8,9},{9,8},{10,11... | collective-permute-start | bytes 2985992 | tf_op jit(solution)/shard_map/ppermute | solution.py:963
  838.5 79.9 %collective-permute-start.9 = (bf16[288,1728]{1,0:T(8,128)(2,1)}, bf16[288,1728]{1,0:T(8,128)(2,1)S(1)}, u32[]{:S(2)}, u32[]{:S(2)}) collective-permute-start(bf16[288,1728]{1,0:T(8,128)(2,1)} %get-tuple-element.103), channel_id=1, source_target_pairs={{0,5},{1,4},{2,7},{3,6},{4,1},{5,0},{6,3},{7,2},{8,13},{9,12},{10,... | collective-permute-start | bytes 2985992 | tf_op jit(solution)/shard_map/ppermute | solution.py:963
  841.2 85.6 %slice-start = ((s8[10616832]{0:T(1024)(128)(4,1)}), s8[4194304]{0:T(1024)(128)(4,1)S(1)}, s32[]{:S(2)}) async-start(s8[10616832]{0:T(1024)(128)(4,1)} %bitcast.113), calls=%async_computation.4 | async-start | bytes 8388608
  843.5 83.3 %slice-start.1 = ((s8[10616832]{0:T(1024)(128)(4,1)}), s8[4194304]{0:T(1024)(128)(4,1)S(1)}, s32[]{:S(2)}) async-start(s8[10616832]{0:T(1024)(128)(4,1)} %bitcast.113), calls=%async_computation.5 | async-start | bytes 8388608
  843.5 83.3 %slice-start.2 = ((s8[10616832]{0:T(1024)(128)(4,1)}), s8[2228224]{0:T(1024)(128)(4,1)S(1)}, s32[]{:S(2)}) async-start(s8[10616832]{0:T(1024)(128)(4,1)} %bitcast.113), calls=%async_computation.6 | async-start | bytes 4456448
  923.3 13.9 %collective-permute-start.10 = (bf16[72,1728]{1,0:T(8,128)(2,1)}, bf16[72,1728]{1,0:T(8,128)(2,1)S(1)}, u32[]{:S(2)}, u32[]{:S(2)}) collective-permute-start(bf16[72,1728]{1,0:T(8,128)(2,1)} %get-tuple-element.119), channel_id=1, source_target_pairs={{0,8},{1,9},{2,10},{3,11},{4,12},{5,13},{6,14},{7,15},{8,16},{9,17... | collective-permute-start | bytes 746504 | tf_op jit(solution)/shard_map/ppermute | solution.py:963
  924.5 21.6 %collective-permute-start.11 = (bf16[72,1728]{1,0:T(8,128)(2,1)}, bf16[72,1728]{1,0:T(8,128)(2,1)S(1)}, u32[]{:S(2)}, u32[]{:S(2)}) collective-permute-start(bf16[72,1728]{1,0:T(8,128)(2,1)} %get-tuple-element.121), channel_id=1, source_target_pairs={{0,16},{1,17},{2,18},{3,19},{4,20},{5,21},{6,22},{7,23},{8,24},{9,... | collective-permute-start | bytes 746504 | tf_op jit(solution)/shard_map/ppermute | solution.py:963
  925.3 52.0 %collective-permute-start.12 = (bf16[72,1728]{1,0:T(8,128)(2,1)}, bf16[72,1728]{1,0:T(8,128)(2,1)S(1)}, u32[]{:S(2)}, u32[]{:S(2)}) collective-permute-start(bf16[72,1728]{1,0:T(8,128)(2,1)} %get-tuple-element.120), channel_id=1, source_target_pairs={{0,24},{1,25},{2,26},{3,27},{4,28},{5,29},{6,30},{7,31},{8,0},{9,1... | collective-permute-start | bytes 746504 | tf_op jit(solution)/shard_map/ppermute | solution.py:963
  933.8 54.9 %collective-permute-start.25 = (bf16[2,72,2304]{2,1,0:T(8,128)(2,1)S(1)}, bf16[2,72,2304]{2,1,0:T(8,128)(2,1)S(1)}, u32[]{:S(2)}, u32[]{:S(2)}) collective-permute-start(bf16[2,72,2304]{2,1,0:T(8,128)(2,1)S(1)} %get-tuple-element.109), channel_id=1, source_target_pairs={{0,8},{1,9},{2,10},{3,11},{4,12},{5,13},{6,14},{7,15},{8,16},{9,17... | collective-permute-start | bytes 1990664 | tf_op jit(solution)/shard_map/ppermute | solution.py:963
  933.8 69.1 %collective-permute-start.26 = (bf16[2,72,2304]{2,1,0:T(8,128)(2,1)S(1)}, bf16[2,72,2304]{2,1,0:T(8,128)(2,1)S(1)}, u32[]{:S(2)}, u32[]{:S(2)}) collective-permute-start(bf16[2,72,2304]{2,1,0:T(8,128)(2,1)S(1)} %get-tuple-element.111), channel_id=1, source_target_pairs={{0,16},{1,17},{2,18},{3,19},{4,20},{5,21},{6,22},{7,23},{8,24},{9,... | collective-permute-start | bytes 1990664 | tf_op jit(solution)/shard_map/ppermute | solution.py:963
  937.2 68.6 %collective-permute-start.27 = (bf16[2,72,2304]{2,1,0:T(8,128)(2,1)S(1)}, bf16[2,72,2304]{2,1,0:T(8,128)(2,1)S(1)}, u32[]{:S(2)}, u32[]{:S(2)}) collective-permute-start(bf16[2,72,2304]{2,1,0:T(8,128)(2,1)S(1)} %get-tuple-element.110), channel_id=1, source_target_pairs={{0,24},{1,25},{2,26},{3,27},{4,28},{5,29},{6,30},{7,31},{8,0},{9,1... | collective-permute-start | bytes 1990664 | tf_op jit(solution)/shard_map/ppermute | solution.py:963
Sparse Core Ops, SparseCore 0:
  12.2 88.5 all-gather.8
  103.7 103.2 all-gather.10
  209.9 86.8 all-gather.12
  721.9 50.1 all-gather.14

commit v2 on v1

--- a/solution.py
+++ b/solution.py
@@ -388,13 +388,20 @@
     return jnp.concatenate([high, middle, rest - middle], axis=-2).astype(BF)
 
 
-def norm_kernel(side, tok_ref, hot_ref, parts_ref, perm_ref, h_ref, ht_ref):
+def norm_kernel(side, tok_ref, hot_ref, parts_ref, perm_ref, h_ref, half_ref, ht_ref):
     width = tok_ref.shape[1]
     normed, _ = layer_norm(tok_ref[...].astype(F32))
     mod = rows_by_columns(hot_ref[...], parts_ref[0, :, : 2 * width])
     hidden = (normed * (1.0 + mod[:, width:]) + mod[:, :width]).astype(BF)
-    h_ref[...] = hidden
     ht_ref[...] = contract_last(perm_ref[...], hidden).astype(BF)
+
+    @pl.when(pl.program_id(0) < 2)
+    def _():
+        h_ref[...] = hidden
+
+    @pl.when(pl.program_id(0) == 2)
+    def _():
+        half_ref[...] = hidden
 
 
 def first_norm(side, tokens, hot, parts, perm, block):
@@ -411,187 +418,324 @@
                 pl.BlockSpec(perm.shape, lambda i, y: (0, 0)),
             ],
             out_specs=[
-                pl.BlockSpec((block, width), lambda i, y: (i, 0)),
+                pl.BlockSpec((block, width), lambda i, y: (jnp.minimum(i, 1), 0)),
+                pl.BlockSpec((block, width), lambda i, y: (0, 0)),
                 pl.BlockSpec((width, block), lambda i, y: (0, i)),
             ],
         ),
-        out_shape=[shape((rows, width), BF), shape((width, rows), BF)],
+        out_shape=[
+            shape((2 * block, width), BF),
+            shape((block, width), BF),
+            shape((width, rows), BF),
+        ],
         compiler_params=params(),
         cost_estimate=cost(2 * rows * width * (width + 512), rows * width * 6),
     )(side, tokens, hot, parts, perm)
 
 
-def project_kernel(side, h_ref, w_ref, bias_ref, out_ref):
-    width = out_ref.shape[2]
-    out_ref[0] = (rows_by_columns(h_ref[...], w_ref[0, :, :width]) + bias_ref[0]).astype(BF)
-
-
-def project(side, hidden, weights, bias, block):
-    rows, width = hidden.shape
-    cols = bias.shape[2]
+def project_kernel(side, full_ref, own_ref, got_ref, w_ref, bias_ref, first, second, own, got):
+    block, padded = own.shape[1:]
+    cols = bias_ref.shape[2]
+
+    def found(hidden):
+        value = (rows_by_columns(hidden, w_ref[0, :, :cols]) + bias_ref[0]).astype(BF)
+        return jnp.concatenate([value, jnp.zeros((block, padded - cols), BF)], axis=1)
+
+    first[0] = found(full_ref[:block])
+    second[0] = found(full_ref[block:])
+
+    @pl.when(pl.program_id(0) == 0)
+    def _():
+        own[0] = found(own_ref[...])
+        got[0] = found(got_ref[...])
+
+
+def project(side, full, own, got, weights, bias, padded):
+    block, width = own.shape
     pick = lambda a, y: a + y[0] - 2 * a * y[0]
+    single = pl.BlockSpec((1, block, padded), lambda a, y: (0, 0, 0))
+    pair = pl.BlockSpec((1, block, padded), lambda a, y: (a, 0, 0))
     return pl.pallas_call(
         project_kernel,
         grid_spec=pltpu.PrefetchScalarGridSpec(
             num_scalar_prefetch=1,
-            grid=(2, rows // block),
+            grid=(2,),
             in_specs=[
-                pl.BlockSpec((block, width), lambda a, i, y: (i, 0)),
-                pl.BlockSpec((1,) + weights.shape[1:], lambda a, i, y: (pick(a, y), 0, 0)),
-                pl.BlockSpec((1, 1, cols), lambda a, i, y: (pick(a, y), 0, 0)),
+                pl.BlockSpec((2 * block, width), lambda a, y: (0, 0)),
+                pl.BlockSpec((block, width), lambda a, y: (0, 0)),
+                pl.BlockSpec((block, width), lambda a, y: (0, 0)),
+                pl.BlockSpec((1,) + weights.shape[1:], lambda a, y: (pick(a, y), 0, 0)),
+                pl.BlockSpec((1,) + bias.shape[1:], lambda a, y: (pick(a, y), 0, 0)),
             ],
-            out_specs=pl.BlockSpec((1, block, cols), lambda a, i, y: (a, i, 0)),
+            out_specs=[pair, pair, single, single],
         ),
-        out_shape=shape((2, rows, cols), BF),
-        compiler_params=params(),
-        cost_estimate=cost(4 * rows * width * cols, 4 * rows * cols + 4 * width * cols),
-    )(side, hidden, weights, bias)
-
-
-def attend_kernel(heads, block, q_ref, kv_ref, code_ref, seg_ref, o_ref, keys, values, bias):
+        out_shape=[shape((2, block, padded), BF)] * 2 + [shape((1, block, padded), BF)] * 2,
+        compiler_params=params(60),
+        cost_estimate=cost(12 * block * width * padded, 12 * block * padded + 4 * width * padded),
+    )(side, full, own, got, weights, bias)
+
+
+MARKS = 16
+DEPTH = 128
+LSE_AT = HEAD_DIM + MARKS - 4
+STEEP = HEAD_DIM**-0.5 * LOG2E
+
+
+def split_three(values):
+    high = values.astype(BF)
+    rest = values - high.astype(F32)
+    middle = rest.astype(BF)
+    return jnp.concatenate([high, middle, (rest - middle.astype(F32)).astype(BF)], axis=1)
+
+
+def at_head(h, part, heads):
+    start = (part * heads + h) * HEAD_DIM
+    return slice(start, start + HEAD_DIM)
+
+
+def both_halves(first, second, columns):
+    return jnp.concatenate([first[0, :, columns], second[0, :, columns]], axis=0)
+
+
+def padded_columns(parts, width):
+    found = jnp.concatenate(parts, axis=1)
+    gap = width - found.shape[1]
+    return jnp.concatenate([found, jnp.zeros((found.shape[0], gap), found.dtype)], axis=1)
+
+
+def attend_kernel(
+    heads, first, second, qm_ref, km_ref, o_first, o_second, l_first, l_second, keys, values, queries
+):
     i = pl.program_id(1)
-    width = heads * HEAD_DIM
+
+    @pl.when((i == 0) & (pl.program_id(0) == 0))
+    def _():
+        keys[...] = jnp.zeros_like(keys)
+        queries[...] = jnp.zeros_like(queries)
 
     @pl.when(i == 0)
     def _():
         for h in range(heads):
-            at = h * HEAD_DIM
-            keys[h] = kv_ref[0, :, width + at : width + at + HEAD_DIM]
-            values[h] = kv_ref[0, :, 2 * width + at : 2 * width + at + HEAD_DIM]
-
-    for t in range(block // TILE):
-        code = code_ref[pl.ds(i * (block // TILE) + t, 1), :]
-        seg = seg_ref[pl.ds(i * block + t * TILE, TILE), :]
-        bias[t * TILE : (t + 1) * TILE, :] = jnp.where(code == seg, 0.0, MASKED_SCORE)
+            keys[h, :, :HEAD_DIM] = both_halves(first, second, at_head(h, 1, heads))
+            keys[h, :, HEAD_DIM : HEAD_DIM + MARKS] = km_ref[...]
+            value = both_halves(first, second, at_head(h, 2, heads))
+            values[h] = value.astype(F32).T.astype(BF)
+
+    for h in range(heads):
+        columns = at_head(h, 0, heads)
+        queries[h, :, :HEAD_DIM] = jnp.where(i == 0, first[0, :, columns], second[0, :, columns])
+        queries[h, :, HEAD_DIM : HEAD_DIM + MARKS] = qm_ref[...]
     parts = []
+    totals = []
+    probs = None
+    scores = contract_last(keys[0], queries[0])
     for h in range(heads):
-        query = q_ref[0, :, h * HEAD_DIM : (h + 1) * HEAD_DIM]
-        scores = contract_last(query, keys[h]) * (HEAD_DIM**-0.5 * LOG2E) + bias[...]
-        powers = jnp.exp2(scores - jnp.max(scores, axis=1, keepdims=True))
-        probs = powers * (1.0 / jnp.sum(powers, axis=1, keepdims=True))
-        parts.append(rows_by_columns(probs.astype(BF), values[h]).astype(BF))
-    o_ref[0] = jnp.concatenate(parts, axis=1)
-
-
-def attend(qkv, code, seg, block):
-    groups, _, cols = qkv.shape
-    length = code.shape[1]
-    heads = cols // (3 * HEAD_DIM)
-    width = heads * HEAD_DIM
+        later = contract_last(keys[h + 1], queries[h + 1]) if h + 1 < heads else None
+        top = jnp.max(scores, axis=0, keepdims=True)
+        powers = jnp.exp2((scores - top) * STEEP)
+        total = jnp.sum(powers, axis=0, keepdims=True)
+        totals.append(top + jnp.log2(total) * (1.0 / STEEP))
+        if h > 0:
+            parts.append(rows_by_columns(values[h - 1], probs).T.astype(BF))
+        probs = (powers * (1.0 / total)).astype(BF)
+        scores = later
+    parts.append(rows_by_columns(values[heads - 1], probs).T.astype(BF))
+    out = padded_columns(parts, o_first.shape[2])
+    log_totals = jnp.concatenate(totals, axis=0)
+
+    @pl.when(i == 0)
+    def _():
+        o_first[0] = out
+        l_first[0] = log_totals
+
+    @pl.when(i == 1)
+    def _():
+        o_second[0] = out
+        l_second[0] = log_totals
+
+
+def attend(first, second, query_marks, key_marks, out_width):
+    groups, half, padded = first.shape
+    heads = out_width // HEAD_DIM
+    pair = lambda *dims: pl.BlockSpec((1,) + dims, lambda a, i: (a, 0, 0))
     return pl.pallas_call(
-        partial(attend_kernel, heads, block),
-        grid=(groups, length // block),
+        partial(attend_kernel, heads),
+        grid=(groups, 2),
         in_specs=[
-            pl.BlockSpec((1, block, cols), lambda a, i: (a, i, 0)),
-            pl.BlockSpec((1, length, cols), lambda a, i: (a, 0, 0)),
-            pl.BlockSpec(code.shape, lambda a, i: (0, 0)),
-            pl.BlockSpec(seg.shape, lambda a, i: (0, 0)),
+            pair(half, padded),
+            pair(half, padded),
+            pl.BlockSpec((half, MARKS), lambda a, i: (i, 0)),
+            pl.BlockSpec((2 * half, MARKS), lambda a, i: (0, 0)),
         ],
-        out_specs=pl.BlockSpec((1, block, width), lambda a, i: (a, i, 0)),
-        out_shape=shape((groups, length, width), BF),
+        out_specs=[pair(half, out_width)] * 2 + [pair(heads, half)] * 2,
+        out_shape=[shape((groups, half, out_width), BF)] * 2 + [shape((groups, heads, half), F32)] * 2,
         scratch_shapes=[
-            pltpu.VMEM((heads, length, HEAD_DIM), BF),
-            pltpu.VMEM((heads, length, HEAD_DIM), BF),
-            pltpu.VMEM((block, length), F32),
+            pltpu.VMEM((heads, 2 * half, DEPTH), BF),
+            pltpu.VMEM((heads, HEAD_DIM, 2 * half), BF),
+            pltpu.VMEM((heads, half, DEPTH), BF),
         ],
         compiler_params=params(),
-        cost_estimate=cost(
-            groups * 16 * length * length * width,
-            groups * length * cols * 4,
-            groups * heads * length * length,
-        ),
-    )(qkv, qkv, code, seg)
+        cost_estimate=cost(groups * 15e9, groups * half * padded * 6, groups * heads * half * half),
+    )(first, second, query_marks, key_marks)
 
 
 def attend_back_kernel(
-    heads, block, qkv_ref, do_ref, code_ref, seg_ref, out_ref, keys, values, turned, dk, dv, bias
+    heads, first, second, do_first, do_second, l_first, l_second, qm_ref, km_ref,
+    out_first, out_second, keys, values, turned, queries, dk, dv,
 ):
     i = pl.program_id(1)
+    half, padded = first.shape[1:]
     width = heads * HEAD_DIM
     scaling = HEAD_DIM**-0.5
 
+    @pl.when((i == 0) & (pl.program_id(0) == 0))
+    def _():
+        keys[...] = jnp.zeros_like(keys)
+        queries[...] = jnp.zeros_like(queries)
+
     @pl.when(i == 0)
     def _():
         for h in range(heads):
-            at = h * HEAD_DIM
-            key = qkv_ref[0, :, width + at : width + at + HEAD_DIM]
-            keys[h] = key
+            key = both_halves(first, second, at_head(h, 1, heads))
+            keys[h, :, :HEAD_DIM] = key
+            keys[h, :, HEAD_DIM : HEAD_DIM + MARKS] = km_ref[...]
             turned[h] = key.astype(F32).T.astype(BF)
-            values[h] = qkv_ref[0, :, 2 * width + at : 2 * width + at + HEAD_DIM]
+            values[h] = both_halves(first, second, at_head(h, 2, heads))
         dk[...] = jnp.zeros_like(dk)
         dv[...] = jnp.zeros_like(dv)
 
-    for t in range(block // TILE):
-        tile = i * (block // TILE) + t
-        seg = seg_ref[pl.ds(tile, 1), :]
-        code = code_ref[pl.ds(tile, 1)].reshape(code_ref.shape[1:])
-        bias[:, t * TILE : (t + 1) * TILE] = jnp.where(code == seg, 0.0, MASKED_SCORE)
-    rows = pl.ds(pl.multiple_of(i * block, block), block)
+    log_totals = jnp.where(i == 0, l_first[0], l_second[0]).T
+    plain = []
+    for h in range(heads):
+        columns = at_head(h, 0, heads)
+        query = jnp.where(i == 0, first[0, :, columns], second[0, :, columns])
+        grad = jnp.where(i == 0, do_first[0, :, columns], do_second[0, :, columns])
+        queries[h, :, :HEAD_DIM] = query
+        queries[h, :, HEAD_DIM : HEAD_DIM + MARKS] = qm_ref[...]
+        queries[h, :, LSE_AT : LSE_AT + 3] = split_three(-log_totals[:, h : h + 1])
+        plain.append((query, grad))
+
+    def scores_of(h):
+        return contract_last(keys[h], queries[h]), contract_last(values[h], plain[h][1])
+
+    def finish(h, probs, grad_scores):
+        query, grad = plain[h]
+        dv[h] += rows_by_columns(probs, grad)
+        dk[h] += rows_by_columns(grad_scores, query)
+        return (rows_by_columns(turned[h], grad_scores) * scaling).T.astype(BF)
+
     parts = []
+    before = None
+    scores, grad_probs = scores_of(0)
     for h in range(heads):
-        query = qkv_ref[0, rows, h * HEAD_DIM : (h + 1) * HEAD_DIM]
-        grad = do_ref[0, rows, h * HEAD_DIM : (h + 1) * HEAD_DIM]
-        scores = contract_last(keys[h], query) * (scaling * LOG2E) + bias[...]
-        powers = jnp.exp2(scores - jnp.max(scores, axis=0, keepdims=True))
-        probs = powers * (1.0 / jnp.sum(powers, axis=0, keepdims=True))
-        grad_probs = contract_last(values[h], grad)
+        later = scores_of(h + 1) if h + 1 < heads else (None, None)
+        probs = jnp.exp2(scores * STEEP)
         centre = jnp.sum(probs * grad_probs, axis=0, keepdims=True)
         grad_scores = (probs * (grad_probs - centre)).astype(BF)
-        dv[h] += rows_by_columns(probs.astype(BF), grad)
-        dk[h] += rows_by_columns(grad_scores, query)
-        parts.append((rows_by_columns(turned[h], grad_scores) * scaling).T.astype(BF))
-    out_ref[0, rows, :width] = jnp.concatenate(parts, axis=1)
-
-    @pl.when(i == pl.num_programs(1) - 1)
-    def _():
-        out_ref[0, :, width:] = jnp.concatenate(
-            [(dk[h] * scaling).astype(BF) for h in range(heads)]
-            + [dv[h].astype(BF) for h in range(heads)],
-            axis=1,
-        )
-
-
-def attend_back(qkv, grad, code, seg, block):
-    groups, _, cols = qkv.shape
-    length = code.shape[1]
-    heads = cols // (3 * HEAD_DIM)
-    width = heads * HEAD_DIM
+        if before is not None:
+            parts.append(finish(h - 1, *before))
+        before = (probs.astype(BF), grad_scores)
+        scores, grad_probs = later
+    parts.append(finish(heads - 1, *before))
+    grad_queries = jnp.concatenate(parts, axis=1)
+
+    @pl.when(i == 0)
+    def _():
+        out_first[0, :, :width] = grad_queries
+
+    @pl.when(i == 1)
+    def _():
+        out_second[0, :, :width] = grad_queries
+        for start, ref in ((0, out_first), (half, out_second)):
+            rows = slice(start, start + half)
+            ref[0, :, width:] = padded_columns(
+                [(dk[h, rows] * scaling).astype(BF) for h in range(heads)]
+                + [dv[h, rows].astype(BF) for h in range(heads)],
+                padded - width,
+            )
+
+
+def attend_back(first, second, do_first, do_second, l_first, l_second, query_marks, key_marks):
+    groups, half, padded = first.shape
+    heads = l_first.shape[1]
+    out_width = do_first.shape[2]
+    pair = lambda *dims: pl.BlockSpec((1,) + dims, lambda a, i: (a, 0, 0))
     return pl.pallas_call(
-        partial(attend_back_kernel, heads, block),
-        grid=(groups, length // block),
-        in_specs=[
-            pl.BlockSpec((1, length, cols), lambda a, i: (a, 0, 0)),
-            pl.BlockSpec((1, length, width), lambda a, i: (a, 0, 0)),
-            pl.BlockSpec(code.shape, lambda a, i: (0, 0, 0)),
-            pl.BlockSpec(seg.shape, lambda a, i: (0, 0)),
+        partial(attend_back_kernel, heads),
+        grid=(groups, 2),
+        in_specs=[pair(half, padded)] * 2
+        + [pair(half, out_width)] * 2
+        + [pair(heads, half)] * 2
+        + [
+            pl.BlockSpec((half, MARKS), lambda a, i: (i, 0)),
+            pl.BlockSpec((2 * half, MARKS), lambda a, i: (0, 0)),
         ],
-        out_specs=pl.BlockSpec((1, length, cols), lambda a, i: (a, 0, 0)),
-        out_shape=shape((groups, length, cols), BF),
+        out_specs=[pair(half, padded)] * 2,
+        out_shape=[shape((groups, half, padded), BF)] * 2,
         scratch_shapes=[
-            pltpu.VMEM((heads, length, HEAD_DIM), BF),
-            pltpu.VMEM((heads, length, HEAD_DIM), BF),
-            pltpu.VMEM((heads, HEAD_DIM, length), BF),
-            pltpu.VMEM((heads, length, HEAD_DIM), F32),
-            pltpu.VMEM((heads, length, HEAD_DIM), F32),
-            pltpu.VMEM((length, block), F32),
+            pltpu.VMEM((heads, 2 * half, DEPTH), BF),
+            pltpu.VMEM((heads, 2 * half, HEAD_DIM), BF),
+            pltpu.VMEM((heads, HEAD_DIM, 2 * half), BF),
+            pltpu.VMEM((heads, half, DEPTH), BF),
+            pltpu.VMEM((heads, 2 * half, HEAD_DIM), F32),
+            pltpu.VMEM((heads, 2 * half, HEAD_DIM), F32),
         ],
-        compiler_params=params(58),
-        cost_estimate=cost(
-            groups * 32 * length * length * width,
-            groups * length * cols * 8,
-            groups * heads * length * length,
-        ),
-    )(qkv, grad, code, seg)
+        compiler_params=params(60),
+        cost_estimate=cost(groups * 12e9, groups * half * padded * 12, groups * heads * half * half),
+    )(first, second, do_first, do_second, l_first, l_second, query_marks, key_marks)
+
+
+def image_sums(hot_turned, values):
+    high = values.astype(BF)
+    low = (values - high.astype(F32)).astype(BF)
+    return rows_by_columns(hot_turned, high) + rows_by_columns(hot_turned, low)
+
+
+def add_up(ref, value):
+    @pl.when(pl.program_id(0) == 0)
+    def _():
+        ref[...] = value
+
+    @pl.when(pl.program_id(0) != 0)
+    def _():
+        ref[...] += value
+
+
+def third_of(first, second, own, other, i, per):
+    half = jnp.stack([own[0], other[0]], axis=0)
+    return jnp.where(i < per, first[...], jnp.where(i < 2 * per, second[...], half))
+
+
+def third_specs(block, columns, per):
+    full = lambda low: pl.BlockSpec(
+        (2, block, columns), lambda i, y: (0, jnp.clip(i - low * per, 0, per - 1), 0)
+    )
+    single = pl.BlockSpec((1, block, columns), lambda i, y: (0, jnp.clip(i - 2 * per, 0, per - 1), 0))
+    return [full(0), full(1), single, single]
+
+
+def out_weight_specs(width, columns):
+    last = columns // (2 * width // 3) - 1
+    return [
+        pl.BlockSpec((1, width, 2 * width // 3), lambda i, y: (y[0], 0, last)),
+        pl.BlockSpec((1, width, 2 * width // 3), lambda i, y: (1 - y[0], 0, last)),
+    ]
 
 
 def middle_kernel(
-    side, tok_ref, dy_ref, full_ref, half_ref, w_own, w_other, b_ref, hot_ref, parts_ref, perm_ref,
+    side, tok_ref, dy_ref, first, second, own, other, w_own, w_other, b_ref, hot_ref, parts_ref, perm_ref,
     branch_ref, h_ref, g_ref, ht_ref, gt_ref, gb_ref,
 ):
     i = pl.program_id(0)
     width = tok_ref.shape[1]
-    att = jnp.where(i < 2, full_ref[...], half_ref[...])
-    branch = contract_last(att[0], w_own[0]) + contract_last(att[1], w_other[0]) + b_ref[...]
+    used = width // 2
+    att = third_of(first, second, own, other, i, pl.num_programs(0) // 3)[:, :, :used]
+    skip = w_own.shape[2] - used
+    branch = (
+        contract_last(att[0], w_own[0, :, skip:])
+        + contract_last(att[1], w_other[0, :, skip:])
+        + b_ref[...]
+    )
     branch_ref[...] = branch
     hot = hot_ref[...]
     gate = rows_by_columns(hot, parts_ref[0, :, 2 * width :])
@@ -603,22 +747,16 @@
     g_ref[...] = grad
     ht_ref[...] = contract_last(perm_ref[...], hidden).astype(BF)
     gt_ref[...] = contract_last(perm_ref[...], grad).astype(BF)
-    total = jnp.sum(grad.astype(F32), axis=0, keepdims=True)
-
-    @pl.when(i == 0)
-    def _():
-        gb_ref[...] = total
-
-    @pl.when(i != 0)
-    def _():
-        gb_ref[...] += total
-
-
-def middle_part(side, tokens, cotangent, full, half, w_out, b_out, hot, parts, perm, block):
+    add_up(gb_ref, jnp.sum(grad.astype(F32), axis=0, keepdims=True))
+
+
+def middle_part(side, tokens, cotangent, thirds, weights, b_out, hot, parts, perm, block):
     rows, width = tokens.shape
-    cols = full.shape[2]
+    per = rows // 3 // block
     spec = lambda dims: pl.BlockSpec(dims, lambda i, y: (0,) * len(dims))
-    placed = pl.BlockSpec((block, width), lambda i, y: ((i + y[0]) % 3, 0))
+    placed = pl.BlockSpec(
+        (block, width), lambda i, y: (((i // per + y[0]) % 3) * per + i % per, 0)
+    )
     plain = pl.BlockSpec((block, width), lambda i, y: (i, 0))
     turned = pl.BlockSpec((width, block), lambda i, y: (0, i))
     return pl.pallas_call(
@@ -629,10 +767,8 @@
             in_specs=[
                 placed,
                 placed,
-                pl.BlockSpec((2, block, cols), lambda i, y: (0, jnp.minimum(i, 1), 0)),
-                spec((2, block, cols)),
-                pl.BlockSpec((1, width, cols), lambda i, y: (y[0], 0, 0)),
-                pl.BlockSpec((1, width, cols), lambda i, y: (1 - y[0], 0, 0)),
+                *third_specs(block, thirds[0].shape[2], per),
+                *out_weight_specs(width, weights.shape[2]),
                 spec((1, width)),
                 pl.BlockSpec((block, hot.shape[1]), lambda i, y: (i, 0)),
                 spec(parts.shape),
@@ -650,18 +786,18 @@
         ],
         compiler_params=params(),
         cost_estimate=cost(2 * rows * width * (3 * width + 1024), rows * width * 22),
-    )(side, tokens, cotangent, full, half, w_out, w_out, b_out, hot, parts, perm)
+    )(side, tokens, cotangent, *thirds, weights, weights, b_out, hot, parts, perm)
 
 
 def feed_kernel(
     chunk, pick, h_ref, g_ref, ht_ref, gt_ref, up_ref, down_ref, bias_ref,
-    branch_ref, back_ref, mine_ref, theirs_ref, gb_ref, act, pre,
+    branch_ref, back_ref, mine_ref, near_ref, far_ref, gb_ref, act, pre,
 ):
     j = pl.program_id(0)
     rows = h_ref.shape[0]
     half = ht_ref.shape[0] // 2
-    up = up_ref[0]
-    down = down_ref[0]
+    up = up_ref[0, 0]
+    down = down_ref[0, 0]
     total = jnp.zeros(gb_ref.shape, F32)
     for start in range(0, rows, chunk):
         at = slice(start, start + chunk)
@@ -690,18 +826,20 @@
             back_ref[at] += back_part
 
     gb_ref[...] = total
-    mine_ref[0] = rows_by_columns(ht_ref[:half], pre[...])
-    theirs_ref[0] = rows_by_columns(ht_ref[half:], pre[...]).astype(BF)
-    mine_ref[1] = rows_by_columns(gt_ref[:half], act[...])
-    theirs_ref[1] = rows_by_columns(gt_ref[half:], act[...]).astype(BF)
-
-
-def feed(pick, hidden, grad, hidden_turned, grad_turned, up, down, bias, chunk, cols):
+    quarter = half // 2
+    for k, (turned, value) in enumerate(((ht_ref, pre), (gt_ref, act))):
+        theirs = rows_by_columns(turned[half:], value[...]).astype(BF)
+        near_ref[k] = theirs[:quarter]
+        far_ref[k] = theirs[quarter:]
+        mine_ref[k] = rows_by_columns(turned[:half], value[...])
+
+
+def feed(pick, hidden, grad, hidden_turned, grad_turned, weights, bias, chunk, cols):
     rows, width = hidden.shape
-    units = up.shape[2]
+    units = weights.shape[3]
     half = width // 2
     whole = lambda dims: pl.BlockSpec(dims, lambda j, y: (0, 0), pipeline_mode=pl.Buffered(1))
-    columns = pl.BlockSpec((1, width, cols), lambda j, y: (y[0], 0, j))
+    columns = lambda k: pl.BlockSpec((1, 1, width, cols), lambda j, y: (k, y[0], 0, j))
     return pl.pallas_call(
         partial(feed_kernel, chunk),
         grid_spec=pltpu.PrefetchScalarGridSpec(
@@ -712,15 +850,16 @@
                 whole((rows, width)),
                 whole((width, rows)),
                 whole((width, rows)),
-                columns,
-                columns,
+                columns(0),
+                columns(1),
                 pl.BlockSpec((1, 1, cols), lambda j, y: (y[0], 0, j)),
             ],
             out_specs=[
                 whole((rows, width)),
                 whole((rows, width)),
                 pl.BlockSpec((2, half, cols), lambda j, y: (0, 0, j)),
-                pl.BlockSpec((2, half, cols), lambda j, y: (0, 0, j)),
+                pl.BlockSpec((2, half // 2, cols), lambda j, y: (0, 0, j)),
+                pl.BlockSpec((2, half // 2, cols), lambda j, y: (0, 0, j)),
                 pl.BlockSpec((1, cols), lambda j, y: (0, j)),
             ],
             scratch_shapes=[pltpu.VMEM((rows, cols), BF), pltpu.VMEM((rows, cols), BF)],
@@ -729,35 +868,21 @@
             shape((rows, width), F32),
             shape((rows, width), F32),
             shape((2, half, units), F32),
-            shape((2, half, units), BF),
+            shape((2, half // 2, units), BF),
+            shape((2, half // 2, units), BF),
             shape((1, units), F32),
         ],
         compiler_params=params(60),
         cost_estimate=cost(
             12 * rows * width * units, rows * width * 16 + width * units * 10, rows * units
         ),
-    )(pick, hidden, grad, hidden_turned, grad_turned, up, down, bias)
-
-
-def image_sums(hot_turned, values):
-    high = values.astype(BF)
-    low = (values - high.astype(F32)).astype(BF)
-    return rows_by_columns(hot_turned, high) + rows_by_columns(hot_turned, low)
-
-
-def add_up(ref, value):
-    @pl.when(pl.program_id(0) == 0)
-    def _():
-        ref[...] = value
-
-    @pl.when(pl.program_id(0) != 0)
-    def _():
-        ref[...] += value
+    )(pick, hidden, grad, hidden_turned, grad_turned, weights, weights, bias)
 
 
 def back_two_kernel(
     side, tok_ref, dy_ref, branch_ref, two_a, two_b, b_ref, back_a, back_b, w_own, w_other, hot_ref,
-    turn_ref, parts_ref, perm_ref, out_ref, middle_ref, gt_ref, att_ref, sums_ref, gb_ref,
+    turn_ref, parts_ref, perm_ref, first, second, half_own, half_other, out_ref, middle_ref, a_first, a_second,
+    a_own, a_other, sums_ref, gb_ref, mine_ref, theirs_ref, outer_ref,
 ):
     width = tok_ref.shape[1]
     hot = hot_ref[...]
@@ -774,9 +899,42 @@
     grad_middle = dy + norm_back(normed, inverse, grad_hidden * (1.0 + mod[:, width : 2 * width]))
     middle_ref[...] = grad_middle
     grad = (grad_middle * gate).astype(BF)
-    gt_ref[...] = contract_last(perm_ref[...], grad).astype(BF)
-    att_ref[0] = rows_by_columns(grad, w_own[0]).astype(BF)
-    att_ref[1] = rows_by_columns(grad, w_other[0]).astype(BF)
+    turned = contract_last(perm_ref[...], grad).astype(BF)
+    att = third_of(first, second, half_own, half_other, pl.program_id(0), pl.num_programs(0) // 3)
+    for k in range(2):
+        product = rows_by_columns(turned, att[k])
+
+        @pl.when(pl.program_id(0) == 0)
+        def _():
+            outer_ref[k] = product
+
+        @pl.when(pl.program_id(0) != 0)
+        def _():
+            outer_ref[k] += product
+
+    @pl.when(pl.program_id(0) == pl.num_programs(0) - 1)
+    def _():
+        for k in range(2):
+            mine_ref[k] = outer_ref[k, : width // 2]
+            theirs_ref[k] = outer_ref[k, width // 2 :].astype(BF)
+
+    skip = w_own.shape[2] - width // 2
+    ours = padded_columns([rows_by_columns(grad, w_own[0, :, skip:]).astype(BF)], a_own.shape[2])
+    theirs = padded_columns([rows_by_columns(grad, w_other[0, :, skip:]).astype(BF)], a_own.shape[2])
+    i = pl.program_id(0)
+    per = pl.num_programs(0) // 3
+    for k, ref in enumerate((a_first, a_second)):
+
+        @pl.when(i // per == k)
+        def _(ref=ref):
+            ref[0] = ours
+            ref[1] = theirs
+
+    @pl.when(i // per == 2)
+    def _():
+        a_own[0] = ours
+        a_other[0] = theirs
+
     sums = [
         image_sums(turn, grad_middle * branch),
         image_sums(turn, grad_hidden),
@@ -788,11 +946,11 @@
 
 
 def back_two(
-    side, tokens, cotangent, branch, two_a, two_b, b_down, back_a, back_b, w_out, hot, turn, parts, perm,
-    block, images,
+    side, tokens, cotangent, branch, two_a, two_b, b_down, back_a, back_b, weights, hot, turn, parts, perm,
+    attended, block, images, out_width,
 ):
     rows, width = tokens.shape
-    cols = w_out.shape[2]
+    third = rows // 3
     per = rows // 3 // block
     spec = lambda dims: pl.BlockSpec(dims, lambda i, y: (0,) * len(dims))
     placed = pl.BlockSpec(
@@ -813,87 +971,82 @@
                 spec((1, width)),
                 plain,
                 plain,
-                pl.BlockSpec((1, width, cols), lambda i, y: (y[0], 0, 0)),
-                pl.BlockSpec((1, width, cols), lambda i, y: (1 - y[0], 0, 0)),
+                *out_weight_specs(width, weights.shape[2]),
                 pl.BlockSpec((block, hot.shape[1]), lambda i, y: (i, 0)),
                 pl.BlockSpec((images, block), lambda i, y: (0, i)),
                 spec(parts.shape),
                 spec(perm.shape),
+                *third_specs(block, out_width, per),
             ],
             out_specs=[
                 placed,
                 plain,
-                pl.BlockSpec((width, block), lambda i, y: (0, i)),
-                pl.BlockSpec((2, block, cols), lambda i, y: (0, i, 0)),
+                *third_specs(block, out_width, per),
                 spec((4, images, width)),
                 spec((1, width)),
+                spec((2, width // 2, out_width)),
+                spec((2, width // 2, out_width)),
             ],
+            scratch_shapes=[pltpu.VMEM((2, width, out_width), F32)],
         ),
         out_shape=[
             shape((rows, width), BF),
             shape((rows, width), F32),
-            shape((width, rows), BF),
-            shape((2, rows, cols), BF),
+            *[shape((2, third, out_width), BF)] * 2,
+            *[shape((1, third, out_width), BF)] * 2,
             shape((4, images, width), F32),
             shape((1, width), F32),
+            shape((2, width // 2, out_width), F32),
+            shape((2, width // 2, out_width), BF),
         ],
-        compiler_params=params(),
-        cost_estimate=cost(2 * rows * width * (3 * width + 1024), rows * width * 34),
-    )(side, tokens, cotangent, branch, two_a, two_b, b_down, back_a, back_b, w_out, w_out, hot, turn, parts, perm)
-
-
-def outer_kernel(ht_ref, full_ref, half_ref, mine_ref, theirs_ref, sums_ref):
-    length = full_ref.shape[1]
-    side = mine_ref.shape[1]
-    full = full_ref[0]
-    rest = half_ref[0]
-
-    def product(start):
-        at = slice(start, start + side)
-        return rows_by_columns(ht_ref[at, :length], full) + rows_by_columns(
-            ht_ref[at, length:], rest
-        )
-
-    mine_ref[0] = product(0)
-    theirs_ref[0] = product(side).astype(BF)
-    sums_ref[0] = jnp.sum(full.astype(F32), axis=0, keepdims=True) + jnp.sum(
-        rest.astype(F32), axis=0, keepdims=True
-    )
-
-
-def outer(turned, full, half):
+        compiler_params=params(62),
+        cost_estimate=cost(2 * rows * width * (4 * width + 1024), rows * width * 34),
+    )(side, tokens, cotangent, branch, two_a, two_b, b_down, back_a, back_b, weights, weights, hot, turn, parts, perm, *attended)
+
+
+def outer_kernel(ht_ref, first, second, rest, mine_ref, theirs_ref, sums_ref):
+    third = first.shape[1]
+    grads = (first[0], second[0], rest[0])
+    found = sum(
+        rows_by_columns(ht_ref[:, k * third : (k + 1) * third], grad)
+        for k, grad in enumerate(grads)
+    )
+
+    @pl.when(pl.program_id(0) == 0)
+    def _():
+        theirs_ref[...] = found.astype(BF)
+        sums_ref[...] = sum(jnp.sum(grad.astype(F32), axis=0, keepdims=True) for grad in grads)
+
+    @pl.when(pl.program_id(0) == 1)
+    def _():
+        mine_ref[...] = found
+
+
+def outer(turned, first, second, rest, group):
     width, rows = turned.shape
-    _, length, cols = full.shape
-    side = width // 2
-    block = pl.BlockSpec((1, side, cols), lambda a: (a, 0, 0))
+    _, third, cols = first.shape
+    block = pl.BlockSpec((width // 2, cols), lambda k: (0, 0))
+    pair = pl.BlockSpec((1, third, cols), lambda k: (group, 0, 0))
+    single = pl.BlockSpec((1, third, cols), lambda k: (0, 0, 0))
     return pl.pallas_call(
         outer_kernel,
         grid=(2,),
-        in_specs=[
-            pl.BlockSpec((width, rows), lambda a: (0, 0)),
-            pl.BlockSpec((1, length, cols), lambda a: (a, 0, 0)),
-            pl.BlockSpec((1, half.shape[1], cols), lambda a: (a, 0, 0)),
-        ],
-        out_specs=[block, block, pl.BlockSpec((1, 1, cols), lambda a: (a, 0, 0))],
-        out_shape=[
-            shape((2, side, cols), F32),
-            shape((2, side, cols), BF),
-            shape((2, 1, cols), F32),
-        ],
+        in_specs=[pl.BlockSpec((width // 2, rows), lambda k: (1 - k, 0)), pair, pair, single],
+        out_specs=[block, block, pl.BlockSpec((1, cols), lambda k: (0, 0))],
+        out_shape=[shape((width // 2, cols), F32), shape((width // 2, cols), BF), shape((1, cols), F32)],
         compiler_params=params(60),
-        cost_estimate=cost(4 * rows * width * cols, rows * width * 2 + rows * cols * 4),
-    )(turned, full, half)
+        cost_estimate=cost(2 * rows * width * cols, rows * width * 2 + rows * cols * 4),
+    )(turned, first, second, rest)
 
 
 def back_one_kernel(
-    side, full_ref, half_ref, w_own, w_other, tok_ref, middle_ref, hot_ref, turn_ref, parts_ref,
+    side, first, second, own, other, w_own, w_other, tok_ref, middle_ref, hot_ref, turn_ref, parts_ref,
     out_ref, sums_ref,
 ):
-    i = pl.program_id(0)
     width = tok_ref.shape[1]
-    cols = full_ref.shape[2]
+    cols = 3 * width // 2
     scale = rows_by_columns(hot_ref[...], parts_ref[0, :, width : 2 * width])
-    grads = jnp.where(i < 2 * pl.num_programs(0) // 3, full_ref[...], half_ref[...])
+    grads = third_of(first, second, own, other, pl.program_id(0), pl.num_programs(0) // 3)[:, :, :cols]
     grad_hidden = contract_last(grads[0], w_own[0, :, :cols]) + contract_last(
         grads[1], w_other[0, :, :cols]
     )
@@ -904,9 +1057,9 @@
     add_up(sums_ref, jnp.stack(sums, axis=0))
 
 
-def back_one(side, full, half, weights, tokens, middle, hot, turn, parts, block, images):
+def back_one(side, thirds, weights, tokens, middle, hot, turn, parts, block, images):
     rows, width = tokens.shape
-    cols = full.shape[2]
+    cols = thirds[0].shape[2]
     per = rows // 3 // block
     spec = lambda dims: pl.BlockSpec(dims, lambda i, y: (0,) * len(dims))
     once = pl.Buffered(1)
@@ -919,8 +1072,7 @@
             num_scalar_prefetch=1,
             grid=(rows // block,),
             in_specs=[
-                pl.BlockSpec((2, block, cols), lambda i, y: (0, jnp.minimum(i, 2 * per - 1), 0)),
-                pl.BlockSpec((2, block, cols), lambda i, y: (0, jnp.maximum(i - 2 * per, 0), 0)),
+                *third_specs(block, cols, per),
                 pl.BlockSpec(
                     (1,) + weights.shape[1:], lambda i, y: (y[0], 0, 0), pipeline_mode=once
                 ),
@@ -938,7 +1090,7 @@
         out_shape=[shape((rows, width), F32), shape((2, images, width), F32)],
         compiler_params=params(),
         cost_estimate=cost(4 * rows * width * cols, rows * width * 10 + rows * cols * 4),
-    )(side, full, half, weights, weights, tokens, middle, hot, turn, parts)
+    )(side, *thirds, weights, weights, tokens, middle, hot, turn, parts)
 
 
 def fast_body(mesh):
@@ -994,16 +1146,19 @@
         cols = w_query.shape[1]
 
         attention_shard = jnp.concatenate([w_query, w_key, w_value, w_out], axis=1).astype(BF)
-        gather = lambda v: lax.all_gather(v, ("heads", "rows"), axis=0, tiled=True).reshape(
-            2, width, v.shape[1]
-        )
-        attention_weights = gather(attention_shard)
-        up = gather(w_up.astype(BF))
-        down = gather(w_down.astype(BF))
-        all_conditions = lax.all_gather(condition, "rows", axis=0, tiled=True)
+        attention_weights = lax.all_gather(
+            attention_shard, ("heads", "rows"), axis=0, tiled=True
+        ).reshape(2, width, attention_shard.shape[1])
+        feed_weights = lax.all_gather(
+            jnp.stack([w_up, w_down]).astype(BF), ("heads", "rows"), axis=1, tiled=True
+        ).reshape(2, 2, width, units)
 
         cond = condition.astype(F32)
         mod_cols = jnp.dot(jax.nn.silu(cond), w_ada, precision=PRECISE) + b_ada
+        flat = jnp.stack([condition] + [send(condition, to_level[k]) for k in range(1, levels)])
+        flat = jnp.concatenate([flat, send(flat, to_x)], axis=0)
+        flat = jnp.concatenate([flat, send(flat, to_core)], axis=0)
+        silu_all = jax.nn.silu(flat.reshape(ring * images, width).astype(F32))
         biases = jnp.concatenate([b_up, b_query, b_value])[None]
         spread = lax.all_gather(jnp.concatenate([mod_cols, biases], axis=0)[None], "heads", axis=0, tiled=True)
         parts = three_parts(spread[:, :images])
@@ -1017,13 +1172,20 @@
             axis=2,
         )
 
+        tiles = length // TILE
         tile_of = jnp.arange(length, dtype=jnp.int32) // TILE
-        tiles = length // TILE
-
-        def pattern(seg, tiles_on):
+        slots = image_index.shape[1]
+
+        def marks_of(seg, tiles_on):
+            own_slot = seg[:, None] == jnp.arange(slots, dtype=jnp.int32)[None, :]
             on = (tiles_on > 0) | jnp.eye(tiles, dtype=bool)
-            code = jnp.where(jnp.repeat(on, TILE, axis=1), seg[None, :], -1)
-            return (code, seg[:, None]), (code[:, :, None], seg.reshape(tiles, TILE))
+            own_tile = tile_of[:, None] == jnp.arange(tiles, dtype=jnp.int32)[None, :]
+            open_to = jnp.broadcast_to(on.T[:, None, :], (tiles, TILE, tiles)).reshape(length, tiles)
+            ends = jnp.zeros((length, MARKS - slots - tiles), F32)
+            query = jnp.concatenate([own_slot, own_tile, ends], axis=1).astype(BF)
+            seen = jnp.concatenate([own_slot, open_to], axis=1)
+            key = jnp.concatenate([jnp.where(seen, 0.0, MASKED_SCORE), ends + 1.0], axis=1).astype(BF)
+            return query, key
 
         seg_full = lax.dynamic_index_in_dim(segment_ids, 2 * y, 0, keepdims=False)
         tile_full = lax.dynamic_index_in_dim(tile_mask, 2 * y, 0, keepdims=False)
@@ -1032,12 +1194,12 @@
         tile_half = jnp.where(
             y == 0, tile_mask[1], jnp.roll(tile_mask[1], (-shift, -shift), axis=(0, 1))
         )
-        full_on, full_back_on = pattern(seg_full, tile_full)
-        half_on, half_back_on = pattern(seg_half, tile_half)
+        marks_full = marks_of(seg_full, tile_full)
+        marks_half = marks_of(seg_half, tile_half)
 
         def image_of(seg, index):
-            slots = jnp.arange(index.shape[0], dtype=jnp.int32)
-            return jnp.sum(jnp.where(seg[:, None] == slots[None, :], index[None, :], 0), axis=1)
+            slot = jnp.arange(slots, dtype=jnp.int32)
+            return jnp.sum(jnp.where(seg[:, None] == slot[None, :], index[None, :], 0), axis=1)
 
         own_image = jnp.concatenate(
             [
@@ -1056,93 +1218,153 @@
         feature = (owner[:, None] * piece + jnp.arange(piece, dtype=jnp.int32)[None, :]).reshape(-1)
         perm = (feature[:, None] == jnp.arange(width, dtype=jnp.int32)[None, :]).astype(BF)
 
-        hidden_one, hidden_one_turned = first_norm(side, tokens, hot, parts, perm, third)
-        qkv = project(side, hidden_one, attention_weights, qkv_bias, third)
-        qkv_got = send(qkv[1, 2 * third :], to_heads)
-        attended_full = attend(qkv, *full_on, third)
-        qkv_shared = jnp.concatenate([qkv[0, 2 * third :], qkv_got], axis=0)[None]
-        attended_shared = attend(qkv_shared, *half_on, third)
-        attended_got = send(attended_shared[0, third:], to_heads)
-        attended_half = jnp.stack([attended_shared[0, :third], attended_got])
-        w_out_all = attention_weights[:, :, 3 * cols :]
+        padded = -(-3 * cols // 128) * 128
+        out_width = -(-cols // 128) * 128
+        hidden_full, hidden_half, hidden_one_turned = first_norm(side, tokens, hot, parts, perm, third)
+        hidden_got = send(hidden_half, to_heads)
+        qkv_first, qkv_second, qkv_own, qkv_got = project(
+            side, hidden_full, hidden_half, hidden_got, attention_weights, qkv_bias, padded
+        )
+        qkv_full = (qkv_first, qkv_second)
+        qkv_half = (qkv_own, qkv_got)
+        out_own, out_theirs, *lse_half = attend(*qkv_half, *marks_half, out_width)
+        out_other = send(out_theirs, to_heads)
+        qkv_first, out_own = lax.optimization_barrier((qkv_first, out_own))
+        out_first, out_second, *lse_full = attend(qkv_first, qkv_second, *marks_full, out_width)
+        attended = (out_first, out_second, out_own, out_other)
         branch_one, hidden_two, grad_two, hidden_two_turned, grad_two_turned, grad_b_down = middle_part(
-            side, tokens, cotangent, attended_full, attended_half, w_out_all, b_out[None], hot, parts, perm, third
-        )
-
-        feed_args = (hidden_two, grad_two, hidden_two_turned, grad_two_turned, up, down, up_bias)
-        two_b, back_b, feed_mine_b, feed_theirs_b, grad_b_up_b = feed(1 - side, *feed_args, third, 768)
-        two_a, back_a, feed_mine_a, feed_theirs_a, grad_b_up_a = feed(side, *feed_args, third, 768)
-
-        def over_cores(mine, theirs):
-            return mine + send(theirs, to_core).astype(F32)
-
-        def over_plane(own_side, other_side):
-            count = own_side.shape[-2] // 2
-            near, far = own_side[..., :count, :], own_side[..., count:, :].astype(BF)
-            over, corner = other_side[..., :count, :].astype(BF), other_side[..., count:, :].astype(BF)
+            side, tokens, cotangent, attended, attention_weights, b_out[None], hot, parts, perm, third // 2
+        )
+
+        def added(mine, got):
+            return mine + got.astype(F32)
+
+        def level_pieces(values):
+            part = lambda k: values[..., k * piece : (k + 1) * piece, :]
+            return part(0), *(part(k).astype(BF) for k in range(1, levels))
+
+        def all_added(kept, got):
+            for part in got:
+                kept = added(kept, part)
+            return kept
+
+        def after(value, *others):
+            return lax.optimization_barrier((value, *others))
+
+        quarter = width // 4
+
+        def plane_pieces(mine_own, got_own, mine_other, got_other):
+            near = lambda mine, got: added(mine[:quarter], got[:quarter])
+            far = lambda mine, got: added(mine[quarter:], got[quarter:]).astype(BF)
             return (
-                near
-                + send(far, to_x).astype(F32)
-                + send(over, to_heads).astype(F32)
-                + send(corner, to_corner).astype(F32)
+                near(mine_own, got_own),
+                far(mine_own, got_own),
+                near(mine_other, got_other).astype(BF),
+                far(mine_other, got_other),
             )
 
-        def over_levels(values):
-            total = values[..., :piece, :]
-            for k in range(1, levels):
-                part = values[..., k * piece : (k + 1) * piece, :].astype(BF)
-                total = total + send(part, to_level[k]).astype(F32)
-            return total
-
-        feed_b = over_cores(feed_mine_b, feed_theirs_b)
-        feed_a = over_cores(feed_mine_a, feed_theirs_a)
-        grad_w_up, grad_w_down = over_levels(over_plane(feed_a, feed_b))
-
-        output, grad_middle, grad_one_turned, grad_attended, sums_two, grad_b_out = back_two(
-            side, tokens, cotangent, branch_one, two_a, two_b, b_down[None], back_a, back_b, w_out_all, hot, turn, parts,
-            perm, third // 2, images,
-        )
-        grad_attended_got = send(grad_attended[1, 2 * third :], to_heads)
-        out_mine, out_theirs, _ = outer(grad_one_turned, attended_full, attended_half)
-        out_sum = over_cores(out_mine, out_theirs)
-        grad_w_out = over_levels(over_plane(out_sum[0], out_sum[1]))
-        grad_qkv_full = attend_back(qkv, grad_attended, *full_back_on, third)
-        shared_grad = jnp.concatenate([grad_attended[0, 2 * third :], grad_attended_got], axis=0)[None]
-        grad_qkv_shared = attend_back(qkv_shared, shared_grad, *half_back_on, third)
-        grad_qkv_got = send(grad_qkv_shared[0, third:], to_heads)
-        grad_qkv_half = jnp.stack([grad_qkv_shared[0, :third], grad_qkv_got])
-        qkv_mine, qkv_theirs, grad_qkv_bias = outer(hidden_one_turned, grad_qkv_full, grad_qkv_half)
-        qkv_sum = over_cores(qkv_mine, qkv_theirs)
-        grad_w_qkv = over_levels(over_plane(qkv_sum[0], qkv_sum[1]))
-        grad_tokens, sums_one = back_one(
-            side, grad_qkv_full, grad_qkv_half, attention_weights, tokens, grad_middle, hot, turn, parts,
-            third // 2, images,
-        )
+        feed_args = (hidden_two_turned, grad_two_turned, feed_weights, up_bias, third, 768)
+        two_b, back_b, mine_b, near_b, far_b, grad_b_up_b = feed(
+            1 - side, hidden_two, grad_two, *feed_args
+        )
+        far_b = added(mine_b[:, quarter:], send(far_b, to_core)).astype(BF)
+        hidden_two, far_b, near_b = after(hidden_two, far_b, near_b)
+        two_a, back_a, mine_a, near_a, far_a, grad_b_up_a, near_b, far_b = after(
+            *feed(side, hidden_two, grad_two, *feed_args),
+            send(near_b, to_core),
+            send(far_b, to_x),
+        )
+        over_b = added(added(mine_b[:, :quarter], near_b), far_b).astype(BF)
+        far_a = added(mine_a[:, quarter:], send(far_a, to_core)).astype(BF)
+        two_a, over_b, far_a, near_a = after(two_a, over_b, far_a, near_a)
+
+        output, grad_middle, *grad_attended, sums_two, grad_b_out, out_mine, out_theirs_sum, over_b, far_a, near_a = after(
+            *back_two(
+                side, tokens, cotangent, branch_one, two_a, two_b, b_down[None], back_a, back_b, attention_weights,
+                hot, turn, parts, perm, attended, third // 2, images, out_width,
+            ),
+            send(over_b, to_heads),
+            send(far_a, to_x),
+            send(near_a, to_core),
+        )
+        grad_first, grad_second, grad_own, grad_theirs = grad_attended
+        grad_other = send(grad_theirs, to_heads)
+        out_got = send(out_theirs_sum, to_core)
+        out_pieces = plane_pieces(out_mine[0], out_got[0], out_mine[1], out_got[1])
+        feed_kept, *feed_sent = level_pieces(
+            added(added(added(mine_a[:, :quarter], near_a), far_a), over_b)
+        )
+        grad_own, feed_kept, *joined = after(grad_own, feed_kept, *feed_sent, *out_pieces)
+        feed_sent, out_pieces = joined[: levels - 1], joined[levels - 1 :]
+        grad_qkv_own, grad_qkv_theirs, *out_pieces = after(
+            *attend_back(*qkv_half, grad_own, grad_other, *lse_half, *marks_half),
+            out_pieces[0],
+            send(out_pieces[1], to_x),
+            send(out_pieces[2], to_heads),
+            send(out_pieces[3], to_corner),
+        )
+        out_kept, *out_sent = level_pieces(
+            added(added(added(out_pieces[0], out_pieces[1]), out_pieces[2]), out_pieces[3])
+        )
+        grad_first, grad_qkv_theirs, feed_kept, out_kept, *joined = after(
+            grad_first, grad_qkv_theirs, feed_kept, out_kept, *feed_sent, *out_sent
+        )
+        grad_qkv_first, grad_qkv_second, grad_qkv_other, *got = after(
+            *attend_back(*qkv_full, grad_first, grad_second, *lse_full, *marks_full),
+            send(grad_qkv_theirs, to_heads),
+            *(send(part, to_level[k % (levels - 1) + 1]) for k, part in enumerate(joined)),
+        )
+        grad_w_up, grad_w_down = all_added(feed_kept, got[: levels - 1])
+        grad_w_out = all_added(out_kept, got[levels - 1 :])
+        qkv_mine_b, qkv_theirs_b, grad_qkv_bias_b = outer(
+            hidden_one_turned, grad_qkv_first, grad_qkv_second, grad_qkv_other, 1
+        )
+        hidden_one_turned, qkv_theirs_b = after(hidden_one_turned, qkv_theirs_b)
+        qkv_mine_a, qkv_theirs_a, grad_qkv_bias_a, qkv_got_b = after(
+            *outer(hidden_one_turned, grad_qkv_first, grad_qkv_second, grad_qkv_own, 0),
+            send(qkv_theirs_b, to_core),
+        )
+        near, *sent = plane_pieces(qkv_mine_a, send(qkv_theirs_a, to_core), qkv_mine_b, qkv_got_b)
+        grad_middle, near, *sent = after(grad_middle, near, *sent)
+        grad_qkv = (grad_qkv_first, grad_qkv_second, grad_qkv_own, grad_qkv_other)
+        grad_tokens, sums_one, *got = after(
+            *back_one(
+                side, grad_qkv, attention_weights, tokens, grad_middle, hot, turn, parts, third // 2, images
+            ),
+            send(sent[0], to_x),
+            send(sent[1], to_heads),
+            send(sent[2], to_corner),
+        )
+        qkv_kept, *qkv_sent = level_pieces(all_added(near, got))
 
         sums = jnp.concatenate([sums_one, sums_two], axis=0).reshape(2, 3, images, width)
         sums = sums.transpose(0, 2, 1, 3).reshape(2, images, 3 * width)
-        grad_b_qkv = grad_qkv_bias[:, 0]
         narrow = jnp.concatenate([grad_b_out, grad_b_down], axis=0).reshape(2, 2, cols)
 
         def packet(which, up_sum, qkv_sum):
-            first = jnp.concatenate([up_sum[0], qkv_sum[:cols], qkv_sum[2 * cols :]])
+            first = jnp.concatenate([up_sum[0], qkv_sum[:cols], qkv_sum[2 * cols : 3 * cols]])
             second = lax.dynamic_index_in_dim(narrow, which, 1, keepdims=False).reshape(-1)
             second = jnp.concatenate([second, jnp.zeros((3 * width - 2 * cols,), F32)])
             chunk = lax.dynamic_index_in_dim(sums, which, 0, keepdims=False)
             return jnp.concatenate([chunk, first[None], second[None]], axis=0)
 
-        own_packet = packet(y, grad_b_up_a, grad_b_qkv[0]) + send(
-            packet(1 - y, grad_b_up_b, grad_b_qkv[1]), to_heads
-        )
-        packets = lax.all_gather(own_packet[None], "rows", axis=0, tiled=True)
+        own_packet = packet(y, grad_b_up_a, grad_qkv_bias_a[0]) + send(
+            packet(1 - y, grad_b_up_b, grad_qkv_bias_b[0]), to_heads
+        )
+        own_packet, qkv_kept, *qkv_sent = after(own_packet, qkv_kept, *qkv_sent)
+        levelled = [own_packet] + [send(own_packet, to_level[k]) for k in range(1, levels)]
+        qkv_kept = all_added(qkv_kept, [send(part, to_level[k + 1]) for k, part in enumerate(qkv_sent)])
+        grad_w_qkv = qkv_kept
+        flat = jnp.stack(levelled)
+        flat = jnp.concatenate([flat, send(flat, to_x)], axis=0)
+        packets = jnp.concatenate([flat, send(flat, to_core)], axis=0)
         grad_mod = packets[:, :images].reshape(ring * images, 3 * width)
-        bias_sums = jnp.sum(packets[:, images:], axis=0)
-        grad_w_ada = lax.dot_general(
-            jax.nn.silu(all_conditions.astype(F32)),
-            grad_mod,
-            (((0,), (0,)), ((), ())),
-            precision=PRECISE,
-            preferred_element_type=F32,
+        bias_sums = jnp.sum(packets[:, images : images + 2], axis=0)
+        s1, s2, s3 = jnp.split(three_parts(silu_all), 3, axis=0)
+        g1, g2, g3 = jnp.split(three_parts(grad_mod), 3, axis=0)
+        grad_w_ada = contract_first(
+            jnp.concatenate([s1, s1, s2, s1, s2, s3], axis=0),
+            jnp.concatenate([g1, g2, g1, g3, g2, g1], axis=0),
         )
         grad_b_ada = jnp.sum(grad_mod, axis=0)
         grad_silu = lax.dot_general(
@@ -1163,10 +1385,10 @@
             grad_b_ada,
             grad_w_qkv[:, :cols],
             grad_w_qkv[:, cols : 2 * cols],
-            grad_w_qkv[:, 2 * cols :],
+            grad_w_qkv[:, 2 * cols : 3 * cols],
             bias_sums[0, units : units + cols],
             bias_sums[0, units + cols :],
-            grad_w_out,
+            grad_w_out[:, :cols],
             bias_sums[1, :cols],
             grad_w_up,
             bias_sums[0, :units],

time: 1020 us -> 843 us (0.83)
  waiting for transfers between devices: 251 us -> 121 us
  local copies, waits for them, and re-layouts: 66.1 us -> 28.2 us
  starting transfers between devices: 30.3 us -> 66.3 us
  other arithmetic: 83.7 us -> 53.7 us
  blocking collectives: 26.5 us -> 7.6 us
  Pallas kernels: 497 us -> 508 us
    ppermute x28 -> x41, waiting for transfers between devices: 216 us -> 71 us  [send(): return lax.ppermute(values, both, pairs)]
    ppermute x28 -> x41, starting transfers between devices: 30.2 us -> 66.2 us  [send(): return lax.ppermute(values, both, pairs)]
    another operation x13 -> x15, other arithmetic: 42.7 us -> 13.9 us
    pallas_call x1, Pallas kernels: 32.5 us -> 58.1 us  [back_two(): pl.pallas_call(back_two_kernel, grid_spec=pltpu.PrefetchScalarGridSpec(nu...]
    pallas_call x6, Pallas kernels: 237 us -> 215 us  [the longest x2 125 us: attend_back(): pl.pallas_call(partial(attend_back_kernel, heads), grid=(groups, 2), in_s...]
    convert_element_type x2 -> x6, other arithmetic: 2.63 us -> 22.6 us  [the longest x3 7.37 us: plane_pieces(): far = lambda mine, got: added(mine[quarter:], got[quarter:]).astype(BF)]
    all_gather x1 -> x0, blocking collectives: 19 us -> none  [body(): all_conditions = lax.all_gather(condition, 'rows', axis=0, tiled=True)]
    slice x10, local copies, waits for them, and re-layouts: 20.7 us -> 4.26 us  [the longest x1 1.97 us: body(): grad_w_qkv[:, 2 * cols:3 * cols]]
  transfers between devices with their start and end apart: 32 -> 43, of which waited for: 12 -> 11; matrix products, arithmetic and copies ran while one was open for 18% -> 10% of each run, Pallas kernels for 32% -> 50%
where the time goes in v2:
time: 843 us; the launch traced here: 839 us
  Pallas kernels  508 us (60%)
  waiting for transfers between devices  121 us (14%)
  starting transfers between devices  66.3 us (8%)
  other arithmetic  53.7 us (6%)
  matrix products  39.7 us (5%)
  local copies, waits for them, and re-layouts  28.2 us (3%)
  between operations  15.2 us (2%)
    pallas_call x2, Pallas kernels, feed(): pl.pallas_call(partial(feed_kernel, chunk), grid_spec=pltpu.PrefetchScala...  141 us
    pallas_call x2, Pallas kernels, attend_back(): pl.pallas_call(partial(attend_back_kernel, heads), grid=(groups, 2), in_s...  125 us
    ppermute x41, waiting for transfers between devices, send(): return lax.ppermute(values, both, pairs)  71 us
    ppermute x41, starting transfers between devices, send(): return lax.ppermute(values, both, pairs)  66.2 us
    pallas_call x2, Pallas kernels, attend(): pl.pallas_call(partial(attend_kernel, heads), grid=(groups, 2), in_specs=...  61.9 us
    pallas_call x1, Pallas kernels, back_two(): pl.pallas_call(back_two_kernel, grid_spec=pltpu.PrefetchScalarGridSpec(nu...  58.1 us
    pallas_call x1, Pallas kernels, back_one(): pl.pallas_call(back_one_kernel, grid_spec=pltpu.PrefetchScalarGridSpec(nu...  31.1 us
    pallas_call x1, Pallas kernels, middle_part(): pl.pallas_call(middle_kernel, grid_spec=pltpu.PrefetchScalarGridSpec(num_...  28.5 us
  transfers between devices with their start and end apart: 43, of which 11 were waited for; matrix products, arithmetic and copies ran while one was open for 10% of the time, Pallas kernels for 50%

profile of v2, /device:TPU:9, one launch (start us, length us, event | category | flops | bytes accessed | tf_op | source)
XLA Modules:
  0.0 838.7 jit_solution(13362496533198422883)
XLA Ops:
  12.0 1.4 convert_bitcast_fusion
  14.9 11.3 %convolution_add_fusion = f32[8,3456]{1,0:T(8,128)S(1)} fusion(f32[1152,3456]{1,0:T(8,128)} %param.24, f32[3456]{0:T(1024)S(1)} %copy-done.10, bf16[8,1152]{1,0:T(8,128)(2,1)S(1)} %copy-done.5), kind=kOutput, calls=%fused_computation.6 | convolution fusion | flops 382279680 | bytes 16068096 | tf_op jit(solution)/shard_map/dot_general | solution.py:1157
  26.2 7.6 all-gather.1
  35.9 2.0 fusion.perm_ref
  37.9 12.5 %shard_map.306 = (bf16[1024,1152]{1,0:T(8,128)(2,1)}, bf16[512,1152]{1,0:T(8,128)(2,1)}, bf16[1152,1536]{1,0:T(8,128)(2,1)}) custom-call(s32[1]{0:T(128)} %bitcast.side.pick, bf16[1536,1152]{1,0:T(8,128)(2,1)} %tok_ref.7, bf16[1536,24]{1,0:T(8,128)(2,1)} %compare_convert_fusion.hot_ref, bf16[2,24,3456]{2,1,0:T(8,128)(2,1)} %pad_maximum_fusion.2.parts_ref, ...), custom_call_target="tpu_custom_call" | custom-call | flops 5888802816 | bytes 10616832 | tf_op jit(solution)/shard_map/pallas_call | solution.py:409
  50.4 1.3 collective-permute-start
  58.1 28.5 %collective-permute-done.got_ref = bf16[512,1152]{1,0:T(8,128)(2,1)S(1)} collective-permute-done((bf16[512,1152]{1,0:T(8,128)(2,1)}, bf16[512,1152]{1,0:T(8,128)(2,1)S(1)}, u32[]{:S(2)}, u32[]{:S(2)}) %collective-permute-start) | collective-permute-done | bytes 1179680 | tf_op jit(solution)/shard_map/ppermute | solution.py:1115
  86.6 26.2 %all-gather.5.cloned.1.call-done = bf16[2304,2304]{1,0:T(8,128)(2,1)} async-done(((bf16[72,2304]{1,0:T(8,128)(2,1)}), bf16[2304,2304]{1,0:T(8,128)(2,1)}) %all-gather.5.cloned.1.call-update) | async-done | bytes 10616848 | tf_op jit(solution)/shard_map/all_gather | solution.py:1149
  112.7 21.8 %shard_map.307 = (bf16[2,512,1792]{2,1,0:T(8,128)(2,1)}, bf16[2,512,1792]{2,1,0:T(8,128)(2,1)}, bf16[1,512,1792]{2,1,0:T(8,128)(2,1)}, bf16[1,512,1792]{2,1,0:T(8,128)(2,1)}) custom-call(s32[1]{0:T(128)} %bitcast.side.pick, bf16[1024,1152]{1,0:T(8,128)(2,1)} %get-tuple-element.156.full_ref, bf16[512,1152]{1,0:T(8,128)(2,1)} %get-tuple-element.157.own_ref, ...), custom_call_target="tpu_custom_call" | custom-call | flops 12683575296 | bytes 19267584 | tf_op jit(solution)/shard_map/pallas_call | solution.py:458
  134.5 21.9 %shard_map.308 = (bf16[1,512,640]{2,1,0:T(8,128)(2,1)}, bf16[1,512,640]{2,1,0:T(8,128)(2,1)}, f32[1,8,512]{2,1,0:T(8,128)}, f32[1,8,512]{2,1,0:T(8,128)}) custom-call(bf16[1,512,1792]{2,1,0:T(8,128)(2,1)} %get-tuple-element.159.first, bf16[1,512,1792]{2,1,0:T(8,128)(2,1)} %get-tuple-element.160.second, bf16[1024,16]{1,0:T(8,128)(2,1)} %copy.98.qm_ref, ...), custom_call_target="tpu_custom_call" | custom-call | flops 15000000512 | bytes 5505024 | tf_op jit(solution)/shard_map/pallas_call | solution.py:561
  156.4 1.2 collective-permute-start.1
  157.6 40.0 %shard_map.309 = (bf16[2,512,640]{2,1,0:T(8,128)(2,1)}, bf16[2,512,640]{2,1,0:T(8,128)(2,1)}, f32[2,8,512]{2,1,0:T(8,128)}, f32[2,8,512]{2,1,0:T(8,128)}) custom-call(bf16[2,512,1792]{2,1,0:T(8,128)(2,1)} %get-tuple-element.162.first, bf16[2,512,1792]{2,1,0:T(8,128)(2,1)} %get-tuple-element.163.second, bf16[1024,16]{1,0:T(8,128)(2,1)} %copy.101.qm_ref, ...), custom_call_target="tpu_custom_call" | custom-call | flops 30000001024 | bytes 11010048 | tf_op jit(solution)/shard_map/pallas_call | solution.py:561
  198.5 28.5 %shard_map.310 = (f32[1536,1152]{1,0:T(8,128)}, bf16[1536,1152]{1,0:T(8,128)(2,1)}, bf16[1536,1152]{1,0:T(8,128)(2,1)}, bf16[1152,1536]{1,0:T(8,128)(2,1)}, bf16...) custom-call(s32[1]{0:T(128)} %bitcast.side.pick, bf16[1536,1152]{1,0:T(8,128)(2,1)} %tok_ref.7, bf16[1536,1152]{1,0:T(8,128)(2,1)} %dy_ref.3, ...), custom_call_target="tpu_custom_call" | custom-call | flops 15854469120 | bytes 38928384 | tf_op jit(solution)/shard_map/pallas_call | solution.py:762
  227.0 23.3 %all-gather.7.cloned.1.call-done = bf16[2,2304,2304]{2,1,0:T(8,128)(2,1)} async-done(((bf16[2,72,2304]{2,1,0:T(8,128)(2,1)}), bf16[2,2304,2304]{2,1,0:T(8,128)(2,1)}) %all-gather.7.cloned.1.call-update) | async-done | bytes 21233680 | tf_op jit(solution)/shard_map/all_gather | solution.py:1152
  250.3 70.2 %shard_map.311 = (f32[1536,1152]{1,0:T(8,128)}, f32[1536,1152]{1,0:T(8,128)}, f32[2,576,2304]{2,1,0:T(8,128)}, bf16[2,288,2304]{2,1,0:T(8,128)(2,1)}, bf16[2,288,2304]{2,1,0:T(8,128)(2,1)}, /*index=5*/f32[1,2304]{1,0:T(1,128)}) custom-call(s32[1]{0:T(128)S(6)} %sub.57.pick, bf16[1536,1152]{1,0:T(8,128)(2,1)} %get-tuple-element.176.h_ref, ...), custom_call_target="tpu_custom_call" | custom-call | flops 48922361856 | bytes 54853632 | tf_op jit(solution)/shard_map/pallas_call | solution.py:843
  320.8 1.8 collective-permute-start.28
  322.7 2.1 collective-permute-start.29
  324.8 1.4 collective-permute-done.29
  326.2 1.3 collective-permute-done.30
  327.5 1.2 collective-permute-start.31
  328.8 4.7 add_convert_fusion.2
  333.5 2.1 collective-permute-start.3
  335.9 70.6 %shard_map.312 = (f32[1536,1152]{1,0:T(8,128)}, f32[1536,1152]{1,0:T(8,128)}, f32[2,576,2304]{2,1,0:T(8,128)}, bf16[2,288,2304]{2,1,0:T(8,128)(2,1)}, bf16[2,288,2304]{2,1,0:T(8,128)(2,1)}, /*index=5*/f32[1,2304]{1,0:T(1,128)}) custom-call(s32[1]{0:T(128)} %bitcast.side.pick, bf16[1536,1152]{1,0:T(8,128)(2,1)} %get-tuple-element.176.h_ref, ...), custom_call_target="tpu_custom_call" | custom-call | flops 48922361856 | bytes 54853632 | tf_op jit(solution)/shard_map/pallas_call | solution.py:843
  408.4 3.3 collective-permute-done.32
  412.6 6.5 add_convert_fusion.1
  419.2 1.5 copy-done
  420.7 3.9 add_convert_fusion
  424.6 1.2 collective-permute-start.6
  428.6 58.1 %shard_map.313 = (bf16[1536,1152]{1,0:T(8,128)(2,1)}, f32[1536,1152]{1,0:T(8,128)}, bf16[2,512,640]{2,1,0:T(8,128)(2,1)}, bf16[2,512,640]{2,1,0:T(8,128)(2,1)}, ...) custom-call(s32[1]{0:T(128)} %bitcast.side.pick, ...), custom_call_target="tpu_custom_call" | custom-call | flops 19931332608 | bytes 60162048 | tf_op jit(solution)/shard_map/pallas_call | solution.py:960
  486.8 1.2 collective-permute-start.10
  488.1 6.0 fusion.49
  494.0 1.3 fusion.50
  495.5 1.1 copy-done.2
  496.6 2.3 fusion.9
  499.2 1.2 collective-permute-start.12
  501.6 1.5 collective-permute-done.10.do_second
  503.1 52.5 %shard_map.314 = (bf16[1,512,1792]{2,1,0:T(8,128)(2,1)}, bf16[1,512,1792]{2,1,0:T(8,128)(2,1)}) custom-call(bf16[1,512,1792]{2,1,0:T(8,128)(2,1)} %get-tuple-element.159.first, bf16[1,512,1792]{2,1,0:T(8,128)(2,1)} %get-tuple-element.160.second, bf16[1,512,640]{2,1,0:T(8,128)(2,1)} %get-tuple-element.216.do_first, ...), custom_call_target="tpu_custom_call" | custom-call | flops 12000000000 | bytes 11010048 | tf_op jit(solution)/shard_map/pallas_call | solution.py:663
  555.6 1.3 fusion.48
  557.0 2.2 collective-permute-start.19
  561.7 3.0 collective-permute-start.16
  564.7 2.5 collective-permute-start.20
  567.1 72.3 %shard_map.315 = (bf16[2,512,1792]{2,1,0:T(8,128)(2,1)}, bf16[2,512,1792]{2,1,0:T(8,128)(2,1)}) custom-call(bf16[2,512,1792]{2,1,0:T(8,128)(2,1)} %get-tuple-element.162.first, bf16[2,512,1792]{2,1,0:T(8,128)(2,1)} %get-tuple-element.163.second, bf16[2,512,640]{2,1,0:T(8,128)(2,1)} %get-tuple-element.235.do_first, ...), custom_call_target="tpu_custom_call" | custom-call | flops 24000000000 | bytes 22020096 | tf_op jit(solution)/shard_map/pallas_call | solution.py:663
  639.6 14.3 %shard_map.316 = (f32[576,1792]{1,0:T(8,128)}, bf16[576,1792]{1,0:T(8,128)(2,1)}, f32[1,1792]{1,0:T(1,128)}) custom-call(bf16[1152,1536]{1,0:T(8,128)(2,1)} %get-tuple-element.255.ht_ref, bf16[2,512,1792]{2,1,0:T(8,128)(2,1)} %get-tuple-element.248.first, bf16[2,512,1792]{2,1,0:T(8,128)(2,1)} %get-tuple-element.249.second, ...), custom_call_target="tpu_custom_call" | custom-call | flops 6341787648 | bytes 14548992 | tf_op jit(solution)/shard_map/pallas_call | solution.py:1031
  653.9 27.0 %collective-permute-start.21 = (bf16[576,1792]{1,0:T(8,128)(2,1)}, bf16[576,1792]{1,0:T(8,128)(2,1)}, u32[]{:S(2)}, u32[]{:S(2)}) collective-permute-start(bf16[576,1792]{1,0:T(8,128)(2,1)} %get-tuple-element.259), channel_id=1, source_target_pairs={{0,2},{1,3},{2,0},{3,1},{4,6},{5,7},{6,4},{7,5},{8,10},{9,11},{10,... | collective-permute-start | bytes 6193160 | tf_op jit(solution)/shard_map/ppermute | solution.py:1115
  684.7 13.8 %shard_map.317 = (f32[576,1792]{1,0:T(8,128)}, bf16[576,1792]{1,0:T(8,128)(2,1)}, f32[1,1792]{1,0:T(1,128)}) custom-call(bf16[1152,1536]{1,0:T(8,128)(2,1)} %get-tuple-element.255.ht_ref, bf16[2,512,1792]{2,1,0:T(8,128)(2,1)} %get-tuple-element.248.first, bf16[2,512,1792]{2,1,0:T(8,128)(2,1)} %get-tuple-element.249.second, ...), custom_call_target="tpu_custom_call" | custom-call | flops 6341787648 | bytes 14548992 | tf_op jit(solution)/shard_map/pallas_call | solution.py:1031
  698.6 1.7 convert_add_fusion.3
  700.4 1.1 slice_bitcast_fusion
  701.6 4.7 add_convert_fusion.3
  706.7 2.3 collective-permute-start.23
  709.0 1.3 collective-permute-start.25
  710.2 31.1 %shard_map.318 = (f32[1536,1152]{1,0:T(8,128)}, f32[2,8,1152]{2,1,0:T(8,128)}) custom-call(s32[1]{0:T(128)} %bitcast.side.pick, bf16[2,512,1792]{2,1,0:T(8,128)(2,1)} %get-tuple-element.248.first, bf16[2,512,1792]{2,1,0:T(8,128)(2,1)} %get-tuple-element.249.second, bf16[1,512,1792]{2,1,0:T(8,128)(2,1)} %get-tuple-element.250.rest.own, ...), custom_call_target="tpu_custom_call" | custom-call | flops 12683575296 | bytes 28704768 | tf_op jit(solution)/shard_map/pallas_call | solution.py:1069
  741.3 13.2 %collective-permute-done.25 = bf16[288,1792]{1,0:T(8,128)(2,1)S(1)} collective-permute-done((bf16[288,1792]{1,0:T(8,128)(2,1)}, bf16[288,1792]{1,0:T(8,128)(2,1)S(1)}, u32[]{:S(2)}, u32[]{:S(2)}) %collective-permute-start.25) | collective-permute-done | bytes 1032224 | tf_op jit(solution)/shard_map/ppermute | solution.py:1115
  756.6 3.7 collective-permute-done.26
  760.5 1.8 collective-permute-start.34
  762.3 16.8 %fusion.14 = f32[8,1152]{1,0:T(8,128)S(1)} fusion(f32[1152,3456]{1,0:T(8,128)} %param.24, f32[10,3456]{1,0:T(8,128)S(1)} %maximum_add_fusion), kind=kOutput, calls=%fused_computation.63 | convolution fusion | flops 382205952 | bytes 16072704 | tf_op jit(solution)/shard_map/dot_general | solution.py:1370
  779.1 1.2 collective-permute-start.27
  780.3 1.5 collective-permute-start.38
  782.6 2.4 collective-permute-start.39
  789.6 12.0 %collective-permute-done.39 = bf16[72,1792]{1,0:T(8,128)(2,1)S(1)} collective-permute-done((bf16[72,1792]{1,0:T(8,128)(2,1)S(1)}, bf16[72,1792]{1,0:T(8,128)(2,1)S(1)}, u32[]{:S(2)}, u32[]{:S(2)}) %collective-permute-start.39) | collective-permute-done | bytes 258080 | tf_op jit(solution)/shard_map/ppermute | solution.py:1115
  801.5 6.0 collective-permute-done.40
  808.4 4.5 concatenate.139
  813.5 2.0 fusion.52
  815.4 1.1 copy_dynamic-update-slice_fusion.1
  820.0 11.6 %fusion.57 = f32[1152,3456]{1,0:T(8,128)} fusion(bf16[768,1152]{1,0:T(8,128)(2,1)} %fusion.10, bf16[768,3456]{1,0:T(8,128)(2,1)S(1)} %constant_dynamic-update-slice_fusion.20), kind=kOutput, calls=%fused_computation.194 | convolution fusion | flops 6115295232 | bytes 23003136 | tf_op jit(solution)/shard_map/dot_general | solution.py:40
  (227 shorter events, 42.4 us)
Async XLA Ops:
  7.2 105.5 %all-gather.5.cloned.1.call-start = ((), (), s32[]{:S(2)}) async-start(), calls=%async_computation | async-start | bytes 10948608 | tf_op jit(solution)/shard_map/all_gather | solution.py:1149
  10.0 4.5 copy-start.13
  11.0 3.7 copy-start.12
  11.0 3.8 copy-start.5
  11.0 3.8 copy-start.10
  12.0 238.4 %all-gather.7.cloned.1.call-start = ((), (), s32[]{:S(2)}) async-start(), calls=%async_computation.1 | async-start | bytes 21897216 | tf_op jit(solution)/shard_map/all_gather | solution.py:1152
  14.8 19.0 %copy-start.23 = (s32[3,4]{1,0:T(4,128)S(1)}, s32[3,4]{1,0:T(4,128)}, u32[]{:S(2)}) copy-start(s32[3,4]{1,0:T(4,128)} %param.23) | copy-start | bytes 148
  34.0 16.4 %copy-start.8 = (s32[1536]{0:T(1024)}, s32[1536]{0:T(1024)S(1)}, u32[]{:S(2)}) copy-start(s32[1536]{0:T(1024)S(1)} %pad_add_fusion) | copy-start | bytes 18436
  37.9 13.9 %copy-start.11 = (s32[3,8,8]{2,1,0:T(8,128)S(1)}, s32[3,8,8]{2,1,0:T(8,128)}, u32[]{:S(2)}) copy-start(s32[3,8,8]{2,1,0:T(8,128)} %param.22) | copy-start | bytes 2308
  37.9 18.8 %copy-start.16 = (f32[1152]{0:T(1024)S(1)}, f32[1152]{0:T(1024)}, u32[]{:S(2)}) copy-start(f32[1152]{0:T(1024)} %param.32) | copy-start | bytes 13828
  50.4 36.2 %collective-permute-start = (bf16[512,1152]{1,0:T(8,128)(2,1)}, bf16[512,1152]{1,0:T(8,128)(2,1)S(1)}, u32[]{:S(2)}, u32[]{:S(2)}) collective-permute-start(bf16[512,1152]{1,0:T(8,128)(2,1)} %get-tuple-element.157.own_ref), channel_id=1, source_target_pairs={{0,1},{1,0},{2,3},{3,2},{4,5},{5,4},{6,7},{7,6},{8,9},{9,8},{10,11... | collective-permute-start | bytes 3538952 | tf_op jit(solution)/shard_map/ppermute | solution.py:1115
  86.5 26.2 %copy-start.24 = (bf16[512,1152]{1,0:T(8,128)(2,1)}, bf16[512,1152]{1,0:T(8,128)(2,1)S(1)}, u32[]{:S(2)}) copy-start(bf16[512,1152]{1,0:T(8,128)(2,1)S(1)} %collective-permute-done.got_ref) | copy-start | bytes 3538948
  156.4 41.3 %collective-permute-start.1 = (bf16[1,512,640]{2,1,0:T(8,128)(2,1)}, bf16[1,512,640]{2,1,0:T(8,128)(2,1)S(1)}, u32[]{:S(2)}, u32[]{:S(2)}) collective-permute-start(bf16[1,512,640]{2,1,0:T(8,128)(2,1)} %get-tuple-element.167), channel_id=1, source_target_pairs={{0,1},{1,0},{2,3},{3,2},{4,5},{5,4},{6,7},{7,6},{8,9},{9,8},{10,11... | collective-permute-start | bytes 1966088 | tf_op jit(solution)/shard_map/ppermute | solution.py:1115
  320.5 8.2 collective-permute-start.2
  320.8 4.0 collective-permute-start.28
  322.7 3.5 collective-permute-start.29
  324.8 2.7 collective-permute-start.30
  327.5 79.4 %collective-permute-start.31 = (bf16[4,8,1152]{2,1,0:T(8,128)(2,1)S(1)}, bf16[4,8,1152]{2,1,0:T(8,128)(2,1)S(1)}, u32[]{:S(2)}, u32[]{:S(2)}) collective-permute-start(bf16[4,8,1152]{2,1,0:T(8,128)(2,1)S(1)} %pad_maximum_fusion.5), channel_id=1, source_target_pairs={{0,4},{1,5},{2,6},{3,7},{4,0},{5,1},{6,2},{7,3},{8,12},{9,13},{10,... | collective-permute-start | bytes 221192 | tf_op jit(solution)/shard_map/ppermute | solution.py:1115
  333.5 73.7 %copy-start.9 = (s32[1536]{0:T(1024)S(1)}, s32[1536]{0:T(1024)}, u32[]{:S(2)}) copy-start(s32[1536]{0:T(1024)} %copy-done.8) | copy-start | bytes 18436
  333.5 74.3 %copy-start.17 = (f32[1152]{0:T(1024)S(1)}, f32[1152]{0:T(1024)}, u32[]{:S(2)}) copy-start(f32[1152]{0:T(1024)} %param.36) | copy-start | bytes 13828
  333.5 73.0 %collective-permute-start.3 = (bf16[2,288,2304]{2,1,0:T(8,128)(2,1)}, bf16[2,288,2304]{2,1,0:T(8,128)(2,1)}, u32[]{:S(2)}, u32[]{:S(2)}) collective-permute-start(bf16[2,288,2304]{2,1,0:T(8,128)(2,1)} %get-tuple-element.183), channel_id=1, source_target_pairs={{0,2},{1,3},{2,0},{3,1},{4,6},{5,7},{6,4},{7,5},{8,10},{9,11},{10,... | collective-permute-start | bytes 7962632 | tf_op jit(solution)/shard_map/ppermute | solution.py:1115
  335.6 70.9 %collective-permute-start.4 = (bf16[2,288,2304]{2,1,0:T(8,128)(2,1)}, bf16[2,288,2304]{2,1,0:T(8,128)(2,1)}, u32[]{:S(2)}, u32[]{:S(2)}) collective-permute-start(bf16[2,288,2304]{2,1,0:T(8,128)(2,1)} %add_convert_fusion.2), channel_id=1, source_target_pairs={{0,4},{1,5},{2,6},{3,7},{4,0},{5,1},{6,2},{7,3},{8,12},{9,13},{10,... | collective-permute-start | bytes 7962632 | tf_op jit(solution)/shard_map/ppermute | solution.py:1115
  406.5 12.7 %collective-permute-start.5 = (bf16[2,288,2304]{2,1,0:T(8,128)(2,1)}, bf16[2,288,2304]{2,1,0:T(8,128)(2,1)}, u32[]{:S(2)}, u32[]{:S(2)}) collective-permute-start(bf16[2,288,2304]{2,1,0:T(8,128)(2,1)} %get-tuple-element.189), channel_id=1, source_target_pairs={{0,2},{1,3},{2,0},{3,1},{4,6},{5,7},{6,4},{7,5},{8,10},{9,11},{10,... | collective-permute-start | bytes 7962632 | tf_op jit(solution)/shard_map/ppermute | solution.py:1115
  406.9 4.8 collective-permute-start.32
  412.6 8.1 copy-start
  424.6 62.1 %collective-permute-start.6 = (bf16[2,288,2304]{2,1,0:T(8,128)(2,1)}, bf16[2,288,2304]{2,1,0:T(8,128)(2,1)}, u32[]{:S(2)}, u32[]{:S(2)}) collective-permute-start(bf16[2,288,2304]{2,1,0:T(8,128)(2,1)} %add_convert_fusion.1), channel_id=1, source_target_pairs={{0,1},{1,0},{2,3},{3,2},{4,5},{5,4},{6,7},{7,6},{8,9},{9,8},{10,11... | collective-permute-start | bytes 7962632 | tf_op jit(solution)/shard_map/ppermute | solution.py:1115
  425.9 60.8 %collective-permute-start.7 = (bf16[2,288,2304]{2,1,0:T(8,128)(2,1)}, bf16[2,288,2304]{2,1,0:T(8,128)(2,1)}, u32[]{:S(2)}, u32[]{:S(2)}) collective-permute-start(bf16[2,288,2304]{2,1,0:T(8,128)(2,1)} %add_convert_fusion), channel_id=1, source_target_pairs={{0,4},{1,5},{2,6},{3,7},{4,0},{5,1},{6,2},{7,3},{8,12},{9,13},{10,... | collective-permute-start | bytes 7962632 | tf_op jit(solution)/shard_map/ppermute | solution.py:1115
  426.1 60.6 %collective-permute-start.8 = (bf16[2,288,2304]{2,1,0:T(8,128)(2,1)}, bf16[2,288,2304]{2,1,0:T(8,128)(2,1)}, u32[]{:S(2)}, u32[]{:S(2)}) collective-permute-start(bf16[2,288,2304]{2,1,0:T(8,128)(2,1)} %get-tuple-element.207), channel_id=1, source_target_pairs={{0,2},{1,3},{2,0},{3,1},{4,6},{5,7},{6,4},{7,5},{8,10},{9,11},{10,... | collective-permute-start | bytes 7962632 | tf_op jit(solution)/shard_map/ppermute | solution.py:1115
  486.8 8.7 %collective-permute-start.9 = (bf16[2,576,640]{2,1,0:T(8,128)(2,1)}, bf16[2,576,640]{2,1,0:T(8,128)(2,1)}, u32[]{:S(2)}, u32[]{:S(2)}) collective-permute-start(bf16[2,576,640]{2,1,0:T(8,128)(2,1)} %get-tuple-element.215), channel_id=1, source_target_pairs={{0,2},{1,3},{2,0},{3,1},{4,6},{5,7},{6,4},{7,5},{8,10},{9,11},{10,... | collective-permute-start | bytes 4423688 | tf_op jit(solution)/shard_map/ppermute | solution.py:1115
  486.8 16.3 %collective-permute-start.10 = (bf16[1,512,640]{2,1,0:T(8,128)(2,1)}, bf16[1,512,640]{2,1,0:T(8,128)(2,1)}, u32[]{:S(2)}, u32[]{:S(2)}) collective-permute-start(bf16[1,512,640]{2,1,0:T(8,128)(2,1)} %get-tuple-element.217), channel_id=1, source_target_pairs={{0,1},{1,0},{2,3},{3,2},{4,5},{5,4},{6,7},{7,6},{8,9},{9,8},{10,11... | collective-permute-start | bytes 1966088 | tf_op jit(solution)/shard_map/ppermute | solution.py:1115
  498.9 56.7 %collective-permute-start.11 = (bf16[288,640]{1,0:T(8,128)(2,1)}, bf16[288,640]{1,0:T(8,128)(2,1)S(1)}, u32[]{:S(2)}, u32[]{:S(2)}) collective-permute-start(bf16[288,640]{1,0:T(8,128)(2,1)} %get-tuple-element.223), channel_id=1, source_target_pairs={{0,4},{1,5},{2,6},{3,7},{4,0},{5,1},{6,2},{7,3},{8,12},{9,13},{10,... | collective-permute-start | bytes 1105928 | tf_op jit(solution)/shard_map/ppermute | solution.py:1115
  499.2 56.4 %collective-permute-start.12 = (bf16[288,640]{1,0:T(8,128)(2,1)S(1)}, bf16[288,640]{1,0:T(8,128)(2,1)}, u32[]{:S(2)}, u32[]{:S(2)}) collective-permute-start(bf16[288,640]{1,0:T(8,128)(2,1)S(1)} %get-tuple-element.224), channel_id=1, source_target_pairs={{0,1},{1,0},{2,3},{3,2},{4,5},{5,4},{6,7},{7,6},{8,9},{9,8},{10,11... | collective-permute-start | bytes 1105928 | tf_op jit(solution)/shard_map/ppermute | solution.py:1115
  500.5 55.2 %collective-permute-start.13 = (bf16[288,640]{1,0:T(8,128)(2,1)S(1)}, bf16[288,640]{1,0:T(8,128)(2,1)}, u32[]{:S(2)}, u32[]{:S(2)}) collective-permute-start(bf16[288,640]{1,0:T(8,128)(2,1)S(1)} %get-tuple-element.225), channel_id=1, source_target_pairs={{0,5},{1,4},{2,7},{3,6},{4,1},{5,0},{6,3},{7,2},{8,13},{9,12},{10,... | collective-permute-start | bytes 1105928 | tf_op jit(solution)/shard_map/ppermute | solution.py:1115
  556.9 7.7 collective-permute-start.18
  557.0 7.7 collective-permute-start.19
  560.1 79.4 %collective-permute-start.14 = (bf16[1,512,1792]{2,1,0:T(8,128)(2,1)}, bf16[1,512,1792]{2,1,0:T(8,128)(2,1)}, u32[]{:S(2)}, u32[]{:S(2)}) collective-permute-start(bf16[1,512,1792]{2,1,0:T(8,128)(2,1)} %get-tuple-element.241), channel_id=1, source_target_pairs={{0,1},{1,0},{2,3},{3,2},{4,5},{5,4},{6,7},{7,6},{8,9},{9,8},{10,11... | collective-permute-start | bytes 5505032 | tf_op jit(solution)/shard_map/ppermute | solution.py:1115
  561.2 78.3 %collective-permute-start.15 = (bf16[2,72,2304]{2,1,0:T(8,128)(2,1)}, bf16[2,72,2304]{2,1,0:T(8,128)(2,1)S(1)}, u32[]{:S(2)}, u32[]{:S(2)}) collective-permute-start(bf16[2,72,2304]{2,1,0:T(8,128)(2,1)} %get-tuple-element.242), channel_id=1, source_target_pairs={{0,8},{1,9},{2,10},{3,11},{4,12},{5,13},{6,14},{7,15},{8,16},{9,17... | collective-permute-start | bytes 1990664 | tf_op jit(solution)/shard_map/ppermute | solution.py:1115
  561.7 77.8 %collective-permute-start.16 = (bf16[2,72,2304]{2,1,0:T(8,128)(2,1)}, bf16[2,72,2304]{2,1,0:T(8,128)(2,1)S(1)}, u32[]{:S(2)}, u32[]{:S(2)}) collective-permute-start(bf16[2,72,2304]{2,1,0:T(8,128)(2,1)} %get-tuple-element.243), channel_id=1, source_target_pairs={{0,16},{1,17},{2,18},{3,19},{4,20},{5,21},{6,22},{7,23},{8,24},{9,... | collective-permute-start | bytes 1990664 | tf_op jit(solution)/shard_map/ppermute | solution.py:1115
  564.7 74.9 %collective-permute-start.17 = (bf16[2,72,2304]{2,1,0:T(8,128)(2,1)}, bf16[2,72,2304]{2,1,0:T(8,128)(2,1)}, u32[]{:S(2)}, u32[]{:S(2)}) collective-permute-start(bf16[2,72,2304]{2,1,0:T(8,128)(2,1)} %get-tuple-element.244), channel_id=1, source_target_pairs={{0,24},{1,25},{2,26},{3,27},{4,28},{5,29},{6,30},{7,31},{8,0},{9,1... | collective-permute-start | bytes 1990664 | tf_op jit(solution)/shard_map/ppermute | solution.py:1115
  564.7 74.8 %collective-permute-start.20 = (bf16[72,640]{1,0:T(8,128)(2,1)S(1)}, bf16[72,640]{1,0:T(8,128)(2,1)S(1)}, u32[]{:S(2)}, u32[]{:S(2)}) collective-permute-start(bf16[72,640]{1,0:T(8,128)(2,1)S(1)} %get-tuple-element.247), channel_id=1, source_target_pairs={{0,24},{1,25},{2,26},{3,27},{4,28},{5,29},{6,30},{7,31},{8,0},{9,1... | collective-permute-start | bytes 276488 | tf_op jit(solution)/shard_map/ppermute | solution.py:1115
  639.5 14.4 %copy-start.3 = (bf16[2,72,2304]{2,1,0:T(8,128)(2,1)}, bf16[2,72,2304]{2,1,0:T(8,128)(2,1)S(1)}, u32[]{:S(2)}) copy-start(bf16[2,72,2304]{2,1,0:T(8,128)(2,1)S(1)} %collective-permute-done.15) | copy-start | bytes 1990660
  639.5 14.4 %copy-start.4 = (bf16[2,72,2304]{2,1,0:T(8,128)(2,1)}, bf16[2,72,2304]{2,1,0:T(8,128)(2,1)S(1)}, u32[]{:S(2)}) copy-start(bf16[2,72,2304]{2,1,0:T(8,128)(2,1)S(1)} %collective-permute-done.16) | copy-start | bytes 1990660
  639.5 43.2 %copy-start.14 = (f32[1,2304]{1,0:T(1,128)S(1)}, f32[1,2304]{1,0:T(1,128)}, u32[]{:S(2)}) copy-start(f32[1,2304]{1,0:T(1,128)} %get-tuple-element.277) | copy-start | bytes 27652
  639.5 43.2 %copy-start.15 = (f32[1,2304]{1,0:T(1,128)S(1)}, f32[1,2304]{1,0:T(1,128)}, u32[]{:S(2)}) copy-start(f32[1,2304]{1,0:T(1,128)} %get-tuple-element.273) | copy-start | bytes 27652
  639.6 43.2 %copy-start.18 = (f32[1,1152]{1,0:T(1,128)S(1)}, f32[1,1152]{1,0:T(1,128)}, u32[]{:S(2)}) copy-start(f32[1,1152]{1,0:T(1,128)} %get-tuple-element.276) | copy-start | bytes 13828
  639.6 43.2 %copy-start.19 = (f32[1,1152]{1,0:T(1,128)S(1)}, f32[1,1152]{1,0:T(1,128)}, u32[]{:S(2)}) copy-start(f32[1,1152]{1,0:T(1,128)} %get-tuple-element.275) | copy-start | bytes 13828
  653.9 44.7 %collective-permute-start.21 = (bf16[576,1792]{1,0:T(8,128)(2,1)}, bf16[576,1792]{1,0:T(8,128)(2,1)}, u32[]{:S(2)}, u32[]{:S(2)}) collective-permute-start(bf16[576,1792]{1,0:T(8,128)(2,1)} %get-tuple-element.259), channel_id=1, source_target_pairs={{0,2},{1,3},{2,0},{3,1},{4,6},{5,7},{6,4},{7,5},{8,10},{9,11},{10,... | collective-permute-start | bytes 6193160 | tf_op jit(solution)/shard_map/ppermute | solution.py:1115
  698.5 7.8 collective-permute-start.22
  701.6 4.7 copy-start.1
  706.7 47.8 %copy-start.7 = (f32[4,8,1152]{2,1,0:T(8,128)S(1)}, f32[4,8,1152]{2,1,0:T(8,128)}, u32[]{:S(2)}) copy-start(f32[4,8,1152]{2,1,0:T(8,128)} %get-tuple-element.272) | copy-start | bytes 442372
  706.7 34.6 %collective-permute-start.23 = (bf16[288,1792]{1,0:T(8,128)(2,1)S(1)}, bf16[288,1792]{1,0:T(8,128)(2,1)S(1)}, u32[]{:S(2)}, u32[]{:S(2)}) collective-permute-start(bf16[288,1792]{1,0:T(8,128)(2,1)S(1)} %get-tuple-element.267), channel_id=1, source_target_pairs={{0,4},{1,5},{2,6},{3,7},{4,0},{5,1},{6,2},{7,3},{8,12},{9,13},{10,... | collective-permute-start | bytes 3096584 | tf_op jit(solution)/shard_map/ppermute | solution.py:1115
  709.0 32.4 %collective-permute-start.24 = (bf16[288,1792]{1,0:T(8,128)(2,1)}, bf16[288,1792]{1,0:T(8,128)(2,1)S(1)}, u32[]{:S(2)}, u32[]{:S(2)}) collective-permute-start(bf16[288,1792]{1,0:T(8,128)(2,1)} %get-tuple-element.268), channel_id=1, source_target_pairs={{0,1},{1,0},{2,3},{3,2},{4,5},{5,4},{6,7},{7,6},{8,9},{9,8},{10,11... | collective-permute-start | bytes 3096584 | tf_op jit(solution)/shard_map/ppermute | solution.py:1115
  709.0 45.6 %collective-permute-start.25 = (bf16[288,1792]{1,0:T(8,128)(2,1)}, bf16[288,1792]{1,0:T(8,128)(2,1)S(1)}, u32[]{:S(2)}, u32[]{:S(2)}) collective-permute-start(bf16[288,1792]{1,0:T(8,128)(2,1)} %get-tuple-element.269), channel_id=1, source_target_pairs={{0,5},{1,4},{2,7},{3,6},{4,1},{5,0},{6,3},{7,2},{8,13},{9,12},{10,... | collective-permute-start | bytes 3096584 | tf_op jit(solution)/shard_map/ppermute | solution.py:1115
  755.5 4.8 collective-permute-start.26
  760.4 24.6 %copy-start.6 = (bf16[8,1152]{1,0:T(8,128)(2,1)S(1)}, bf16[8,1152]{1,0:T(8,128)(2,1)}, u32[]{:S(2)}) copy-start(bf16[8,1152]{1,0:T(8,128)(2,1)} %param.20) | copy-start | bytes 55300
  760.4 25.3 %collective-permute-start.33 = (f32[10,3456]{1,0:T(8,128)S(1)}, f32[10,3456]{1,0:T(8,128)S(1)}, u32[]{:S(2)}, u32[]{:S(2)}) collective-permute-start(f32[10,3456]{1,0:T(8,128)S(1)} %maximum_add_fusion), channel_id=1, source_target_pairs={{0,8},{1,9},{2,10},{3,11},{4,12},{5,13},{6,14},{7,15},{8,16},{9,17... | collective-permute-start | bytes 414728 | tf_op jit(solution)/shard_map/ppermute | solution.py:1115
  760.5 25.2 %collective-permute-start.34 = (f32[10,3456]{1,0:T(8,128)S(1)}, f32[10,3456]{1,0:T(8,128)S(1)}, u32[]{:S(2)}, u32[]{:S(2)}) collective-permute-start(f32[10,3456]{1,0:T(8,128)S(1)} %maximum_add_fusion), channel_id=1, source_target_pairs={{0,16},{1,17},{2,18},{3,19},{4,20},{5,21},{6,22},{7,23},{8,24},{9,... | collective-permute-start | bytes 414728 | tf_op jit(solution)/shard_map/ppermute | solution.py:1115
  762.3 23.4 %collective-permute-start.35 = (f32[10,3456]{1,0:T(8,128)S(1)}, f32[10,3456]{1,0:T(8,128)S(1)}, u32[]{:S(2)}, u32[]{:S(2)}) collective-permute-start(f32[10,3456]{1,0:T(8,128)S(1)} %maximum_add_fusion), channel_id=1, source_target_pairs={{0,24},{1,25},{2,26},{3,27},{4,28},{5,29},{6,30},{7,31},{8,0},{9,1... | collective-permute-start | bytes 414728 | tf_op jit(solution)/shard_map/ppermute | solution.py:1115
  779.1 3.5 collective-permute-start.27
  780.3 9.3 %collective-permute-start.38 = (bf16[72,1792]{1,0:T(8,128)(2,1)S(1)}, bf16[72,1792]{1,0:T(8,128)(2,1)S(1)}, u32[]{:S(2)}, u32[]{:S(2)}) collective-permute-start(bf16[72,1792]{1,0:T(8,128)(2,1)S(1)} %get-tuple-element.285), channel_id=1, source_target_pairs={{0,8},{1,9},{2,10},{3,11},{4,12},{5,13},{6,14},{7,15},{8,16},{9,17... | collective-permute-start | bytes 774152 | tf_op jit(solution)/shard_map/ppermute | solution.py:1115
  782.6 18.9 %collective-permute-start.39 = (bf16[72,1792]{1,0:T(8,128)(2,1)S(1)}, bf16[72,1792]{1,0:T(8,128)(2,1)S(1)}, u32[]{:S(2)}, u32[]{:S(2)}) collective-permute-start(bf16[72,1792]{1,0:T(8,128)(2,1)S(1)} %get-tuple-element.286), channel_id=1, source_target_pairs={{0,16},{1,17},{2,18},{3,19},{4,20},{5,21},{6,22},{7,23},{8,24},{9,... | collective-permute-start | bytes 774152 | tf_op jit(solution)/shard_map/ppermute | solution.py:1115
  785.7 21.9 %collective-permute-start.40 = (bf16[72,1792]{1,0:T(8,128)(2,1)S(1)}, bf16[72,1792]{1,0:T(8,128)(2,1)S(1)}, u32[]{:S(2)}, u32[]{:S(2)}) collective-permute-start(bf16[72,1792]{1,0:T(8,128)(2,1)S(1)} %get-tuple-element.287), channel_id=1, source_target_pairs={{0,24},{1,25},{2,26},{3,27},{4,28},{5,29},{6,30},{7,31},{8,0},{9,1... | collective-permute-start | bytes 774152 | tf_op jit(solution)/shard_map/ppermute | solution.py:1115
  786.0 22.4 %collective-permute-start.36 = (f32[4,10,3456]{2,0,1:T(4,128)S(1)}, f32[4,10,3456]{2,0,1:T(4,128)}, u32[]{:S(2)}, u32[]{:S(2)}) collective-permute-start(f32[4,10,3456]{2,0,1:T(4,128)S(1)} %copy.104), channel_id=1, source_target_pairs={{0,4},{1,5},{2,6},{3,7},{4,0},{5,1},{6,2},{7,3},{8,12},{9,13},{10,... | collective-permute-start | bytes 1658888 | tf_op jit(solution)/shard_map/ppermute | solution.py:1115
  813.0 3.6 collective-permute-start.37
  (5 other events, 13.8 us)
Sparse Core Ops, SparseCore 0:
  12.1 100.5 all-gather.4
  116.2 134.0 all-gather.6

commit v3 on v2

--- a/solution.py
+++ b/solution.py
@@ -388,12 +388,60 @@
     return jnp.concatenate([high, middle, rest - middle], axis=-2).astype(BF)
 
 
-def norm_kernel(side, tok_ref, hot_ref, parts_ref, perm_ref, h_ref, half_ref, ht_ref):
+def collect_kernel(core, over_x, x_got, over_y, y_got, last, last_got, whole, sems):
+    heads, levels, xs = whole.shape[:3]
+    count = over_x.shape[-1]
+    place_of = (lambda h, z, x: (h, x, z), lambda h, z, x: (x, h, z), lambda h, z, x: (z, h, x))
+    copies = []
+    for k, pair in enumerate(((over_x, x_got), (over_y, y_got), (last, last_got))):
+        for got, source in enumerate(pair):
+            c = core[0] if got == 0 else 1 - core[0]
+            for h in range(heads):
+                for z in range(levels):
+                    for x in range(xs):
+                        copy = pltpu.make_async_copy(
+                            source.at[place_of[k](h, z, x)],
+                            whole.at[h, z, x, c, :, pl.ds(k * count, count)],
+                            sems.at[len(copies)],
+                        )
+                        copy.start()
+                        copies.append(copy)
+    for copy in copies:
+        copy.wait()
+
+
+def collected(core, over_x, x_got, over_y, y_got, last, last_got):
+    levels, heads, xs, piece, count = last.shape
+    whole = (heads, levels, xs, 2, piece, 3 * count)
+    anywhere = pl.BlockSpec(memory_space=pl.ANY)
+    return pl.pallas_call(
+        collect_kernel,
+        grid_spec=pltpu.PrefetchScalarGridSpec(
+            num_scalar_prefetch=1,
+            grid=(1,),
+            in_specs=[anywhere] * 6,
+            out_specs=anywhere,
+            scratch_shapes=[pltpu.SemaphoreType.DMA((6 * heads * levels * xs,))],
+        ),
+        out_shape=shape(whole, BF),
+        compiler_params=params(16),
+        cost_estimate=cost(0, 24 * heads * levels * xs * piece * count),
+    )(core, over_x, x_got, over_y, y_got, last, last_got)
+
+
+def turn_in_order(places, turned_ref, values):
+    turned = values.astype(F32).T
+    piece = turned_ref.shape[1]
+    for k in range(turned_ref.shape[0]):
+        turned_ref[places[1 + k]] = turned[k * piece : (k + 1) * piece].astype(BF)
+
+
+def norm_kernel(side, tok_ref, hot_ref, parts_ref, h_ref, half_ref, ht_ref):
     width = tok_ref.shape[1]
     normed, _ = layer_norm(tok_ref[...].astype(F32))
     mod = rows_by_columns(hot_ref[...], parts_ref[0, :, : 2 * width])
     hidden = (normed * (1.0 + mod[:, width:]) + mod[:, :width]).astype(BF)
-    ht_ref[...] = contract_last(perm_ref[...], hidden).astype(BF)
+    turn_in_order(side, ht_ref, hidden)
 
     @pl.when(pl.program_id(0) < 2)
     def _():
@@ -404,7 +452,8 @@
         half_ref[...] = hidden
 
 
-def first_norm(side, tokens, hot, parts, perm, block):
+def first_norm(side, tokens, hot, parts, block):
+    ring = side.shape[0] // 2
     rows, width = tokens.shape
     return pl.pallas_call(
         norm_kernel,
@@ -415,22 +464,21 @@
                 pl.BlockSpec((block, width), lambda i, y: ((i + y[0]) % 3, 0)),
                 pl.BlockSpec((block, hot.shape[1]), lambda i, y: (i, 0)),
                 pl.BlockSpec((1,) + parts.shape[1:], lambda i, y: (0, 0, 0)),
-                pl.BlockSpec(perm.shape, lambda i, y: (0, 0)),
             ],
             out_specs=[
                 pl.BlockSpec((block, width), lambda i, y: (jnp.minimum(i, 1), 0)),
                 pl.BlockSpec((block, width), lambda i, y: (0, 0)),
-                pl.BlockSpec((width, block), lambda i, y: (0, i)),
+                pl.BlockSpec((ring, width // ring, block), lambda i, y: (0, 0, i)),
             ],
         ),
         out_shape=[
             shape((2 * block, width), BF),
             shape((block, width), BF),
-            shape((width, rows), BF),
+            shape((ring, width // ring, rows), BF),
         ],
         compiler_params=params(),
         cost_estimate=cost(2 * rows * width * (width + 512), rows * width * 6),
-    )(side, tokens, hot, parts, perm)
+    )(side, tokens, hot, parts)
 
 
 def project_kernel(side, full_ref, own_ref, got_ref, w_ref, bias_ref, first, second, own, got):
@@ -723,7 +771,7 @@
 
 
 def middle_kernel(
-    side, tok_ref, dy_ref, first, second, own, other, w_own, w_other, b_ref, hot_ref, parts_ref, perm_ref,
+    side, tok_ref, dy_ref, first, second, own, other, w_own, w_other, b_ref, hot_ref, parts_ref,
     branch_ref, h_ref, g_ref, ht_ref, gt_ref, gb_ref,
 ):
     i = pl.program_id(0)
@@ -745,12 +793,13 @@
     grad = (dy_ref[...].astype(F32) * mod[:, 2 * width :]).astype(BF)
     h_ref[...] = hidden
     g_ref[...] = grad
-    ht_ref[...] = contract_last(perm_ref[...], hidden).astype(BF)
-    gt_ref[...] = contract_last(perm_ref[...], grad).astype(BF)
+    turn_in_order(side, ht_ref, hidden)
+    turn_in_order(side, gt_ref, grad)
     add_up(gb_ref, jnp.sum(grad.astype(F32), axis=0, keepdims=True))
 
 
-def middle_part(side, tokens, cotangent, thirds, weights, b_out, hot, parts, perm, block):
+def middle_part(side, tokens, cotangent, thirds, weights, b_out, hot, parts, block):
+    ring = side.shape[0] // 2
     rows, width = tokens.shape
     per = rows // 3 // block
     spec = lambda dims: pl.BlockSpec(dims, lambda i, y: (0,) * len(dims))
@@ -758,7 +807,7 @@
         (block, width), lambda i, y: (((i // per + y[0]) % 3) * per + i % per, 0)
     )
     plain = pl.BlockSpec((block, width), lambda i, y: (i, 0))
-    turned = pl.BlockSpec((width, block), lambda i, y: (0, i))
+    turned = pl.BlockSpec((ring, width // ring, block), lambda i, y: (0, 0, i))
     return pl.pallas_call(
         middle_kernel,
         grid_spec=pltpu.PrefetchScalarGridSpec(
@@ -772,7 +821,6 @@
                 spec((1, width)),
                 pl.BlockSpec((block, hot.shape[1]), lambda i, y: (i, 0)),
                 spec(parts.shape),
-                spec(perm.shape),
             ],
             out_specs=[plain, plain, plain, turned, turned, spec((1, width))],
         ),
@@ -780,13 +828,13 @@
             shape((rows, width), F32),
             shape((rows, width), BF),
             shape((rows, width), BF),
-            shape((width, rows), BF),
-            shape((width, rows), BF),
+            shape((ring, width // ring, rows), BF),
+            shape((ring, width // ring, rows), BF),
             shape((1, width), F32),
         ],
         compiler_params=params(),
         cost_estimate=cost(2 * rows * width * (3 * width + 1024), rows * width * 22),
-    )(side, tokens, cotangent, *thirds, weights, weights, b_out, hot, parts, perm)
+    )(side, tokens, cotangent, *thirds, weights, weights, b_out, hot, parts)
 
 
 def feed_kernel(
@@ -881,7 +929,7 @@
 
 def back_two_kernel(
     side, tok_ref, dy_ref, branch_ref, two_a, two_b, b_ref, back_a, back_b, w_own, w_other, hot_ref,
-    turn_ref, parts_ref, perm_ref, first, second, half_own, half_other, out_ref, middle_ref, a_first, a_second,
+    turn_ref, parts_ref, first, second, half_own, half_other, out_ref, middle_ref, a_first, a_second,
     a_own, a_other, sums_ref, gb_ref, mine_ref, theirs_ref, outer_ref,
 ):
     width = tok_ref.shape[1]
@@ -899,7 +947,7 @@
     grad_middle = dy + norm_back(normed, inverse, grad_hidden * (1.0 + mod[:, width : 2 * width]))
     middle_ref[...] = grad_middle
     grad = (grad_middle * gate).astype(BF)
-    turned = contract_last(perm_ref[...], grad).astype(BF)
+    turned = grad.astype(F32).T.astype(BF)
     att = third_of(first, second, half_own, half_other, pl.program_id(0), pl.num_programs(0) // 3)
     for k in range(2):
         product = rows_by_columns(turned, att[k])
@@ -914,9 +962,15 @@
 
     @pl.when(pl.program_id(0) == pl.num_programs(0) - 1)
     def _():
+        ring = side.shape[0] // 2
+        piece = width // ring
         for k in range(2):
-            mine_ref[k] = outer_ref[k, : width // 2]
-            theirs_ref[k] = outer_ref[k, width // 2 :].astype(BF)
+            pieces = [
+                outer_ref[k, pl.ds(pl.multiple_of(side[1 + ring + j] * piece, 8), piece)]
+                for j in range(ring)
+            ]
+            mine_ref[k] = jnp.concatenate(pieces[: ring // 2], axis=0)
+            theirs_ref[k] = jnp.concatenate(pieces[ring // 2 :], axis=0).astype(BF)
 
     skip = w_own.shape[2] - width // 2
     ours = padded_columns([rows_by_columns(grad, w_own[0, :, skip:]).astype(BF)], a_own.shape[2])
@@ -946,7 +1000,7 @@
 
 
 def back_two(
-    side, tokens, cotangent, branch, two_a, two_b, b_down, back_a, back_b, weights, hot, turn, parts, perm,
+    side, tokens, cotangent, branch, two_a, two_b, b_down, back_a, back_b, weights, hot, turn, parts,
     attended, block, images, out_width,
 ):
     rows, width = tokens.shape
@@ -975,7 +1029,6 @@
                 pl.BlockSpec((block, hot.shape[1]), lambda i, y: (i, 0)),
                 pl.BlockSpec((images, block), lambda i, y: (0, i)),
                 spec(parts.shape),
-                spec(perm.shape),
                 *third_specs(block, out_width, per),
             ],
             out_specs=[
@@ -1001,7 +1054,7 @@
         ],
         compiler_params=params(62),
         cost_estimate=cost(2 * rows * width * (4 * width + 1024), rows * width * 34),
-    )(side, tokens, cotangent, branch, two_a, two_b, b_down, back_a, back_b, weights, weights, hot, turn, parts, perm, *attended)
+    )(side, tokens, cotangent, branch, two_a, two_b, b_down, back_a, back_b, weights, weights, hot, turn, parts, *attended)
 
 
 def outer_kernel(ht_ref, first, second, rest, mine_ref, theirs_ref, sums_ref):
@@ -1113,6 +1166,9 @@
 
     def send(values, pairs):
         return lax.ppermute(values, both, pairs)
+
+    def after(*values):
+        return lax.optimization_barrier(values)
 
     def body(
         tokens,
@@ -1141,36 +1197,8 @@
         length = segment_ids.shape[1]
         third = rows // 3
         images = condition.shape[0]
-        side = y.reshape(1)
         units = w_up.shape[1]
         cols = w_query.shape[1]
-
-        attention_shard = jnp.concatenate([w_query, w_key, w_value, w_out], axis=1).astype(BF)
-        attention_weights = lax.all_gather(
-            attention_shard, ("heads", "rows"), axis=0, tiled=True
-        ).reshape(2, width, attention_shard.shape[1])
-        feed_weights = lax.all_gather(
-            jnp.stack([w_up, w_down]).astype(BF), ("heads", "rows"), axis=1, tiled=True
-        ).reshape(2, 2, width, units)
-
-        cond = condition.astype(F32)
-        mod_cols = jnp.dot(jax.nn.silu(cond), w_ada, precision=PRECISE) + b_ada
-        flat = jnp.stack([condition] + [send(condition, to_level[k]) for k in range(1, levels)])
-        flat = jnp.concatenate([flat, send(flat, to_x)], axis=0)
-        flat = jnp.concatenate([flat, send(flat, to_core)], axis=0)
-        silu_all = jax.nn.silu(flat.reshape(ring * images, width).astype(F32))
-        biases = jnp.concatenate([b_up, b_query, b_value])[None]
-        spread = lax.all_gather(jnp.concatenate([mod_cols, biases], axis=0)[None], "heads", axis=0, tiled=True)
-        parts = three_parts(spread[:, :images])
-        up_bias = spread[:, images:, :units]
-        qkv_bias = jnp.concatenate(
-            [
-                spread[:, images:, units : units + cols],
-                jnp.zeros((2, 1, cols), F32),
-                spread[:, images:, units + cols :],
-            ],
-            axis=2,
-        )
 
         tiles = length // TILE
         tile_of = jnp.arange(length, dtype=jnp.int32) // TILE
@@ -1215,25 +1243,117 @@
         core_of, x_of, level_of = order // (ring // 2), (order // levels) % 2, order % levels
         owner = ((r // 4 + level_of) % levels) * 4 + ((r // 2 % 2) ^ x_of) * 2 + ((r % 2) ^ core_of)
         piece = width // ring
-        feature = (owner[:, None] * piece + jnp.arange(piece, dtype=jnp.int32)[None, :]).reshape(-1)
-        perm = (feature[:, None] == jnp.arange(width, dtype=jnp.int32)[None, :]).astype(BF)
+        place = jnp.sum(jnp.where(owner[None, :] == order[:, None], order[None, :], 0), axis=1)
+        side = jnp.concatenate([y.reshape(1), place, owner])
 
         padded = -(-3 * cols // 128) * 128
         out_width = -(-cols // 128) * 128
-        hidden_full, hidden_half, hidden_one_turned = first_norm(side, tokens, hot, parts, perm, third)
-        hidden_got = send(hidden_half, to_heads)
-        qkv_first, qkv_second, qkv_own, qkv_got = project(
-            side, hidden_full, hidden_half, hidden_got, attention_weights, qkv_bias, padded
-        )
+        level, x_bit, core_bit = r // 4, (r // 2) % 2, r % 2
+        next_level = to_level[levels - 1]
+
+        def placed(bit, own, got):
+            return jnp.where(bit == 0, jnp.stack([own, got]), jnp.stack([got, own]))
+
+        def round_of(found):
+            return lax.dynamic_slice_in_dim(
+                jnp.stack(found + found), (levels - level) % levels, levels, axis=0
+            )
+
+        shard = jnp.concatenate([w_query, w_key, w_value, w_out], axis=1).astype(BF)
+        count = shard.shape[1] // 3
+        steps = [shard[:, : 2 * count]]
+        last = shard[:, 2 * count :]
+        cond = condition.astype(F32)
+        mod_cols, got, last_got = after(
+            jnp.dot(jax.nn.silu(cond), w_ada, precision=PRECISE) + b_ada,
+            send(steps[0], next_level),
+            send(last, to_x),
+        )
+        steps.append(got)
+        last = placed(x_bit, last, last_got)
+        biases = jnp.concatenate([b_up, b_query, b_value])[None]
+        own_spread = jnp.concatenate([mod_cols, biases], axis=0)
+        got_spread, got, last_got, hot, turn, side, *marks = after(
+            send(own_spread, to_heads),
+            send(steps[1], next_level),
+            send(last, to_heads),
+            hot,
+            turn,
+            side,
+            *marks_full,
+            *marks_half,
+        )
+        marks_full, marks_half = marks[:2], marks[2:]
+        steps.append(got)
+        last = [placed(y, last, last_got)]
+        spread = placed(y, own_spread, got_spread)
+        parts = three_parts(spread[:, :images])
+        up_bias = spread[:, images:, :units]
+        qkv_bias = jnp.concatenate(
+            [
+                spread[:, images:, units : units + cols],
+                jnp.zeros((2, 1, cols), F32),
+                spread[:, images:, units + cols :],
+            ],
+            axis=2,
+        )
+        hidden_full, hidden_half, hidden_one_turned, got, last_got = after(
+            *first_norm(side, tokens, hot, parts, third),
+            send(steps[2], next_level),
+            send(last[0], next_level),
+        )
+        first = round_of([*steps, got])
+        last.append(last_got)
+        over_x, over_y = first[..., :count], first[..., count:]
+        x_got, y_got, last_got = after(
+            send(over_x, to_x), send(over_y, to_heads), send(last[1], next_level)
+        )
+        over_x, over_y = placed(x_bit, over_x, x_got), placed(y, over_y, y_got)
+        last.append(last_got)
+        hidden_got, x_got, y_got, last_got = after(
+            send(hidden_half, to_heads),
+            send(over_x, to_heads),
+            send(over_y, to_x),
+            send(last[2], next_level),
+        )
+        over_x, over_y = placed(y, over_x, x_got), placed(x_bit, over_y, y_got)
+        last = round_of([*last, last_got])
+        feed_shard = jnp.stack([w_up, w_down]).astype(BF)
+        over_x, over_y, last, feed_shard = after(over_x, over_y, last, feed_shard)
+        feed_weights = lax.all_gather(
+            feed_shard, ("heads", "rows"), axis=1, tiled=True
+        ).reshape(2, 2, width, units)
+        x_got, y_got, last_got = after(
+            send(over_x, to_core), send(over_y, to_core), send(last, to_core)
+        )
+        attention_weights = collected(
+            core_bit.reshape(1), over_x, x_got, over_y, y_got, last, last_got
+        ).reshape(2, width, shard.shape[1])
+
+        qkv_first, qkv_second, qkv_own, qkv_got, *got = after(
+            *project(
+                side, hidden_full, hidden_half, hidden_got, attention_weights, qkv_bias, padded
+            ),
+            *(send(condition, to_level[k]) for k in range(1, levels)),
+        )
+        flat = jnp.stack([condition, *got])
         qkv_full = (qkv_first, qkv_second)
         qkv_half = (qkv_own, qkv_got)
-        out_own, out_theirs, *lse_half = attend(*qkv_half, *marks_half, out_width)
-        out_other = send(out_theirs, to_heads)
-        qkv_first, out_own = lax.optimization_barrier((qkv_first, out_own))
-        out_first, out_second, *lse_full = attend(qkv_first, qkv_second, *marks_full, out_width)
+        out_own, out_theirs, *lse_half, got = after(
+            *attend(*qkv_half, *marks_half, out_width), send(flat, to_x)
+        )
+        flat = jnp.concatenate([flat, got], axis=0)
+        qkv_first, out_theirs, flat = after(qkv_first, out_theirs, flat)
+        out_first, out_second, *lse_full, out_other, got = after(
+            *attend(qkv_first, qkv_second, *marks_full, out_width),
+            send(out_theirs, to_heads),
+            send(flat, to_core),
+        )
+        flat = jnp.concatenate([flat, got], axis=0)
+        silu_all = jax.nn.silu(flat.reshape(ring * images, width).astype(F32))
         attended = (out_first, out_second, out_own, out_other)
         branch_one, hidden_two, grad_two, hidden_two_turned, grad_two_turned, grad_b_down = middle_part(
-            side, tokens, cotangent, attended, attention_weights, b_out[None], hot, parts, perm, third // 2
+            side, tokens, cotangent, attended, attention_weights, b_out[None], hot, parts, third // 2
         )
 
         def added(mine, got):
@@ -1247,9 +1367,6 @@
             for part in got:
                 kept = added(kept, part)
             return kept
-
-        def after(value, *others):
-            return lax.optimization_barrier((value, *others))
 
         quarter = width // 4
 
@@ -1263,14 +1380,16 @@
                 far(mine_other, got_other),
             )
 
-        feed_args = (hidden_two_turned, grad_two_turned, feed_weights, up_bias, third, 768)
+        flat_turned = lambda values: values.reshape(width, rows)
+        hidden_one_turned = flat_turned(hidden_one_turned)
+        feed_args = (flat_turned(hidden_two_turned), flat_turned(grad_two_turned), feed_weights, up_bias, third, 768)
         two_b, back_b, mine_b, near_b, far_b, grad_b_up_b = feed(
-            1 - side, hidden_two, grad_two, *feed_args
+            1 - y.reshape(1), hidden_two, grad_two, *feed_args
         )
         far_b = added(mine_b[:, quarter:], send(far_b, to_core)).astype(BF)
         hidden_two, far_b, near_b = after(hidden_two, far_b, near_b)
         two_a, back_a, mine_a, near_a, far_a, grad_b_up_a, near_b, far_b = after(
-            *feed(side, hidden_two, grad_two, *feed_args),
+            *feed(y.reshape(1), hidden_two, grad_two, *feed_args),
             send(near_b, to_core),
             send(far_b, to_x),
         )
@@ -1281,7 +1400,7 @@
         output, grad_middle, *grad_attended, sums_two, grad_b_out, out_mine, out_theirs_sum, over_b, far_a, near_a = after(
             *back_two(
                 side, tokens, cotangent, branch_one, two_a, two_b, b_down[None], back_a, back_b, attention_weights,
-                hot, turn, parts, perm, attended, third // 2, images, out_width,
+                hot, turn, parts, attended, third // 2, images, out_width,
             ),
             send(over_b, to_heads),
             send(far_a, to_x),
@@ -1296,34 +1415,35 @@
         )
         grad_own, feed_kept, *joined = after(grad_own, feed_kept, *feed_sent, *out_pieces)
         feed_sent, out_pieces = joined[: levels - 1], joined[levels - 1 :]
-        grad_qkv_own, grad_qkv_theirs, *out_pieces = after(
-            *attend_back(*qkv_half, grad_own, grad_other, *lse_half, *marks_half),
-            out_pieces[0],
+        grad_qkv_own, grad_qkv_theirs = attend_back(
+            *qkv_half, grad_own, grad_other, *lse_half, *marks_half
+        )
+        grad_first, grad_qkv_theirs, feed_kept, *joined = after(
+            grad_first, grad_qkv_theirs, feed_kept, *feed_sent, *out_pieces
+        )
+        feed_sent, out_pieces = joined[: levels - 1], joined[levels - 1 :]
+        grad_qkv_first, grad_qkv_second, grad_qkv_other, *got = after(
+            *attend_back(*qkv_full, grad_first, grad_second, *lse_full, *marks_full),
+            send(grad_qkv_theirs, to_heads),
+            *(send(part, to_level[k + 1]) for k, part in enumerate(feed_sent)),
+        )
+        grad_w_up, grad_w_down = all_added(feed_kept, got)
+        qkv_mine_b, qkv_theirs_b, grad_qkv_bias_b, *got = after(
+            *outer(hidden_one_turned, grad_qkv_first, grad_qkv_second, grad_qkv_other, 1),
             send(out_pieces[1], to_x),
             send(out_pieces[2], to_heads),
             send(out_pieces[3], to_corner),
         )
-        out_kept, *out_sent = level_pieces(
-            added(added(added(out_pieces[0], out_pieces[1]), out_pieces[2]), out_pieces[3])
-        )
-        grad_first, grad_qkv_theirs, feed_kept, out_kept, *joined = after(
-            grad_first, grad_qkv_theirs, feed_kept, out_kept, *feed_sent, *out_sent
-        )
-        grad_qkv_first, grad_qkv_second, grad_qkv_other, *got = after(
-            *attend_back(*qkv_full, grad_first, grad_second, *lse_full, *marks_full),
-            send(grad_qkv_theirs, to_heads),
-            *(send(part, to_level[k % (levels - 1) + 1]) for k, part in enumerate(joined)),
-        )
-        grad_w_up, grad_w_down = all_added(feed_kept, got[: levels - 1])
-        grad_w_out = all_added(out_kept, got[levels - 1 :])
-        qkv_mine_b, qkv_theirs_b, grad_qkv_bias_b = outer(
-            hidden_one_turned, grad_qkv_first, grad_qkv_second, grad_qkv_other, 1
-        )
-        hidden_one_turned, qkv_theirs_b = after(hidden_one_turned, qkv_theirs_b)
-        qkv_mine_a, qkv_theirs_a, grad_qkv_bias_a, qkv_got_b = after(
+        out_kept, *out_sent = level_pieces(all_added(out_pieces[0], got))
+        hidden_one_turned, qkv_theirs_b, out_kept, *out_sent = after(
+            hidden_one_turned, qkv_theirs_b, out_kept, *out_sent
+        )
+        qkv_mine_a, qkv_theirs_a, grad_qkv_bias_a, qkv_got_b, *got = after(
             *outer(hidden_one_turned, grad_qkv_first, grad_qkv_second, grad_qkv_own, 0),
             send(qkv_theirs_b, to_core),
-        )
+            *(send(part, to_level[k + 1]) for k, part in enumerate(out_sent)),
+        )
+        grad_w_out = all_added(out_kept, got)
         near, *sent = plane_pieces(qkv_mine_a, send(qkv_theirs_a, to_core), qkv_mine_b, qkv_got_b)
         grad_middle, near, *sent = after(grad_middle, near, *sent)
         grad_qkv = (grad_qkv_first, grad_qkv_second, grad_qkv_own, grad_qkv_other)
@@ -1342,39 +1462,48 @@
         narrow = jnp.concatenate([grad_b_out, grad_b_down], axis=0).reshape(2, 2, cols)
 
         def packet(which, up_sum, qkv_sum):
-            first = jnp.concatenate([up_sum[0], qkv_sum[:cols], qkv_sum[2 * cols : 3 * cols]])
             second = lax.dynamic_index_in_dim(narrow, which, 1, keepdims=False).reshape(-1)
-            second = jnp.concatenate([second, jnp.zeros((3 * width - 2 * cols,), F32)])
+            short = [up_sum[0], qkv_sum[:cols], qkv_sum[2 * cols : 3 * cols], second]
+            short = jnp.concatenate(short).reshape(images, -1)
             chunk = lax.dynamic_index_in_dim(sums, which, 0, keepdims=False)
-            return jnp.concatenate([chunk, first[None], second[None]], axis=0)
+            gap = -(chunk.shape[1] + short.shape[1]) % 128
+            return jnp.concatenate([chunk, short, jnp.zeros((images, gap), F32)], axis=1)
 
         own_packet = packet(y, grad_b_up_a, grad_qkv_bias_a[0]) + send(
             packet(1 - y, grad_b_up_b, grad_qkv_bias_b[0]), to_heads
         )
         own_packet, qkv_kept, *qkv_sent = after(own_packet, qkv_kept, *qkv_sent)
-        levelled = [own_packet] + [send(own_packet, to_level[k]) for k in range(1, levels)]
-        qkv_kept = all_added(qkv_kept, [send(part, to_level[k + 1]) for k, part in enumerate(qkv_sent)])
-        grad_w_qkv = qkv_kept
-        flat = jnp.stack(levelled)
-        flat = jnp.concatenate([flat, send(flat, to_x)], axis=0)
-        packets = jnp.concatenate([flat, send(flat, to_core)], axis=0)
-        grad_mod = packets[:, :images].reshape(ring * images, 3 * width)
-        bias_sums = jnp.sum(packets[:, images : images + 2], axis=0)
-        s1, s2, s3 = jnp.split(three_parts(silu_all), 3, axis=0)
-        g1, g2, g3 = jnp.split(three_parts(grad_mod), 3, axis=0)
-        grad_w_ada = contract_first(
-            jnp.concatenate([s1, s1, s2, s1, s2, s3], axis=0),
-            jnp.concatenate([g1, g2, g1, g3, g2, g1], axis=0),
-        )
-        grad_b_ada = jnp.sum(grad_mod, axis=0)
         grad_silu = lax.dot_general(
-            own_packet[:images],
+            own_packet[:, : 3 * width],
             w_ada,
             (((1,), (1,)), ((), ())),
             precision=PRECISE,
             preferred_element_type=F32,
         )
-        grad_silu = grad_silu + send(grad_silu, to_heads)
+        grad_silu, *got = after(
+            grad_silu, *(send(own_packet, to_level[k]) for k in range(1, levels))
+        )
+        flat = jnp.concatenate([own_packet, *got], axis=0)
+        flat, *qkv_sent = after(flat, *qkv_sent)
+        silu_got, flat_got, *got = after(
+            send(grad_silu, to_heads),
+            send(flat, to_x),
+            *(send(part, to_level[k + 1]) for k, part in enumerate(qkv_sent)),
+        )
+        grad_w_qkv = all_added(qkv_kept, got)
+        flat = jnp.concatenate([flat, flat_got], axis=0)
+        packets = jnp.concatenate([flat, send(flat, to_core)], axis=0)
+        grad_mod = packets[:, : 3 * width]
+        count = units + 4 * cols
+        short = packets[:, 3 * width : 3 * width + count // images]
+        bias_sums = jnp.sum(short.reshape(ring, images, count // images), axis=0).reshape(-1)
+        s1, s2, _ = jnp.split(three_parts(silu_all), 3, axis=0)
+        g1, g2, _ = jnp.split(three_parts(grad_mod), 3, axis=0)
+        grad_w_ada = contract_first(
+            jnp.concatenate([s1, s1, s2], axis=0), jnp.concatenate([g1, g2, g1], axis=0)
+        )
+        grad_b_ada = jnp.sum(grad_mod, axis=0)
+        grad_silu = grad_silu + silu_got
         _, silu_back = jax.vjp(jax.nn.silu, cond)
         grad_condition = silu_back(grad_silu)[0]
         return (
@@ -1386,14 +1515,14 @@
             grad_w_qkv[:, :cols],
             grad_w_qkv[:, cols : 2 * cols],
             grad_w_qkv[:, 2 * cols : 3 * cols],
-            bias_sums[0, units : units + cols],
-            bias_sums[0, units + cols :],
+            bias_sums[units : units + cols],
+            bias_sums[units + cols : units + 2 * cols],
             grad_w_out[:, :cols],
-            bias_sums[1, :cols],
+            bias_sums[units + 2 * cols : units + 3 * cols],
             grad_w_up,
-            bias_sums[0, :units],
+            bias_sums[:units],
             grad_w_down,
-            bias_sums[1, cols : 2 * cols],
+            bias_sums[units + 3 * cols :],
         )
 
     return body

time: 843 us -> 822 us (0.975)
  Pallas kernels: 508 us -> 492 us
    ppermute x41 -> x57, waiting for transfers between devices: 71 us -> 109 us  [send(): return lax.ppermute(values, both, pairs)]
    all_gather x2 -> x1, waiting for transfers between devices: 49.5 us -> 12.7 us  [body(): lax.all_gather(feed_shard, ('heads', 'rows'), axis=1, tiled=True)]
    pallas_call x1, Pallas kernels: 58.1 us -> 47.8 us  [back_two(): pl.pallas_call(back_two_kernel, grid_spec=pltpu.PrefetchScalarGridSpec(nu...]
    unnamed x61 -> x99, local copies, waits for them, and re-layouts: 4.85 us -> 15 us
    ppermute x41 -> x57, starting transfers between devices: 66.2 us -> 62.1 us  [send(): return lax.ppermute(values, both, pairs)]
  transfers between devices with their start and end apart: 43 -> 58, of which waited for: 11 -> 19; matrix products, arithmetic and copies ran while one was open for 10% -> 10% of each run, Pallas kernels for 50% -> 46%
where the time goes in v3:
time: 822 us; the launch traced here: 812 us
  Pallas kernels  492 us (60%)
  waiting for transfers between devices  122 us (15%)
  starting transfers between devices  62.1 us (8%)
  other arithmetic  50.6 us (6%)
  matrix products  36.5 us (4%)
  local copies, waits for them, and re-layouts  34.3 us (4%)
  between operations  15.2 us (2%)
    pallas_call x2, Pallas kernels, feed(): pl.pallas_call(partial(feed_kernel, chunk), grid_spec=pltpu.PrefetchScala...  141 us
    pallas_call x2, Pallas kernels, attend_back(): pl.pallas_call(partial(attend_back_kernel, heads), grid=(groups, 2), in_s...  124 us
    ppermute x57, waiting for transfers between devices, send(): return lax.ppermute(values, both, pairs)  109 us
    pallas_call x2, Pallas kernels, attend(): pl.pallas_call(partial(attend_kernel, heads), grid=(groups, 2), in_specs=...  62.5 us
    ppermute x57, starting transfers between devices, send(): return lax.ppermute(values, both, pairs)  62.1 us
    pallas_call x1, Pallas kernels, back_two(): pl.pallas_call(back_two_kernel, grid_spec=pltpu.PrefetchScalarGridSpec(nu...  47.8 us
    pallas_call x1, Pallas kernels, back_one(): pl.pallas_call(back_one_kernel, grid_spec=pltpu.PrefetchScalarGridSpec(nu...  31.6 us
    pallas_call x2, Pallas kernels, outer(): pl.pallas_call(outer_kernel, grid=(2,), in_specs=[pl.BlockSpec((width //...  27.6 us
  transfers between devices with their start and end apart: 58, of which 19 were waited for; matrix products, arithmetic and copies ran while one was open for 10% of the time, Pallas kernels for 46%

profile of v3, /device:TPU:9, one launch (start us, length us, event | category | flops | bytes accessed | tf_op | source)
XLA Modules:
  0.0 812.2 jit_solution(1337315273447238954)
XLA Ops:
  19.3 11.3 %convolution_add_fusion = f32[8,3456]{1,0:T(8,128)S(1)} fusion(f32[1152,3456]{1,0:T(8,128)} %param.24, f32[3456]{0:T(1024)S(1)} %copy-done.26, bf16[8,1152]{1,0:T(8,128)(2,1)S(1)} %copy-done.16), kind=kOutput, calls=%fused_computation.4 | convolution fusion | flops 382279680 | bytes 16068096 | tf_op jit(solution)/shard_map/dot_general | solution.py:1268
  33.3 3.3 collective-permute-start.3
  38.0 4.2 collective-permute-done.2
  42.4 3.7 collective-permute-start.6
  47.0 9.1 %shard_map.306 = (bf16[1024,1152]{1,0:T(8,128)(2,1)}, bf16[512,1152]{1,0:T(8,128)(2,1)}, bf16[16,72,1536]{2,1,0:T(8,128)(2,1)}) custom-call(s32[33]{0:T(128)} %pad_add_fusion.2.side, bf16[1536,1152]{1,0:T(8,128)(2,1)} %tok_ref.7, bf16[1536,24]{1,0:T(8,128)(2,1)} %compare_convert_fusion.hot_ref, bf16[2,24,3456]{2,1,0:T(8,128)(2,1)} %pad_maximum_fusion.3.parts_ref), custom_call_target="tpu_custom_call" | custom-call | flops 5888802816 | bytes 10616832 | tf_op jit(solution)/shard_map/pallas_call | solution.py:458
  56.2 1.9 collective-permute-done.5
  59.9 2.2 collective-permute-start.10
  63.2 3.7 collective-permute-done.8
  69.9 2.3 collective-permute-start.13
  72.5 5.5 collective-permute-done.13
  78.0 14.2 %collective-permute-done.7.got_ref = bf16[512,1152]{1,0:T(8,128)(2,1)S(1)} collective-permute-done((bf16[512,1152]{1,0:T(8,128)(2,1)}, bf16[512,1152]{1,0:T(8,128)(2,1)S(1)}, u32[]{:S(2)}, u32[]{:S(2)}) %collective-permute-start.7) | collective-permute-done | bytes 1179680 | tf_op jit(solution)/shard_map/ppermute | solution.py:1168
  92.2 19.0 %collective-permute-done.11 = bf16[2,4,72,768]{3,2,1,0:T(8,128)(2,1)S(1)} collective-permute-done((bf16[2,4,72,768]{3,2,1,0:T(8,128)(2,1)S(1)}, bf16[2,4,72,768]{3,2,1,0:T(8,128)(2,1)S(1)}, u32[]{:S(2)}, u32[]{:S(2)}) %collective-permute-start.11) | collective-permute-done | bytes 884768 | tf_op jit(solution)/shard_map/ppermute | solution.py:1168
  111.9 1.5 maximum_select_fusion.over_x
  113.4 4.3 collective-permute-start.14
  118.4 4.1 collective-permute-start.18
  124.5 1.5 slice.367.bias_ref
  126.0 1.6 copy.65.qm_ref
  127.6 1.6 copy.66.qm_ref
  132.7 1.5 copy-done.1
  134.2 3.8 shard_map.307
  138.0 4.1 copy-done
  142.2 22.5 %shard_map.308 = (bf16[2,512,1792]{2,1,0:T(8,128)(2,1)}, bf16[2,512,1792]{2,1,0:T(8,128)(2,1)}, bf16[1,512,1792]{2,1,0:T(8,128)(2,1)}, bf16[1,512,1792]{2,1,0:T(8,128)(2,1)}) custom-call(s32[33]{0:T(128)} %pad_add_fusion.2.side, bf16[1024,1152]{1,0:T(8,128)(2,1)} %get-tuple-element.235.full_ref, bf16[512,1152]{1,0:T(8,128)(2,1)} %get-tuple-element.236.own_ref, ...), custom_call_target="tpu_custom_call" | custom-call | flops 12683575296 | bytes 19267584 | tf_op jit(solution)/shard_map/pallas_call | solution.py:506
  168.2 21.9 %shard_map.309 = (bf16[1,512,640]{2,1,0:T(8,128)(2,1)}, bf16[1,512,640]{2,1,0:T(8,128)(2,1)}, f32[1,8,512]{2,1,0:T(8,128)}, f32[1,8,512]{2,1,0:T(8,128)}) custom-call(bf16[1,512,1792]{2,1,0:T(8,128)(2,1)} %get-tuple-element.257.first, bf16[1,512,1792]{2,1,0:T(8,128)(2,1)} %get-tuple-element.258.second, bf16[1024,16]{1,0:T(8,128)(2,1)} %copy.65.qm_ref, ...), custom_call_target="tpu_custom_call" | custom-call | flops 15000000512 | bytes 5505024 | tf_op jit(solution)/shard_map/pallas_call | solution.py:609
  191.5 1.5 collective-permute-start.22
  192.9 40.6 %shard_map.310 = (bf16[2,512,640]{2,1,0:T(8,128)(2,1)}, bf16[2,512,640]{2,1,0:T(8,128)(2,1)}, f32[2,8,512]{2,1,0:T(8,128)}, f32[2,8,512]{2,1,0:T(8,128)}) custom-call(bf16[2,512,1792]{2,1,0:T(8,128)(2,1)} %get-tuple-element.270.first, bf16[2,512,1792]{2,1,0:T(8,128)(2,1)} %get-tuple-element.271.second, bf16[1024,16]{1,0:T(8,128)(2,1)} %copy.66.qm_ref, ...), custom_call_target="tpu_custom_call" | custom-call | flops 30000001024 | bytes 11010048 | tf_op jit(solution)/shard_map/pallas_call | solution.py:609
  235.1 21.6 %shard_map.311 = (f32[1536,1152]{1,0:T(8,128)}, bf16[1536,1152]{1,0:T(8,128)(2,1)}, bf16[1536,1152]{1,0:T(8,128)(2,1)}, bf16[16,72,1536]{2,1,0:T(8,128)(2,1)}, b...) custom-call(s32[33]{0:T(128)} %pad_add_fusion.2.side, bf16[1536,1152]{1,0:T(8,128)(2,1)} %tok_ref.7, ...), custom_call_target="tpu_custom_call" | custom-call | flops 15854469120 | bytes 38928384 | tf_op jit(solution)/shard_map/pallas_call | solution.py:811
  256.7 12.7 %all-gather.2.cloned.1.call-done = bf16[2,2304,2304]{2,1,0:T(8,128)(2,1)} async-done(((bf16[2,72,2304]{2,1,0:T(8,128)(2,1)}), bf16[2,2304,2304]{2,1,0:T(8,128)(2,1)}) %all-gather.2.cloned.1.call-update) | async-done | bytes 21233680 | tf_op jit(solution)/shard_map/all_gather | solution.py:1323
  269.4 70.1 %shard_map.312 = (f32[1536,1152]{1,0:T(8,128)}, f32[1536,1152]{1,0:T(8,128)}, f32[2,576,2304]{2,1,0:T(8,128)}, bf16[2,288,2304]{2,1,0:T(8,128)(2,1)}, bf16[2,288,2304]{2,1,0:T(8,128)(2,1)}, /*index=5*/f32[1,2304]{1,0:T(1,128)}) custom-call(s32[1]{0:T(128)S(6)} %sub.60.pick, bf16[1536,1152]{1,0:T(8,128)(2,1)} %get-tuple-element.293.h_ref, ...), custom_call_target="tpu_custom_call" | custom-call | flops 48922361856 | bytes 54853632 | tf_op jit(solution)/shard_map/pallas_call | solution.py:891
  339.8 4.9 collective-permute-done.23
  344.7 4.7 add_convert_fusion.2
  350.5 70.6 %shard_map.313 = (f32[1536,1152]{1,0:T(8,128)}, f32[1536,1152]{1,0:T(8,128)}, f32[2,576,2304]{2,1,0:T(8,128)}, bf16[2,288,2304]{2,1,0:T(8,128)(2,1)}, bf16[2,288,2304]{2,1,0:T(8,128)(2,1)}, /*index=5*/f32[1,2304]{1,0:T(1,128)}) custom-call(s32[1]{0:T(128)} %bitcast.8.pick, bf16[1536,1152]{1,0:T(8,128)(2,1)} %get-tuple-element.293.h_ref, ...), custom_call_target="tpu_custom_call" | custom-call | flops 48922361856 | bytes 54853632 | tf_op jit(solution)/shard_map/pallas_call | solution.py:891
  421.7 5.8 add_convert_fusion.1
  427.5 1.5 copy-done.2
  428.9 2.1 add_convert_fusion
  433.0 47.8 %shard_map.314 = (bf16[1536,1152]{1,0:T(8,128)(2,1)}, f32[1536,1152]{1,0:T(8,128)}, bf16[2,512,640]{2,1,0:T(8,128)(2,1)}, bf16[2,512,640]{2,1,0:T(8,128)(2,1)}, ...) custom-call(s32[33]{0:T(128)} %pad_add_fusion.2.side, ...), custom_call_target="tpu_custom_call" | custom-call | flops 19931332608 | bytes 60162048 | tf_op jit(solution)/shard_map/pallas_call | solution.py:1014
  480.9 9.7 %collective-permute-done.27 = bf16[2,288,2304]{2,1,0:T(8,128)(2,1)} collective-permute-done((bf16[2,288,2304]{2,1,0:T(8,128)(2,1)}, bf16[2,288,2304]{2,1,0:T(8,128)(2,1)}, u32[]{:S(2)}, u32[]{:S(2)}) %collective-permute-start.27) | collective-permute-done | bytes 2654240 | tf_op jit(solution)/shard_map/ppermute | solution.py:1168
  492.8 6.0 fusion.62
  502.5 6.1 collective-permute-done.31.do_second
  508.7 52.1 %shard_map.315 = (bf16[1,512,1792]{2,1,0:T(8,128)(2,1)}, bf16[1,512,1792]{2,1,0:T(8,128)(2,1)}) custom-call(bf16[1,512,1792]{2,1,0:T(8,128)(2,1)} %get-tuple-element.257.first, bf16[1,512,1792]{2,1,0:T(8,128)(2,1)} %get-tuple-element.258.second, bf16[1,512,640]{2,1,0:T(8,128)(2,1)} %get-tuple-element.334.do_first, ...), custom_call_target="tpu_custom_call" | custom-call | flops 12000000000 | bytes 11010048 | tf_op jit(solution)/shard_map/pallas_call | solution.py:711
  561.7 2.4 collective-permute-start.34
  565.8 72.4 %shard_map.316 = (bf16[2,512,1792]{2,1,0:T(8,128)(2,1)}, bf16[2,512,1792]{2,1,0:T(8,128)(2,1)}) custom-call(bf16[2,512,1792]{2,1,0:T(8,128)(2,1)} %get-tuple-element.270.first, bf16[2,512,1792]{2,1,0:T(8,128)(2,1)} %get-tuple-element.271.second, bf16[2,512,640]{2,1,0:T(8,128)(2,1)} %get-tuple-element.347.do_first, ...), custom_call_target="tpu_custom_call" | custom-call | flops 24000000000 | bytes 22020096 | tf_op jit(solution)/shard_map/pallas_call | solution.py:711
  639.8 13.8 %shard_map.317 = (f32[576,1792]{1,0:T(8,128)}, bf16[576,1792]{1,0:T(8,128)(2,1)}, f32[1,1792]{1,0:T(1,128)}) custom-call(bf16[1152,1536]{1,0:T(8,128)(2,1)} %bitcast.166, bf16[2,512,1792]{2,1,0:T(8,128)(2,1)} %get-tuple-element.357.first, bf16[2,512,1792]{2,1,0:T(8,128)(2,1)} %get-tuple-element.358.second, ...), custom_call_target="tpu_custom_call" | custom-call | flops 6341787648 | bytes 14548992 | tf_op jit(solution)/shard_map/pallas_call | solution.py:1084
  653.6 1.9 collective-permute-done.37
  658.2 2.0 collective-permute-start.39
  660.3 2.0 reduce-precision_convert_fusion.1
  664.9 1.8 collective-permute-start.41
  666.7 13.8 %shard_map.318 = (f32[576,1792]{1,0:T(8,128)}, bf16[576,1792]{1,0:T(8,128)(2,1)}, f32[1,1792]{1,0:T(1,128)}) custom-call(bf16[1152,1536]{1,0:T(8,128)(2,1)} %bitcast.167, bf16[2,512,1792]{2,1,0:T(8,128)(2,1)} %get-tuple-element.357.first, bf16[2,512,1792]{2,1,0:T(8,128)(2,1)} %get-tuple-element.358.second, bf16[1,512,1792]{2,1,0:T(8,128)(2,1)} %get-tuple-element.359.rest.own), custom_call_target="tpu_custom_call" | custom-call | flops 6341787648 | bytes 14548992 | tf_op jit(solution)/shard_map/pallas_call | solution.py:1084
  681.4 1.7 convert_add_fusion.3
  684.5 2.8 add_convert_fusion.3
  687.9 1.9 add_convert_fusion.5
  692.6 31.6 %shard_map.319 = (f32[1536,1152]{1,0:T(8,128)}, f32[2,8,1152]{2,1,0:T(8,128)}) custom-call(s32[33]{0:T(128)} %pad_add_fusion.2.side, bf16[2,512,1792]{2,1,0:T(8,128)(2,1)} %get-tuple-element.357.first, bf16[2,512,1792]{2,1,0:T(8,128)(2,1)} %get-tuple-element.358.second, bf16[1,512,1792]{2,1,0:T(8,128)(2,1)} %get-tuple-element.359.rest.own, ...), custom_call_target="tpu_custom_call" | custom-call | flops 12683575296 | bytes 28704768 | tf_op jit(solution)/shard_map/pallas_call | solution.py:1122
  724.2 13.3 %collective-permute-done.46 = bf16[288,1792]{1,0:T(8,128)(2,1)} collective-permute-done((bf16[288,1792]{1,0:T(8,128)(2,1)S(1)}, bf16[288,1792]{1,0:T(8,128)(2,1)}, u32[]{:S(2)}, u32[]{:S(2)}) %collective-permute-start.46) | collective-permute-done | bytes 1032224 | tf_op jit(solution)/shard_map/ppermute | solution.py:1168
  738.8 2.0 fusion.60
  741.0 1.7 collective-permute-done.47
  742.8 1.8 collective-permute-start.48
  744.6 2.4 collective-permute-start.49
  746.9 16.9 %fusion.25 = f32[8,1152]{1,0:T(8,128)S(1)} fusion(f32[1152,3456]{1,0:T(8,128)} %param.24, f32[8,4096]{1,0:T(8,128)S(1)} %add.263), kind=kOutput, calls=%fused_computation.92 | convolution fusion | flops 382205952 | bytes 16072704 | tf_op jit(solution)/shard_map/dot_general | solution.py:1476
  764.1 1.7 fusion.24
  765.7 1.5 collective-permute-start.53
  767.2 1.8 collective-permute-start.54
  770.0 2.1 collective-permute-done.51
  772.1 14.9 %collective-permute-done.54 = bf16[72,1792]{1,0:T(8,128)(2,1)S(1)} collective-permute-done((bf16[72,1792]{1,0:T(8,128)(2,1)S(1)}, bf16[72,1792]{1,0:T(8,128)(2,1)S(1)}, u32[]{:S(2)}, u32[]{:S(2)}) %collective-permute-start.54) | collective-permute-done | bytes 258080 | tf_op jit(solution)/shard_map/ppermute | solution.py:1168
  787.0 4.0 collective-permute-done.55
  796.9 8.2 %fusion = f32[1152,3456]{1,0:T(8,128)} fusion(bf16[128,3456]{1,0:T(8,128)(2,1)S(1)} %get-tuple-element.461, bf16[128,3456]{1,0:T(8,128)(2,1)S(1)} %get-tuple-element.460, bf16[128,1152]{1,0:T(8,128)(2,1)S(1)} %copy-done.7, bf16[128,1152]{1,0:T(8,128)(2,1)S(1)} %copy-done.6), kind=kOutput, calls=%fused_computation.5 | convolution fusion | flops 3068264448 | bytes 18284544 | tf_op jit(solution)/shard_map/dot_general | solution.py:40
  (294 shorter events, 70.0 us)
Async XLA Ops:
  7.3 262.1 %all-gather.2.cloned.1.call-start = ((), (), s32[]{:S(2)}) async-start(), calls=%async_computation | async-start | bytes 21897216 | tf_op jit(solution)/shard_map/all_gather | solution.py:1323
  10.4 21.6 %collective-permute-start = (bf16[72,1536]{1,0:T(8,128)(2,1)S(1)}, bf16[72,1536]{1,0:T(8,128)(2,1)S(1)}, u32[]{:S(2)}, u32[]{:S(2)}) collective-permute-start(bf16[72,1536]{1,0:T(8,128)(2,1)S(1)} %slice.363), channel_id=1, source_target_pairs={{0,24},{1,25},{2,26},{3,27},{4,28},{5,29},{6,30},{7,31},{8,0},{9,1... | collective-permute-start | bytes 663560 | tf_op jit(solution)/shard_map/ppermute | solution.py:1168
  11.5 20.5 %collective-permute-start.1 = (bf16[72,768]{1,0:T(8,128)(2,1)S(1)}, bf16[72,768]{1,0:T(8,128)(2,1)S(1)}, u32[]{:S(2)}, u32[]{:S(2)}) collective-permute-start(bf16[72,768]{1,0:T(8,128)(2,1)S(1)} %pad_maximum_fusion.5), channel_id=1, source_target_pairs={{0,4},{1,5},{2,6},{3,7},{4,0},{5,1},{6,2},{7,3},{8,12},{9,13},{10,... | collective-permute-start | bytes 331784 | tf_op jit(solution)/shard_map/ppermute | solution.py:1168
  32.0 10.2 %collective-permute-start.4 = (bf16[2,72,768]{2,1,0:T(8,128)(2,1)S(1)}, bf16[2,72,768]{2,1,0:T(8,128)(2,1)S(1)}, u32[]{:S(2)}, u32[]{:S(2)}) collective-permute-start(bf16[2,72,768]{2,1,0:T(8,128)(2,1)S(1)} %maximum_select_fusion.9), channel_id=1, source_target_pairs={{0,1},{1,0},{2,3},{3,2},{4,5},{5,4},{6,7},{7,6},{8,9},{9,8},{10,11... | collective-permute-start | bytes 663560 | tf_op jit(solution)/shard_map/ppermute | solution.py:1168
  33.3 8.9 %collective-permute-start.3 = (bf16[72,1536]{1,0:T(8,128)(2,1)S(1)}, bf16[72,1536]{1,0:T(8,128)(2,1)S(1)}, u32[]{:S(2)}, u32[]{:S(2)}) collective-permute-start(bf16[72,1536]{1,0:T(8,128)(2,1)S(1)} %collective-permute-done), channel_id=1, source_target_pairs={{0,24},{1,25},{2,26},{3,27},{4,28},{5,29},{6,30},{7,31},{8,0},{9,1... | collective-permute-start | bytes 663560 | tf_op jit(solution)/shard_map/ppermute | solution.py:1168
  37.0 5.2 collective-permute-start.2
  42.4 15.7 %collective-permute-start.6 = (bf16[2,2,72,768]{3,2,1,0:T(8,128)(2,1)S(1)}, bf16[2,2,72,768]{3,2,1,0:T(8,128)(2,1)S(1)}, u32[]{:S(2)}, u32[]{:S(2)}) collective-permute-start(bf16[2,2,72,768]{3,2,1,0:T(8,128)(2,1)S(1)} %maximum_select_fusion.7), channel_id=1, source_target_pairs={{0,24},{1,25},{2,26},{3,27},{4,28},{5,29},{6,30},{7,31},{8,0},{9,1... | collective-permute-start | bytes 1327112 | tf_op jit(solution)/shard_map/ppermute | solution.py:1168
  46.1 12.0 %collective-permute-start.5 = (bf16[72,1536]{1,0:T(8,128)(2,1)S(1)}, bf16[72,1536]{1,0:T(8,128)(2,1)S(1)}, u32[]{:S(2)}, u32[]{:S(2)}) collective-permute-start(bf16[72,1536]{1,0:T(8,128)(2,1)S(1)} %collective-permute-done.3), channel_id=1, source_target_pairs={{0,24},{1,25},{2,26},{3,27},{4,28},{5,29},{6,30},{7,31},{8,0},{9,1... | collective-permute-start | bytes 663560 | tf_op jit(solution)/shard_map/ppermute | solution.py:1168
  58.3 8.6 %collective-permute-start.8 = (bf16[4,72,768]{2,1,0:T(8,128)(2,1)S(1)}, bf16[4,72,768]{2,1,0:T(8,128)(2,1)S(1)}, u32[]{:S(2)}, u32[]{:S(2)}) collective-permute-start(bf16[4,72,768]{2,1,0:T(8,128)(2,1)S(1)} %get-tuple-element.463), channel_id=1, source_target_pairs={{0,4},{1,5},{2,6},{3,7},{4,0},{5,1},{6,2},{7,3},{8,12},{9,13},{10,... | collective-permute-start | bytes 1327112 | tf_op jit(solution)/shard_map/ppermute | solution.py:1168
  58.6 8.3 %collective-permute-start.9 = (bf16[4,72,768]{2,1,0:T(8,128)(2,1)S(1)}, bf16[4,72,768]{2,1,0:T(8,128)(2,1)S(1)}, u32[]{:S(2)}, u32[]{:S(2)}) collective-permute-start(bf16[4,72,768]{2,1,0:T(8,128)(2,1)S(1)} %get-tuple-element.462), channel_id=1, source_target_pairs={{0,1},{1,0},{2,3},{3,2},{4,5},{5,4},{6,7},{7,6},{8,9},{9,8},{10,11... | collective-permute-start | bytes 1327112 | tf_op jit(solution)/shard_map/ppermute | solution.py:1168
  59.9 8.0 collective-permute-start.10
  63.0 29.2 %collective-permute-start.7 = (bf16[512,1152]{1,0:T(8,128)(2,1)}, bf16[512,1152]{1,0:T(8,128)(2,1)S(1)}, u32[]{:S(2)}, u32[]{:S(2)}) collective-permute-start(bf16[512,1152]{1,0:T(8,128)(2,1)} %get-tuple-element.236.own_ref), channel_id=1, source_target_pairs={{0,1},{1,0},{2,3},{3,2},{4,5},{5,4},{6,7},{7,6},{8,9},{9,8},{10,11... | collective-permute-start | bytes 3538952 | tf_op jit(solution)/shard_map/ppermute | solution.py:1168
  68.0 24.2 %collective-permute-start.12 = (bf16[2,4,72,768]{3,2,1,0:T(8,128)(2,1)S(1)}, bf16[2,4,72,768]{3,2,1,0:T(8,128)(2,1)S(1)}, u32[]{:S(2)}, u32[]{:S(2)}) collective-permute-start(bf16[2,4,72,768]{3,2,1,0:T(8,128)(2,1)S(1)} %maximum_select_fusion.3), channel_id=1, source_target_pairs={{0,4},{1,5},{2,6},{3,7},{4,0},{5,1},{6,2},{7,3},{8,12},{9,13},{10,... | collective-permute-start | bytes 2654216 | tf_op jit(solution)/shard_map/ppermute | solution.py:1168
  69.5 41.7 %collective-permute-start.11 = (bf16[2,4,72,768]{3,2,1,0:T(8,128)(2,1)S(1)}, bf16[2,4,72,768]{3,2,1,0:T(8,128)(2,1)S(1)}, u32[]{:S(2)}, u32[]{:S(2)}) collective-permute-start(bf16[2,4,72,768]{3,2,1,0:T(8,128)(2,1)S(1)} %maximum_select_fusion.2), channel_id=1, source_target_pairs={{0,1},{1,0},{2,3},{3,2},{4,5},{5,4},{6,7},{7,6},{8,9},{9,8},{10,11... | collective-permute-start | bytes 2654216 | tf_op jit(solution)/shard_map/ppermute | solution.py:1168
  69.9 8.1 collective-permute-start.13
  113.4 18.7 %collective-permute-start.14 = (bf16[2,2,4,72,768]{4,3,2,1,0:T(8,128)(2,1)}, bf16[2,2,4,72,768]{4,3,2,1,0:T(8,128)(2,1)}, u32[]{:S(2)}, u32[]{:S(2)}) collective-permute-start(bf16[2,2,4,72,768]{4,3,2,1,0:T(8,128)(2,1)} %maximum_select_fusion.over_x), channel_id=1, source_target_pairs={{0,2},{1,3},{2,0},{3,1},{4,6},{5,7},{6,4},{7,5},{8,10},{9,11},{10,... | collective-permute-start | bytes 5308424 | tf_op jit(solution)/shard_map/ppermute | solution.py:1168
  117.7 15.0 %collective-permute-start.15 = (bf16[2,2,4,72,768]{4,3,2,1,0:T(8,128)(2,1)S(1)}, bf16[2,2,4,72,768]{4,3,2,1,0:T(8,128)(2,1)}, u32[]{:S(2)}, u32[]{:S(2)}) collective-permute-start(bf16[2,2,4,72,768]{4,3,2,1,0:T(8,128)(2,1)S(1)} %maximum_select_fusion.1.over_y), channel_id=1, source_target_pairs={{0,2},{1,3},{2,0},{3,1},{4,6},{5,7},{6,4},{7,5},{8,10},{9,11},{10,... | collective-permute-start | bytes 5308424 | tf_op jit(solution)/shard_map/ppermute | solution.py:1168
  117.8 14.9 %collective-permute-start.16 = (bf16[4,2,2,72,768]{4,3,2,1,0:T(8,128)(2,1)S(1)}, bf16[4,2,2,72,768]{4,3,2,1,0:T(8,128)(2,1)}, u32[]{:S(2)}, u32[]{:S(2)}) collective-permute-start(bf16[4,2,2,72,768]{4,3,2,1,0:T(8,128)(2,1)S(1)} %constant_dynamic-slice_fusion.last), channel_id=1, source_target_pairs={{0,2},{1,3},{2,0},{3,1},{4,6},{5,7},{6,4},{7,5},{8,10},{9,11},{10,... | collective-permute-start | bytes 5308424 | tf_op jit(solution)/shard_map/ppermute | solution.py:1168
  118.2 46.5 %collective-permute-start.17 = (bf16[8,1152]{1,0:T(8,128)(2,1)}, bf16[8,1152]{1,0:T(8,128)(2,1)}, u32[]{:S(2)}, u32[]{:S(2)}) collective-permute-start(bf16[8,1152]{1,0:T(8,128)(2,1)} %param.20), channel_id=1, source_target_pairs={{0,8},{1,9},{2,10},{3,11},{4,12},{5,13},{6,14},{7,15},{8,16},{9,17... | collective-permute-start | bytes 55304 | tf_op jit(solution)/shard_map/ppermute | solution.py:1168
  118.4 46.3 %collective-permute-start.18 = (bf16[8,1152]{1,0:T(8,128)(2,1)}, bf16[8,1152]{1,0:T(8,128)(2,1)}, u32[]{:S(2)}, u32[]{:S(2)}) collective-permute-start(bf16[8,1152]{1,0:T(8,128)(2,1)} %param.20), channel_id=1, source_target_pairs={{0,16},{1,17},{2,18},{3,19},{4,20},{5,21},{6,22},{7,23},{8,24},{9,... | collective-permute-start | bytes 55304 | tf_op jit(solution)/shard_map/ppermute | solution.py:1168
  132.1 32.6 %collective-permute-start.19 = (bf16[8,1152]{1,0:T(8,128)(2,1)}, bf16[8,1152]{1,0:T(8,128)(2,1)S(1)}, u32[]{:S(2)}, u32[]{:S(2)}) collective-permute-start(bf16[8,1152]{1,0:T(8,128)(2,1)} %param.20), channel_id=1, source_target_pairs={{0,24},{1,25},{2,26},{3,27},{4,28},{5,29},{6,30},{7,31},{8,0},{9,1... | collective-permute-start | bytes 55304 | tf_op jit(solution)/shard_map/ppermute | solution.py:1168
  142.2 22.6 %copy-start.17 = (bf16[8,1152]{1,0:T(8,128)(2,1)S(1)}, bf16[8,1152]{1,0:T(8,128)(2,1)}, u32[]{:S(2)}) copy-start(bf16[8,1152]{1,0:T(8,128)(2,1)} %param.20) | copy-start | bytes 55300
  142.2 24.6 %copy-start.19 = (bf16[8,8,1152]{2,1,0:T(8,128)(2,1)S(1)}, bf16[8,8,1152]{2,1,0:T(8,128)(2,1)}, u32[]{:S(2)}) copy-start(bf16[8,8,1152]{2,1,0:T(8,128)(2,1)} %constant_dynamic-update-slice_fusion.5) | copy-start | bytes 442372
  165.5 24.6 %collective-permute-start.20 = (bf16[4,8,1152]{2,1,0:T(8,128)(2,1)S(1)}, bf16[4,8,1152]{2,1,0:T(8,128)(2,1)S(1)}, u32[]{:S(2)}, u32[]{:S(2)}) collective-permute-start(bf16[4,8,1152]{2,1,0:T(8,128)(2,1)S(1)} %pad_maximum_fusion.6), channel_id=1, source_target_pairs={{0,4},{1,5},{2,6},{3,7},{4,0},{5,1},{6,2},{7,3},{8,12},{9,13},{10,... | collective-permute-start | bytes 221192 | tf_op jit(solution)/shard_map/ppermute | solution.py:1168
  190.1 43.4 %copy-start.20 = (bf16[8,8,1152]{2,1,0:T(8,128)(2,1)}, bf16[8,8,1152]{2,1,0:T(8,128)(2,1)S(1)}, u32[]{:S(2)}) copy-start(bf16[8,8,1152]{2,1,0:T(8,128)(2,1)S(1)} %constant_dynamic-update-slice_fusion.1) | copy-start | bytes 442372
  190.1 44.1 %collective-permute-start.21 = (bf16[1,512,640]{2,1,0:T(8,128)(2,1)}, bf16[1,512,640]{2,1,0:T(8,128)(2,1)S(1)}, u32[]{:S(2)}, u32[]{:S(2)}) collective-permute-start(bf16[1,512,640]{2,1,0:T(8,128)(2,1)} %get-tuple-element.278), channel_id=1, source_target_pairs={{0,1},{1,0},{2,3},{3,2},{4,5},{5,4},{6,7},{7,6},{8,9},{9,8},{10,11... | collective-permute-start | bytes 1966088 | tf_op jit(solution)/shard_map/ppermute | solution.py:1168
  191.5 42.1 %collective-permute-start.22 = (bf16[8,8,1152]{2,1,0:T(8,128)(2,1)S(1)}, bf16[8,8,1152]{2,1,0:T(8,128)(2,1)S(1)}, u32[]{:S(2)}, u32[]{:S(2)}) collective-permute-start(bf16[8,8,1152]{2,1,0:T(8,128)(2,1)S(1)} %constant_dynamic-update-slice_fusion.1), channel_id=1, source_target_pairs={{0,2},{1,3},{2,0},{3,1},{4,6},{5,7},{6,4},{7,5},{8,10},{9,11},{10,... | collective-permute-start | bytes 442376 | tf_op jit(solution)/shard_map/ppermute | solution.py:1168
  339.4 5.2 collective-permute-start.23
  349.4 71.8 %collective-permute-start.24 = (bf16[2,288,2304]{2,1,0:T(8,128)(2,1)}, bf16[2,288,2304]{2,1,0:T(8,128)(2,1)S(1)}, u32[]{:S(2)}, u32[]{:S(2)}) collective-permute-start(bf16[2,288,2304]{2,1,0:T(8,128)(2,1)} %get-tuple-element.300), channel_id=1, source_target_pairs={{0,2},{1,3},{2,0},{3,1},{4,6},{5,7},{6,4},{7,5},{8,10},{9,11},{10,... | collective-permute-start | bytes 7962632 | tf_op jit(solution)/shard_map/ppermute | solution.py:1168
  349.6 71.5 %collective-permute-start.25 = (bf16[2,288,2304]{2,1,0:T(8,128)(2,1)}, bf16[2,288,2304]{2,1,0:T(8,128)(2,1)}, u32[]{:S(2)}, u32[]{:S(2)}) collective-permute-start(bf16[2,288,2304]{2,1,0:T(8,128)(2,1)} %add_convert_fusion.2), channel_id=1, source_target_pairs={{0,4},{1,5},{2,6},{3,7},{4,0},{5,1},{6,2},{7,3},{8,12},{9,13},{10,... | collective-permute-start | bytes 7962632 | tf_op jit(solution)/shard_map/ppermute | solution.py:1168
  421.1 6.3 collective-permute-start.26
  431.0 59.5 %collective-permute-start.27 = (bf16[2,288,2304]{2,1,0:T(8,128)(2,1)}, bf16[2,288,2304]{2,1,0:T(8,128)(2,1)}, u32[]{:S(2)}, u32[]{:S(2)}) collective-permute-start(bf16[2,288,2304]{2,1,0:T(8,128)(2,1)} %add_convert_fusion.1), channel_id=1, source_target_pairs={{0,1},{1,0},{2,3},{3,2},{4,5},{5,4},{6,7},{7,6},{8,9},{9,8},{10,11... | collective-permute-start | bytes 7962632 | tf_op jit(solution)/shard_map/ppermute | solution.py:1168
  431.7 59.2 %collective-permute-start.28 = (bf16[2,288,2304]{2,1,0:T(8,128)(2,1)}, bf16[2,288,2304]{2,1,0:T(8,128)(2,1)}, u32[]{:S(2)}, u32[]{:S(2)}) collective-permute-start(bf16[2,288,2304]{2,1,0:T(8,128)(2,1)} %add_convert_fusion), channel_id=1, source_target_pairs={{0,4},{1,5},{2,6},{3,7},{4,0},{5,1},{6,2},{7,3},{8,12},{9,13},{10,... | collective-permute-start | bytes 7962632 | tf_op jit(solution)/shard_map/ppermute | solution.py:1168
  431.9 59.0 %collective-permute-start.29 = (bf16[2,288,2304]{2,1,0:T(8,128)(2,1)}, bf16[2,288,2304]{2,1,0:T(8,128)(2,1)}, u32[]{:S(2)}, u32[]{:S(2)}) collective-permute-start(bf16[2,288,2304]{2,1,0:T(8,128)(2,1)} %get-tuple-element.325), channel_id=1, source_target_pairs={{0,2},{1,3},{2,0},{3,1},{4,6},{5,7},{6,4},{7,5},{8,10},{9,11},{10,... | collective-permute-start | bytes 7962632 | tf_op jit(solution)/shard_map/ppermute | solution.py:1168
  490.8 9.5 %collective-permute-start.30 = (bf16[2,576,640]{2,1,0:T(8,128)(2,1)}, bf16[2,576,640]{2,1,0:T(8,128)(2,1)S(1)}, u32[]{:S(2)}, u32[]{:S(2)}) collective-permute-start(bf16[2,576,640]{2,1,0:T(8,128)(2,1)} %get-tuple-element.333), channel_id=1, source_target_pairs={{0,2},{1,3},{2,0},{3,1},{4,6},{5,7},{6,4},{7,5},{8,10},{9,11},{10,... | collective-permute-start | bytes 4423688 | tf_op jit(solution)/shard_map/ppermute | solution.py:1168
  492.0 16.7 %collective-permute-start.31 = (bf16[1,512,640]{2,1,0:T(8,128)(2,1)}, bf16[1,512,640]{2,1,0:T(8,128)(2,1)}, u32[]{:S(2)}, u32[]{:S(2)}) collective-permute-start(bf16[1,512,640]{2,1,0:T(8,128)(2,1)} %get-tuple-element.335), channel_id=1, source_target_pairs={{0,1},{1,0},{2,3},{3,2},{4,5},{5,4},{6,7},{7,6},{8,9},{9,8},{10,11... | collective-permute-start | bytes 1966088 | tf_op jit(solution)/shard_map/ppermute | solution.py:1168
  560.7 78.2 %copy-start.15 = (bf16[288,640]{1,0:T(8,128)(2,1)S(1)}, bf16[288,640]{1,0:T(8,128)(2,1)}, u32[]{:S(2)}) copy-start(bf16[288,640]{1,0:T(8,128)(2,1)} %get-tuple-element.368) | copy-start | bytes 1105924
  560.8 79.0 %collective-permute-start.32 = (bf16[1,512,1792]{2,1,0:T(8,128)(2,1)}, bf16[1,512,1792]{2,1,0:T(8,128)(2,1)}, u32[]{:S(2)}, u32[]{:S(2)}) collective-permute-start(bf16[1,512,1792]{2,1,0:T(8,128)(2,1)} %get-tuple-element.353), channel_id=1, source_target_pairs={{0,1},{1,0},{2,3},{3,2},{4,5},{5,4},{6,7},{7,6},{8,9},{9,8},{10,11... | collective-permute-start | bytes 5505032 | tf_op jit(solution)/shard_map/ppermute | solution.py:1168
  561.7 76.5 %collective-permute-start.33 = (bf16[2,72,2304]{2,1,0:T(8,128)(2,1)}, bf16[2,72,2304]{2,1,0:T(8,128)(2,1)S(1)}, u32[]{:S(2)}, u32[]{:S(2)}) collective-permute-start(bf16[2,72,2304]{2,1,0:T(8,128)(2,1)} %get-tuple-element.354), channel_id=1, source_target_pairs={{0,8},{1,9},{2,10},{3,11},{4,12},{5,13},{6,14},{7,15},{8,16},{9,17... | collective-permute-start | bytes 1990664 | tf_op jit(solution)/shard_map/ppermute | solution.py:1168
  561.7 77.3 %collective-permute-start.34 = (bf16[2,72,2304]{2,1,0:T(8,128)(2,1)}, bf16[2,72,2304]{2,1,0:T(8,128)(2,1)S(1)}, u32[]{:S(2)}, u32[]{:S(2)}) collective-permute-start(bf16[2,72,2304]{2,1,0:T(8,128)(2,1)} %get-tuple-element.355), channel_id=1, source_target_pairs={{0,16},{1,17},{2,18},{3,19},{4,20},{5,21},{6,22},{7,23},{8,24},{9,... | collective-permute-start | bytes 1990664 | tf_op jit(solution)/shard_map/ppermute | solution.py:1168
  564.1 75.7 %collective-permute-start.35 = (bf16[2,72,2304]{2,1,0:T(8,128)(2,1)}, bf16[2,72,2304]{2,1,0:T(8,128)(2,1)}, u32[]{:S(2)}, u32[]{:S(2)}) collective-permute-start(bf16[2,72,2304]{2,1,0:T(8,128)(2,1)} %get-tuple-element.356), channel_id=1, source_target_pairs={{0,24},{1,25},{2,26},{3,27},{4,28},{5,29},{6,30},{7,31},{8,0},{9,1... | collective-permute-start | bytes 1990664 | tf_op jit(solution)/shard_map/ppermute | solution.py:1168
  564.6 89.0 %collective-permute-start.36 = (bf16[288,640]{1,0:T(8,128)(2,1)}, bf16[288,640]{1,0:T(8,128)(2,1)}, u32[]{:S(2)}, u32[]{:S(2)}) collective-permute-start(bf16[288,640]{1,0:T(8,128)(2,1)} %get-tuple-element.366), channel_id=1, source_target_pairs={{0,4},{1,5},{2,6},{3,7},{4,0},{5,1},{6,2},{7,3},{8,12},{9,13},{10,... | collective-permute-start | bytes 1105928 | tf_op jit(solution)/shard_map/ppermute | solution.py:1168
  638.2 17.3 %collective-permute-start.37 = (bf16[288,640]{1,0:T(8,128)(2,1)}, bf16[288,640]{1,0:T(8,128)(2,1)}, u32[]{:S(2)}, u32[]{:S(2)}) collective-permute-start(bf16[288,640]{1,0:T(8,128)(2,1)} %get-tuple-element.367), channel_id=1, source_target_pairs={{0,1},{1,0},{2,3},{3,2},{4,5},{5,4},{6,7},{7,6},{8,9},{9,8},{10,11... | collective-permute-start | bytes 1105928 | tf_op jit(solution)/shard_map/ppermute | solution.py:1168
  639.0 16.5 %collective-permute-start.38 = (bf16[288,640]{1,0:T(8,128)(2,1)S(1)}, bf16[288,640]{1,0:T(8,128)(2,1)}, u32[]{:S(2)}, u32[]{:S(2)}) collective-permute-start(bf16[288,640]{1,0:T(8,128)(2,1)S(1)} %copy-done.15), channel_id=1, source_target_pairs={{0,5},{1,4},{2,7},{3,6},{4,1},{5,0},{6,3},{7,2},{8,13},{9,12},{10,... | collective-permute-start | bytes 1105928 | tf_op jit(solution)/shard_map/ppermute | solution.py:1168
  658.2 22.5 %collective-permute-start.39 = (bf16[576,1792]{1,0:T(8,128)(2,1)}, bf16[576,1792]{1,0:T(8,128)(2,1)S(1)}, u32[]{:S(2)}, u32[]{:S(2)}) collective-permute-start(bf16[576,1792]{1,0:T(8,128)(2,1)} %get-tuple-element.378), channel_id=1, source_target_pairs={{0,2},{1,3},{2,0},{3,1},{4,6},{5,7},{6,4},{7,5},{8,10},{9,11},{10,... | collective-permute-start | bytes 6193160 | tf_op jit(solution)/shard_map/ppermute | solution.py:1168
  664.0 16.8 %collective-permute-start.40 = (bf16[72,640]{1,0:T(8,128)(2,1)}, bf16[72,640]{1,0:T(8,128)(2,1)S(1)}, u32[]{:S(2)}, u32[]{:S(2)}) collective-permute-start(bf16[72,640]{1,0:T(8,128)(2,1)} %get-tuple-element.379), channel_id=1, source_target_pairs={{0,8},{1,9},{2,10},{3,11},{4,12},{5,13},{6,14},{7,15},{8,16},{9,17... | collective-permute-start | bytes 276488 | tf_op jit(solution)/shard_map/ppermute | solution.py:1168
  664.9 15.8 %collective-permute-start.41 = (bf16[72,640]{1,0:T(8,128)(2,1)}, bf16[72,640]{1,0:T(8,128)(2,1)}, u32[]{:S(2)}, u32[]{:S(2)}) collective-permute-start(bf16[72,640]{1,0:T(8,128)(2,1)} %get-tuple-element.380), channel_id=1, source_target_pairs={{0,16},{1,17},{2,18},{3,19},{4,20},{5,21},{6,22},{7,23},{8,24},{9,... | collective-permute-start | bytes 276488 | tf_op jit(solution)/shard_map/ppermute | solution.py:1168
  666.7 14.0 %collective-permute-start.42 = (bf16[72,640]{1,0:T(8,128)(2,1)}, bf16[72,640]{1,0:T(8,128)(2,1)}, u32[]{:S(2)}, u32[]{:S(2)}) collective-permute-start(bf16[72,640]{1,0:T(8,128)(2,1)} %get-tuple-element.381), channel_id=1, source_target_pairs={{0,24},{1,25},{2,26},{3,27},{4,28},{5,29},{6,30},{7,31},{8,0},{9,1... | collective-permute-start | bytes 276488 | tf_op jit(solution)/shard_map/ppermute | solution.py:1168
  680.8 6.5 collective-permute-start.43
  689.8 47.6 %copy-start.22 = (f32[4,8,1152]{2,1,0:T(8,128)S(1)}, f32[4,8,1152]{2,1,0:T(8,128)}, u32[]{:S(2)}) copy-start(f32[4,8,1152]{2,1,0:T(8,128)} %get-tuple-element.394) | copy-start | bytes 442372
  689.8 34.3 %collective-permute-start.44 = (bf16[288,1792]{1,0:T(8,128)(2,1)S(1)}, bf16[288,1792]{1,0:T(8,128)(2,1)S(1)}, u32[]{:S(2)}, u32[]{:S(2)}) collective-permute-start(bf16[288,1792]{1,0:T(8,128)(2,1)S(1)} %get-tuple-element.389), channel_id=1, source_target_pairs={{0,4},{1,5},{2,6},{3,7},{4,0},{5,1},{6,2},{7,3},{8,12},{9,13},{10,... | collective-permute-start | bytes 3096584 | tf_op jit(solution)/shard_map/ppermute | solution.py:1168
  690.2 34.0 %collective-permute-start.45 = (bf16[288,1792]{1,0:T(8,128)(2,1)S(1)}, bf16[288,1792]{1,0:T(8,128)(2,1)}, u32[]{:S(2)}, u32[]{:S(2)}) collective-permute-start(bf16[288,1792]{1,0:T(8,128)(2,1)S(1)} %get-tuple-element.390), channel_id=1, source_target_pairs={{0,1},{1,0},{2,3},{3,2},{4,5},{5,4},{6,7},{7,6},{8,9},{9,8},{10,11... | collective-permute-start | bytes 3096584 | tf_op jit(solution)/shard_map/ppermute | solution.py:1168
  691.4 46.1 %collective-permute-start.46 = (bf16[288,1792]{1,0:T(8,128)(2,1)S(1)}, bf16[288,1792]{1,0:T(8,128)(2,1)}, u32[]{:S(2)}, u32[]{:S(2)}) collective-permute-start(bf16[288,1792]{1,0:T(8,128)(2,1)S(1)} %get-tuple-element.391), channel_id=1, source_target_pairs={{0,5},{1,4},{2,7},{3,6},{4,1},{5,0},{6,3},{7,2},{8,13},{9,12},{10,... | collective-permute-start | bytes 3096584 | tf_op jit(solution)/shard_map/ppermute | solution.py:1168
  738.5 4.2 collective-permute-start.47
  742.8 21.1 %collective-permute-start.48 = (f32[8,4096]{1,0:T(8,128)S(1)}, f32[8,4096]{1,0:T(8,128)S(1)}, u32[]{:S(2)}, u32[]{:S(2)}) collective-permute-start(f32[8,4096]{1,0:T(8,128)S(1)} %add.263), channel_id=1, source_target_pairs={{0,8},{1,9},{2,10},{3,11},{4,12},{5,13},{6,14},{7,15},{8,16},{9,17... | collective-permute-start | bytes 393224 | tf_op jit(solution)/shard_map/ppermute | solution.py:1168
  744.6 19.3 %collective-permute-start.49 = (f32[8,4096]{1,0:T(8,128)S(1)}, f32[8,4096]{1,0:T(8,128)S(1)}, u32[]{:S(2)}, u32[]{:S(2)}) collective-permute-start(f32[8,4096]{1,0:T(8,128)S(1)} %add.263), channel_id=1, source_target_pairs={{0,16},{1,17},{2,18},{3,19},{4,20},{5,21},{6,22},{7,23},{8,24},{9,... | collective-permute-start | bytes 393224 | tf_op jit(solution)/shard_map/ppermute | solution.py:1168
  746.9 17.0 %collective-permute-start.50 = (f32[8,4096]{1,0:T(8,128)S(1)}, f32[8,4096]{1,0:T(8,128)S(1)}, u32[]{:S(2)}, u32[]{:S(2)}) collective-permute-start(f32[8,4096]{1,0:T(8,128)S(1)} %add.263), channel_id=1, source_target_pairs={{0,24},{1,25},{2,26},{3,27},{4,28},{5,29},{6,30},{7,31},{8,0},{9,1... | collective-permute-start | bytes 393224 | tf_op jit(solution)/shard_map/ppermute | solution.py:1168
  764.0 27.1 %collective-permute-start.52 = (f32[32,4096]{1,0:T(8,128)S(1)}, f32[32,4096]{1,0:T(8,128)S(1)}, u32[]{:S(2)}, u32[]{:S(2)}) collective-permute-start(f32[32,4096]{1,0:T(8,128)S(1)} %pad_maximum_fusion.2), channel_id=1, source_target_pairs={{0,4},{1,5},{2,6},{3,7},{4,0},{5,1},{6,2},{7,3},{8,12},{9,13},{10,... | collective-permute-start | bytes 1572872 | tf_op jit(solution)/shard_map/ppermute | solution.py:1168
  765.7 6.4 collective-permute-start.53
  767.2 19.8 %collective-permute-start.54 = (bf16[72,1792]{1,0:T(8,128)(2,1)S(1)}, bf16[72,1792]{1,0:T(8,128)(2,1)S(1)}, u32[]{:S(2)}, u32[]{:S(2)}) collective-permute-start(bf16[72,1792]{1,0:T(8,128)(2,1)S(1)} %get-tuple-element.415), channel_id=1, source_target_pairs={{0,16},{1,17},{2,18},{3,19},{4,20},{5,21},{6,22},{7,23},{8,24},{9,... | collective-permute-start | bytes 774152 | tf_op jit(solution)/shard_map/ppermute | solution.py:1168
  769.0 22.1 %collective-permute-start.55 = (bf16[72,1792]{1,0:T(8,128)(2,1)S(1)}, bf16[72,1792]{1,0:T(8,128)(2,1)S(1)}, u32[]{:S(2)}, u32[]{:S(2)}) collective-permute-start(bf16[72,1792]{1,0:T(8,128)(2,1)S(1)} %get-tuple-element.416), channel_id=1, source_target_pairs={{0,24},{1,25},{2,26},{3,27},{4,28},{5,29},{6,30},{7,31},{8,0},{9,1... | collective-permute-start | bytes 774152 | tf_op jit(solution)/shard_map/ppermute | solution.py:1168
  769.0 3.1 collective-permute-start.51
  770.0 23.3 %copy-start.18 = (bf16[8,1152]{1,0:T(8,128)(2,1)S(1)}, bf16[8,1152]{1,0:T(8,128)(2,1)}, u32[]{:S(2)}) copy-start(bf16[8,1152]{1,0:T(8,128)(2,1)} %param.20) | copy-start | bytes 55300
  791.1 3.5 collective-permute-start.56
  (34 other events, 291.6 us)
Sparse Core Ops, SparseCore 0:
  113.5 155.8 all-gather.1

commit v4 on v3

--- a/solution.py
+++ b/solution.py
@@ -388,45 +388,49 @@
     return jnp.concatenate([high, middle, rest - middle], axis=-2).astype(BF)
 
 
-def collect_kernel(core, over_x, x_got, over_y, y_got, last, last_got, whole, sems):
-    heads, levels, xs = whole.shape[:3]
-    count = over_x.shape[-1]
-    place_of = (lambda h, z, x: (h, x, z), lambda h, z, x: (x, h, z), lambda h, z, x: (z, h, x))
+def collect_kernel(here, *refs):
+    sources, whole, sems = refs[:10], refs[10], refs[11]
+    levels, xs = whole.shape[2:4]
+    count = sources[0].shape[-1]
+    y, level, x, core = (here[k] for k in range(4))
+    flip = lambda bit, other: bit + other - 2 * bit * other
     copies = []
-    for k, pair in enumerate(((over_x, x_got), (over_y, y_got), (last, last_got))):
-        for got, source in enumerate(pair):
-            c = core[0] if got == 0 else 1 - core[0]
-            for h in range(heads):
-                for z in range(levels):
-                    for x in range(xs):
-                        copy = pltpu.make_async_copy(
-                            source.at[place_of[k](h, z, x)],
-                            whole.at[h, z, x, c, :, pl.ds(k * count, count)],
-                            sems.at[len(copies)],
-                        )
-                        copy.start()
-                        copies.append(copy)
+    for dc in range(2):
+        x_near, x_far, y_near, y_far, last = sources[5 * dc : 5 * dc + 5]
+        for dz in range(levels):
+            for i in range(2):
+                for j in range(2):
+                    at = (flip(y, i), lax.rem(level + dz, levels), flip(x, j), flip(core, dc))
+                    found = (
+                        (x_near, x_far)[i].at[j, dz],
+                        (y_near, y_far)[j].at[i, dz],
+                        last.at[dz, i, j],
+                    )
+                    for k, source in enumerate(found):
+                        place = whole.at[(slice(None), *at, slice(None), pl.ds(k * count, count))]
+                        copies.append(pltpu.make_async_copy(source, place, sems.at[len(copies)]))
+                        copies[-1].start()
     for copy in copies:
         copy.wait()
 
 
-def collected(core, over_x, x_got, over_y, y_got, last, last_got):
-    levels, heads, xs, piece, count = last.shape
-    whole = (heads, levels, xs, 2, piece, 3 * count)
+def collected(here, sources):
+    levels, heads, xs, parts, piece, count = sources[4].shape
+    whole = (parts, heads, levels, xs, 2, piece, 3 * count)
     anywhere = pl.BlockSpec(memory_space=pl.ANY)
     return pl.pallas_call(
         collect_kernel,
         grid_spec=pltpu.PrefetchScalarGridSpec(
             num_scalar_prefetch=1,
             grid=(1,),
-            in_specs=[anywhere] * 6,
+            in_specs=[anywhere] * 10,
             out_specs=anywhere,
             scratch_shapes=[pltpu.SemaphoreType.DMA((6 * heads * levels * xs,))],
         ),
         out_shape=shape(whole, BF),
         compiler_params=params(16),
-        cost_estimate=cost(0, 24 * heads * levels * xs * piece * count),
-    )(core, over_x, x_got, over_y, y_got, last, last_got)
+        cost_estimate=cost(0, 24 * parts * heads * levels * xs * piece * count),
+    )(here, *sources)
 
 
 def turn_in_order(places, turned_ref, values):
@@ -481,52 +485,76 @@
     )(side, tokens, hot, parts)
 
 
-def project_kernel(side, full_ref, own_ref, got_ref, w_ref, bias_ref, first, second, own, got):
-    block, padded = own.shape[1:]
+def project_kernel(side, first_in, second_in, w_ref, bias_ref, first, second):
+    padded = first.shape[2]
     cols = bias_ref.shape[2]
-
-    def found(hidden):
-        value = (rows_by_columns(hidden, w_ref[0, :, :cols]) + bias_ref[0]).astype(BF)
-        return jnp.concatenate([value, jnp.zeros((block, padded - cols), BF)], axis=1)
-
-    first[0] = found(full_ref[:block])
-    second[0] = found(full_ref[block:])
-
-    @pl.when(pl.program_id(0) == 0)
-    def _():
-        own[0] = found(own_ref[...])
-        got[0] = found(got_ref[...])
-
-
-def project(side, full, own, got, weights, bias, padded):
-    block, width = own.shape
+    for hidden, ref in ((first_in, first), (second_in, second)):
+        value = (rows_by_columns(hidden[...], w_ref[0, :, :cols]) + bias_ref[0]).astype(BF)
+        ref[0] = jnp.concatenate([value, jnp.zeros((value.shape[0], padded - cols), BF)], axis=1)
+
+
+def project(side, first, second, weights, bias, padded, block, groups):
+    width = first.shape[1]
     pick = lambda a, y: a + y[0] - 2 * a * y[0]
-    single = pl.BlockSpec((1, block, padded), lambda a, y: (0, 0, 0))
+    last = second.shape[0] // block - 1
     pair = pl.BlockSpec((1, block, padded), lambda a, y: (a, 0, 0))
     return pl.pallas_call(
         project_kernel,
         grid_spec=pltpu.PrefetchScalarGridSpec(
             num_scalar_prefetch=1,
-            grid=(2,),
+            grid=(groups,),
             in_specs=[
-                pl.BlockSpec((2 * block, width), lambda a, y: (0, 0)),
                 pl.BlockSpec((block, width), lambda a, y: (0, 0)),
-                pl.BlockSpec((block, width), lambda a, y: (0, 0)),
+                pl.BlockSpec((block, width), lambda a, y: (last, 0)),
                 pl.BlockSpec((1,) + weights.shape[1:], lambda a, y: (pick(a, y), 0, 0)),
                 pl.BlockSpec((1,) + bias.shape[1:], lambda a, y: (pick(a, y), 0, 0)),
             ],
-            out_specs=[pair, pair, single, single],
+            out_specs=[pair, pair],
         ),
-        out_shape=[shape((2, block, padded), BF)] * 2 + [shape((1, block, padded), BF)] * 2,
+        out_shape=[shape((groups, block, padded), BF)] * 2,
         compiler_params=params(60),
-        cost_estimate=cost(12 * block * width * padded, 12 * block * padded + 4 * width * padded),
-    )(side, full, own, got, weights, bias)
+        cost_estimate=cost(
+            4 * groups * block * width * padded, 4 * groups * (block + width) * padded
+        ),
+    )(side, first, second, weights, bias)
 
 
 MARKS = 16
 DEPTH = 128
 LSE_AT = HEAD_DIM + MARKS - 4
 STEEP = HEAD_DIM**-0.5 * LOG2E
+
+
+def marks_kernel(*refs):
+    count = len(refs) // 4
+    for n in range(count):
+        seg_ref, open_ref = refs[2 * n : 2 * n + 2]
+        query_ref, key_ref = refs[2 * count + 2 * n : 2 * count + 2 * n + 2]
+        tiles, length = open_ref.shape
+        slots = MARKS - 4 - tiles
+        slot = lax.broadcasted_iota(jnp.int32, (slots, length), 0)
+        own_slot = slot == seg_ref[...]
+        tile = lax.broadcasted_iota(jnp.int32, (tiles, length), 0)
+        own_tile = tile == lax.broadcasted_iota(jnp.int32, (tiles, length), 1) // TILE
+        seen = jnp.concatenate(
+            [jnp.where(own_slot, 0.0, MASKED_SCORE), jnp.where(open_ref[...] > 0, 0.0, MASKED_SCORE)],
+            axis=0,
+        )
+        chosen = jnp.concatenate(
+            [jnp.where(own_slot, 1.0, 0.0), jnp.where(own_tile, 1.0, 0.0)], axis=0
+        )
+        rest = (MARKS - slots - tiles, length)
+        query_ref[...] = jnp.concatenate([chosen, jnp.zeros(rest, F32)], axis=0).T.astype(BF)
+        key_ref[...] = jnp.concatenate([seen, jnp.ones(rest, F32)], axis=0).T.astype(BF)
+
+
+def marks_of(*rows):
+    length = rows[1].shape[1]
+    return pl.pallas_call(
+        marks_kernel,
+        out_shape=[shape((length, MARKS), BF)] * len(rows),
+        compiler_params=params(16),
+    )(*rows)
 
 
 def split_three(values):
@@ -1201,19 +1229,11 @@
         cols = w_query.shape[1]
 
         tiles = length // TILE
-        tile_of = jnp.arange(length, dtype=jnp.int32) // TILE
         slots = image_index.shape[1]
 
-        def marks_of(seg, tiles_on):
-            own_slot = seg[:, None] == jnp.arange(slots, dtype=jnp.int32)[None, :]
+        def open_to(tiles_on):
             on = (tiles_on > 0) | jnp.eye(tiles, dtype=bool)
-            own_tile = tile_of[:, None] == jnp.arange(tiles, dtype=jnp.int32)[None, :]
-            open_to = jnp.broadcast_to(on.T[:, None, :], (tiles, TILE, tiles)).reshape(length, tiles)
-            ends = jnp.zeros((length, MARKS - slots - tiles), F32)
-            query = jnp.concatenate([own_slot, own_tile, ends], axis=1).astype(BF)
-            seen = jnp.concatenate([own_slot, open_to], axis=1)
-            key = jnp.concatenate([jnp.where(seen, 0.0, MASKED_SCORE), ends + 1.0], axis=1).astype(BF)
-            return query, key
+            return jnp.repeat(on.astype(jnp.int32), TILE, axis=1)
 
         seg_full = lax.dynamic_index_in_dim(segment_ids, 2 * y, 0, keepdims=False)
         tile_full = lax.dynamic_index_in_dim(tile_mask, 2 * y, 0, keepdims=False)
@@ -1222,8 +1242,7 @@
         tile_half = jnp.where(
             y == 0, tile_mask[1], jnp.roll(tile_mask[1], (-shift, -shift), axis=(0, 1))
         )
-        marks_full = marks_of(seg_full, tile_full)
-        marks_half = marks_of(seg_half, tile_half)
+        marks = marks_of(seg_full[None], open_to(tile_full), seg_half[None], open_to(tile_half))
 
         def image_of(seg, index):
             slot = jnp.arange(slots, dtype=jnp.int32)
@@ -1248,45 +1267,70 @@
 
         padded = -(-3 * cols // 128) * 128
         out_width = -(-cols // 128) * 128
-        level, x_bit, core_bit = r // 4, (r // 2) % 2, r % 2
+        here = jnp.stack([y, r // 4, (r // 2) % 2, r % 2]).astype(jnp.int32)
         next_level = to_level[levels - 1]
 
-        def placed(bit, own, got):
-            return jnp.where(bit == 0, jnp.stack([own, got]), jnp.stack([got, own]))
-
-        def round_of(found):
-            return lax.dynamic_slice_in_dim(
-                jnp.stack(found + found), (levels - level) % levels, levels, axis=0
-            )
+        class Tree:
+            def __init__(self, shard):
+                self.count = shard.shape[-1] // 3
+                self.first = [shard[..., : 2 * self.count]]
+                self.last = [shard[..., 2 * self.count :]]
+                self.step = 0
+
+            def sends(self):
+                moves = (
+                    (next_level, to_x),
+                    (next_level, to_heads),
+                    (next_level, next_level),
+                    (to_x, to_heads, next_level),
+                    (to_heads, to_x, next_level),
+                    (to_core,) * 5,
+                )[self.step]
+                if self.step < 3:
+                    self.sent = (self.first[-1], self.last[-1])
+                elif self.step < 5:
+                    self.sent = (self.over_x, self.over_y, self.last[-1])
+                else:
+                    self.sent = (*self.over_x, *self.over_y, self.last)
+                return [send(value, move) for value, move in zip(self.sent, moves)]
+
+            def take(self, got):
+                if self.step < 2:
+                    self.first.append(got[0])
+                    self.last = [jnp.stack([self.last[0], got[1]])]
+                elif self.step == 2:
+                    whole = jnp.stack([*self.first, got[0]])
+                    self.over_x, self.over_y = whole[..., : self.count], whole[..., self.count :]
+                    self.last.append(got[1])
+                elif self.step == 3:
+                    self.over_x = jnp.stack([self.over_x, got[0]])
+                    self.over_y = jnp.stack([self.over_y, got[1]])
+                    self.last.append(got[2])
+                elif self.step == 4:
+                    self.over_x = (self.over_x, got[0])
+                    self.over_y = (self.over_y, got[1])
+                    self.last = jnp.stack([*self.last, got[2]])
+                else:
+                    self.whole = collected(here, (*self.sent, *got))
+                self.step += 1
 
         shard = jnp.concatenate([w_query, w_key, w_value, w_out], axis=1).astype(BF)
-        count = shard.shape[1] // 3
-        steps = [shard[:, : 2 * count]]
-        last = shard[:, 2 * count :]
+        tree = Tree(shard[None])
         cond = condition.astype(F32)
-        mod_cols, got, last_got = after(
-            jnp.dot(jax.nn.silu(cond), w_ada, precision=PRECISE) + b_ada,
-            send(steps[0], next_level),
-            send(last, to_x),
-        )
-        steps.append(got)
-        last = placed(x_bit, last, last_got)
+        mod_cols, *got = after(
+            jnp.dot(jax.nn.silu(cond), w_ada, precision=PRECISE) + b_ada, *tree.sends()
+        )
+        tree.take(got)
         biases = jnp.concatenate([b_up, b_query, b_value])[None]
         own_spread = jnp.concatenate([mod_cols, biases], axis=0)
-        got_spread, got, last_got, hot, turn, side, *marks = after(
-            send(own_spread, to_heads),
-            send(steps[1], next_level),
-            send(last, to_heads),
-            hot,
-            turn,
-            side,
-            *marks_full,
-            *marks_half,
-        )
-        marks_full, marks_half = marks[:2], marks[2:]
-        steps.append(got)
-        last = [placed(y, last, last_got)]
-        spread = placed(y, own_spread, got_spread)
+        got_spread, hot, turn, side, *joined = after(
+            send(own_spread, to_heads), hot, turn, side, *marks, *tree.sends()
+        )
+        marks_full, marks_half = joined[:2], joined[2:4]
+        tree.take(joined[4:])
+        spread = jnp.where(
+            y == 0, jnp.stack([own_spread, got_spread]), jnp.stack([got_spread, own_spread])
+        )
         parts = three_parts(spread[:, :images])
         up_bias = spread[:, images:, :units]
         qkv_bias = jnp.concatenate(
@@ -1297,64 +1341,57 @@
             ],
             axis=2,
         )
-        hidden_full, hidden_half, hidden_one_turned, got, last_got = after(
-            *first_norm(side, tokens, hot, parts, third),
-            send(steps[2], next_level),
-            send(last[0], next_level),
-        )
-        first = round_of([*steps, got])
-        last.append(last_got)
-        over_x, over_y = first[..., :count], first[..., count:]
-        x_got, y_got, last_got = after(
-            send(over_x, to_x), send(over_y, to_heads), send(last[1], next_level)
-        )
-        over_x, over_y = placed(x_bit, over_x, x_got), placed(y, over_y, y_got)
-        last.append(last_got)
-        hidden_got, x_got, y_got, last_got = after(
-            send(hidden_half, to_heads),
-            send(over_x, to_heads),
-            send(over_y, to_x),
-            send(last[2], next_level),
-        )
-        over_x, over_y = placed(y, over_x, x_got), placed(x_bit, over_y, y_got)
-        last = round_of([*last, last_got])
+        hidden_full, hidden_half, hidden_one_turned, qkv_bias, up_bias, *got = after(
+            *first_norm(side, tokens, hot, parts, third), qkv_bias, up_bias, *tree.sends()
+        )
+        tree.take(got)
         feed_shard = jnp.stack([w_up, w_down]).astype(BF)
-        over_x, over_y, last, feed_shard = after(over_x, over_y, last, feed_shard)
+        hidden_full, hidden_half, feed_shard, *got = after(
+            hidden_full, hidden_half, feed_shard, *tree.sends()
+        )
+        tree.take(got)
+        hidden_full, hidden_half, *got = after(hidden_full, hidden_half, *tree.sends())
+        tree.take(got)
         feed_weights = lax.all_gather(
             feed_shard, ("heads", "rows"), axis=1, tiled=True
         ).reshape(2, 2, width, units)
-        x_got, y_got, last_got = after(
-            send(over_x, to_core), send(over_y, to_core), send(last, to_core)
-        )
-        attention_weights = collected(
-            core_bit.reshape(1), over_x, x_got, over_y, y_got, last, last_got
-        ).reshape(2, width, shard.shape[1])
-
-        qkv_first, qkv_second, qkv_own, qkv_got, *got = after(
+        hidden_full, hidden_half, *got = after(hidden_full, hidden_half, *tree.sends())
+        tree.take(got)
+        attention_weights = tree.whole.reshape(2, width, shard.shape[1])
+
+        qkv_first, qkv_second, hidden_got = after(
             *project(
-                side, hidden_full, hidden_half, hidden_got, attention_weights, qkv_bias, padded
+                side, hidden_full, hidden_full, attention_weights, qkv_bias, padded, third, 2
             ),
+            send(hidden_half, to_heads),
+        )
+        qkv_full = (qkv_first, qkv_second)
+        qkv_half = project(
+            side, hidden_half, hidden_got, attention_weights, qkv_bias, padded, third, 1
+        )
+        qkv_own, qkv_got, condition = after(*qkv_half, condition)
+        qkv_half = (qkv_own, qkv_got)
+        out_own, out_theirs, l_own, l_other, *got = after(
+            *attend(*qkv_half, *marks_half, out_width),
             *(send(condition, to_level[k]) for k in range(1, levels)),
         )
-        flat = jnp.stack([condition, *got])
-        qkv_full = (qkv_first, qkv_second)
-        qkv_half = (qkv_own, qkv_got)
-        out_own, out_theirs, *lse_half, got = after(
-            *attend(*qkv_half, *marks_half, out_width), send(flat, to_x)
-        )
-        flat = jnp.concatenate([flat, got], axis=0)
-        qkv_first, out_theirs, flat = after(qkv_first, out_theirs, flat)
+        lse_half = (l_own, l_other)
+        qkv_first, out_theirs, flat = after(qkv_first, out_theirs, jnp.stack([condition, *got]))
         out_first, out_second, *lse_full, out_other, got = after(
             *attend(qkv_first, qkv_second, *marks_full, out_width),
             send(out_theirs, to_heads),
+            send(flat, to_x),
+        )
+        out_first, flat = after(out_first, jnp.concatenate([flat, got], axis=0))
+        attended = (out_first, out_second, out_own, out_other)
+        branch_one, hidden_two, grad_two, hidden_two_turned, grad_two_turned, grad_b_down, got = after(
+            *middle_part(
+                side, tokens, cotangent, attended, attention_weights, b_out[None], hot, parts, third // 2
+            ),
             send(flat, to_core),
         )
         flat = jnp.concatenate([flat, got], axis=0)
         silu_all = jax.nn.silu(flat.reshape(ring * images, width).astype(F32))
-        attended = (out_first, out_second, out_own, out_other)
-        branch_one, hidden_two, grad_two, hidden_two_turned, grad_two_turned, grad_b_down = middle_part(
-            side, tokens, cotangent, attended, attention_weights, b_out[None], hot, parts, third // 2
-        )
 
         def added(mine, got):
             return mine + got.astype(F32)

time: 822 us -> 795 us (0.967)
  waiting for transfers between devices: 122 us -> 103 us
  local copies, waits for them, and re-layouts: 34.3 us -> 25.8 us
    all_gather x1, waiting for transfers between devices: 12.7 us -> 0.01 us  [body(): lax.all_gather(feed_shard, ('heads', 'rows'), axis=1, tiled=True)]
    ppermute x57 -> x59, waiting for transfers between devices: 109 us -> 103 us  [send(): return lax.ppermute(values, both, pairs)]
    ppermute x57 -> x59, starting transfers between devices: 62.1 us -> 66.5 us  [send(): return lax.ppermute(values, both, pairs)]
    pallas_call x1 -> x2, Pallas kernels: 22.5 us -> 25.4 us  [project(): pl.pallas_call(project_kernel, grid_spec=pltpu.PrefetchScalarGridSpec(num...]
  transfers between devices with their start and end apart: 58 -> 60, of which waited for: 19 -> 23; matrix products, arithmetic and copies ran while one was open for 10% -> 9% of each run, Pallas kernels for 46% -> 47%
where the time goes in v4:
time: 795 us; the launch traced here: 788 us
  Pallas kernels  494 us (62%)
  waiting for transfers between devices  103 us (13%)
  starting transfers between devices  66.5 us (8%)
  other arithmetic  47.6 us (6%)
  matrix products  36.5 us (5%)
  local copies, waits for them, and re-layouts  25.8 us (3%)
  between operations  15.1 us (2%)
    pallas_call x2, Pallas kernels, feed(): pl.pallas_call(partial(feed_kernel, chunk), grid_spec=pltpu.PrefetchScala...  141 us
    pallas_call x2, Pallas kernels, attend_back(): pl.pallas_call(partial(attend_back_kernel, heads), grid=(groups, 2), in_s...  124 us
    ppermute x59, waiting for transfers between devices, send(): return lax.ppermute(values, both, pairs)  103 us
    ppermute x59, starting transfers between devices, send(): return lax.ppermute(values, both, pairs)  66.5 us
    pallas_call x2, Pallas kernels, attend(): pl.pallas_call(partial(attend_kernel, heads), grid=(groups, 2), in_specs=...  61.8 us
    pallas_call x1, Pallas kernels, back_two(): pl.pallas_call(back_two_kernel, grid_spec=pltpu.PrefetchScalarGridSpec(nu...  47.9 us
    pallas_call x1, Pallas kernels, back_one(): pl.pallas_call(back_one_kernel, grid_spec=pltpu.PrefetchScalarGridSpec(nu...  31.6 us
    pallas_call x2, Pallas kernels, outer(): pl.pallas_call(outer_kernel, grid=(2,), in_specs=[pl.BlockSpec((width //...  27.6 us
  transfers between devices with their start and end apart: 60, of which 23 were waited for; matrix products, arithmetic and copies ran while one was open for 9% of the time, Pallas kernels for 47%

profile of v4, /device:TPU:9, one launch (start us, length us, event | category | flops | bytes accessed | tf_op | source)
XLA Modules:
  0.0 787.8 jit_solution(16146810026505907040)
XLA Ops:
  10.5 1.4 collective-permute-start.1
  15.1 11.3 %convolution_add_fusion = f32[8,3456]{1,0:T(8,128)S(1)} fusion(f32[1152,3456]{1,0:T(8,128)} %param.24, f32[3456]{0:T(1024)S(1)} %copy-done.25, bf16[8,1152]{1,0:T(8,128)(2,1)S(1)} %copy-done.18), kind=kOutput, calls=%fused_computation.4 | convolution fusion | flops 382279680 | bytes 16068096 | tf_op jit(solution)/shard_map/dot_general | solution.py:1321
  28.7 3.3 collective-permute-start.3
  37.4 3.4 collective-permute-start.6
  41.7 9.0 %shard_map.307 = (bf16[1024,1152]{1,0:T(8,128)(2,1)}, bf16[512,1152]{1,0:T(8,128)(2,1)}, bf16[16,72,1536]{2,1,0:T(8,128)(2,1)}) custom-call(s32[33]{0:T(128)} %pad_add_fusion.2.side, bf16[1536,1152]{1,0:T(8,128)(2,1)} %tok_ref.7, bf16[1536,24]{1,0:T(8,128)(2,1)} %compare_convert_fusion.hot_ref, bf16[2,24,3456]{2,1,0:T(8,128)(2,1)} %pad_maximum_fusion.8.parts_ref), custom_call_target="tpu_custom_call" | custom-call | flops 5888802816 | bytes 10616832 | tf_op jit(solution)/shard_map/pallas_call | solution.py:462
  56.0 1.7 collective-permute-start.9
  58.6 5.1 collective-permute-done.7
  68.7 1.7 collective-permute-start.12
  70.4 6.2 collective-permute-done.12
  76.6 7.0 collective-permute-done.11
  83.6 4.3 collective-permute-done.10
  88.1 7.2 collective-permute-start.17
  96.3 3.6 collective-permute-done.15
  104.9 3.4 shard_map.308
  108.3 4.1 copy-done
  112.4 15.2 %shard_map.309 = (bf16[2,512,1792]{2,1,0:T(8,128)(2,1)}, bf16[2,512,1792]{2,1,0:T(8,128)(2,1)}) custom-call(s32[33]{0:T(128)} %pad_add_fusion.2.side, bf16[1024,1152]{1,0:T(8,128)(2,1)} %get-tuple-element.273.first_in.second_in, bf16[1024,1152]{1,0:T(8,128)(2,1)} %get-tuple-element.273.first_in.second_in, bf16[2,1152,2304]{2,1,0:T(8,128)(2,1)} %bitcast.134, ...), custom_call_target="tpu_custom_call" | custom-call | flops 8455716864 | bytes 23855104 | tf_op jit(solution)/shard_map/pallas_call | solution.py:501
  127.6 12.9 %collective-permute-done.18.second_in = bf16[512,1152]{1,0:T(8,128)(2,1)S(1)} collective-permute-done((bf16[512,1152]{1,0:T(8,128)(2,1)S(1)}, bf16[512,1152]{1,0:T(8,128)(2,1)S(1)}, u32[]{:S(2)}, u32[]{:S(2)}) %collective-permute-start.18) | collective-permute-done | bytes 1179680 | tf_op jit(solution)/shard_map/ppermute | solution.py:1196
  141.5 10.2 %shard_map.310 = (bf16[1,512,1792]{2,1,0:T(8,128)(2,1)}, bf16[1,512,1792]{2,1,0:T(8,128)(2,1)}) custom-call(s32[33]{0:T(128)} %pad_add_fusion.2.side, bf16[512,1152]{1,0:T(8,128)(2,1)} %get-tuple-element.282.first_in, bf16[512,1152]{1,0:T(8,128)(2,1)} %copy-done.38, bf16[2,1152,2304]{2,1,0:T(8,128)(2,1)} %bitcast.135, f32[2,1,1728]{2,1,0:T(1,128)} %concatenate.122.bias_ref), custom_call_target="tpu_custom_call" | custom-call | flops 4227858432 | bytes 11927552 | tf_op jit(solution)/shard_map/pallas_call | solution.py:501
  153.0 3.1 collective-permute-start.20
  157.3 21.8 %shard_map.311 = (bf16[1,512,640]{2,1,0:T(8,128)(2,1)}, bf16[1,512,640]{2,1,0:T(8,128)(2,1)}, f32[1,8,512]{2,1,0:T(8,128)}, f32[1,8,512]{2,1,0:T(8,128)}) custom-call(bf16[1,512,1792]{2,1,0:T(8,128)(2,1)} %get-tuple-element.287.first, bf16[1,512,1792]{2,1,0:T(8,128)(2,1)} %get-tuple-element.288.second, bf16[1024,16]{1,0:T(8,128)(2,1)} %copy-done.3, ...), custom_call_target="tpu_custom_call" | custom-call | flops 15000000512 | bytes 5505024 | tf_op jit(solution)/shard_map/pallas_call | solution.py:637
  179.6 40.0 %shard_map.312 = (bf16[2,512,640]{2,1,0:T(8,128)(2,1)}, bf16[2,512,640]{2,1,0:T(8,128)(2,1)}, f32[2,8,512]{2,1,0:T(8,128)}, f32[2,8,512]{2,1,0:T(8,128)}) custom-call(bf16[2,512,1792]{2,1,0:T(8,128)(2,1)} %get-tuple-element.300.first, bf16[2,512,1792]{2,1,0:T(8,128)(2,1)} %get-tuple-element.301.second, bf16[1024,16]{1,0:T(8,128)(2,1)} %copy-done.1, ...), custom_call_target="tpu_custom_call" | custom-call | flops 30000001024 | bytes 11010048 | tf_op jit(solution)/shard_map/pallas_call | solution.py:637
  219.6 2.4 collective-permute-start.24
  222.0 21.4 %shard_map.313 = (f32[1536,1152]{1,0:T(8,128)}, bf16[1536,1152]{1,0:T(8,128)(2,1)}, bf16[1536,1152]{1,0:T(8,128)(2,1)}, bf16[16,72,1536]{2,1,0:T(8,128)(2,1)}, b...) custom-call(s32[33]{0:T(128)} %pad_add_fusion.2.side, bf16[1536,1152]{1,0:T(8,128)(2,1)} %tok_ref.7, ...), custom_call_target="tpu_custom_call" | custom-call | flops 15854469120 | bytes 38928384 | tf_op jit(solution)/shard_map/pallas_call | solution.py:839
  244.1 70.1 %shard_map.314 = (f32[1536,1152]{1,0:T(8,128)}, f32[1536,1152]{1,0:T(8,128)}, f32[2,576,2304]{2,1,0:T(8,128)}, bf16[2,288,2304]{2,1,0:T(8,128)(2,1)}, bf16[2,288,2304]{2,1,0:T(8,128)(2,1)}, /*index=5*/f32[1,2304]{1,0:T(1,128)}) custom-call(s32[1]{0:T(128)S(6)} %sub.46.pick, bf16[1536,1152]{1,0:T(8,128)(2,1)} %get-tuple-element.333.h_ref, ...), custom_call_target="tpu_custom_call" | custom-call | flops 48922361856 | bytes 54853632 | tf_op jit(solution)/shard_map/pallas_call | solution.py:919
  315.0 4.8 collective-permute-done.25
  319.8 4.6 add_convert_fusion.2
  325.8 70.7 %shard_map.315 = (f32[1536,1152]{1,0:T(8,128)}, f32[1536,1152]{1,0:T(8,128)}, f32[2,576,2304]{2,1,0:T(8,128)}, bf16[2,288,2304]{2,1,0:T(8,128)(2,1)}, bf16[2,288,2304]{2,1,0:T(8,128)(2,1)}, /*index=5*/f32[1,2304]{1,0:T(1,128)}) custom-call(s32[1]{0:T(128)} %bitcast.10.pick, bf16[1536,1152]{1,0:T(8,128)(2,1)} %get-tuple-element.333.h_ref, ...), custom_call_target="tpu_custom_call" | custom-call | flops 48922361856 | bytes 54853632 | tf_op jit(solution)/shard_map/pallas_call | solution.py:919
  396.9 5.8 add_convert_fusion.1
  402.7 1.5 copy-done.5
  404.2 2.1 add_convert_fusion
  406.3 1.6 collective-permute-start.29
  409.4 47.9 %shard_map.316 = (bf16[1536,1152]{1,0:T(8,128)(2,1)}, f32[1536,1152]{1,0:T(8,128)}, bf16[2,512,640]{2,1,0:T(8,128)(2,1)}, bf16[2,512,640]{2,1,0:T(8,128)(2,1)}, ...) custom-call(s32[33]{0:T(128)} %pad_add_fusion.2.side, ...), custom_call_target="tpu_custom_call" | custom-call | flops 19931332608 | bytes 60162048 | tf_op jit(solution)/shard_map/pallas_call | solution.py:1042
  457.4 8.6 %collective-permute-done.29 = bf16[2,288,2304]{2,1,0:T(8,128)(2,1)} collective-permute-done((bf16[2,288,2304]{2,1,0:T(8,128)(2,1)}, bf16[2,288,2304]{2,1,0:T(8,128)(2,1)}, u32[]{:S(2)}, u32[]{:S(2)}) %collective-permute-start.29) | collective-permute-done | bytes 2654240 | tf_op jit(solution)/shard_map/ppermute | solution.py:1196
  468.2 6.0 fusion.59
  474.3 1.4 fusion.60
  477.9 7.0 collective-permute-done.33.do_second
  484.9 52.1 %shard_map.317 = (bf16[1,512,1792]{2,1,0:T(8,128)(2,1)}, bf16[1,512,1792]{2,1,0:T(8,128)(2,1)}) custom-call(bf16[1,512,1792]{2,1,0:T(8,128)(2,1)} %get-tuple-element.287.first, bf16[1,512,1792]{2,1,0:T(8,128)(2,1)} %get-tuple-element.288.second, bf16[1,512,640]{2,1,0:T(8,128)(2,1)} %get-tuple-element.374.do_first, ...), custom_call_target="tpu_custom_call" | custom-call | flops 12000000000 | bytes 11010048 | tf_op jit(solution)/shard_map/pallas_call | solution.py:739
  537.3 1.8 collective-permute-start.36
  539.4 72.4 %shard_map.318 = (bf16[2,512,1792]{2,1,0:T(8,128)(2,1)}, bf16[2,512,1792]{2,1,0:T(8,128)(2,1)}) custom-call(bf16[2,512,1792]{2,1,0:T(8,128)(2,1)} %get-tuple-element.300.first, bf16[2,512,1792]{2,1,0:T(8,128)(2,1)} %get-tuple-element.301.second, bf16[2,512,640]{2,1,0:T(8,128)(2,1)} %get-tuple-element.387.do_first, ...), custom_call_target="tpu_custom_call" | custom-call | flops 24000000000 | bytes 22020096 | tf_op jit(solution)/shard_map/pallas_call | solution.py:739
  614.2 13.8 %shard_map.319 = (f32[576,1792]{1,0:T(8,128)}, bf16[576,1792]{1,0:T(8,128)(2,1)}, f32[1,1792]{1,0:T(1,128)}) custom-call(bf16[1152,1536]{1,0:T(8,128)(2,1)} %bitcast.172, bf16[2,512,1792]{2,1,0:T(8,128)(2,1)} %get-tuple-element.397.first, bf16[2,512,1792]{2,1,0:T(8,128)(2,1)} %get-tuple-element.398.second, ...), custom_call_target="tpu_custom_call" | custom-call | flops 6341787648 | bytes 14548992 | tf_op jit(solution)/shard_map/pallas_call | solution.py:1112
  631.4 2.4 collective-permute-start.41
  633.8 2.0 reduce-precision_convert_fusion.1
  637.6 1.5 collective-permute-start.42
  639.0 2.2 collective-permute-start.43
  641.2 13.8 %shard_map.320 = (f32[576,1792]{1,0:T(8,128)}, bf16[576,1792]{1,0:T(8,128)(2,1)}, f32[1,1792]{1,0:T(1,128)}) custom-call(bf16[1152,1536]{1,0:T(8,128)(2,1)} %bitcast.173, bf16[2,512,1792]{2,1,0:T(8,128)(2,1)} %get-tuple-element.397.first, bf16[2,512,1792]{2,1,0:T(8,128)(2,1)} %get-tuple-element.398.second, bf16[1,512,1792]{2,1,0:T(8,128)(2,1)} %get-tuple-element.399.rest.own), custom_call_target="tpu_custom_call" | custom-call | flops 6341787648 | bytes 14548992 | tf_op jit(solution)/shard_map/pallas_call | solution.py:1112
  655.9 1.7 convert_add_fusion.3
  659.0 2.8 add_convert_fusion.3
  662.4 1.9 add_convert_fusion.5
  664.3 1.4 collective-permute-start.46
  667.1 31.6 %shard_map.321 = (f32[1536,1152]{1,0:T(8,128)}, f32[2,8,1152]{2,1,0:T(8,128)}) custom-call(s32[33]{0:T(128)} %pad_add_fusion.2.side, bf16[2,512,1792]{2,1,0:T(8,128)(2,1)} %get-tuple-element.397.first, bf16[2,512,1792]{2,1,0:T(8,128)(2,1)} %get-tuple-element.398.second, bf16[1,512,1792]{2,1,0:T(8,128)(2,1)} %get-tuple-element.399.rest.own, ...), custom_call_target="tpu_custom_call" | custom-call | flops 12683575296 | bytes 28704768 | tf_op jit(solution)/shard_map/pallas_call | solution.py:1150
  698.7 12.3 %collective-permute-done.47 = bf16[288,1792]{1,0:T(8,128)(2,1)} collective-permute-done((bf16[288,1792]{1,0:T(8,128)(2,1)S(1)}, bf16[288,1792]{1,0:T(8,128)(2,1)}, u32[]{:S(2)}, u32[]{:S(2)}) %collective-permute-start.47) | collective-permute-done | bytes 1032224 | tf_op jit(solution)/shard_map/ppermute | solution.py:1196
  714.5 2.0 fusion.57
  717.1 1.8 collective-permute-start.50
  718.9 1.7 collective-permute-start.51
  720.6 16.9 %fusion.25 = f32[8,1152]{1,0:T(8,128)S(1)} fusion(f32[1152,3456]{1,0:T(8,128)} %param.24, f32[8,4096]{1,0:T(8,128)S(1)} %add.244), kind=kOutput, calls=%fused_computation.79 | convolution fusion | flops 382205952 | bytes 16072704 | tf_op jit(solution)/shard_map/dot_general | solution.py:1513
  737.6 1.7 collective-permute-start.54
  739.2 1.7 fusion.24
  740.9 1.5 collective-permute-start.55
  742.4 2.6 collective-permute-start.56
  745.0 3.0 collective-permute-done.53
  748.1 13.8 %collective-permute-done.56 = bf16[72,1792]{1,0:T(8,128)(2,1)S(1)} collective-permute-done((bf16[72,1792]{1,0:T(8,128)(2,1)S(1)}, bf16[72,1792]{1,0:T(8,128)(2,1)S(1)}, u32[]{:S(2)}, u32[]{:S(2)}) %collective-permute-start.56) | collective-permute-done | bytes 258080 | tf_op jit(solution)/shard_map/ppermute | solution.py:1196
  761.8 4.5 collective-permute-done.57
  766.5 1.5 collective-permute-start.58
  772.6 8.2 %fusion = f32[1152,3456]{1,0:T(8,128)} fusion(bf16[128,3456]{1,0:T(8,128)(2,1)S(1)} %get-tuple-element.501, bf16[128,3456]{1,0:T(8,128)(2,1)S(1)} %get-tuple-element.500, bf16[128,1152]{1,0:T(8,128)(2,1)S(1)} %copy-done.9, bf16[128,1152]{1,0:T(8,128)(2,1)S(1)} %copy-done.8), kind=kOutput, calls=%fused_computation.5 | convolution fusion | flops 3068264448 | bytes 18284544 | tf_op jit(solution)/shard_map/dot_general | solution.py:40
  (260 shorter events, 66.6 us)
Async XLA Ops:
  7.2 236.9 %all-gather.2.cloned.1.call-start = ((), (), s32[]{:S(2)}) async-start(), calls=%async_computation | async-start | bytes 21897216 | tf_op jit(solution)/shard_map/all_gather | solution.py:1355
  9.4 17.2 %collective-permute-start = (bf16[1,72,1536]{2,1,0:T(8,128)(2,1)S(1)}, bf16[1,72,1536]{2,1,0:T(8,128)(2,1)S(1)}, u32[]{:S(2)}, u32[]{:S(2)}) collective-permute-start(bf16[1,72,1536]{2,1,0:T(8,128)(2,1)S(1)} %get-tuple-element.531), channel_id=1, source_target_pairs={{0,24},{1,25},{2,26},{3,27},{4,28},{5,29},{6,30},{7,31},{8,0},{9,1... | collective-permute-start | bytes 663560 | tf_op jit(solution)/shard_map/ppermute | solution.py:1196
  10.5 16.1 %collective-permute-start.1 = (bf16[1,72,768]{2,1,0:T(8,128)(2,1)S(1)}, bf16[1,72,768]{2,1,0:T(8,128)(2,1)S(1)}, u32[]{:S(2)}, u32[]{:S(2)}) collective-permute-start(bf16[1,72,768]{2,1,0:T(8,128)(2,1)S(1)} %pad_maximum_fusion.12), channel_id=1, source_target_pairs={{0,4},{1,5},{2,6},{3,7},{4,0},{5,1},{6,2},{7,3},{8,12},{9,13},{10,... | collective-permute-start | bytes 331784 | tf_op jit(solution)/shard_map/ppermute | solution.py:1196
  26.7 10.5 %collective-permute-start.4 = (bf16[2,1,72,768]{3,2,0,1:T(8,128)(2,1)S(1)}, bf16[2,1,72,768]{3,2,0,1:T(8,128)(2,1)S(1)}, u32[]{:S(2)}, u32[]{:S(2)}) collective-permute-start(bf16[2,1,72,768]{3,2,0,1:T(8,128)(2,1)S(1)} %get-tuple-element.535), channel_id=1, source_target_pairs={{0,1},{1,0},{2,3},{3,2},{4,5},{5,4},{6,7},{7,6},{8,9},{9,8},{10,11... | collective-permute-start | bytes 663560 | tf_op jit(solution)/shard_map/ppermute | solution.py:1196
  28.4 8.8 %collective-permute-start.2 = (f32[9,3456]{1,0:T(8,128)S(1)}, f32[9,3456]{1,0:T(8,128)S(1)}, u32[]{:S(2)}, u32[]{:S(2)}) collective-permute-start(f32[9,3456]{1,0:T(8,128)S(1)} %dynamic-update-slice.4), channel_id=1, source_target_pairs={{0,1},{1,0},{2,3},{3,2},{4,5},{5,4},{6,7},{7,6},{8,9},{9,8},{10,11... | collective-permute-start | bytes 373256 | tf_op jit(solution)/shard_map/ppermute | solution.py:1196
  28.7 8.5 %collective-permute-start.3 = (bf16[1,72,1536]{2,1,0:T(8,128)(2,1)S(1)}, bf16[1,72,1536]{2,1,0:T(8,128)(2,1)S(1)}, u32[]{:S(2)}, u32[]{:S(2)}) collective-permute-start(bf16[1,72,1536]{2,1,0:T(8,128)(2,1)S(1)} %collective-permute-done), channel_id=1, source_target_pairs={{0,24},{1,25},{2,26},{3,27},{4,28},{5,29},{6,30},{7,31},{8,0},{9,1... | collective-permute-start | bytes 663560 | tf_op jit(solution)/shard_map/ppermute | solution.py:1196
  37.4 16.0 %collective-permute-start.6 = (bf16[2,2,1,72,768]{4,3,1,0,2:T(8,128)(2,1)S(1)}, bf16[2,2,1,72,768]{4,3,1,0,2:T(8,128)(2,1)S(1)}, u32[]{:S(2)}, u32[]{:S(2)}) collective-permute-start(bf16[2,2,1,72,768]{4,3,1,0,2:T(8,128)(2,1)S(1)} %get-tuple-element.519), channel_id=1, source_target_pairs={{0,24},{1,25},{2,26},{3,27},{4,28},{5,29},{6,30},{7,31},{8,0},{9,1... | collective-permute-start | bytes 1327112 | tf_op jit(solution)/shard_map/ppermute | solution.py:1196
  40.8 12.6 %collective-permute-start.5 = (bf16[1,72,1536]{2,1,0:T(8,128)(2,1)S(1)}, bf16[1,72,1536]{2,1,0:T(8,128)(2,1)S(1)}, u32[]{:S(2)}, u32[]{:S(2)}) collective-permute-start(bf16[1,72,1536]{2,1,0:T(8,128)(2,1)S(1)} %collective-permute-done.3), channel_id=1, source_target_pairs={{0,24},{1,25},{2,26},{3,27},{4,28},{5,29},{6,30},{7,31},{8,0},{9,1... | collective-permute-start | bytes 663560 | tf_op jit(solution)/shard_map/ppermute | solution.py:1196
  54.5 9.3 %collective-permute-start.7 = (bf16[4,1,72,768]{3,2,0,1:T(8,128)(2,1)}, bf16[4,1,72,768]{3,2,0,1:T(8,128)(2,1)}, u32[]{:S(2)}, u32[]{:S(2)}) collective-permute-start(bf16[4,1,72,768]{3,2,0,1:T(8,128)(2,1)} %get-tuple-element.514), channel_id=1, source_target_pairs={{0,4},{1,5},{2,6},{3,7},{4,0},{5,1},{6,2},{7,3},{8,12},{9,13},{10,... | collective-permute-start | bytes 1327112 | tf_op jit(solution)/shard_map/ppermute | solution.py:1196
  54.7 9.0 %collective-permute-start.8 = (bf16[4,1,72,768]{3,2,0,1:T(8,128)(2,1)}, bf16[4,1,72,768]{3,2,0,1:T(8,128)(2,1)}, u32[]{:S(2)}, u32[]{:S(2)}) collective-permute-start(bf16[4,1,72,768]{3,2,0,1:T(8,128)(2,1)} %get-tuple-element.513), channel_id=1, source_target_pairs={{0,1},{1,0},{2,3},{3,2},{4,5},{5,4},{6,7},{7,6},{8,9},{9,8},{10,11... | collective-permute-start | bytes 1327112 | tf_op jit(solution)/shard_map/ppermute | solution.py:1196
  56.0 8.5 %collective-permute-start.9 = (bf16[2,2,1,72,768]{4,3,1,0,2:T(8,128)(2,1)S(1)}, bf16[2,2,1,72,768]{4,3,1,0,2:T(8,128)(2,1)S(1)}, u32[]{:S(2)}, u32[]{:S(2)}) collective-permute-start(bf16[2,2,1,72,768]{4,3,1,0,2:T(8,128)(2,1)S(1)} %collective-permute-done.6), channel_id=1, source_target_pairs={{0,24},{1,25},{2,26},{3,27},{4,28},{5,29},{6,30},{7,31},{8,0},{9,1... | collective-permute-start | bytes 1327112 | tf_op jit(solution)/shard_map/ppermute | solution.py:1196
  65.6 18.0 %collective-permute-start.11 = (bf16[2,4,1,72,768]{4,3,1,2,0:T(8,128)(2,1)S(1)}, bf16[2,4,1,72,768]{4,3,1,2,0:T(8,128)(2,1)S(1)}, u32[]{:S(2)}, u32[]{:S(2)}) collective-permute-start(bf16[2,4,1,72,768]{4,3,1,2,0:T(8,128)(2,1)S(1)} %get-tuple-element.508), channel_id=1, source_target_pairs={{0,4},{1,5},{2,6},{3,7},{4,0},{5,1},{6,2},{7,3},{8,12},{9,13},{10,... | collective-permute-start | bytes 2654216 | tf_op jit(solution)/shard_map/ppermute | solution.py:1196
  66.9 36.8 %copy-start.37 = (bf16[512,1152]{1,0:T(8,128)(2,1)S(1)}, bf16[512,1152]{1,0:T(8,128)(2,1)}, u32[]{:S(2)}) copy-start(bf16[512,1152]{1,0:T(8,128)(2,1)} %get-tuple-element.282.first_in) | copy-start | bytes 3538948
  66.9 37.3 %copy-start.30 = (f32[1152]{0:T(1024)S(1)}, f32[1152]{0:T(1024)}, u32[]{:S(2)}) copy-start(f32[1152]{0:T(1024)} %param.32) | copy-start | bytes 13828
  68.2 19.7 %collective-permute-start.10 = (bf16[2,4,1,72,768]{4,3,1,2,0:T(8,128)(2,1)S(1)}, bf16[2,4,1,72,768]{4,3,1,2,0:T(8,128)(2,1)S(1)}, u32[]{:S(2)}, u32[]{:S(2)}) collective-permute-start(bf16[2,4,1,72,768]{4,3,1,2,0:T(8,128)(2,1)S(1)} %get-tuple-element.510), channel_id=1, source_target_pairs={{0,1},{1,0},{2,3},{3,2},{4,5},{5,4},{6,7},{7,6},{8,9},{9,8},{10,11... | collective-permute-start | bytes 2654216 | tf_op jit(solution)/shard_map/ppermute | solution.py:1196
  68.7 7.9 %collective-permute-start.12 = (bf16[2,2,1,72,768]{4,3,1,0,2:T(8,128)(2,1)S(1)}, bf16[2,2,1,72,768]{4,3,1,0,2:T(8,128)(2,1)S(1)}, u32[]{:S(2)}, u32[]{:S(2)}) collective-permute-start(bf16[2,2,1,72,768]{4,3,1,0,2:T(8,128)(2,1)S(1)} %collective-permute-done.9), channel_id=1, source_target_pairs={{0,24},{1,25},{2,26},{3,27},{4,28},{5,29},{6,30},{7,31},{8,0},{9,1... | collective-permute-start | bytes 1327112 | tf_op jit(solution)/shard_map/ppermute | solution.py:1196
  88.1 15.6 %collective-permute-start.17 = (bf16[4,2,2,1,72,768]{5,4,3,2,1,0:T(8,128)(2,1)S(1)}, bf16[4,2,2,1,72,768]{5,4,3,2,1,0:T(8,128)(2,1)S(1)}, u32[]{:S(2)}, u32[]{:S(2)}) collective-permute-start(bf16[4,2,2,1,72,768]{5,4,3,2,1,0:T(8,128)(2,1)S(1)} %pad_maximum_fusion.refs_4_), channel_id=1, source_target_pairs={{0,2},{1,3},{2,0},{3,1},{4,6},{5,7},{6,4},{7,5},{8,10},{9,11},{10,... | collective-permute-start | bytes 5308424 | tf_op jit(solution)/shard_map/ppermute | solution.py:1196
  95.3 4.6 collective-permute-start.15
  95.4 5.8 collective-permute-start.13
  95.8 6.6 collective-permute-start.14
  95.9 7.8 collective-permute-start.16
  103.7 36.8 %collective-permute-start.18 = (bf16[512,1152]{1,0:T(8,128)(2,1)S(1)}, bf16[512,1152]{1,0:T(8,128)(2,1)S(1)}, u32[]{:S(2)}, u32[]{:S(2)}) collective-permute-start(bf16[512,1152]{1,0:T(8,128)(2,1)S(1)} %copy-done.37), channel_id=1, source_target_pairs={{0,1},{1,0},{2,3},{3,2},{4,5},{5,4},{6,7},{7,6},{8,9},{9,8},{10,11... | collective-permute-start | bytes 3538952 | tf_op jit(solution)/shard_map/ppermute | solution.py:1196
  151.7 27.4 %collective-permute-start.19 = (bf16[8,1152]{1,0:T(8,128)(2,1)S(1)}, bf16[8,1152]{1,0:T(8,128)(2,1)S(1)}, u32[]{:S(2)}, u32[]{:S(2)}) collective-permute-start(bf16[8,1152]{1,0:T(8,128)(2,1)S(1)} %copy-done.19), channel_id=1, source_target_pairs={{0,8},{1,9},{2,10},{3,11},{4,12},{5,13},{6,14},{7,15},{8,16},{9,17... | collective-permute-start | bytes 55304 | tf_op jit(solution)/shard_map/ppermute | solution.py:1196
  153.0 26.1 %collective-permute-start.20 = (bf16[8,1152]{1,0:T(8,128)(2,1)S(1)}, bf16[8,1152]{1,0:T(8,128)(2,1)S(1)}, u32[]{:S(2)}, u32[]{:S(2)}) collective-permute-start(bf16[8,1152]{1,0:T(8,128)(2,1)S(1)} %copy-done.19), channel_id=1, source_target_pairs={{0,16},{1,17},{2,18},{3,19},{4,20},{5,21},{6,22},{7,23},{8,24},{9,... | collective-permute-start | bytes 55304 | tf_op jit(solution)/shard_map/ppermute | solution.py:1196
  156.0 23.1 %collective-permute-start.21 = (bf16[8,1152]{1,0:T(8,128)(2,1)S(1)}, bf16[8,1152]{1,0:T(8,128)(2,1)S(1)}, u32[]{:S(2)}, u32[]{:S(2)}) collective-permute-start(bf16[8,1152]{1,0:T(8,128)(2,1)S(1)} %copy-done.19), channel_id=1, source_target_pairs={{0,24},{1,25},{2,26},{3,27},{4,28},{5,29},{6,30},{7,31},{8,0},{9,1... | collective-permute-start | bytes 55304 | tf_op jit(solution)/shard_map/ppermute | solution.py:1196
  179.1 40.4 %collective-permute-start.22 = (bf16[1,512,640]{2,1,0:T(8,128)(2,1)}, bf16[1,512,640]{2,1,0:T(8,128)(2,1)S(1)}, u32[]{:S(2)}, u32[]{:S(2)}) collective-permute-start(bf16[1,512,640]{2,1,0:T(8,128)(2,1)} %get-tuple-element.308), channel_id=1, source_target_pairs={{0,1},{1,0},{2,3},{3,2},{4,5},{5,4},{6,7},{7,6},{8,9},{9,8},{10,11... | collective-permute-start | bytes 1966088 | tf_op jit(solution)/shard_map/ppermute | solution.py:1196
  179.2 40.3 %collective-permute-start.23 = (bf16[4,8,1152]{2,1,0:T(8,128)(2,1)S(1)}, bf16[4,8,1152]{2,1,0:T(8,128)(2,1)S(1)}, u32[]{:S(2)}, u32[]{:S(2)}) collective-permute-start(bf16[4,8,1152]{2,1,0:T(8,128)(2,1)S(1)} %pad_maximum_fusion.13), channel_id=1, source_target_pairs={{0,4},{1,5},{2,6},{3,7},{4,0},{5,1},{6,2},{7,3},{8,12},{9,13},{10,... | collective-permute-start | bytes 221192 | tf_op jit(solution)/shard_map/ppermute | solution.py:1196
  219.6 23.8 %collective-permute-start.24 = (bf16[8,8,1152]{2,1,0:T(8,128)(2,1)S(1)}, bf16[8,8,1152]{2,1,0:T(8,128)(2,1)S(1)}, u32[]{:S(2)}, u32[]{:S(2)}) collective-permute-start(bf16[8,8,1152]{2,1,0:T(8,128)(2,1)S(1)} %pad_maximum_fusion.11), channel_id=1, source_target_pairs={{0,2},{1,3},{2,0},{3,1},{4,6},{5,7},{6,4},{7,5},{8,10},{9,11},{10,... | collective-permute-start | bytes 442376 | tf_op jit(solution)/shard_map/ppermute | solution.py:1196
  314.2 5.6 collective-permute-start.25
  324.4 72.0 %collective-permute-start.26 = (bf16[2,288,2304]{2,1,0:T(8,128)(2,1)}, bf16[2,288,2304]{2,1,0:T(8,128)(2,1)S(1)}, u32[]{:S(2)}, u32[]{:S(2)}) collective-permute-start(bf16[2,288,2304]{2,1,0:T(8,128)(2,1)} %get-tuple-element.340), channel_id=1, source_target_pairs={{0,2},{1,3},{2,0},{3,1},{4,6},{5,7},{6,4},{7,5},{8,10},{9,11},{10,... | collective-permute-start | bytes 7962632 | tf_op jit(solution)/shard_map/ppermute | solution.py:1196
  324.8 71.7 %collective-permute-start.27 = (bf16[2,288,2304]{2,1,0:T(8,128)(2,1)}, bf16[2,288,2304]{2,1,0:T(8,128)(2,1)}, u32[]{:S(2)}, u32[]{:S(2)}) collective-permute-start(bf16[2,288,2304]{2,1,0:T(8,128)(2,1)} %add_convert_fusion.2), channel_id=1, source_target_pairs={{0,4},{1,5},{2,6},{3,7},{4,0},{5,1},{6,2},{7,3},{8,12},{9,13},{10,... | collective-permute-start | bytes 7962632 | tf_op jit(solution)/shard_map/ppermute | solution.py:1196
  396.5 6.2 collective-permute-start.28
  406.3 59.7 %collective-permute-start.29 = (bf16[2,288,2304]{2,1,0:T(8,128)(2,1)}, bf16[2,288,2304]{2,1,0:T(8,128)(2,1)}, u32[]{:S(2)}, u32[]{:S(2)}) collective-permute-start(bf16[2,288,2304]{2,1,0:T(8,128)(2,1)} %add_convert_fusion.1), channel_id=1, source_target_pairs={{0,1},{1,0},{2,3},{3,2},{4,5},{5,4},{6,7},{7,6},{8,9},{9,8},{10,11... | collective-permute-start | bytes 7962632 | tf_op jit(solution)/shard_map/ppermute | solution.py:1196
  407.9 59.0 %collective-permute-start.30 = (bf16[2,288,2304]{2,1,0:T(8,128)(2,1)}, bf16[2,288,2304]{2,1,0:T(8,128)(2,1)}, u32[]{:S(2)}, u32[]{:S(2)}) collective-permute-start(bf16[2,288,2304]{2,1,0:T(8,128)(2,1)} %add_convert_fusion), channel_id=1, source_target_pairs={{0,4},{1,5},{2,6},{3,7},{4,0},{5,1},{6,2},{7,3},{8,12},{9,13},{10,... | collective-permute-start | bytes 7962632 | tf_op jit(solution)/shard_map/ppermute | solution.py:1196
  408.1 58.8 %collective-permute-start.31 = (bf16[2,288,2304]{2,1,0:T(8,128)(2,1)}, bf16[2,288,2304]{2,1,0:T(8,128)(2,1)}, u32[]{:S(2)}, u32[]{:S(2)}) collective-permute-start(bf16[2,288,2304]{2,1,0:T(8,128)(2,1)} %get-tuple-element.365), channel_id=1, source_target_pairs={{0,2},{1,3},{2,0},{3,1},{4,6},{5,7},{6,4},{7,5},{8,10},{9,11},{10,... | collective-permute-start | bytes 7962632 | tf_op jit(solution)/shard_map/ppermute | solution.py:1196
  466.9 8.8 %collective-permute-start.32 = (bf16[2,576,640]{2,1,0:T(8,128)(2,1)}, bf16[2,576,640]{2,1,0:T(8,128)(2,1)S(1)}, u32[]{:S(2)}, u32[]{:S(2)}) collective-permute-start(bf16[2,576,640]{2,1,0:T(8,128)(2,1)} %get-tuple-element.373), channel_id=1, source_target_pairs={{0,2},{1,3},{2,0},{3,1},{4,6},{5,7},{6,4},{7,5},{8,10},{9,11},{10,... | collective-permute-start | bytes 4423688 | tf_op jit(solution)/shard_map/ppermute | solution.py:1196
  468.2 16.7 %collective-permute-start.33 = (bf16[1,512,640]{2,1,0:T(8,128)(2,1)}, bf16[1,512,640]{2,1,0:T(8,128)(2,1)}, u32[]{:S(2)}, u32[]{:S(2)}) collective-permute-start(bf16[1,512,640]{2,1,0:T(8,128)(2,1)} %get-tuple-element.375), channel_id=1, source_target_pairs={{0,1},{1,0},{2,3},{3,2},{4,5},{5,4},{6,7},{7,6},{8,9},{9,8},{10,11... | collective-permute-start | bytes 1966088 | tf_op jit(solution)/shard_map/ppermute | solution.py:1196
  537.0 76.0 %copy-start.17 = (bf16[288,640]{1,0:T(8,128)(2,1)S(1)}, bf16[288,640]{1,0:T(8,128)(2,1)}, u32[]{:S(2)}) copy-start(bf16[288,640]{1,0:T(8,128)(2,1)} %get-tuple-element.408) | copy-start | bytes 1105924
  537.0 77.2 %collective-permute-start.34 = (bf16[1,512,1792]{2,1,0:T(8,128)(2,1)}, bf16[1,512,1792]{2,1,0:T(8,128)(2,1)}, u32[]{:S(2)}, u32[]{:S(2)}) collective-permute-start(bf16[1,512,1792]{2,1,0:T(8,128)(2,1)} %get-tuple-element.393), channel_id=1, source_target_pairs={{0,1},{1,0},{2,3},{3,2},{4,5},{5,4},{6,7},{7,6},{8,9},{9,8},{10,11... | collective-permute-start | bytes 5505032 | tf_op jit(solution)/shard_map/ppermute | solution.py:1196
  537.1 74.7 %collective-permute-start.35 = (bf16[2,72,2304]{2,1,0:T(8,128)(2,1)}, bf16[2,72,2304]{2,1,0:T(8,128)(2,1)S(1)}, u32[]{:S(2)}, u32[]{:S(2)}) collective-permute-start(bf16[2,72,2304]{2,1,0:T(8,128)(2,1)} %get-tuple-element.394), channel_id=1, source_target_pairs={{0,8},{1,9},{2,10},{3,11},{4,12},{5,13},{6,14},{7,15},{8,16},{9,17... | collective-permute-start | bytes 1990664 | tf_op jit(solution)/shard_map/ppermute | solution.py:1196
  537.3 75.7 %collective-permute-start.36 = (bf16[2,72,2304]{2,1,0:T(8,128)(2,1)}, bf16[2,72,2304]{2,1,0:T(8,128)(2,1)S(1)}, u32[]{:S(2)}, u32[]{:S(2)}) collective-permute-start(bf16[2,72,2304]{2,1,0:T(8,128)(2,1)} %get-tuple-element.395), channel_id=1, source_target_pairs={{0,16},{1,17},{2,18},{3,19},{4,20},{5,21},{6,22},{7,23},{8,24},{9,... | collective-permute-start | bytes 1990664 | tf_op jit(solution)/shard_map/ppermute | solution.py:1196
  539.1 75.2 %collective-permute-start.37 = (bf16[2,72,2304]{2,1,0:T(8,128)(2,1)}, bf16[2,72,2304]{2,1,0:T(8,128)(2,1)}, u32[]{:S(2)}, u32[]{:S(2)}) collective-permute-start(bf16[2,72,2304]{2,1,0:T(8,128)(2,1)} %get-tuple-element.396), channel_id=1, source_target_pairs={{0,24},{1,25},{2,26},{3,27},{4,28},{5,29},{6,30},{7,31},{8,0},{9,1... | collective-permute-start | bytes 1990664 | tf_op jit(solution)/shard_map/ppermute | solution.py:1196
  539.1 89.0 %collective-permute-start.38 = (bf16[288,640]{1,0:T(8,128)(2,1)}, bf16[288,640]{1,0:T(8,128)(2,1)}, u32[]{:S(2)}, u32[]{:S(2)}) collective-permute-start(bf16[288,640]{1,0:T(8,128)(2,1)} %get-tuple-element.406), channel_id=1, source_target_pairs={{0,4},{1,5},{2,6},{3,7},{4,0},{5,1},{6,2},{7,3},{8,12},{9,13},{10,... | collective-permute-start | bytes 1105928 | tf_op jit(solution)/shard_map/ppermute | solution.py:1196
  611.8 16.9 %collective-permute-start.39 = (bf16[288,640]{1,0:T(8,128)(2,1)}, bf16[288,640]{1,0:T(8,128)(2,1)}, u32[]{:S(2)}, u32[]{:S(2)}) collective-permute-start(bf16[288,640]{1,0:T(8,128)(2,1)} %get-tuple-element.407), channel_id=1, source_target_pairs={{0,1},{1,0},{2,3},{3,2},{4,5},{5,4},{6,7},{7,6},{8,9},{9,8},{10,11... | collective-permute-start | bytes 1105928 | tf_op jit(solution)/shard_map/ppermute | solution.py:1196
  613.0 15.7 %collective-permute-start.40 = (bf16[288,640]{1,0:T(8,128)(2,1)S(1)}, bf16[288,640]{1,0:T(8,128)(2,1)}, u32[]{:S(2)}, u32[]{:S(2)}) collective-permute-start(bf16[288,640]{1,0:T(8,128)(2,1)S(1)} %copy-done.17), channel_id=1, source_target_pairs={{0,5},{1,4},{2,7},{3,6},{4,1},{5,0},{6,3},{7,2},{8,13},{9,12},{10,... | collective-permute-start | bytes 1105928 | tf_op jit(solution)/shard_map/ppermute | solution.py:1196
  631.4 23.8 %collective-permute-start.41 = (bf16[576,1792]{1,0:T(8,128)(2,1)}, bf16[576,1792]{1,0:T(8,128)(2,1)S(1)}, u32[]{:S(2)}, u32[]{:S(2)}) collective-permute-start(bf16[576,1792]{1,0:T(8,128)(2,1)} %get-tuple-element.418), channel_id=1, source_target_pairs={{0,2},{1,3},{2,0},{3,1},{4,6},{5,7},{6,4},{7,5},{8,10},{9,11},{10,... | collective-permute-start | bytes 6193160 | tf_op jit(solution)/shard_map/ppermute | solution.py:1196
  637.6 17.6 %collective-permute-start.42 = (bf16[72,640]{1,0:T(8,128)(2,1)}, bf16[72,640]{1,0:T(8,128)(2,1)S(1)}, u32[]{:S(2)}, u32[]{:S(2)}) collective-permute-start(bf16[72,640]{1,0:T(8,128)(2,1)} %get-tuple-element.419), channel_id=1, source_target_pairs={{0,8},{1,9},{2,10},{3,11},{4,12},{5,13},{6,14},{7,15},{8,16},{9,17... | collective-permute-start | bytes 276488 | tf_op jit(solution)/shard_map/ppermute | solution.py:1196
  639.0 16.2 %collective-permute-start.43 = (bf16[72,640]{1,0:T(8,128)(2,1)}, bf16[72,640]{1,0:T(8,128)(2,1)}, u32[]{:S(2)}, u32[]{:S(2)}) collective-permute-start(bf16[72,640]{1,0:T(8,128)(2,1)} %get-tuple-element.420), channel_id=1, source_target_pairs={{0,16},{1,17},{2,18},{3,19},{4,20},{5,21},{6,22},{7,23},{8,24},{9,... | collective-permute-start | bytes 276488 | tf_op jit(solution)/shard_map/ppermute | solution.py:1196
  641.2 14.0 %collective-permute-start.44 = (bf16[72,640]{1,0:T(8,128)(2,1)}, bf16[72,640]{1,0:T(8,128)(2,1)}, u32[]{:S(2)}, u32[]{:S(2)}) collective-permute-start(bf16[72,640]{1,0:T(8,128)(2,1)} %get-tuple-element.421), channel_id=1, source_target_pairs={{0,24},{1,25},{2,26},{3,27},{4,28},{5,29},{6,30},{7,31},{8,0},{9,1... | collective-permute-start | bytes 276488 | tf_op jit(solution)/shard_map/ppermute | solution.py:1196
  655.3 6.5 collective-permute-start.45
  664.3 47.9 %copy-start.21 = (f32[4,8,1152]{2,1,0:T(8,128)S(1)}, f32[4,8,1152]{2,1,0:T(8,128)}, u32[]{:S(2)}) copy-start(f32[4,8,1152]{2,1,0:T(8,128)} %get-tuple-element.434) | copy-start | bytes 442372
  664.3 34.4 %collective-permute-start.46 = (bf16[288,1792]{1,0:T(8,128)(2,1)S(1)}, bf16[288,1792]{1,0:T(8,128)(2,1)S(1)}, u32[]{:S(2)}, u32[]{:S(2)}) collective-permute-start(bf16[288,1792]{1,0:T(8,128)(2,1)S(1)} %get-tuple-element.429), channel_id=1, source_target_pairs={{0,4},{1,5},{2,6},{3,7},{4,0},{5,1},{6,2},{7,3},{8,12},{9,13},{10,... | collective-permute-start | bytes 3096584 | tf_op jit(solution)/shard_map/ppermute | solution.py:1196
  665.7 45.3 %collective-permute-start.47 = (bf16[288,1792]{1,0:T(8,128)(2,1)S(1)}, bf16[288,1792]{1,0:T(8,128)(2,1)}, u32[]{:S(2)}, u32[]{:S(2)}) collective-permute-start(bf16[288,1792]{1,0:T(8,128)(2,1)S(1)} %get-tuple-element.430), channel_id=1, source_target_pairs={{0,1},{1,0},{2,3},{3,2},{4,5},{5,4},{6,7},{7,6},{8,9},{9,8},{10,11... | collective-permute-start | bytes 3096584 | tf_op jit(solution)/shard_map/ppermute | solution.py:1196
  667.1 45.0 %collective-permute-start.48 = (bf16[288,1792]{1,0:T(8,128)(2,1)S(1)}, bf16[288,1792]{1,0:T(8,128)(2,1)}, u32[]{:S(2)}, u32[]{:S(2)}) collective-permute-start(bf16[288,1792]{1,0:T(8,128)(2,1)S(1)} %get-tuple-element.431), channel_id=1, source_target_pairs={{0,5},{1,4},{2,7},{3,6},{4,1},{5,0},{6,3},{7,2},{8,13},{9,12},{10,... | collective-permute-start | bytes 3096584 | tf_op jit(solution)/shard_map/ppermute | solution.py:1196
  713.2 3.8 collective-permute-start.49
  717.1 20.4 %collective-permute-start.50 = (f32[8,4096]{1,0:T(8,128)S(1)}, f32[8,4096]{1,0:T(8,128)S(1)}, u32[]{:S(2)}, u32[]{:S(2)}) collective-permute-start(f32[8,4096]{1,0:T(8,128)S(1)} %add.244), channel_id=1, source_target_pairs={{0,8},{1,9},{2,10},{3,11},{4,12},{5,13},{6,14},{7,15},{8,16},{9,17... | collective-permute-start | bytes 393224 | tf_op jit(solution)/shard_map/ppermute | solution.py:1196
  718.9 18.7 %collective-permute-start.51 = (f32[8,4096]{1,0:T(8,128)S(1)}, f32[8,4096]{1,0:T(8,128)S(1)}, u32[]{:S(2)}, u32[]{:S(2)}) collective-permute-start(f32[8,4096]{1,0:T(8,128)S(1)} %add.244), channel_id=1, source_target_pairs={{0,16},{1,17},{2,18},{3,19},{4,20},{5,21},{6,22},{7,23},{8,24},{9,... | collective-permute-start | bytes 393224 | tf_op jit(solution)/shard_map/ppermute | solution.py:1196
  720.6 17.0 %collective-permute-start.52 = (f32[8,4096]{1,0:T(8,128)S(1)}, f32[8,4096]{1,0:T(8,128)S(1)}, u32[]{:S(2)}, u32[]{:S(2)}) collective-permute-start(f32[8,4096]{1,0:T(8,128)S(1)} %add.244), channel_id=1, source_target_pairs={{0,24},{1,25},{2,26},{3,27},{4,28},{5,29},{6,30},{7,31},{8,0},{9,1... | collective-permute-start | bytes 393224 | tf_op jit(solution)/shard_map/ppermute | solution.py:1196
  737.6 28.8 %collective-permute-start.54 = (f32[32,4096]{1,0:T(8,128)S(1)}, f32[32,4096]{1,0:T(8,128)S(1)}, u32[]{:S(2)}, u32[]{:S(2)}) collective-permute-start(f32[32,4096]{1,0:T(8,128)S(1)} %pad_maximum_fusion.6), channel_id=1, source_target_pairs={{0,4},{1,5},{2,6},{3,7},{4,0},{5,1},{6,2},{7,3},{8,12},{9,13},{10,... | collective-permute-start | bytes 1572872 | tf_op jit(solution)/shard_map/ppermute | solution.py:1196
  740.9 7.2 collective-permute-start.55
  742.4 19.5 %collective-permute-start.56 = (bf16[72,1792]{1,0:T(8,128)(2,1)S(1)}, bf16[72,1792]{1,0:T(8,128)(2,1)S(1)}, u32[]{:S(2)}, u32[]{:S(2)}) collective-permute-start(bf16[72,1792]{1,0:T(8,128)(2,1)S(1)} %get-tuple-element.455), channel_id=1, source_target_pairs={{0,16},{1,17},{2,18},{3,19},{4,20},{5,21},{6,22},{7,23},{8,24},{9,... | collective-permute-start | bytes 774152 | tf_op jit(solution)/shard_map/ppermute | solution.py:1196
  744.9 21.4 %collective-permute-start.57 = (bf16[72,1792]{1,0:T(8,128)(2,1)S(1)}, bf16[72,1792]{1,0:T(8,128)(2,1)S(1)}, u32[]{:S(2)}, u32[]{:S(2)}) collective-permute-start(bf16[72,1792]{1,0:T(8,128)(2,1)S(1)} %get-tuple-element.456), channel_id=1, source_target_pairs={{0,24},{1,25},{2,26},{3,27},{4,28},{5,29},{6,30},{7,31},{8,0},{9,1... | collective-permute-start | bytes 774152 | tf_op jit(solution)/shard_map/ppermute | solution.py:1196
  744.9 3.1 collective-permute-start.53
  766.5 3.8 collective-permute-start.58
  (36 other events, 285.8 us)
Sparse Core Ops, SparseCore 0:
  64.6 151.8 all-gather.1

commit v5 on v4

--- a/solution.py
+++ b/solution.py
@@ -630,16 +630,17 @@
         l_second[0] = log_totals
 
 
-def attend(first, second, query_marks, key_marks, out_width):
-    groups, half, padded = first.shape
+def attend(first, second, query_marks, key_marks, out_width, group):
+    groups = 1
+    _, half, padded = first.shape
     heads = out_width // HEAD_DIM
     pair = lambda *dims: pl.BlockSpec((1,) + dims, lambda a, i: (a, 0, 0))
     return pl.pallas_call(
         partial(attend_kernel, heads),
         grid=(groups, 2),
         in_specs=[
-            pair(half, padded),
-            pair(half, padded),
+            pl.BlockSpec((1, half, padded), lambda a, i: (group, 0, 0)),
+            pl.BlockSpec((1, half, padded), lambda a, i: (group, 0, 0)),
             pl.BlockSpec((half, MARKS), lambda a, i: (i, 0)),
             pl.BlockSpec((2 * half, MARKS), lambda a, i: (0, 0)),
         ],
@@ -782,6 +783,22 @@
     return jnp.where(i < per, first[...], jnp.where(i < 2 * per, second[...], half))
 
 
+def thirds_of(first, second, half, i, per):
+    return [
+        jnp.where(i < per, a[0], jnp.where(i < 2 * per, b[0], c[0]))
+        for a, b, c in zip(first, second, half)
+    ]
+
+
+def single_specs(block, columns, per):
+    return [
+        pl.BlockSpec(
+            (1, block, columns), lambda i, y, k=k: (0, jnp.clip(i - k * per, 0, per - 1), 0)
+        )
+        for k in (0, 0, 1, 1, 2, 2)
+    ]
+
+
 def third_specs(block, columns, per):
     full = lambda low: pl.BlockSpec(
         (2, block, columns), lambda i, y: (0, jnp.clip(i - low * per, 0, per - 1), 0)
@@ -799,17 +816,18 @@
 
 
 def middle_kernel(
-    side, tok_ref, dy_ref, first, second, own, other, w_own, w_other, b_ref, hot_ref, parts_ref,
-    branch_ref, h_ref, g_ref, ht_ref, gt_ref, gb_ref,
+    side, tok_ref, dy_ref, first, first_other, second, second_other, own, other, w_own, w_other, b_ref, hot_ref,
+    parts_ref, branch_ref, h_ref, g_ref, ht_ref, gt_ref, gb_ref,
 ):
     i = pl.program_id(0)
     width = tok_ref.shape[1]
     used = width // 2
-    att = third_of(first, second, own, other, i, pl.num_programs(0) // 3)[:, :, :used]
+    per = pl.num_programs(0) // 3
+    att = thirds_of((first, first_other), (second, second_other), (own, other), i, per)
     skip = w_own.shape[2] - used
     branch = (
-        contract_last(att[0], w_own[0, :, skip:])
-        + contract_last(att[1], w_other[0, :, skip:])
+        contract_last(att[0][:, :used], w_own[0, :, skip:])
+        + contract_last(att[1][:, :used], w_other[0, :, skip:])
         + b_ref[...]
     )
     branch_ref[...] = branch
@@ -844,7 +862,7 @@
             in_specs=[
                 placed,
                 placed,
-                *third_specs(block, thirds[0].shape[2], per),
+                *single_specs(block, thirds[0].shape[2], per),
                 *out_weight_specs(width, weights.shape[2]),
                 spec((1, width)),
                 pl.BlockSpec((block, hot.shape[1]), lambda i, y: (i, 0)),
@@ -957,7 +975,7 @@
 
 def back_two_kernel(
     side, tok_ref, dy_ref, branch_ref, two_a, two_b, b_ref, back_a, back_b, w_own, w_other, hot_ref,
-    turn_ref, parts_ref, first, second, half_own, half_other, out_ref, middle_ref, a_first, a_second,
+    turn_ref, parts_ref, first, first_other, second, second_other, half_own, half_other, out_ref, middle_ref, a_first, a_second,
     a_own, a_other, sums_ref, gb_ref, mine_ref, theirs_ref, outer_ref,
 ):
     width = tok_ref.shape[1]
@@ -976,7 +994,13 @@
     middle_ref[...] = grad_middle
     grad = (grad_middle * gate).astype(BF)
     turned = grad.astype(F32).T.astype(BF)
-    att = third_of(first, second, half_own, half_other, pl.program_id(0), pl.num_programs(0) // 3)
+    att = thirds_of(
+        (first, first_other),
+        (second, second_other),
+        (half_own, half_other),
+        pl.program_id(0),
+        pl.num_programs(0) // 3,
+    )
     for k in range(2):
         product = rows_by_columns(turned, att[k])
 
@@ -1057,7 +1081,7 @@
                 pl.BlockSpec((block, hot.shape[1]), lambda i, y: (i, 0)),
                 pl.BlockSpec((images, block), lambda i, y: (0, i)),
                 spec(parts.shape),
-                *third_specs(block, out_width, per),
+                *single_specs(block, out_width, per),
             ],
             out_specs=[
                 placed,
@@ -1359,31 +1383,34 @@
         tree.take(got)
         attention_weights = tree.whole.reshape(2, width, shard.shape[1])
 
-        qkv_first, qkv_second, hidden_got = after(
-            *project(
-                side, hidden_full, hidden_full, attention_weights, qkv_bias, padded, third, 2
-            ),
+        qkv_first, qkv_second = project(
+            side, hidden_full, hidden_full, attention_weights, qkv_bias, padded, third, 2
+        )
+        qkv_full = (qkv_first, qkv_second)
+        qkv_first, hidden_half, condition = after(qkv_first, hidden_half, condition)
+        first_0, second_0, l_first_0, l_second_0, hidden_got, *got = after(
+            *attend(qkv_first, qkv_second, *marks_full, out_width, 0),
             send(hidden_half, to_heads),
-        )
-        qkv_full = (qkv_first, qkv_second)
+            *(send(condition, to_level[k]) for k in range(1, levels)),
+        )
+        flat = jnp.stack([condition, *got])
         qkv_half = project(
             side, hidden_half, hidden_got, attention_weights, qkv_bias, padded, third, 1
         )
-        qkv_own, qkv_got, condition = after(*qkv_half, condition)
-        qkv_half = (qkv_own, qkv_got)
-        out_own, out_theirs, l_own, l_other, *got = after(
-            *attend(*qkv_half, *marks_half, out_width),
-            *(send(condition, to_level[k]) for k in range(1, levels)),
+        out_own, out_theirs, l_own, l_other, got = after(
+            *attend(*qkv_half, *marks_half, out_width, 0), send(flat, to_x)
         )
         lse_half = (l_own, l_other)
-        qkv_first, out_theirs, flat = after(qkv_first, out_theirs, jnp.stack([condition, *got]))
-        out_first, out_second, *lse_full, out_other, got = after(
-            *attend(qkv_first, qkv_second, *marks_full, out_width),
-            send(out_theirs, to_heads),
-            send(flat, to_x),
-        )
-        out_first, flat = after(out_first, jnp.concatenate([flat, got], axis=0))
-        attended = (out_first, out_second, out_own, out_other)
+        flat = jnp.concatenate([flat, got], axis=0)
+        qkv_first, out_theirs, flat = after(qkv_first, out_theirs, flat)
+        first_1, second_1, l_first_1, l_second_1, out_other = after(
+            *attend(qkv_first, qkv_second, *marks_full, out_width, 1), send(out_theirs, to_heads)
+        )
+        lse_full = (
+            jnp.concatenate([l_first_0, l_first_1], axis=0),
+            jnp.concatenate([l_second_0, l_second_1], axis=0),
+        )
+        attended = (first_0, first_1, second_0, second_1, out_own, out_other)
         branch_one, hidden_two, grad_two, hidden_two_turned, grad_two_turned, grad_b_down, got = after(
             *middle_part(
                 side, tokens, cotangent, attended, attention_weights, b_out[None], hot, parts, third // 2
@@ -1419,7 +1446,7 @@
 
         flat_turned = lambda values: values.reshape(width, rows)
         hidden_one_turned = flat_turned(hidden_one_turned)
-        feed_args = (flat_turned(hidden_two_turned), flat_turned(grad_two_turned), feed_weights, up_bias, third, 768)
+        feed_args = (flat_turned(hidden_two_turned), flat_turned(grad_two_turned), feed_weights, up_bias, rows // 2, 768)
         two_b, back_b, mine_b, near_b, far_b, grad_b_up_b = feed(
             1 - y.reshape(1), hidden_two, grad_two, *feed_args
         )
@@ -1452,13 +1479,17 @@
         )
         grad_own, feed_kept, *joined = after(grad_own, feed_kept, *feed_sent, *out_pieces)
         feed_sent, out_pieces = joined[: levels - 1], joined[levels - 1 :]
-        grad_qkv_own, grad_qkv_theirs = attend_back(
-            *qkv_half, grad_own, grad_other, *lse_half, *marks_half
-        )
-        grad_first, grad_qkv_theirs, feed_kept, *joined = after(
-            grad_first, grad_qkv_theirs, feed_kept, *feed_sent, *out_pieces
-        )
-        feed_sent, out_pieces = joined[: levels - 1], joined[levels - 1 :]
+        grad_qkv_own, grad_qkv_theirs, *got = after(
+            *attend_back(*qkv_half, grad_own, grad_other, *lse_half, *marks_half),
+            send(out_pieces[1], to_x),
+            send(out_pieces[2], to_heads),
+            send(out_pieces[3], to_corner),
+        )
+        out_kept, *out_sent = level_pieces(all_added(out_pieces[0], got))
+        grad_first, grad_qkv_theirs, feed_kept, out_kept, *joined = after(
+            grad_first, grad_qkv_theirs, feed_kept, out_kept, *feed_sent, *out_sent
+        )
+        feed_sent, out_sent = joined[: levels - 1], joined[levels - 1 :]
         grad_qkv_first, grad_qkv_second, grad_qkv_other, *got = after(
             *attend_back(*qkv_full, grad_first, grad_second, *lse_full, *marks_full),
             send(grad_qkv_theirs, to_heads),
@@ -1467,20 +1498,14 @@
         grad_w_up, grad_w_down = all_added(feed_kept, got)
         qkv_mine_b, qkv_theirs_b, grad_qkv_bias_b, *got = after(
             *outer(hidden_one_turned, grad_qkv_first, grad_qkv_second, grad_qkv_other, 1),
-            send(out_pieces[1], to_x),
-            send(out_pieces[2], to_heads),
-            send(out_pieces[3], to_corner),
-        )
-        out_kept, *out_sent = level_pieces(all_added(out_pieces[0], got))
-        hidden_one_turned, qkv_theirs_b, out_kept, *out_sent = after(
-            hidden_one_turned, qkv_theirs_b, out_kept, *out_sent
-        )
-        qkv_mine_a, qkv_theirs_a, grad_qkv_bias_a, qkv_got_b, *got = after(
+            *(send(part, to_level[k + 1]) for k, part in enumerate(out_sent)),
+        )
+        grad_w_out = all_added(out_kept, got)
+        hidden_one_turned, qkv_theirs_b = after(hidden_one_turned, qkv_theirs_b)
+        qkv_mine_a, qkv_theirs_a, grad_qkv_bias_a, qkv_got_b = after(
             *outer(hidden_one_turned, grad_qkv_first, grad_qkv_second, grad_qkv_own, 0),
             send(qkv_theirs_b, to_core),
-            *(send(part, to_level[k + 1]) for k, part in enumerate(out_sent)),
-        )
-        grad_w_out = all_added(out_kept, got)
+        )
         near, *sent = plane_pieces(qkv_mine_a, send(qkv_theirs_a, to_core), qkv_mine_b, qkv_got_b)
         grad_middle, near, *sent = after(grad_middle, near, *sent)
         grad_qkv = (grad_qkv_first, grad_qkv_second, grad_qkv_own, grad_qkv_other)

time: 795 us -> 814 us (1.024)
  starting transfers between devices: 66.5 us -> 81 us
    ppermute x59, starting transfers between devices: 66.5 us -> 81 us  [send(): return lax.ppermute(values, both, pairs)]
    pallas_call x2 -> x3, Pallas kernels: 61.8 us -> 65.7 us  [attend(): pl.pallas_call(partial(attend_kernel, heads), grid=(groups, 2), in_specs=...]
  transfers between devices with their start and end apart: 60 -> 60, of which waited for: 23 -> 18; matrix products, arithmetic and copies ran while one was open for 9% -> 9% of each run, Pallas kernels for 47% -> 53%
where the time goes in v5:
time: 814 us; the launch traced here: 806 us
  Pallas kernels  498 us (61%)
  waiting for transfers between devices  103 us (13%)
  starting transfers between devices  81 us (10%)
  other arithmetic  46.5 us (6%)
  matrix products  36.3 us (4%)
  local copies, waits for them, and re-layouts  26.4 us (3%)
  between operations  15.2 us (2%)
    pallas_call x2, Pallas kernels, feed(): pl.pallas_call(partial(feed_kernel, chunk), grid_spec=pltpu.PrefetchScala...  140 us
    pallas_call x2, Pallas kernels, attend_back(): pl.pallas_call(partial(attend_back_kernel, heads), grid=(groups, 2), in_s...  124 us
    ppermute x59, waiting for transfers between devices, send(): return lax.ppermute(values, both, pairs)  103 us
    ppermute x59, starting transfers between devices, send(): return lax.ppermute(values, both, pairs)  81 us
    pallas_call x3, Pallas kernels, attend(): pl.pallas_call(partial(attend_kernel, heads), grid=(groups, 2), in_specs=...  65.7 us
    pallas_call x1, Pallas kernels, back_two(): pl.pallas_call(back_two_kernel, grid_spec=pltpu.PrefetchScalarGridSpec(nu...  47.9 us
    pallas_call x1, Pallas kernels, back_one(): pl.pallas_call(back_one_kernel, grid_spec=pltpu.PrefetchScalarGridSpec(nu...  31.7 us
    pallas_call x2, Pallas kernels, outer(): pl.pallas_call(outer_kernel, grid=(2,), in_specs=[pl.BlockSpec((width //...  28.1 us
  transfers between devices with their start and end apart: 60, of which 18 were waited for; matrix products, arithmetic and copies ran while one was open for 9% of the time, Pallas kernels for 53%

profile of v5, /device:TPU:9, one launch (start us, length us, event | category | flops | bytes accessed | tf_op | source)
XLA Modules:
  0.0 806.2 jit_solution(5466482522460869161)
XLA Ops:
  10.5 1.4 collective-permute-start.1
  15.1 11.3 %convolution_add_fusion = f32[8,3456]{1,0:T(8,128)S(1)} fusion(f32[1152,3456]{1,0:T(8,128)} %param.24, f32[3456]{0:T(1024)S(1)} %copy-done.33, bf16[8,1152]{1,0:T(8,128)(2,1)S(1)} %copy-done.16), kind=kOutput, calls=%fused_computation.4 | convolution fusion | flops 382279680 | bytes 16068096 | tf_op jit(solution)/shard_map/dot_general | solution.py:1345
  28.7 3.3 collective-permute-start.3
  37.4 3.4 collective-permute-start.6
  41.7 9.0 %shard_map.307 = (bf16[1024,1152]{1,0:T(8,128)(2,1)}, bf16[512,1152]{1,0:T(8,128)(2,1)}, bf16[16,72,1536]{2,1,0:T(8,128)(2,1)}) custom-call(s32[33]{0:T(128)} %pad_add_fusion.2.side, bf16[1536,1152]{1,0:T(8,128)(2,1)} %tok_ref.7, bf16[1536,24]{1,0:T(8,128)(2,1)} %compare_convert_fusion.hot_ref, bf16[2,24,3456]{2,1,0:T(8,128)(2,1)} %pad_maximum_fusion.8.parts_ref), custom_call_target="tpu_custom_call" | custom-call | flops 5888802816 | bytes 10616832 | tf_op jit(solution)/shard_map/pallas_call | solution.py:462
  52.0 1.4 concatenate.129.bias_ref
  56.0 1.6 collective-permute-start.9
  58.6 5.1 collective-permute-done.7
  68.6 13.9 %collective-permute-start.12 = (bf16[2,2,1,72,768]{4,3,1,0,2:T(8,128)(2,1)S(1)}, bf16[2,2,1,72,768]{4,3,1,0,2:T(8,128)(2,1)S(1)}, u32[]{:S(2)}, u32[]{:S(2)}) collective-permute-start(bf16[2,2,1,72,768]{4,3,1,0,2:T(8,128)(2,1)S(1)} %collective-permute-done.9), channel_id=1, source_target_pairs={{0,24},{1,25},{2,26},{3,27},{4,28},{5,29},{6,30},{7,31},{8,0},{9,1... | collective-permute-start | bytes 1327112 | tf_op jit(solution)/shard_map/ppermute | solution.py:1220
  82.5 21.9 %collective-permute-done.12 = bf16[2,2,1,72,768]{4,3,1,0,2:T(8,128)(2,1)S(1)} collective-permute-done((bf16[2,2,1,72,768]{4,3,1,0,2:T(8,128)(2,1)S(1)}, bf16[2,2,1,72,768]{4,3,1,0,2:T(8,128)(2,1)S(1)}, u32[]{:S(2)}, u32[]{:S(2)}) %collective-permute-start.12) | collective-permute-done | bytes 442400 | tf_op jit(solution)/shard_map/ppermute | solution.py:1220
  104.6 2.2 collective-permute-start.17
  108.5 2.9 collective-permute-done.15
  115.2 3.4 shard_map.308
  118.6 4.1 copy-done
  122.7 15.3 %shard_map.309 = (bf16[2,512,1792]{2,1,0:T(8,128)(2,1)}, bf16[2,512,1792]{2,1,0:T(8,128)(2,1)}) custom-call(s32[33]{0:T(128)} %pad_add_fusion.2.side, bf16[1024,1152]{1,0:T(8,128)(2,1)} %get-tuple-element.275.first_in.second_in, bf16[1024,1152]{1,0:T(8,128)(2,1)} %get-tuple-element.275.first_in.second_in, bf16[2,1152,2304]{2,1,0:T(8,128)(2,1)} %bitcast.138, ...), custom_call_target="tpu_custom_call" | custom-call | flops 8455716864 | bytes 23855104 | tf_op jit(solution)/shard_map/pallas_call | solution.py:501
  141.8 21.7 %shard_map.310 = (bf16[1,512,640]{2,1,0:T(8,128)(2,1)}, bf16[1,512,640]{2,1,0:T(8,128)(2,1)}, f32[1,8,512]{2,1,0:T(8,128)}, f32[1,8,512]{2,1,0:T(8,128)}) custom-call(bf16[2,512,1792]{2,1,0:T(8,128)(2,1)} %get-tuple-element.309.first, bf16[2,512,1792]{2,1,0:T(8,128)(2,1)} %get-tuple-element.285.second, bf16[1024,16]{1,0:T(8,128)(2,1)} %copy-done.1, ...), custom_call_target="tpu_custom_call" | custom-call | flops 15000000512 | bytes 5505024 | tf_op jit(solution)/shard_map/pallas_call | solution.py:638
  163.5 17.5 %collective-permute-done.18.second_in = bf16[512,1152]{1,0:T(8,128)(2,1)S(1)} collective-permute-done((bf16[512,1152]{1,0:T(8,128)(2,1)S(1)}, bf16[512,1152]{1,0:T(8,128)(2,1)S(1)}, u32[]{:S(2)}, u32[]{:S(2)}) %collective-permute-start.18) | collective-permute-done | bytes 1179680 | tf_op jit(solution)/shard_map/ppermute | solution.py:1220
  182.0 10.1 %shard_map.311 = (bf16[1,512,1792]{2,1,0:T(8,128)(2,1)}, bf16[1,512,1792]{2,1,0:T(8,128)(2,1)}) custom-call(s32[33]{0:T(128)} %pad_add_fusion.2.side, bf16[512,1152]{1,0:T(8,128)(2,1)} %get-tuple-element.292.first_in, bf16[512,1152]{1,0:T(8,128)(2,1)} %copy-done.45, bf16[2,1152,2304]{2,1,0:T(8,128)(2,1)} %bitcast.139, f32[2,1,1728]{2,1,0:T(1,128)} %concatenate.129.bias_ref), custom_call_target="tpu_custom_call" | custom-call | flops 4227858432 | bytes 11927552 | tf_op jit(solution)/shard_map/pallas_call | solution.py:501
  192.1 22.1 %shard_map.312 = (bf16[1,512,640]{2,1,0:T(8,128)(2,1)}, bf16[1,512,640]{2,1,0:T(8,128)(2,1)}, f32[1,8,512]{2,1,0:T(8,128)}, f32[1,8,512]{2,1,0:T(8,128)}) custom-call(bf16[1,512,1792]{2,1,0:T(8,128)(2,1)} %get-tuple-element.296.first, bf16[1,512,1792]{2,1,0:T(8,128)(2,1)} %get-tuple-element.297.second, bf16[1024,16]{1,0:T(8,128)(2,1)} %copy-done.3, ...), custom_call_target="tpu_custom_call" | custom-call | flops 15000000512 | bytes 5505024 | tf_op jit(solution)/shard_map/pallas_call | solution.py:638
  214.3 1.8 collective-permute-start.23
  216.0 21.9 %shard_map.313 = (bf16[1,512,640]{2,1,0:T(8,128)(2,1)}, bf16[1,512,640]{2,1,0:T(8,128)(2,1)}, f32[1,8,512]{2,1,0:T(8,128)}, f32[1,8,512]{2,1,0:T(8,128)}) custom-call(bf16[2,512,1792]{2,1,0:T(8,128)(2,1)} %get-tuple-element.309.first, bf16[2,512,1792]{2,1,0:T(8,128)(2,1)} %get-tuple-element.285.second, bf16[1024,16]{1,0:T(8,128)(2,1)} %copy-done.1, ...), custom_call_target="tpu_custom_call" | custom-call | flops 15000000512 | bytes 5505024 | tf_op jit(solution)/shard_map/pallas_call | solution.py:638
  238.0 6.2 collective-permute-start.24
  245.0 21.8 %shard_map.314 = (f32[1536,1152]{1,0:T(8,128)}, bf16[1536,1152]{1,0:T(8,128)(2,1)}, bf16[1536,1152]{1,0:T(8,128)(2,1)}, bf16[16,72,1536]{2,1,0:T(8,128)(2,1)}, b...) custom-call(s32[33]{0:T(128)} %pad_add_fusion.2.side, bf16[1536,1152]{1,0:T(8,128)(2,1)} %tok_ref.7, ...), custom_call_target="tpu_custom_call" | custom-call | flops 15854469120 | bytes 38928384 | tf_op jit(solution)/shard_map/pallas_call | solution.py:857
  267.5 69.7 %shard_map.315 = (f32[1536,1152]{1,0:T(8,128)}, f32[1536,1152]{1,0:T(8,128)}, f32[2,576,2304]{2,1,0:T(8,128)}, bf16[2,288,2304]{2,1,0:T(8,128)(2,1)}, bf16[2,288,2304]{2,1,0:T(8,128)(2,1)}, /*index=5*/f32[1,2304]{1,0:T(1,128)}) custom-call(s32[1]{0:T(128)S(6)} %sub.46.pick, bf16[1536,1152]{1,0:T(8,128)(2,1)} %get-tuple-element.337.h_ref, ...), custom_call_target="tpu_custom_call" | custom-call | flops 48922361856 | bytes 54853632 | tf_op jit(solution)/shard_map/pallas_call | solution.py:937
  337.3 5.1 collective-permute-done.25
  342.5 4.6 add_convert_fusion.2
  348.0 70.2 %shard_map.316 = (f32[1536,1152]{1,0:T(8,128)}, f32[1536,1152]{1,0:T(8,128)}, f32[2,576,2304]{2,1,0:T(8,128)}, bf16[2,288,2304]{2,1,0:T(8,128)(2,1)}, bf16[2,288,2304]{2,1,0:T(8,128)(2,1)}, /*index=5*/f32[1,2304]{1,0:T(1,128)}) custom-call(s32[1]{0:T(128)} %bitcast.10.pick, bf16[1536,1152]{1,0:T(8,128)(2,1)} %get-tuple-element.337.h_ref, ...), custom_call_target="tpu_custom_call" | custom-call | flops 48922361856 | bytes 54853632 | tf_op jit(solution)/shard_map/pallas_call | solution.py:937
  418.9 5.7 add_convert_fusion.1
  424.7 1.5 copy-done.5
  426.2 2.1 add_convert_fusion
  431.4 47.9 %shard_map.317 = (bf16[1536,1152]{1,0:T(8,128)(2,1)}, f32[1536,1152]{1,0:T(8,128)}, bf16[2,512,640]{2,1,0:T(8,128)(2,1)}, bf16[2,512,640]{2,1,0:T(8,128)(2,1)}, ...) custom-call(s32[33]{0:T(128)} %pad_add_fusion.2.side, ...), custom_call_target="tpu_custom_call" | custom-call | flops 19931332608 | bytes 60162048 | tf_op jit(solution)/shard_map/pallas_call | solution.py:1066
  479.4 8.4 %collective-permute-done.29 = bf16[2,288,2304]{2,1,0:T(8,128)(2,1)} collective-permute-done((bf16[2,288,2304]{2,1,0:T(8,128)(2,1)}, bf16[2,288,2304]{2,1,0:T(8,128)(2,1)}, u32[]{:S(2)}, u32[]{:S(2)}) %collective-permute-start.29) | collective-permute-done | bytes 2654240 | tf_op jit(solution)/shard_map/ppermute | solution.py:1220
  488.6 1.4 collective-permute-start.33
  490.0 6.0 fusion.59
  496.0 1.4 fusion.60
  500.4 1.9 collective-permute-start.36
  502.3 3.0 collective-permute-done.33.do_second
  505.3 52.1 %shard_map.318 = (bf16[1,512,1792]{2,1,0:T(8,128)(2,1)}, bf16[1,512,1792]{2,1,0:T(8,128)(2,1)}) custom-call(bf16[1,512,1792]{2,1,0:T(8,128)(2,1)} %get-tuple-element.296.first, bf16[1,512,1792]{2,1,0:T(8,128)(2,1)} %get-tuple-element.297.second, bf16[1,512,640]{2,1,0:T(8,128)(2,1)} %get-tuple-element.378.do_first, ...), custom_call_target="tpu_custom_call" | custom-call | flops 12000000000 | bytes 11010048 | tf_op jit(solution)/shard_map/pallas_call | solution.py:740
  558.3 1.4 collective-permute-start.37
  560.8 5.1 collective-permute-start.39
  565.9 1.5 collective-permute-start.41
  567.3 72.3 %shard_map.319 = (bf16[2,512,1792]{2,1,0:T(8,128)(2,1)}, bf16[2,512,1792]{2,1,0:T(8,128)(2,1)}) custom-call(bf16[2,512,1792]{2,1,0:T(8,128)(2,1)} %get-tuple-element.309.first, bf16[2,512,1792]{2,1,0:T(8,128)(2,1)} %get-tuple-element.285.second, bf16[2,512,640]{2,1,0:T(8,128)(2,1)} %get-tuple-element.396.do_first, ...), custom_call_target="tpu_custom_call" | custom-call | flops 24000000000 | bytes 22020096 | tf_op jit(solution)/shard_map/pallas_call | solution.py:740
  639.7 1.9 collective-permute-start.42
  641.6 14.3 %shard_map.320 = (f32[576,1792]{1,0:T(8,128)}, bf16[576,1792]{1,0:T(8,128)(2,1)}, f32[1,1792]{1,0:T(1,128)}) custom-call(bf16[1152,1536]{1,0:T(8,128)(2,1)} %bitcast.176, bf16[2,512,1792]{2,1,0:T(8,128)(2,1)} %get-tuple-element.408.first, bf16[2,512,1792]{2,1,0:T(8,128)(2,1)} %get-tuple-element.409.second, ...), custom_call_target="tpu_custom_call" | custom-call | flops 6341787648 | bytes 14548992 | tf_op jit(solution)/shard_map/pallas_call | solution.py:1136
  656.6 2.6 collective-permute-start.44
  659.2 1.9 reduce-precision_convert_fusion.1
  663.8 13.8 %shard_map.321 = (f32[576,1792]{1,0:T(8,128)}, bf16[576,1792]{1,0:T(8,128)(2,1)}, f32[1,1792]{1,0:T(1,128)}) custom-call(bf16[1152,1536]{1,0:T(8,128)(2,1)} %bitcast.177, bf16[2,512,1792]{2,1,0:T(8,128)(2,1)} %get-tuple-element.408.first, bf16[2,512,1792]{2,1,0:T(8,128)(2,1)} %get-tuple-element.409.second, bf16[1,512,1792]{2,1,0:T(8,128)(2,1)} %get-tuple-element.410.rest.own), custom_call_target="tpu_custom_call" | custom-call | flops 6341787648 | bytes 14548992 | tf_op jit(solution)/shard_map/pallas_call | solution.py:1136
  677.7 1.8 convert_add_fusion.3
  680.8 2.8 add_convert_fusion.3
  684.2 1.9 add_convert_fusion.5
  687.0 1.8 collective-permute-start.48
  688.8 31.7 %shard_map.322 = (f32[1536,1152]{1,0:T(8,128)}, f32[2,8,1152]{2,1,0:T(8,128)}) custom-call(s32[33]{0:T(128)} %pad_add_fusion.2.side, bf16[2,512,1792]{2,1,0:T(8,128)(2,1)} %get-tuple-element.408.first, bf16[2,512,1792]{2,1,0:T(8,128)(2,1)} %get-tuple-element.409.second, bf16[1,512,1792]{2,1,0:T(8,128)(2,1)} %get-tuple-element.410.rest.own, ...), custom_call_target="tpu_custom_call" | custom-call | flops 12683575296 | bytes 28704768 | tf_op jit(solution)/shard_map/pallas_call | solution.py:1174
  720.6 11.6 %collective-permute-done.48 = bf16[288,1792]{1,0:T(8,128)(2,1)} collective-permute-done((bf16[288,1792]{1,0:T(8,128)(2,1)S(1)}, bf16[288,1792]{1,0:T(8,128)(2,1)}, u32[]{:S(2)}, u32[]{:S(2)}) %collective-permute-start.48) | collective-permute-done | bytes 1032224 | tf_op jit(solution)/shard_map/ppermute | solution.py:1220
  733.2 1.3 collective-permute-start.49
  734.5 2.0 fusion.57
  737.1 1.6 collective-permute-start.50
  738.6 2.6 collective-permute-start.51
  741.3 16.8 %fusion.25 = f32[8,1152]{1,0:T(8,128)S(1)} fusion(f32[1152,3456]{1,0:T(8,128)} %param.24, f32[8,4096]{1,0:T(8,128)S(1)} %add.244), kind=kOutput, calls=%fused_computation.78 | convolution fusion | flops 382205952 | bytes 16072704 | tf_op jit(solution)/shard_map/dot_general | solution.py:1538
  759.7 1.5 collective-permute-start.55
  761.2 1.8 collective-permute-start.56
  764.3 1.7 collective-permute-done.53
  766.1 14.9 %collective-permute-done.56 = bf16[72,1792]{1,0:T(8,128)(2,1)S(1)} collective-permute-done((bf16[72,1792]{1,0:T(8,128)(2,1)S(1)}, bf16[72,1792]{1,0:T(8,128)(2,1)S(1)}, u32[]{:S(2)}, u32[]{:S(2)}) %collective-permute-start.56) | collective-permute-done | bytes 258080 | tf_op jit(solution)/shard_map/ppermute | solution.py:1220
  780.9 4.1 collective-permute-done.57
  790.9 8.2 %fusion = f32[1152,3456]{1,0:T(8,128)} fusion(bf16[128,3456]{1,0:T(8,128)(2,1)S(1)} %get-tuple-element.505, bf16[128,3456]{1,0:T(8,128)(2,1)S(1)} %get-tuple-element.504, bf16[128,1152]{1,0:T(8,128)(2,1)S(1)} %copy-done.9, bf16[128,1152]{1,0:T(8,128)(2,1)S(1)} %copy-done.8), kind=kOutput, calls=%fused_computation.5 | convolution fusion | flops 3068264448 | bytes 18284544 | tf_op jit(solution)/shard_map/dot_general | solution.py:40
  (281 shorter events, 64.1 us)
Async XLA Ops:
  7.2 260.3 %all-gather.2.cloned.1.call-start = ((), (), s32[]{:S(2)}) async-start(), calls=%async_computation | async-start | bytes 21897216 | tf_op jit(solution)/shard_map/all_gather | solution.py:1379
  9.4 17.2 %collective-permute-start = (bf16[1,72,1536]{2,1,0:T(8,128)(2,1)S(1)}, bf16[1,72,1536]{2,1,0:T(8,128)(2,1)S(1)}, u32[]{:S(2)}, u32[]{:S(2)}) collective-permute-start(bf16[1,72,1536]{2,1,0:T(8,128)(2,1)S(1)} %get-tuple-element.535), channel_id=1, source_target_pairs={{0,24},{1,25},{2,26},{3,27},{4,28},{5,29},{6,30},{7,31},{8,0},{9,1... | collective-permute-start | bytes 663560 | tf_op jit(solution)/shard_map/ppermute | solution.py:1220
  10.5 16.1 %collective-permute-start.1 = (bf16[1,72,768]{2,1,0:T(8,128)(2,1)S(1)}, bf16[1,72,768]{2,1,0:T(8,128)(2,1)S(1)}, u32[]{:S(2)}, u32[]{:S(2)}) collective-permute-start(bf16[1,72,768]{2,1,0:T(8,128)(2,1)S(1)} %pad_maximum_fusion.11), channel_id=1, source_target_pairs={{0,4},{1,5},{2,6},{3,7},{4,0},{5,1},{6,2},{7,3},{8,12},{9,13},{10,... | collective-permute-start | bytes 331784 | tf_op jit(solution)/shard_map/ppermute | solution.py:1220
  26.7 10.5 %collective-permute-start.4 = (bf16[2,1,72,768]{3,2,0,1:T(8,128)(2,1)S(1)}, bf16[2,1,72,768]{3,2,0,1:T(8,128)(2,1)S(1)}, u32[]{:S(2)}, u32[]{:S(2)}) collective-permute-start(bf16[2,1,72,768]{3,2,0,1:T(8,128)(2,1)S(1)} %get-tuple-element.539), channel_id=1, source_target_pairs={{0,1},{1,0},{2,3},{3,2},{4,5},{5,4},{6,7},{7,6},{8,9},{9,8},{10,11... | collective-permute-start | bytes 663560 | tf_op jit(solution)/shard_map/ppermute | solution.py:1220
  28.4 8.8 %collective-permute-start.2 = (f32[9,3456]{1,0:T(8,128)S(1)}, f32[9,3456]{1,0:T(8,128)S(1)}, u32[]{:S(2)}, u32[]{:S(2)}) collective-permute-start(f32[9,3456]{1,0:T(8,128)S(1)} %dynamic-update-slice.9), channel_id=1, source_target_pairs={{0,1},{1,0},{2,3},{3,2},{4,5},{5,4},{6,7},{7,6},{8,9},{9,8},{10,11... | collective-permute-start | bytes 373256 | tf_op jit(solution)/shard_map/ppermute | solution.py:1220
  28.7 8.5 %collective-permute-start.3 = (bf16[1,72,1536]{2,1,0:T(8,128)(2,1)S(1)}, bf16[1,72,1536]{2,1,0:T(8,128)(2,1)S(1)}, u32[]{:S(2)}, u32[]{:S(2)}) collective-permute-start(bf16[1,72,1536]{2,1,0:T(8,128)(2,1)S(1)} %collective-permute-done), channel_id=1, source_target_pairs={{0,24},{1,25},{2,26},{3,27},{4,28},{5,29},{6,30},{7,31},{8,0},{9,1... | collective-permute-start | bytes 663560 | tf_op jit(solution)/shard_map/ppermute | solution.py:1220
  37.4 16.0 %collective-permute-start.6 = (bf16[2,2,1,72,768]{4,3,1,0,2:T(8,128)(2,1)S(1)}, bf16[2,2,1,72,768]{4,3,1,0,2:T(8,128)(2,1)S(1)}, u32[]{:S(2)}, u32[]{:S(2)}) collective-permute-start(bf16[2,2,1,72,768]{4,3,1,0,2:T(8,128)(2,1)S(1)} %get-tuple-element.523), channel_id=1, source_target_pairs={{0,24},{1,25},{2,26},{3,27},{4,28},{5,29},{6,30},{7,31},{8,0},{9,1... | collective-permute-start | bytes 1327112 | tf_op jit(solution)/shard_map/ppermute | solution.py:1220
  40.7 12.6 %collective-permute-start.5 = (bf16[1,72,1536]{2,1,0:T(8,128)(2,1)S(1)}, bf16[1,72,1536]{2,1,0:T(8,128)(2,1)S(1)}, u32[]{:S(2)}, u32[]{:S(2)}) collective-permute-start(bf16[1,72,1536]{2,1,0:T(8,128)(2,1)S(1)} %collective-permute-done.3), channel_id=1, source_target_pairs={{0,24},{1,25},{2,26},{3,27},{4,28},{5,29},{6,30},{7,31},{8,0},{9,1... | collective-permute-start | bytes 663560 | tf_op jit(solution)/shard_map/ppermute | solution.py:1220
  54.5 9.2 %collective-permute-start.7 = (bf16[4,1,72,768]{3,2,0,1:T(8,128)(2,1)}, bf16[4,1,72,768]{3,2,0,1:T(8,128)(2,1)}, u32[]{:S(2)}, u32[]{:S(2)}) collective-permute-start(bf16[4,1,72,768]{3,2,0,1:T(8,128)(2,1)} %get-tuple-element.518), channel_id=1, source_target_pairs={{0,4},{1,5},{2,6},{3,7},{4,0},{5,1},{6,2},{7,3},{8,12},{9,13},{10,... | collective-permute-start | bytes 1327112 | tf_op jit(solution)/shard_map/ppermute | solution.py:1220
  54.8 9.0 %collective-permute-start.8 = (bf16[4,1,72,768]{3,2,0,1:T(8,128)(2,1)}, bf16[4,1,72,768]{3,2,0,1:T(8,128)(2,1)}, u32[]{:S(2)}, u32[]{:S(2)}) collective-permute-start(bf16[4,1,72,768]{3,2,0,1:T(8,128)(2,1)} %get-tuple-element.517), channel_id=1, source_target_pairs={{0,1},{1,0},{2,3},{3,2},{4,5},{5,4},{6,7},{7,6},{8,9},{9,8},{10,11... | collective-permute-start | bytes 1327112 | tf_op jit(solution)/shard_map/ppermute | solution.py:1220
  56.0 8.5 %collective-permute-start.9 = (bf16[2,2,1,72,768]{4,3,1,0,2:T(8,128)(2,1)S(1)}, bf16[2,2,1,72,768]{4,3,1,0,2:T(8,128)(2,1)S(1)}, u32[]{:S(2)}, u32[]{:S(2)}) collective-permute-start(bf16[2,2,1,72,768]{4,3,1,0,2:T(8,128)(2,1)S(1)} %collective-permute-done.6), channel_id=1, source_target_pairs={{0,24},{1,25},{2,26},{3,27},{4,28},{5,29},{6,30},{7,31},{8,0},{9,1... | collective-permute-start | bytes 1327112 | tf_op jit(solution)/shard_map/ppermute | solution.py:1220
  65.6 38.8 %collective-permute-start.11 = (bf16[2,4,1,72,768]{4,3,1,2,0:T(8,128)(2,1)S(1)}, bf16[2,4,1,72,768]{4,3,1,2,0:T(8,128)(2,1)S(1)}, u32[]{:S(2)}, u32[]{:S(2)}) collective-permute-start(bf16[2,4,1,72,768]{4,3,1,2,0:T(8,128)(2,1)S(1)} %get-tuple-element.512), channel_id=1, source_target_pairs={{0,4},{1,5},{2,6},{3,7},{4,0},{5,1},{6,2},{7,3},{8,12},{9,13},{10,... | collective-permute-start | bytes 2654216 | tf_op jit(solution)/shard_map/ppermute | solution.py:1220
  66.9 40.9 %copy-start.38 = (f32[1152]{0:T(1024)S(1)}, f32[1152]{0:T(1024)}, u32[]{:S(2)}) copy-start(f32[1152]{0:T(1024)} %param.32) | copy-start | bytes 13828
  68.1 36.3 %collective-permute-start.10 = (bf16[2,4,1,72,768]{4,3,1,2,0:T(8,128)(2,1)S(1)}, bf16[2,4,1,72,768]{4,3,1,2,0:T(8,128)(2,1)S(1)}, u32[]{:S(2)}, u32[]{:S(2)}) collective-permute-start(bf16[2,4,1,72,768]{4,3,1,2,0:T(8,128)(2,1)S(1)} %get-tuple-element.514), channel_id=1, source_target_pairs={{0,1},{1,0},{2,3},{3,2},{4,5},{5,4},{6,7},{7,6},{8,9},{9,8},{10,11... | collective-permute-start | bytes 2654216 | tf_op jit(solution)/shard_map/ppermute | solution.py:1220
  68.6 35.8 %collective-permute-start.12 = (bf16[2,2,1,72,768]{4,3,1,0,2:T(8,128)(2,1)S(1)}, bf16[2,2,1,72,768]{4,3,1,0,2:T(8,128)(2,1)S(1)}, u32[]{:S(2)}, u32[]{:S(2)}) collective-permute-start(bf16[2,2,1,72,768]{4,3,1,0,2:T(8,128)(2,1)S(1)} %collective-permute-done.9), channel_id=1, source_target_pairs={{0,24},{1,25},{2,26},{3,27},{4,28},{5,29},{6,30},{7,31},{8,0},{9,1... | collective-permute-start | bytes 1327112 | tf_op jit(solution)/shard_map/ppermute | solution.py:1220
  104.6 10.5 %collective-permute-start.17 = (bf16[4,2,2,1,72,768]{5,4,3,2,1,0:T(8,128)(2,1)S(1)}, bf16[4,2,2,1,72,768]{5,4,3,2,1,0:T(8,128)(2,1)S(1)}, u32[]{:S(2)}, u32[]{:S(2)}) collective-permute-start(bf16[4,2,2,1,72,768]{5,4,3,2,1,0:T(8,128)(2,1)S(1)} %pad_maximum_fusion.refs_4_), channel_id=1, source_target_pairs={{0,2},{1,3},{2,0},{3,1},{4,6},{5,7},{6,4},{7,5},{8,10},{9,11},{10,... | collective-permute-start | bytes 5308424 | tf_op jit(solution)/shard_map/ppermute | solution.py:1220
  106.8 4.6 collective-permute-start.15
  106.9 5.8 collective-permute-start.13
  107.3 6.6 collective-permute-start.14
  107.4 7.8 collective-permute-start.16
  138.0 25.4 %collective-permute-start.19 = (bf16[8,1152]{1,0:T(8,128)(2,1)S(1)}, bf16[8,1152]{1,0:T(8,128)(2,1)S(1)}, u32[]{:S(2)}, u32[]{:S(2)}) collective-permute-start(bf16[8,1152]{1,0:T(8,128)(2,1)S(1)} %copy-done.17), channel_id=1, source_target_pairs={{0,8},{1,9},{2,10},{3,11},{4,12},{5,13},{6,14},{7,15},{8,16},{9,17... | collective-permute-start | bytes 55304 | tf_op jit(solution)/shard_map/ppermute | solution.py:1220
  139.1 24.4 %collective-permute-start.20 = (bf16[8,1152]{1,0:T(8,128)(2,1)S(1)}, bf16[8,1152]{1,0:T(8,128)(2,1)S(1)}, u32[]{:S(2)}, u32[]{:S(2)}) collective-permute-start(bf16[8,1152]{1,0:T(8,128)(2,1)S(1)} %copy-done.17), channel_id=1, source_target_pairs={{0,16},{1,17},{2,18},{3,19},{4,20},{5,21},{6,22},{7,23},{8,24},{9,... | collective-permute-start | bytes 55304 | tf_op jit(solution)/shard_map/ppermute | solution.py:1220
  140.3 23.2 %collective-permute-start.21 = (bf16[8,1152]{1,0:T(8,128)(2,1)S(1)}, bf16[8,1152]{1,0:T(8,128)(2,1)S(1)}, u32[]{:S(2)}, u32[]{:S(2)}) collective-permute-start(bf16[8,1152]{1,0:T(8,128)(2,1)S(1)} %copy-done.17), channel_id=1, source_target_pairs={{0,24},{1,25},{2,26},{3,27},{4,28},{5,29},{6,30},{7,31},{8,0},{9,1... | collective-permute-start | bytes 55304 | tf_op jit(solution)/shard_map/ppermute | solution.py:1220
  140.9 40.1 %collective-permute-start.18 = (bf16[512,1152]{1,0:T(8,128)(2,1)S(1)}, bf16[512,1152]{1,0:T(8,128)(2,1)S(1)}, u32[]{:S(2)}, u32[]{:S(2)}) collective-permute-start(bf16[512,1152]{1,0:T(8,128)(2,1)S(1)} %copy-done.44), channel_id=1, source_target_pairs={{0,1},{1,0},{2,3},{3,2},{4,5},{5,4},{6,7},{7,6},{8,9},{9,8},{10,11... | collective-permute-start | bytes 3538952 | tf_op jit(solution)/shard_map/ppermute | solution.py:1220
  181.1 33.2 %collective-permute-start.22 = (bf16[4,8,1152]{2,1,0:T(8,128)(2,1)S(1)}, bf16[4,8,1152]{2,1,0:T(8,128)(2,1)S(1)}, u32[]{:S(2)}, u32[]{:S(2)}) collective-permute-start(bf16[4,8,1152]{2,1,0:T(8,128)(2,1)S(1)} %pad_maximum_fusion.12), channel_id=1, source_target_pairs={{0,4},{1,5},{2,6},{3,7},{4,0},{5,1},{6,2},{7,3},{8,12},{9,13},{10,... | collective-permute-start | bytes 221192 | tf_op jit(solution)/shard_map/ppermute | solution.py:1220
  214.3 23.7 %copy-start.19 = (bf16[8,8,1152]{2,1,0:T(8,128)(2,1)}, bf16[8,8,1152]{2,1,0:T(8,128)(2,1)S(1)}, u32[]{:S(2)}) copy-start(bf16[8,8,1152]{2,1,0:T(8,128)(2,1)S(1)} %constant_dynamic-update-slice_fusion.1) | copy-start | bytes 442372
  214.3 29.9 %collective-permute-start.23 = (bf16[1,512,640]{2,1,0:T(8,128)(2,1)}, bf16[1,512,640]{2,1,0:T(8,128)(2,1)S(1)}, u32[]{:S(2)}, u32[]{:S(2)}) collective-permute-start(bf16[1,512,640]{2,1,0:T(8,128)(2,1)} %get-tuple-element.314), channel_id=1, source_target_pairs={{0,1},{1,0},{2,3},{3,2},{4,5},{5,4},{6,7},{7,6},{8,9},{9,8},{10,11... | collective-permute-start | bytes 1966088 | tf_op jit(solution)/shard_map/ppermute | solution.py:1220
  238.0 28.8 %collective-permute-start.24 = (bf16[8,8,1152]{2,1,0:T(8,128)(2,1)S(1)}, bf16[8,8,1152]{2,1,0:T(8,128)(2,1)S(1)}, u32[]{:S(2)}, u32[]{:S(2)}) collective-permute-start(bf16[8,8,1152]{2,1,0:T(8,128)(2,1)S(1)} %constant_dynamic-update-slice_fusion.1), channel_id=1, source_target_pairs={{0,2},{1,3},{2,0},{3,1},{4,6},{5,7},{6,4},{7,5},{8,10},{9,11},{10,... | collective-permute-start | bytes 442376 | tf_op jit(solution)/shard_map/ppermute | solution.py:1220
  337.2 5.2 collective-permute-start.25
  347.1 71.1 %collective-permute-start.26 = (bf16[2,288,2304]{2,1,0:T(8,128)(2,1)}, bf16[2,288,2304]{2,1,0:T(8,128)(2,1)S(1)}, u32[]{:S(2)}, u32[]{:S(2)}) collective-permute-start(bf16[2,288,2304]{2,1,0:T(8,128)(2,1)} %get-tuple-element.344), channel_id=1, source_target_pairs={{0,2},{1,3},{2,0},{3,1},{4,6},{5,7},{6,4},{7,5},{8,10},{9,11},{10,... | collective-permute-start | bytes 7962632 | tf_op jit(solution)/shard_map/ppermute | solution.py:1220
  347.2 71.0 %collective-permute-start.27 = (bf16[2,288,2304]{2,1,0:T(8,128)(2,1)}, bf16[2,288,2304]{2,1,0:T(8,128)(2,1)}, u32[]{:S(2)}, u32[]{:S(2)}) collective-permute-start(bf16[2,288,2304]{2,1,0:T(8,128)(2,1)} %add_convert_fusion.2), channel_id=1, source_target_pairs={{0,4},{1,5},{2,6},{3,7},{4,0},{5,1},{6,2},{7,3},{8,12},{9,13},{10,... | collective-permute-start | bytes 7962632 | tf_op jit(solution)/shard_map/ppermute | solution.py:1220
  418.2 6.5 collective-permute-start.28
  428.2 59.5 %collective-permute-start.29 = (bf16[2,288,2304]{2,1,0:T(8,128)(2,1)}, bf16[2,288,2304]{2,1,0:T(8,128)(2,1)}, u32[]{:S(2)}, u32[]{:S(2)}) collective-permute-start(bf16[2,288,2304]{2,1,0:T(8,128)(2,1)} %add_convert_fusion.1), channel_id=1, source_target_pairs={{0,1},{1,0},{2,3},{3,2},{4,5},{5,4},{6,7},{7,6},{8,9},{9,8},{10,11... | collective-permute-start | bytes 7962632 | tf_op jit(solution)/shard_map/ppermute | solution.py:1220
  428.3 59.4 %collective-permute-start.30 = (bf16[2,288,2304]{2,1,0:T(8,128)(2,1)}, bf16[2,288,2304]{2,1,0:T(8,128)(2,1)}, u32[]{:S(2)}, u32[]{:S(2)}) collective-permute-start(bf16[2,288,2304]{2,1,0:T(8,128)(2,1)} %add_convert_fusion), channel_id=1, source_target_pairs={{0,4},{1,5},{2,6},{3,7},{4,0},{5,1},{6,2},{7,3},{8,12},{9,13},{10,... | collective-permute-start | bytes 7962632 | tf_op jit(solution)/shard_map/ppermute | solution.py:1220
  429.0 58.7 %collective-permute-start.31 = (bf16[2,288,2304]{2,1,0:T(8,128)(2,1)}, bf16[2,288,2304]{2,1,0:T(8,128)(2,1)}, u32[]{:S(2)}, u32[]{:S(2)}) collective-permute-start(bf16[2,288,2304]{2,1,0:T(8,128)(2,1)} %get-tuple-element.369), channel_id=1, source_target_pairs={{0,2},{1,3},{2,0},{3,1},{4,6},{5,7},{6,4},{7,5},{8,10},{9,11},{10,... | collective-permute-start | bytes 7962632 | tf_op jit(solution)/shard_map/ppermute | solution.py:1220
  487.8 9.7 %collective-permute-start.32 = (bf16[2,576,640]{2,1,0:T(8,128)(2,1)}, bf16[2,576,640]{2,1,0:T(8,128)(2,1)S(1)}, u32[]{:S(2)}, u32[]{:S(2)}) collective-permute-start(bf16[2,576,640]{2,1,0:T(8,128)(2,1)} %get-tuple-element.377), channel_id=1, source_target_pairs={{0,2},{1,3},{2,0},{3,1},{4,6},{5,7},{6,4},{7,5},{8,10},{9,11},{10,... | collective-permute-start | bytes 4423688 | tf_op jit(solution)/shard_map/ppermute | solution.py:1220
  488.6 16.6 %collective-permute-start.33 = (bf16[1,512,640]{2,1,0:T(8,128)(2,1)}, bf16[1,512,640]{2,1,0:T(8,128)(2,1)}, u32[]{:S(2)}, u32[]{:S(2)}) collective-permute-start(bf16[1,512,640]{2,1,0:T(8,128)(2,1)} %get-tuple-element.379), channel_id=1, source_target_pairs={{0,1},{1,0},{2,3},{3,2},{4,5},{5,4},{6,7},{7,6},{8,9},{9,8},{10,11... | collective-permute-start | bytes 1966088 | tf_op jit(solution)/shard_map/ppermute | solution.py:1220
  499.6 57.8 %collective-permute-start.34 = (bf16[288,640]{1,0:T(8,128)(2,1)}, bf16[288,640]{1,0:T(8,128)(2,1)S(1)}, u32[]{:S(2)}, u32[]{:S(2)}) collective-permute-start(bf16[288,640]{1,0:T(8,128)(2,1)} %get-tuple-element.384), channel_id=1, source_target_pairs={{0,4},{1,5},{2,6},{3,7},{4,0},{5,1},{6,2},{7,3},{8,12},{9,13},{10,... | collective-permute-start | bytes 1105928 | tf_op jit(solution)/shard_map/ppermute | solution.py:1220
  500.3 57.1 %collective-permute-start.35 = (bf16[288,640]{1,0:T(8,128)(2,1)}, bf16[288,640]{1,0:T(8,128)(2,1)S(1)}, u32[]{:S(2)}, u32[]{:S(2)}) collective-permute-start(bf16[288,640]{1,0:T(8,128)(2,1)} %get-tuple-element.385), channel_id=1, source_target_pairs={{0,1},{1,0},{2,3},{3,2},{4,5},{5,4},{6,7},{7,6},{8,9},{9,8},{10,11... | collective-permute-start | bytes 1105928 | tf_op jit(solution)/shard_map/ppermute | solution.py:1220
  500.4 57.0 %collective-permute-start.36 = (bf16[288,640]{1,0:T(8,128)(2,1)}, bf16[288,640]{1,0:T(8,128)(2,1)S(1)}, u32[]{:S(2)}, u32[]{:S(2)}) collective-permute-start(bf16[288,640]{1,0:T(8,128)(2,1)} %get-tuple-element.386), channel_id=1, source_target_pairs={{0,5},{1,4},{2,7},{3,6},{4,1},{5,0},{6,3},{7,2},{8,13},{9,12},{10,... | collective-permute-start | bytes 1105928 | tf_op jit(solution)/shard_map/ppermute | solution.py:1220
  558.3 83.3 %collective-permute-start.37 = (bf16[1,512,1792]{2,1,0:T(8,128)(2,1)}, bf16[1,512,1792]{2,1,0:T(8,128)(2,1)}, u32[]{:S(2)}, u32[]{:S(2)}) collective-permute-start(bf16[1,512,1792]{2,1,0:T(8,128)(2,1)} %get-tuple-element.404), channel_id=1, source_target_pairs={{0,1},{1,0},{2,3},{3,2},{4,5},{5,4},{6,7},{7,6},{8,9},{9,8},{10,11... | collective-permute-start | bytes 5505032 | tf_op jit(solution)/shard_map/ppermute | solution.py:1220
  559.8 79.9 %collective-permute-start.38 = (bf16[2,72,2304]{2,1,0:T(8,128)(2,1)}, bf16[2,72,2304]{2,1,0:T(8,128)(2,1)S(1)}, u32[]{:S(2)}, u32[]{:S(2)}) collective-permute-start(bf16[2,72,2304]{2,1,0:T(8,128)(2,1)} %get-tuple-element.405), channel_id=1, source_target_pairs={{0,8},{1,9},{2,10},{3,11},{4,12},{5,13},{6,14},{7,15},{8,16},{9,17... | collective-permute-start | bytes 1990664 | tf_op jit(solution)/shard_map/ppermute | solution.py:1220
  560.8 80.8 %collective-permute-start.39 = (bf16[2,72,2304]{2,1,0:T(8,128)(2,1)}, bf16[2,72,2304]{2,1,0:T(8,128)(2,1)S(1)}, u32[]{:S(2)}, u32[]{:S(2)}) collective-permute-start(bf16[2,72,2304]{2,1,0:T(8,128)(2,1)} %get-tuple-element.406), channel_id=1, source_target_pairs={{0,16},{1,17},{2,18},{3,19},{4,20},{5,21},{6,22},{7,23},{8,24},{9,... | collective-permute-start | bytes 1990664 | tf_op jit(solution)/shard_map/ppermute | solution.py:1220
  565.9 75.7 %collective-permute-start.40 = (bf16[2,72,2304]{2,1,0:T(8,128)(2,1)}, bf16[2,72,2304]{2,1,0:T(8,128)(2,1)S(1)}, u32[]{:S(2)}, u32[]{:S(2)}) collective-permute-start(bf16[2,72,2304]{2,1,0:T(8,128)(2,1)} %get-tuple-element.407), channel_id=1, source_target_pairs={{0,24},{1,25},{2,26},{3,27},{4,28},{5,29},{6,30},{7,31},{8,0},{9,1... | collective-permute-start | bytes 1990664 | tf_op jit(solution)/shard_map/ppermute | solution.py:1220
  565.9 90.1 %collective-permute-start.41 = (bf16[72,640]{1,0:T(8,128)(2,1)S(1)}, bf16[72,640]{1,0:T(8,128)(2,1)S(1)}, u32[]{:S(2)}, u32[]{:S(2)}) collective-permute-start(bf16[72,640]{1,0:T(8,128)(2,1)S(1)} %get-tuple-element.417), channel_id=1, source_target_pairs={{0,8},{1,9},{2,10},{3,11},{4,12},{5,13},{6,14},{7,15},{8,16},{9,17... | collective-permute-start | bytes 276488 | tf_op jit(solution)/shard_map/ppermute | solution.py:1220
  639.7 16.3 %collective-permute-start.42 = (bf16[72,640]{1,0:T(8,128)(2,1)S(1)}, bf16[72,640]{1,0:T(8,128)(2,1)S(1)}, u32[]{:S(2)}, u32[]{:S(2)}) collective-permute-start(bf16[72,640]{1,0:T(8,128)(2,1)S(1)} %get-tuple-element.418), channel_id=1, source_target_pairs={{0,16},{1,17},{2,18},{3,19},{4,20},{5,21},{6,22},{7,23},{8,24},{9,... | collective-permute-start | bytes 276488 | tf_op jit(solution)/shard_map/ppermute | solution.py:1220
  641.6 14.4 %collective-permute-start.43 = (bf16[72,640]{1,0:T(8,128)(2,1)S(1)}, bf16[72,640]{1,0:T(8,128)(2,1)S(1)}, u32[]{:S(2)}, u32[]{:S(2)}) collective-permute-start(bf16[72,640]{1,0:T(8,128)(2,1)S(1)} %get-tuple-element.419), channel_id=1, source_target_pairs={{0,24},{1,25},{2,26},{3,27},{4,28},{5,29},{6,30},{7,31},{8,0},{9,1... | collective-permute-start | bytes 276488 | tf_op jit(solution)/shard_map/ppermute | solution.py:1220
  656.6 21.0 %collective-permute-start.44 = (bf16[576,1792]{1,0:T(8,128)(2,1)}, bf16[576,1792]{1,0:T(8,128)(2,1)S(1)}, u32[]{:S(2)}, u32[]{:S(2)}) collective-permute-start(bf16[576,1792]{1,0:T(8,128)(2,1)} %get-tuple-element.425), channel_id=1, source_target_pairs={{0,2},{1,3},{2,0},{3,1},{4,6},{5,7},{6,4},{7,5},{8,10},{9,11},{10,... | collective-permute-start | bytes 6193160 | tf_op jit(solution)/shard_map/ppermute | solution.py:1220
  677.6 5.9 collective-permute-start.45
  686.1 46.0 %copy-start.21 = (f32[4,8,1152]{2,1,0:T(8,128)S(1)}, f32[4,8,1152]{2,1,0:T(8,128)}, u32[]{:S(2)}) copy-start(f32[4,8,1152]{2,1,0:T(8,128)} %get-tuple-element.438) | copy-start | bytes 442372
  686.1 34.5 %collective-permute-start.46 = (bf16[288,1792]{1,0:T(8,128)(2,1)S(1)}, bf16[288,1792]{1,0:T(8,128)(2,1)S(1)}, u32[]{:S(2)}, u32[]{:S(2)}) collective-permute-start(bf16[288,1792]{1,0:T(8,128)(2,1)S(1)} %get-tuple-element.433), channel_id=1, source_target_pairs={{0,4},{1,5},{2,6},{3,7},{4,0},{5,1},{6,2},{7,3},{8,12},{9,13},{10,... | collective-permute-start | bytes 3096584 | tf_op jit(solution)/shard_map/ppermute | solution.py:1220
  687.0 33.6 %collective-permute-start.47 = (bf16[288,1792]{1,0:T(8,128)(2,1)S(1)}, bf16[288,1792]{1,0:T(8,128)(2,1)}, u32[]{:S(2)}, u32[]{:S(2)}) collective-permute-start(bf16[288,1792]{1,0:T(8,128)(2,1)S(1)} %get-tuple-element.434), channel_id=1, source_target_pairs={{0,1},{1,0},{2,3},{3,2},{4,5},{5,4},{6,7},{7,6},{8,9},{9,8},{10,11... | collective-permute-start | bytes 3096584 | tf_op jit(solution)/shard_map/ppermute | solution.py:1220
  687.0 45.1 %collective-permute-start.48 = (bf16[288,1792]{1,0:T(8,128)(2,1)S(1)}, bf16[288,1792]{1,0:T(8,128)(2,1)}, u32[]{:S(2)}, u32[]{:S(2)}) collective-permute-start(bf16[288,1792]{1,0:T(8,128)(2,1)S(1)} %get-tuple-element.435), channel_id=1, source_target_pairs={{0,5},{1,4},{2,7},{3,6},{4,1},{5,0},{6,3},{7,2},{8,13},{9,12},{10,... | collective-permute-start | bytes 3096584 | tf_op jit(solution)/shard_map/ppermute | solution.py:1220
  733.2 3.8 collective-permute-start.49
  737.1 21.0 %collective-permute-start.50 = (f32[8,4096]{1,0:T(8,128)S(1)}, f32[8,4096]{1,0:T(8,128)S(1)}, u32[]{:S(2)}, u32[]{:S(2)}) collective-permute-start(f32[8,4096]{1,0:T(8,128)S(1)} %add.244), channel_id=1, source_target_pairs={{0,8},{1,9},{2,10},{3,11},{4,12},{5,13},{6,14},{7,15},{8,16},{9,17... | collective-permute-start | bytes 393224 | tf_op jit(solution)/shard_map/ppermute | solution.py:1220
  738.6 19.4 %collective-permute-start.51 = (f32[8,4096]{1,0:T(8,128)S(1)}, f32[8,4096]{1,0:T(8,128)S(1)}, u32[]{:S(2)}, u32[]{:S(2)}) collective-permute-start(f32[8,4096]{1,0:T(8,128)S(1)} %add.244), channel_id=1, source_target_pairs={{0,16},{1,17},{2,18},{3,19},{4,20},{5,21},{6,22},{7,23},{8,24},{9,... | collective-permute-start | bytes 393224 | tf_op jit(solution)/shard_map/ppermute | solution.py:1220
  741.3 16.8 %collective-permute-start.52 = (f32[8,4096]{1,0:T(8,128)S(1)}, f32[8,4096]{1,0:T(8,128)S(1)}, u32[]{:S(2)}, u32[]{:S(2)}) collective-permute-start(f32[8,4096]{1,0:T(8,128)S(1)} %add.244), channel_id=1, source_target_pairs={{0,24},{1,25},{2,26},{3,27},{4,28},{5,29},{6,30},{7,31},{8,0},{9,1... | collective-permute-start | bytes 393224 | tf_op jit(solution)/shard_map/ppermute | solution.py:1220
  758.1 26.9 %collective-permute-start.54 = (f32[32,4096]{1,0:T(8,128)S(1)}, f32[32,4096]{1,0:T(8,128)S(1)}, u32[]{:S(2)}, u32[]{:S(2)}) collective-permute-start(f32[32,4096]{1,0:T(8,128)S(1)} %pad_maximum_fusion.6), channel_id=1, source_target_pairs={{0,4},{1,5},{2,6},{3,7},{4,0},{5,1},{6,2},{7,3},{8,12},{9,13},{10,... | collective-permute-start | bytes 1572872 | tf_op jit(solution)/shard_map/ppermute | solution.py:1220
  759.7 6.4 collective-permute-start.55
  761.2 19.8 %collective-permute-start.56 = (bf16[72,1792]{1,0:T(8,128)(2,1)S(1)}, bf16[72,1792]{1,0:T(8,128)(2,1)S(1)}, u32[]{:S(2)}, u32[]{:S(2)}) collective-permute-start(bf16[72,1792]{1,0:T(8,128)(2,1)S(1)} %get-tuple-element.459), channel_id=1, source_target_pairs={{0,16},{1,17},{2,18},{3,19},{4,20},{5,21},{6,22},{7,23},{8,24},{9,... | collective-permute-start | bytes 774152 | tf_op jit(solution)/shard_map/ppermute | solution.py:1220
  763.0 22.1 %collective-permute-start.57 = (bf16[72,1792]{1,0:T(8,128)(2,1)S(1)}, bf16[72,1792]{1,0:T(8,128)(2,1)S(1)}, u32[]{:S(2)}, u32[]{:S(2)}) collective-permute-start(bf16[72,1792]{1,0:T(8,128)(2,1)S(1)} %get-tuple-element.460), channel_id=1, source_target_pairs={{0,24},{1,25},{2,26},{3,27},{4,28},{5,29},{6,30},{7,31},{8,0},{9,1... | collective-permute-start | bytes 774152 | tf_op jit(solution)/shard_map/ppermute | solution.py:1220
  763.0 3.1 collective-permute-start.53
  764.3 23.0 %copy-start.18 = (bf16[8,1152]{1,0:T(8,128)(2,1)S(1)}, bf16[8,1152]{1,0:T(8,128)(2,1)}, u32[]{:S(2)}) copy-start(bf16[8,1152]{1,0:T(8,128)(2,1)} %param.20) | copy-start | bytes 55300
  785.1 3.5 collective-permute-start.58
  (43 other events, 346.7 us)
Sparse Core Ops, SparseCore 0:
  64.6 167.8 all-gather.1

commit v6 on v4

--- a/solution.py
+++ b/solution.py
@@ -1419,7 +1419,7 @@
 
         flat_turned = lambda values: values.reshape(width, rows)
         hidden_one_turned = flat_turned(hidden_one_turned)
-        feed_args = (flat_turned(hidden_two_turned), flat_turned(grad_two_turned), feed_weights, up_bias, third, 768)
+        feed_args = (flat_turned(hidden_two_turned), flat_turned(grad_two_turned), feed_weights, up_bias, rows // 2, 768)
         two_b, back_b, mine_b, near_b, far_b, grad_b_up_b = feed(
             1 - y.reshape(1), hidden_two, grad_two, *feed_args
         )
@@ -1452,13 +1452,17 @@
         )
         grad_own, feed_kept, *joined = after(grad_own, feed_kept, *feed_sent, *out_pieces)
         feed_sent, out_pieces = joined[: levels - 1], joined[levels - 1 :]
-        grad_qkv_own, grad_qkv_theirs = attend_back(
-            *qkv_half, grad_own, grad_other, *lse_half, *marks_half
-        )
-        grad_first, grad_qkv_theirs, feed_kept, *joined = after(
-            grad_first, grad_qkv_theirs, feed_kept, *feed_sent, *out_pieces
-        )
-        feed_sent, out_pieces = joined[: levels - 1], joined[levels - 1 :]
+        grad_qkv_own, grad_qkv_theirs, *got = after(
+            *attend_back(*qkv_half, grad_own, grad_other, *lse_half, *marks_half),
+            send(out_pieces[1], to_x),
+            send(out_pieces[2], to_heads),
+            send(out_pieces[3], to_corner),
+        )
+        out_kept, *out_sent = level_pieces(all_added(out_pieces[0], got))
+        grad_first, grad_qkv_theirs, feed_kept, out_kept, *joined = after(
+            grad_first, grad_qkv_theirs, feed_kept, out_kept, *feed_sent, *out_sent
+        )
+        feed_sent, out_sent = joined[: levels - 1], joined[levels - 1 :]
         grad_qkv_first, grad_qkv_second, grad_qkv_other, *got = after(
             *attend_back(*qkv_full, grad_first, grad_second, *lse_full, *marks_full),
             send(grad_qkv_theirs, to_heads),
@@ -1467,20 +1471,14 @@
         grad_w_up, grad_w_down = all_added(feed_kept, got)
         qkv_mine_b, qkv_theirs_b, grad_qkv_bias_b, *got = after(
             *outer(hidden_one_turned, grad_qkv_first, grad_qkv_second, grad_qkv_other, 1),
-            send(out_pieces[1], to_x),
-            send(out_pieces[2], to_heads),
-            send(out_pieces[3], to_corner),
-        )
-        out_kept, *out_sent = level_pieces(all_added(out_pieces[0], got))
-        hidden_one_turned, qkv_theirs_b, out_kept, *out_sent = after(
-            hidden_one_turned, qkv_theirs_b, out_kept, *out_sent
-        )
-        qkv_mine_a, qkv_theirs_a, grad_qkv_bias_a, qkv_got_b, *got = after(
+            *(send(part, to_level[k + 1]) for k, part in enumerate(out_sent)),
+        )
+        grad_w_out = all_added(out_kept, got)
+        hidden_one_turned, qkv_theirs_b = after(hidden_one_turned, qkv_theirs_b)
+        qkv_mine_a, qkv_theirs_a, grad_qkv_bias_a, qkv_got_b = after(
             *outer(hidden_one_turned, grad_qkv_first, grad_qkv_second, grad_qkv_own, 0),
             send(qkv_theirs_b, to_core),
-            *(send(part, to_level[k + 1]) for k, part in enumerate(out_sent)),
-        )
-        grad_w_out = all_added(out_kept, got)
+        )
         near, *sent = plane_pieces(qkv_mine_a, send(qkv_theirs_a, to_core), qkv_mine_b, qkv_got_b)
         grad_middle, near, *sent = after(grad_middle, near, *sent)
         grad_qkv = (grad_qkv_first, grad_qkv_second, grad_qkv_own, grad_qkv_other)

time: 795 us -> 788 us (level)
  transfers between devices with their start and end apart: 60 -> 60, of which waited for: 23 -> 21; matrix products, arithmetic and copies ran while one was open for 9% -> 9% of each run, Pallas kernels for 47% -> 54%
where the time goes in v6:
time: 788 us; the launch traced here: 780 us
  Pallas kernels  493 us (63%)
  waiting for transfers between devices  98.8 us (13%)
  starting transfers between devices  64.6 us (8%)
  other arithmetic  45.5 us (6%)
  matrix products  36.3 us (5%)
  local copies, waits for them, and re-layouts  26.5 us (3%)
  between operations  15.2 us (2%)
    pallas_call x2, Pallas kernels, feed(): pl.pallas_call(partial(feed_kernel, chunk), grid_spec=pltpu.PrefetchScala...  140 us
    pallas_call x2, Pallas kernels, attend_back(): pl.pallas_call(partial(attend_back_kernel, heads), grid=(groups, 2), in_s...  125 us
    ppermute x59, waiting for transfers between devices, send(): return lax.ppermute(values, both, pairs)  98.7 us
    ppermute x59, starting transfers between devices, send(): return lax.ppermute(values, both, pairs)  64.6 us
    pallas_call x2, Pallas kernels, attend(): pl.pallas_call(partial(attend_kernel, heads), grid=(groups, 2), in_specs=...  61.8 us
    pallas_call x1, Pallas kernels, back_two(): pl.pallas_call(back_two_kernel, grid_spec=pltpu.PrefetchScalarGridSpec(nu...  47.9 us
    pallas_call x1, Pallas kernels, back_one(): pl.pallas_call(back_one_kernel, grid_spec=pltpu.PrefetchScalarGridSpec(nu...  31.8 us
    pallas_call x2, Pallas kernels, outer(): pl.pallas_call(outer_kernel, grid=(2,), in_specs=[pl.BlockSpec((width //...  28.1 us
  transfers between devices with their start and end apart: 60, of which 21 were waited for; matrix products, arithmetic and copies ran while one was open for 9% of the time, Pallas kernels for 54%

profile of v6, /device:TPU:9, one launch (start us, length us, event | category | flops | bytes accessed | tf_op | source)
XLA Modules:
  0.0 780.3 jit_solution(2597577625787872014)
XLA Ops:
  10.5 1.4 collective-permute-start.1
  15.1 11.3 %convolution_add_fusion = f32[8,3456]{1,0:T(8,128)S(1)} fusion(f32[1152,3456]{1,0:T(8,128)} %param.24, f32[3456]{0:T(1024)S(1)} %copy-done.29, bf16[8,1152]{1,0:T(8,128)(2,1)S(1)} %copy-done.18), kind=kOutput, calls=%fused_computation.4 | convolution fusion | flops 382279680 | bytes 16068096 | tf_op jit(solution)/shard_map/dot_general | solution.py:1321
  28.7 3.3 collective-permute-start.3
  37.4 3.4 collective-permute-start.6
  41.7 9.0 %shard_map.307 = (bf16[1024,1152]{1,0:T(8,128)(2,1)}, bf16[512,1152]{1,0:T(8,128)(2,1)}, bf16[16,72,1536]{2,1,0:T(8,128)(2,1)}) custom-call(s32[33]{0:T(128)} %pad_add_fusion.2.side, bf16[1536,1152]{1,0:T(8,128)(2,1)} %tok_ref.7, bf16[1536,24]{1,0:T(8,128)(2,1)} %compare_convert_fusion.hot_ref, bf16[2,24,3456]{2,1,0:T(8,128)(2,1)} %pad_maximum_fusion.8.parts_ref), custom_call_target="tpu_custom_call" | custom-call | flops 5888802816 | bytes 10616832 | tf_op jit(solution)/shard_map/pallas_call | solution.py:462
  52.0 1.4 concatenate.122.bias_ref
  56.0 1.6 collective-permute-start.9
  58.6 5.1 collective-permute-done.7
  68.7 1.7 collective-permute-start.12
  70.4 6.2 collective-permute-done.12
  76.6 7.1 collective-permute-done.11
  83.7 4.2 collective-permute-done.10
  88.0 7.2 collective-permute-start.17
  96.3 3.6 collective-permute-done.15
  104.8 3.4 shard_map.308
  108.2 4.1 copy-done
  112.3 15.2 %shard_map.309 = (bf16[2,512,1792]{2,1,0:T(8,128)(2,1)}, bf16[2,512,1792]{2,1,0:T(8,128)(2,1)}) custom-call(s32[33]{0:T(128)} %pad_add_fusion.2.side, bf16[1024,1152]{1,0:T(8,128)(2,1)} %get-tuple-element.271.first_in.second_in, bf16[1024,1152]{1,0:T(8,128)(2,1)} %get-tuple-element.271.first_in.second_in, bf16[2,1152,2304]{2,1,0:T(8,128)(2,1)} %bitcast.134, ...), custom_call_target="tpu_custom_call" | custom-call | flops 8455716864 | bytes 23855104 | tf_op jit(solution)/shard_map/pallas_call | solution.py:501
  127.6 12.9 %collective-permute-done.18.second_in = bf16[512,1152]{1,0:T(8,128)(2,1)S(1)} collective-permute-done((bf16[512,1152]{1,0:T(8,128)(2,1)S(1)}, bf16[512,1152]{1,0:T(8,128)(2,1)S(1)}, u32[]{:S(2)}, u32[]{:S(2)}) %collective-permute-start.18) | collective-permute-done | bytes 1179680 | tf_op jit(solution)/shard_map/ppermute | solution.py:1196
  141.5 10.2 %shard_map.310 = (bf16[1,512,1792]{2,1,0:T(8,128)(2,1)}, bf16[1,512,1792]{2,1,0:T(8,128)(2,1)}) custom-call(s32[33]{0:T(128)} %pad_add_fusion.2.side, bf16[512,1152]{1,0:T(8,128)(2,1)} %get-tuple-element.280.first_in, bf16[512,1152]{1,0:T(8,128)(2,1)} %copy-done.41, bf16[2,1152,2304]{2,1,0:T(8,128)(2,1)} %bitcast.135, f32[2,1,1728]{2,1,0:T(1,128)} %concatenate.122.bias_ref), custom_call_target="tpu_custom_call" | custom-call | flops 4227858432 | bytes 11927552 | tf_op jit(solution)/shard_map/pallas_call | solution.py:501
  153.0 3.1 collective-permute-start.20
  157.3 21.8 %shard_map.311 = (bf16[1,512,640]{2,1,0:T(8,128)(2,1)}, bf16[1,512,640]{2,1,0:T(8,128)(2,1)}, f32[1,8,512]{2,1,0:T(8,128)}, f32[1,8,512]{2,1,0:T(8,128)}) custom-call(bf16[1,512,1792]{2,1,0:T(8,128)(2,1)} %get-tuple-element.285.first, bf16[1,512,1792]{2,1,0:T(8,128)(2,1)} %get-tuple-element.286.second, bf16[1024,16]{1,0:T(8,128)(2,1)} %copy-done.3, ...), custom_call_target="tpu_custom_call" | custom-call | flops 15000000512 | bytes 5505024 | tf_op jit(solution)/shard_map/pallas_call | solution.py:637
  179.6 40.0 %shard_map.312 = (bf16[2,512,640]{2,1,0:T(8,128)(2,1)}, bf16[2,512,640]{2,1,0:T(8,128)(2,1)}, f32[2,8,512]{2,1,0:T(8,128)}, f32[2,8,512]{2,1,0:T(8,128)}) custom-call(bf16[2,512,1792]{2,1,0:T(8,128)(2,1)} %get-tuple-element.298.first, bf16[2,512,1792]{2,1,0:T(8,128)(2,1)} %get-tuple-element.299.second, bf16[1024,16]{1,0:T(8,128)(2,1)} %copy-done.1, ...), custom_call_target="tpu_custom_call" | custom-call | flops 30000001024 | bytes 11010048 | tf_op jit(solution)/shard_map/pallas_call | solution.py:637
  219.6 2.4 collective-permute-start.24
  222.0 21.5 %shard_map.313 = (f32[1536,1152]{1,0:T(8,128)}, bf16[1536,1152]{1,0:T(8,128)(2,1)}, bf16[1536,1152]{1,0:T(8,128)(2,1)}, bf16[16,72,1536]{2,1,0:T(8,128)(2,1)}, b...) custom-call(s32[33]{0:T(128)} %pad_add_fusion.2.side, bf16[1536,1152]{1,0:T(8,128)(2,1)} %tok_ref.7, ...), custom_call_target="tpu_custom_call" | custom-call | flops 15854469120 | bytes 38928384 | tf_op jit(solution)/shard_map/pallas_call | solution.py:839
  244.2 69.5 %shard_map.314 = (f32[1536,1152]{1,0:T(8,128)}, f32[1536,1152]{1,0:T(8,128)}, f32[2,576,2304]{2,1,0:T(8,128)}, bf16[2,288,2304]{2,1,0:T(8,128)(2,1)}, bf16[2,288,2304]{2,1,0:T(8,128)(2,1)}, /*index=5*/f32[1,2304]{1,0:T(1,128)}) custom-call(s32[1]{0:T(128)S(6)} %sub.46.pick, bf16[1536,1152]{1,0:T(8,128)(2,1)} %get-tuple-element.331.h_ref, ...), custom_call_target="tpu_custom_call" | custom-call | flops 48922361856 | bytes 54853632 | tf_op jit(solution)/shard_map/pallas_call | solution.py:919
  314.5 4.8 collective-permute-done.25
  319.3 4.6 add_convert_fusion.2
  325.3 70.1 %shard_map.315 = (f32[1536,1152]{1,0:T(8,128)}, f32[1536,1152]{1,0:T(8,128)}, f32[2,576,2304]{2,1,0:T(8,128)}, bf16[2,288,2304]{2,1,0:T(8,128)(2,1)}, bf16[2,288,2304]{2,1,0:T(8,128)(2,1)}, /*index=5*/f32[1,2304]{1,0:T(1,128)}) custom-call(s32[1]{0:T(128)} %bitcast.10.pick, bf16[1536,1152]{1,0:T(8,128)(2,1)} %get-tuple-element.331.h_ref, ...), custom_call_target="tpu_custom_call" | custom-call | flops 48922361856 | bytes 54853632 | tf_op jit(solution)/shard_map/pallas_call | solution.py:919
  396.0 5.7 add_convert_fusion.1
  401.7 1.5 copy-done.5
  403.2 2.1 add_convert_fusion
  405.3 1.6 collective-permute-start.29
  408.4 47.9 %shard_map.316 = (bf16[1536,1152]{1,0:T(8,128)(2,1)}, f32[1536,1152]{1,0:T(8,128)}, bf16[2,512,640]{2,1,0:T(8,128)(2,1)}, bf16[2,512,640]{2,1,0:T(8,128)(2,1)}, ...) custom-call(s32[33]{0:T(128)} %pad_add_fusion.2.side, ...), custom_call_target="tpu_custom_call" | custom-call | flops 19931332608 | bytes 60162048 | tf_op jit(solution)/shard_map/pallas_call | solution.py:1042
  456.3 8.8 %collective-permute-done.29 = bf16[2,288,2304]{2,1,0:T(8,128)(2,1)} collective-permute-done((bf16[2,288,2304]{2,1,0:T(8,128)(2,1)}, bf16[2,288,2304]{2,1,0:T(8,128)(2,1)}, u32[]{:S(2)}, u32[]{:S(2)}) %collective-permute-start.29) | collective-permute-done | bytes 2654240 | tf_op jit(solution)/shard_map/ppermute | solution.py:1196
  467.2 6.0 fusion.59
  473.3 1.4 fusion.60
  479.6 4.3 collective-permute-done.33.do_second
  483.9 52.2 %shard_map.317 = (bf16[1,512,1792]{2,1,0:T(8,128)(2,1)}, bf16[1,512,1792]{2,1,0:T(8,128)(2,1)}) custom-call(bf16[1,512,1792]{2,1,0:T(8,128)(2,1)} %get-tuple-element.285.first, bf16[1,512,1792]{2,1,0:T(8,128)(2,1)} %get-tuple-element.286.second, bf16[1,512,640]{2,1,0:T(8,128)(2,1)} %get-tuple-element.372.do_first, ...), custom_call_target="tpu_custom_call" | custom-call | flops 12000000000 | bytes 11010048 | tf_op jit(solution)/shard_map/pallas_call | solution.py:739
  537.3 1.9 collective-permute-start.39
  539.1 1.5 collective-permute-start.41
  540.6 72.3 %shard_map.318 = (bf16[2,512,1792]{2,1,0:T(8,128)(2,1)}, bf16[2,512,1792]{2,1,0:T(8,128)(2,1)}) custom-call(bf16[2,512,1792]{2,1,0:T(8,128)(2,1)} %get-tuple-element.298.first, bf16[2,512,1792]{2,1,0:T(8,128)(2,1)} %get-tuple-element.299.second, bf16[2,512,640]{2,1,0:T(8,128)(2,1)} %get-tuple-element.390.do_first, ...), custom_call_target="tpu_custom_call" | custom-call | flops 24000000000 | bytes 22020096 | tf_op jit(solution)/shard_map/pallas_call | solution.py:739
  613.0 2.3 collective-permute-start.42
  615.4 14.3 %shard_map.319 = (f32[576,1792]{1,0:T(8,128)}, bf16[576,1792]{1,0:T(8,128)(2,1)}, f32[1,1792]{1,0:T(1,128)}) custom-call(bf16[1152,1536]{1,0:T(8,128)(2,1)} %bitcast.172, bf16[2,512,1792]{2,1,0:T(8,128)(2,1)} %get-tuple-element.400.first, bf16[2,512,1792]{2,1,0:T(8,128)(2,1)} %get-tuple-element.401.second, ...), custom_call_target="tpu_custom_call" | custom-call | flops 6341787648 | bytes 14548992 | tf_op jit(solution)/shard_map/pallas_call | solution.py:1112
  630.4 2.9 collective-permute-start.44
  633.4 2.0 reduce-precision_convert_fusion.1
  638.0 13.8 %shard_map.320 = (f32[576,1792]{1,0:T(8,128)}, bf16[576,1792]{1,0:T(8,128)(2,1)}, f32[1,1792]{1,0:T(1,128)}) custom-call(bf16[1152,1536]{1,0:T(8,128)(2,1)} %bitcast.173, bf16[2,512,1792]{2,1,0:T(8,128)(2,1)} %get-tuple-element.400.first, bf16[2,512,1792]{2,1,0:T(8,128)(2,1)} %get-tuple-element.401.second, bf16[1,512,1792]{2,1,0:T(8,128)(2,1)} %get-tuple-element.402.rest.own), custom_call_target="tpu_custom_call" | custom-call | flops 6341787648 | bytes 14548992 | tf_op jit(solution)/shard_map/pallas_call | solution.py:1112
  651.9 1.8 convert_add_fusion.3
  655.0 2.8 add_convert_fusion.3
  658.4 1.9 add_convert_fusion.5
  660.4 1.4 collective-permute-start.47
  663.0 31.8 %shard_map.321 = (f32[1536,1152]{1,0:T(8,128)}, f32[2,8,1152]{2,1,0:T(8,128)}) custom-call(s32[33]{0:T(128)} %pad_add_fusion.2.side, bf16[2,512,1792]{2,1,0:T(8,128)(2,1)} %get-tuple-element.400.first, bf16[2,512,1792]{2,1,0:T(8,128)(2,1)} %get-tuple-element.401.second, bf16[1,512,1792]{2,1,0:T(8,128)(2,1)} %get-tuple-element.402.rest.own, ...), custom_call_target="tpu_custom_call" | custom-call | flops 12683575296 | bytes 28704768 | tf_op jit(solution)/shard_map/pallas_call | solution.py:1150
  694.8 12.8 %collective-permute-done.48 = bf16[288,1792]{1,0:T(8,128)(2,1)} collective-permute-done((bf16[288,1792]{1,0:T(8,128)(2,1)S(1)}, bf16[288,1792]{1,0:T(8,128)(2,1)}, u32[]{:S(2)}, u32[]{:S(2)}) %collective-permute-start.48) | collective-permute-done | bytes 1032224 | tf_op jit(solution)/shard_map/ppermute | solution.py:1196
  708.8 2.0 fusion.57
  710.9 1.5 collective-permute-done.49
  712.5 1.6 collective-permute-start.50
  714.1 1.6 collective-permute-start.51
  715.7 16.8 %fusion.25 = f32[8,1152]{1,0:T(8,128)S(1)} fusion(f32[1152,3456]{1,0:T(8,128)} %param.24, f32[8,4096]{1,0:T(8,128)S(1)} %add.244), kind=kOutput, calls=%fused_computation.79 | convolution fusion | flops 382205952 | bytes 16072704 | tf_op jit(solution)/shard_map/dot_general | solution.py:1511
  733.6 1.5 collective-permute-start.55
  735.0 2.4 collective-permute-start.56
  738.8 1.7 collective-permute-done.53
  740.5 14.1 %collective-permute-done.56 = bf16[72,1792]{1,0:T(8,128)(2,1)S(1)} collective-permute-done((bf16[72,1792]{1,0:T(8,128)(2,1)S(1)}, bf16[72,1792]{1,0:T(8,128)(2,1)S(1)}, u32[]{:S(2)}, u32[]{:S(2)}) %collective-permute-start.56) | collective-permute-done | bytes 258080 | tf_op jit(solution)/shard_map/ppermute | solution.py:1196
  754.6 4.3 collective-permute-done.57
  759.0 1.5 collective-permute-start.58
  765.1 8.2 %fusion = f32[1152,3456]{1,0:T(8,128)} fusion(bf16[128,3456]{1,0:T(8,128)(2,1)S(1)} %get-tuple-element.497, bf16[128,3456]{1,0:T(8,128)(2,1)S(1)} %get-tuple-element.496, bf16[128,1152]{1,0:T(8,128)(2,1)S(1)} %copy-done.9, bf16[128,1152]{1,0:T(8,128)(2,1)S(1)} %copy-done.8), kind=kOutput, calls=%fused_computation.5 | convolution fusion | flops 3068264448 | bytes 18284544 | tf_op jit(solution)/shard_map/dot_general | solution.py:40
  (266 shorter events, 62.8 us)
Async XLA Ops:
  7.2 237.0 %all-gather.2.cloned.1.call-start = ((), (), s32[]{:S(2)}) async-start(), calls=%async_computation | async-start | bytes 21897216 | tf_op jit(solution)/shard_map/all_gather | solution.py:1355
  9.4 17.2 %collective-permute-start = (bf16[1,72,1536]{2,1,0:T(8,128)(2,1)S(1)}, bf16[1,72,1536]{2,1,0:T(8,128)(2,1)S(1)}, u32[]{:S(2)}, u32[]{:S(2)}) collective-permute-start(bf16[1,72,1536]{2,1,0:T(8,128)(2,1)S(1)} %get-tuple-element.527), channel_id=1, source_target_pairs={{0,24},{1,25},{2,26},{3,27},{4,28},{5,29},{6,30},{7,31},{8,0},{9,1... | collective-permute-start | bytes 663560 | tf_op jit(solution)/shard_map/ppermute | solution.py:1196
  10.5 16.1 %collective-permute-start.1 = (bf16[1,72,768]{2,1,0:T(8,128)(2,1)S(1)}, bf16[1,72,768]{2,1,0:T(8,128)(2,1)S(1)}, u32[]{:S(2)}, u32[]{:S(2)}) collective-permute-start(bf16[1,72,768]{2,1,0:T(8,128)(2,1)S(1)} %pad_maximum_fusion.12), channel_id=1, source_target_pairs={{0,4},{1,5},{2,6},{3,7},{4,0},{5,1},{6,2},{7,3},{8,12},{9,13},{10,... | collective-permute-start | bytes 331784 | tf_op jit(solution)/shard_map/ppermute | solution.py:1196
  26.7 10.5 %collective-permute-start.4 = (bf16[2,1,72,768]{3,2,0,1:T(8,128)(2,1)S(1)}, bf16[2,1,72,768]{3,2,0,1:T(8,128)(2,1)S(1)}, u32[]{:S(2)}, u32[]{:S(2)}) collective-permute-start(bf16[2,1,72,768]{3,2,0,1:T(8,128)(2,1)S(1)} %get-tuple-element.531), channel_id=1, source_target_pairs={{0,1},{1,0},{2,3},{3,2},{4,5},{5,4},{6,7},{7,6},{8,9},{9,8},{10,11... | collective-permute-start | bytes 663560 | tf_op jit(solution)/shard_map/ppermute | solution.py:1196
  28.4 8.8 %collective-permute-start.2 = (f32[9,3456]{1,0:T(8,128)S(1)}, f32[9,3456]{1,0:T(8,128)S(1)}, u32[]{:S(2)}, u32[]{:S(2)}) collective-permute-start(f32[9,3456]{1,0:T(8,128)S(1)} %dynamic-update-slice.4), channel_id=1, source_target_pairs={{0,1},{1,0},{2,3},{3,2},{4,5},{5,4},{6,7},{7,6},{8,9},{9,8},{10,11... | collective-permute-start | bytes 373256 | tf_op jit(solution)/shard_map/ppermute | solution.py:1196
  28.7 8.5 %collective-permute-start.3 = (bf16[1,72,1536]{2,1,0:T(8,128)(2,1)S(1)}, bf16[1,72,1536]{2,1,0:T(8,128)(2,1)S(1)}, u32[]{:S(2)}, u32[]{:S(2)}) collective-permute-start(bf16[1,72,1536]{2,1,0:T(8,128)(2,1)S(1)} %collective-permute-done), channel_id=1, source_target_pairs={{0,24},{1,25},{2,26},{3,27},{4,28},{5,29},{6,30},{7,31},{8,0},{9,1... | collective-permute-start | bytes 663560 | tf_op jit(solution)/shard_map/ppermute | solution.py:1196
  37.4 16.0 %collective-permute-start.6 = (bf16[2,2,1,72,768]{4,3,1,0,2:T(8,128)(2,1)S(1)}, bf16[2,2,1,72,768]{4,3,1,0,2:T(8,128)(2,1)S(1)}, u32[]{:S(2)}, u32[]{:S(2)}) collective-permute-start(bf16[2,2,1,72,768]{4,3,1,0,2:T(8,128)(2,1)S(1)} %get-tuple-element.515), channel_id=1, source_target_pairs={{0,24},{1,25},{2,26},{3,27},{4,28},{5,29},{6,30},{7,31},{8,0},{9,1... | collective-permute-start | bytes 1327112 | tf_op jit(solution)/shard_map/ppermute | solution.py:1196
  40.7 12.6 %collective-permute-start.5 = (bf16[1,72,1536]{2,1,0:T(8,128)(2,1)S(1)}, bf16[1,72,1536]{2,1,0:T(8,128)(2,1)S(1)}, u32[]{:S(2)}, u32[]{:S(2)}) collective-permute-start(bf16[1,72,1536]{2,1,0:T(8,128)(2,1)S(1)} %collective-permute-done.3), channel_id=1, source_target_pairs={{0,24},{1,25},{2,26},{3,27},{4,28},{5,29},{6,30},{7,31},{8,0},{9,1... | collective-permute-start | bytes 663560 | tf_op jit(solution)/shard_map/ppermute | solution.py:1196
  54.5 9.3 %collective-permute-start.7 = (bf16[4,1,72,768]{3,2,0,1:T(8,128)(2,1)}, bf16[4,1,72,768]{3,2,0,1:T(8,128)(2,1)}, u32[]{:S(2)}, u32[]{:S(2)}) collective-permute-start(bf16[4,1,72,768]{3,2,0,1:T(8,128)(2,1)} %get-tuple-element.510), channel_id=1, source_target_pairs={{0,4},{1,5},{2,6},{3,7},{4,0},{5,1},{6,2},{7,3},{8,12},{9,13},{10,... | collective-permute-start | bytes 1327112 | tf_op jit(solution)/shard_map/ppermute | solution.py:1196
  54.8 9.0 %collective-permute-start.8 = (bf16[4,1,72,768]{3,2,0,1:T(8,128)(2,1)}, bf16[4,1,72,768]{3,2,0,1:T(8,128)(2,1)}, u32[]{:S(2)}, u32[]{:S(2)}) collective-permute-start(bf16[4,1,72,768]{3,2,0,1:T(8,128)(2,1)} %get-tuple-element.509), channel_id=1, source_target_pairs={{0,1},{1,0},{2,3},{3,2},{4,5},{5,4},{6,7},{7,6},{8,9},{9,8},{10,11... | collective-permute-start | bytes 1327112 | tf_op jit(solution)/shard_map/ppermute | solution.py:1196
  56.0 8.5 %collective-permute-start.9 = (bf16[2,2,1,72,768]{4,3,1,0,2:T(8,128)(2,1)S(1)}, bf16[2,2,1,72,768]{4,3,1,0,2:T(8,128)(2,1)S(1)}, u32[]{:S(2)}, u32[]{:S(2)}) collective-permute-start(bf16[2,2,1,72,768]{4,3,1,0,2:T(8,128)(2,1)S(1)} %collective-permute-done.6), channel_id=1, source_target_pairs={{0,24},{1,25},{2,26},{3,27},{4,28},{5,29},{6,30},{7,31},{8,0},{9,1... | collective-permute-start | bytes 1327112 | tf_op jit(solution)/shard_map/ppermute | solution.py:1196
  65.6 18.0 %collective-permute-start.11 = (bf16[2,4,1,72,768]{4,3,1,2,0:T(8,128)(2,1)S(1)}, bf16[2,4,1,72,768]{4,3,1,2,0:T(8,128)(2,1)S(1)}, u32[]{:S(2)}, u32[]{:S(2)}) collective-permute-start(bf16[2,4,1,72,768]{4,3,1,2,0:T(8,128)(2,1)S(1)} %get-tuple-element.504), channel_id=1, source_target_pairs={{0,4},{1,5},{2,6},{3,7},{4,0},{5,1},{6,2},{7,3},{8,12},{9,13},{10,... | collective-permute-start | bytes 2654216 | tf_op jit(solution)/shard_map/ppermute | solution.py:1196
  66.9 36.8 %copy-start.40 = (bf16[512,1152]{1,0:T(8,128)(2,1)S(1)}, bf16[512,1152]{1,0:T(8,128)(2,1)}, u32[]{:S(2)}) copy-start(bf16[512,1152]{1,0:T(8,128)(2,1)} %get-tuple-element.280.first_in) | copy-start | bytes 3538948
  66.9 37.3 %copy-start.34 = (f32[1152]{0:T(1024)S(1)}, f32[1152]{0:T(1024)}, u32[]{:S(2)}) copy-start(f32[1152]{0:T(1024)} %param.32) | copy-start | bytes 13828
  68.1 19.7 %collective-permute-start.10 = (bf16[2,4,1,72,768]{4,3,1,2,0:T(8,128)(2,1)S(1)}, bf16[2,4,1,72,768]{4,3,1,2,0:T(8,128)(2,1)S(1)}, u32[]{:S(2)}, u32[]{:S(2)}) collective-permute-start(bf16[2,4,1,72,768]{4,3,1,2,0:T(8,128)(2,1)S(1)} %get-tuple-element.506), channel_id=1, source_target_pairs={{0,1},{1,0},{2,3},{3,2},{4,5},{5,4},{6,7},{7,6},{8,9},{9,8},{10,11... | collective-permute-start | bytes 2654216 | tf_op jit(solution)/shard_map/ppermute | solution.py:1196
  68.7 7.9 %collective-permute-start.12 = (bf16[2,2,1,72,768]{4,3,1,0,2:T(8,128)(2,1)S(1)}, bf16[2,2,1,72,768]{4,3,1,0,2:T(8,128)(2,1)S(1)}, u32[]{:S(2)}, u32[]{:S(2)}) collective-permute-start(bf16[2,2,1,72,768]{4,3,1,0,2:T(8,128)(2,1)S(1)} %collective-permute-done.9), channel_id=1, source_target_pairs={{0,24},{1,25},{2,26},{3,27},{4,28},{5,29},{6,30},{7,31},{8,0},{9,1... | collective-permute-start | bytes 1327112 | tf_op jit(solution)/shard_map/ppermute | solution.py:1196
  88.0 15.6 %collective-permute-start.17 = (bf16[4,2,2,1,72,768]{5,4,3,2,1,0:T(8,128)(2,1)S(1)}, bf16[4,2,2,1,72,768]{5,4,3,2,1,0:T(8,128)(2,1)S(1)}, u32[]{:S(2)}, u32[]{:S(2)}) collective-permute-start(bf16[4,2,2,1,72,768]{5,4,3,2,1,0:T(8,128)(2,1)S(1)} %pad_maximum_fusion.refs_4_), channel_id=1, source_target_pairs={{0,2},{1,3},{2,0},{3,1},{4,6},{5,7},{6,4},{7,5},{8,10},{9,11},{10,... | collective-permute-start | bytes 5308424 | tf_op jit(solution)/shard_map/ppermute | solution.py:1196
  95.3 4.6 collective-permute-start.15
  95.4 5.8 collective-permute-start.13
  95.8 6.6 collective-permute-start.14
  95.9 7.8 collective-permute-start.16
  103.7 36.8 %collective-permute-start.18 = (bf16[512,1152]{1,0:T(8,128)(2,1)S(1)}, bf16[512,1152]{1,0:T(8,128)(2,1)S(1)}, u32[]{:S(2)}, u32[]{:S(2)}) collective-permute-start(bf16[512,1152]{1,0:T(8,128)(2,1)S(1)} %copy-done.40), channel_id=1, source_target_pairs={{0,1},{1,0},{2,3},{3,2},{4,5},{5,4},{6,7},{7,6},{8,9},{9,8},{10,11... | collective-permute-start | bytes 3538952 | tf_op jit(solution)/shard_map/ppermute | solution.py:1196
  151.7 27.5 %collective-permute-start.19 = (bf16[8,1152]{1,0:T(8,128)(2,1)S(1)}, bf16[8,1152]{1,0:T(8,128)(2,1)S(1)}, u32[]{:S(2)}, u32[]{:S(2)}) collective-permute-start(bf16[8,1152]{1,0:T(8,128)(2,1)S(1)} %copy-done.19), channel_id=1, source_target_pairs={{0,8},{1,9},{2,10},{3,11},{4,12},{5,13},{6,14},{7,15},{8,16},{9,17... | collective-permute-start | bytes 55304 | tf_op jit(solution)/shard_map/ppermute | solution.py:1196
  153.0 26.2 %collective-permute-start.20 = (bf16[8,1152]{1,0:T(8,128)(2,1)S(1)}, bf16[8,1152]{1,0:T(8,128)(2,1)S(1)}, u32[]{:S(2)}, u32[]{:S(2)}) collective-permute-start(bf16[8,1152]{1,0:T(8,128)(2,1)S(1)} %copy-done.19), channel_id=1, source_target_pairs={{0,16},{1,17},{2,18},{3,19},{4,20},{5,21},{6,22},{7,23},{8,24},{9,... | collective-permute-start | bytes 55304 | tf_op jit(solution)/shard_map/ppermute | solution.py:1196
  156.1 23.1 %collective-permute-start.21 = (bf16[8,1152]{1,0:T(8,128)(2,1)S(1)}, bf16[8,1152]{1,0:T(8,128)(2,1)S(1)}, u32[]{:S(2)}, u32[]{:S(2)}) collective-permute-start(bf16[8,1152]{1,0:T(8,128)(2,1)S(1)} %copy-done.19), channel_id=1, source_target_pairs={{0,24},{1,25},{2,26},{3,27},{4,28},{5,29},{6,30},{7,31},{8,0},{9,1... | collective-permute-start | bytes 55304 | tf_op jit(solution)/shard_map/ppermute | solution.py:1196
  179.2 40.4 %collective-permute-start.22 = (bf16[1,512,640]{2,1,0:T(8,128)(2,1)}, bf16[1,512,640]{2,1,0:T(8,128)(2,1)S(1)}, u32[]{:S(2)}, u32[]{:S(2)}) collective-permute-start(bf16[1,512,640]{2,1,0:T(8,128)(2,1)} %get-tuple-element.306), channel_id=1, source_target_pairs={{0,1},{1,0},{2,3},{3,2},{4,5},{5,4},{6,7},{7,6},{8,9},{9,8},{10,11... | collective-permute-start | bytes 1966088 | tf_op jit(solution)/shard_map/ppermute | solution.py:1196
  179.3 40.3 %collective-permute-start.23 = (bf16[4,8,1152]{2,1,0:T(8,128)(2,1)S(1)}, bf16[4,8,1152]{2,1,0:T(8,128)(2,1)S(1)}, u32[]{:S(2)}, u32[]{:S(2)}) collective-permute-start(bf16[4,8,1152]{2,1,0:T(8,128)(2,1)S(1)} %pad_maximum_fusion.13), channel_id=1, source_target_pairs={{0,4},{1,5},{2,6},{3,7},{4,0},{5,1},{6,2},{7,3},{8,12},{9,13},{10,... | collective-permute-start | bytes 221192 | tf_op jit(solution)/shard_map/ppermute | solution.py:1196
  219.6 23.9 %copy-start.16 = (bf16[8,8,1152]{2,1,0:T(8,128)(2,1)}, bf16[8,8,1152]{2,1,0:T(8,128)(2,1)S(1)}, u32[]{:S(2)}) copy-start(bf16[8,8,1152]{2,1,0:T(8,128)(2,1)S(1)} %pad_maximum_fusion.11) | copy-start | bytes 442372
  219.6 23.9 %collective-permute-start.24 = (bf16[8,8,1152]{2,1,0:T(8,128)(2,1)S(1)}, bf16[8,8,1152]{2,1,0:T(8,128)(2,1)S(1)}, u32[]{:S(2)}, u32[]{:S(2)}) collective-permute-start(bf16[8,8,1152]{2,1,0:T(8,128)(2,1)S(1)} %pad_maximum_fusion.11), channel_id=1, source_target_pairs={{0,2},{1,3},{2,0},{3,1},{4,6},{5,7},{6,4},{7,5},{8,10},{9,11},{10,... | collective-permute-start | bytes 442376 | tf_op jit(solution)/shard_map/ppermute | solution.py:1196
  313.7 5.6 collective-permute-start.25
  323.9 71.5 %collective-permute-start.26 = (bf16[2,288,2304]{2,1,0:T(8,128)(2,1)}, bf16[2,288,2304]{2,1,0:T(8,128)(2,1)S(1)}, u32[]{:S(2)}, u32[]{:S(2)}) collective-permute-start(bf16[2,288,2304]{2,1,0:T(8,128)(2,1)} %get-tuple-element.338), channel_id=1, source_target_pairs={{0,2},{1,3},{2,0},{3,1},{4,6},{5,7},{6,4},{7,5},{8,10},{9,11},{10,... | collective-permute-start | bytes 7962632 | tf_op jit(solution)/shard_map/ppermute | solution.py:1196
  324.3 71.1 %collective-permute-start.27 = (bf16[2,288,2304]{2,1,0:T(8,128)(2,1)}, bf16[2,288,2304]{2,1,0:T(8,128)(2,1)}, u32[]{:S(2)}, u32[]{:S(2)}) collective-permute-start(bf16[2,288,2304]{2,1,0:T(8,128)(2,1)} %add_convert_fusion.2), channel_id=1, source_target_pairs={{0,4},{1,5},{2,6},{3,7},{4,0},{5,1},{6,2},{7,3},{8,12},{9,13},{10,... | collective-permute-start | bytes 7962632 | tf_op jit(solution)/shard_map/ppermute | solution.py:1196
  395.5 6.2 collective-permute-start.28
  405.3 59.7 %collective-permute-start.29 = (bf16[2,288,2304]{2,1,0:T(8,128)(2,1)}, bf16[2,288,2304]{2,1,0:T(8,128)(2,1)}, u32[]{:S(2)}, u32[]{:S(2)}) collective-permute-start(bf16[2,288,2304]{2,1,0:T(8,128)(2,1)} %add_convert_fusion.1), channel_id=1, source_target_pairs={{0,1},{1,0},{2,3},{3,2},{4,5},{5,4},{6,7},{7,6},{8,9},{9,8},{10,11... | collective-permute-start | bytes 7962632 | tf_op jit(solution)/shard_map/ppermute | solution.py:1196
  406.9 59.1 %collective-permute-start.30 = (bf16[2,288,2304]{2,1,0:T(8,128)(2,1)}, bf16[2,288,2304]{2,1,0:T(8,128)(2,1)}, u32[]{:S(2)}, u32[]{:S(2)}) collective-permute-start(bf16[2,288,2304]{2,1,0:T(8,128)(2,1)} %add_convert_fusion), channel_id=1, source_target_pairs={{0,4},{1,5},{2,6},{3,7},{4,0},{5,1},{6,2},{7,3},{8,12},{9,13},{10,... | collective-permute-start | bytes 7962632 | tf_op jit(solution)/shard_map/ppermute | solution.py:1196
  407.1 58.9 %collective-permute-start.31 = (bf16[2,288,2304]{2,1,0:T(8,128)(2,1)}, bf16[2,288,2304]{2,1,0:T(8,128)(2,1)}, u32[]{:S(2)}, u32[]{:S(2)}) collective-permute-start(bf16[2,288,2304]{2,1,0:T(8,128)(2,1)} %get-tuple-element.363), channel_id=1, source_target_pairs={{0,2},{1,3},{2,0},{3,1},{4,6},{5,7},{6,4},{7,5},{8,10},{9,11},{10,... | collective-permute-start | bytes 7962632 | tf_op jit(solution)/shard_map/ppermute | solution.py:1196
  466.1 8.7 %collective-permute-start.32 = (bf16[2,576,640]{2,1,0:T(8,128)(2,1)}, bf16[2,576,640]{2,1,0:T(8,128)(2,1)S(1)}, u32[]{:S(2)}, u32[]{:S(2)}) collective-permute-start(bf16[2,576,640]{2,1,0:T(8,128)(2,1)} %get-tuple-element.371), channel_id=1, source_target_pairs={{0,2},{1,3},{2,0},{3,1},{4,6},{5,7},{6,4},{7,5},{8,10},{9,11},{10,... | collective-permute-start | bytes 4423688 | tf_op jit(solution)/shard_map/ppermute | solution.py:1196
  467.2 16.7 %collective-permute-start.33 = (bf16[1,512,640]{2,1,0:T(8,128)(2,1)}, bf16[1,512,640]{2,1,0:T(8,128)(2,1)}, u32[]{:S(2)}, u32[]{:S(2)}) collective-permute-start(bf16[1,512,640]{2,1,0:T(8,128)(2,1)} %get-tuple-element.373), channel_id=1, source_target_pairs={{0,1},{1,0},{2,3},{3,2},{4,5},{5,4},{6,7},{7,6},{8,9},{9,8},{10,11... | collective-permute-start | bytes 1966088 | tf_op jit(solution)/shard_map/ppermute | solution.py:1196
  476.9 59.2 %collective-permute-start.34 = (bf16[288,640]{1,0:T(8,128)(2,1)}, bf16[288,640]{1,0:T(8,128)(2,1)S(1)}, u32[]{:S(2)}, u32[]{:S(2)}) collective-permute-start(bf16[288,640]{1,0:T(8,128)(2,1)} %get-tuple-element.378), channel_id=1, source_target_pairs={{0,4},{1,5},{2,6},{3,7},{4,0},{5,1},{6,2},{7,3},{8,12},{9,13},{10,... | collective-permute-start | bytes 1105928 | tf_op jit(solution)/shard_map/ppermute | solution.py:1196
  477.3 58.9 %collective-permute-start.35 = (bf16[288,640]{1,0:T(8,128)(2,1)}, bf16[288,640]{1,0:T(8,128)(2,1)S(1)}, u32[]{:S(2)}, u32[]{:S(2)}) collective-permute-start(bf16[288,640]{1,0:T(8,128)(2,1)} %get-tuple-element.379), channel_id=1, source_target_pairs={{0,1},{1,0},{2,3},{3,2},{4,5},{5,4},{6,7},{7,6},{8,9},{9,8},{10,11... | collective-permute-start | bytes 1105928 | tf_op jit(solution)/shard_map/ppermute | solution.py:1196
  478.6 57.6 %collective-permute-start.36 = (bf16[288,640]{1,0:T(8,128)(2,1)}, bf16[288,640]{1,0:T(8,128)(2,1)S(1)}, u32[]{:S(2)}, u32[]{:S(2)}) collective-permute-start(bf16[288,640]{1,0:T(8,128)(2,1)} %get-tuple-element.380), channel_id=1, source_target_pairs={{0,5},{1,4},{2,7},{3,6},{4,1},{5,0},{6,3},{7,2},{8,13},{9,12},{10,... | collective-permute-start | bytes 1105928 | tf_op jit(solution)/shard_map/ppermute | solution.py:1196
  537.1 78.2 %collective-permute-start.37 = (bf16[1,512,1792]{2,1,0:T(8,128)(2,1)}, bf16[1,512,1792]{2,1,0:T(8,128)(2,1)}, u32[]{:S(2)}, u32[]{:S(2)}) collective-permute-start(bf16[1,512,1792]{2,1,0:T(8,128)(2,1)} %get-tuple-element.396), channel_id=1, source_target_pairs={{0,1},{1,0},{2,3},{3,2},{4,5},{5,4},{6,7},{7,6},{8,9},{9,8},{10,11... | collective-permute-start | bytes 5505032 | tf_op jit(solution)/shard_map/ppermute | solution.py:1196
  537.1 75.9 %collective-permute-start.38 = (bf16[2,72,2304]{2,1,0:T(8,128)(2,1)}, bf16[2,72,2304]{2,1,0:T(8,128)(2,1)S(1)}, u32[]{:S(2)}, u32[]{:S(2)}) collective-permute-start(bf16[2,72,2304]{2,1,0:T(8,128)(2,1)} %get-tuple-element.397), channel_id=1, source_target_pairs={{0,8},{1,9},{2,10},{3,11},{4,12},{5,13},{6,14},{7,15},{8,16},{9,17... | collective-permute-start | bytes 1990664 | tf_op jit(solution)/shard_map/ppermute | solution.py:1196
  537.3 78.1 %collective-permute-start.39 = (bf16[2,72,2304]{2,1,0:T(8,128)(2,1)}, bf16[2,72,2304]{2,1,0:T(8,128)(2,1)S(1)}, u32[]{:S(2)}, u32[]{:S(2)}) collective-permute-start(bf16[2,72,2304]{2,1,0:T(8,128)(2,1)} %get-tuple-element.398), channel_id=1, source_target_pairs={{0,16},{1,17},{2,18},{3,19},{4,20},{5,21},{6,22},{7,23},{8,24},{9,... | collective-permute-start | bytes 1990664 | tf_op jit(solution)/shard_map/ppermute | solution.py:1196
  539.1 76.2 %collective-permute-start.40 = (bf16[2,72,2304]{2,1,0:T(8,128)(2,1)}, bf16[2,72,2304]{2,1,0:T(8,128)(2,1)S(1)}, u32[]{:S(2)}, u32[]{:S(2)}) collective-permute-start(bf16[2,72,2304]{2,1,0:T(8,128)(2,1)} %get-tuple-element.399), channel_id=1, source_target_pairs={{0,24},{1,25},{2,26},{3,27},{4,28},{5,29},{6,30},{7,31},{8,0},{9,1... | collective-permute-start | bytes 1990664 | tf_op jit(solution)/shard_map/ppermute | solution.py:1196
  539.1 90.5 %collective-permute-start.41 = (bf16[72,640]{1,0:T(8,128)(2,1)S(1)}, bf16[72,640]{1,0:T(8,128)(2,1)S(1)}, u32[]{:S(2)}, u32[]{:S(2)}) collective-permute-start(bf16[72,640]{1,0:T(8,128)(2,1)S(1)} %get-tuple-element.409), channel_id=1, source_target_pairs={{0,8},{1,9},{2,10},{3,11},{4,12},{5,13},{6,14},{7,15},{8,16},{9,17... | collective-permute-start | bytes 276488 | tf_op jit(solution)/shard_map/ppermute | solution.py:1196
  613.0 16.7 %collective-permute-start.42 = (bf16[72,640]{1,0:T(8,128)(2,1)S(1)}, bf16[72,640]{1,0:T(8,128)(2,1)S(1)}, u32[]{:S(2)}, u32[]{:S(2)}) collective-permute-start(bf16[72,640]{1,0:T(8,128)(2,1)S(1)} %get-tuple-element.410), channel_id=1, source_target_pairs={{0,16},{1,17},{2,18},{3,19},{4,20},{5,21},{6,22},{7,23},{8,24},{9,... | collective-permute-start | bytes 276488 | tf_op jit(solution)/shard_map/ppermute | solution.py:1196
  615.3 14.4 %collective-permute-start.43 = (bf16[72,640]{1,0:T(8,128)(2,1)S(1)}, bf16[72,640]{1,0:T(8,128)(2,1)S(1)}, u32[]{:S(2)}, u32[]{:S(2)}) collective-permute-start(bf16[72,640]{1,0:T(8,128)(2,1)S(1)} %get-tuple-element.411), channel_id=1, source_target_pairs={{0,24},{1,25},{2,26},{3,27},{4,28},{5,29},{6,30},{7,31},{8,0},{9,1... | collective-permute-start | bytes 276488 | tf_op jit(solution)/shard_map/ppermute | solution.py:1196
  630.4 21.4 %collective-permute-start.44 = (bf16[576,1792]{1,0:T(8,128)(2,1)}, bf16[576,1792]{1,0:T(8,128)(2,1)S(1)}, u32[]{:S(2)}, u32[]{:S(2)}) collective-permute-start(bf16[576,1792]{1,0:T(8,128)(2,1)} %get-tuple-element.417), channel_id=1, source_target_pairs={{0,2},{1,3},{2,0},{3,1},{4,6},{5,7},{6,4},{7,5},{8,10},{9,11},{10,... | collective-permute-start | bytes 6193160 | tf_op jit(solution)/shard_map/ppermute | solution.py:1196
  651.8 5.9 collective-permute-start.45
  660.3 47.3 %copy-start.21 = (f32[4,8,1152]{2,1,0:T(8,128)S(1)}, f32[4,8,1152]{2,1,0:T(8,128)}, u32[]{:S(2)}) copy-start(f32[4,8,1152]{2,1,0:T(8,128)} %get-tuple-element.430) | copy-start | bytes 442372
  660.3 34.5 %collective-permute-start.46 = (bf16[288,1792]{1,0:T(8,128)(2,1)S(1)}, bf16[288,1792]{1,0:T(8,128)(2,1)S(1)}, u32[]{:S(2)}, u32[]{:S(2)}) collective-permute-start(bf16[288,1792]{1,0:T(8,128)(2,1)S(1)} %get-tuple-element.425), channel_id=1, source_target_pairs={{0,4},{1,5},{2,6},{3,7},{4,0},{5,1},{6,2},{7,3},{8,12},{9,13},{10,... | collective-permute-start | bytes 3096584 | tf_op jit(solution)/shard_map/ppermute | solution.py:1196
  660.4 34.4 %collective-permute-start.47 = (bf16[288,1792]{1,0:T(8,128)(2,1)S(1)}, bf16[288,1792]{1,0:T(8,128)(2,1)}, u32[]{:S(2)}, u32[]{:S(2)}) collective-permute-start(bf16[288,1792]{1,0:T(8,128)(2,1)S(1)} %get-tuple-element.426), channel_id=1, source_target_pairs={{0,1},{1,0},{2,3},{3,2},{4,5},{5,4},{6,7},{7,6},{8,9},{9,8},{10,11... | collective-permute-start | bytes 3096584 | tf_op jit(solution)/shard_map/ppermute | solution.py:1196
  661.8 45.7 %collective-permute-start.48 = (bf16[288,1792]{1,0:T(8,128)(2,1)S(1)}, bf16[288,1792]{1,0:T(8,128)(2,1)}, u32[]{:S(2)}, u32[]{:S(2)}) collective-permute-start(bf16[288,1792]{1,0:T(8,128)(2,1)S(1)} %get-tuple-element.427), channel_id=1, source_target_pairs={{0,5},{1,4},{2,7},{3,6},{4,1},{5,0},{6,3},{7,2},{8,13},{9,12},{10,... | collective-permute-start | bytes 3096584 | tf_op jit(solution)/shard_map/ppermute | solution.py:1196
  708.6 3.8 collective-permute-start.49
  712.5 19.9 %collective-permute-start.50 = (f32[8,4096]{1,0:T(8,128)S(1)}, f32[8,4096]{1,0:T(8,128)S(1)}, u32[]{:S(2)}, u32[]{:S(2)}) collective-permute-start(f32[8,4096]{1,0:T(8,128)S(1)} %add.244), channel_id=1, source_target_pairs={{0,8},{1,9},{2,10},{3,11},{4,12},{5,13},{6,14},{7,15},{8,16},{9,17... | collective-permute-start | bytes 393224 | tf_op jit(solution)/shard_map/ppermute | solution.py:1196
  714.1 18.4 %collective-permute-start.51 = (f32[8,4096]{1,0:T(8,128)S(1)}, f32[8,4096]{1,0:T(8,128)S(1)}, u32[]{:S(2)}, u32[]{:S(2)}) collective-permute-start(f32[8,4096]{1,0:T(8,128)S(1)} %add.244), channel_id=1, source_target_pairs={{0,16},{1,17},{2,18},{3,19},{4,20},{5,21},{6,22},{7,23},{8,24},{9,... | collective-permute-start | bytes 393224 | tf_op jit(solution)/shard_map/ppermute | solution.py:1196
  715.7 16.8 %collective-permute-start.52 = (f32[8,4096]{1,0:T(8,128)S(1)}, f32[8,4096]{1,0:T(8,128)S(1)}, u32[]{:S(2)}, u32[]{:S(2)}) collective-permute-start(f32[8,4096]{1,0:T(8,128)S(1)} %add.244), channel_id=1, source_target_pairs={{0,24},{1,25},{2,26},{3,27},{4,28},{5,29},{6,30},{7,31},{8,0},{9,1... | collective-permute-start | bytes 393224 | tf_op jit(solution)/shard_map/ppermute | solution.py:1196
  732.5 26.4 %collective-permute-start.54 = (f32[32,4096]{1,0:T(8,128)S(1)}, f32[32,4096]{1,0:T(8,128)S(1)}, u32[]{:S(2)}, u32[]{:S(2)}) collective-permute-start(f32[32,4096]{1,0:T(8,128)S(1)} %pad_maximum_fusion.6), channel_id=1, source_target_pairs={{0,4},{1,5},{2,6},{3,7},{4,0},{5,1},{6,2},{7,3},{8,12},{9,13},{10,... | collective-permute-start | bytes 1572872 | tf_op jit(solution)/shard_map/ppermute | solution.py:1196
  733.6 7.0 collective-permute-start.55
  735.0 19.6 %collective-permute-start.56 = (bf16[72,1792]{1,0:T(8,128)(2,1)S(1)}, bf16[72,1792]{1,0:T(8,128)(2,1)S(1)}, u32[]{:S(2)}, u32[]{:S(2)}) collective-permute-start(bf16[72,1792]{1,0:T(8,128)(2,1)S(1)} %get-tuple-element.451), channel_id=1, source_target_pairs={{0,16},{1,17},{2,18},{3,19},{4,20},{5,21},{6,22},{7,23},{8,24},{9,... | collective-permute-start | bytes 774152 | tf_op jit(solution)/shard_map/ppermute | solution.py:1196
  737.4 21.5 %collective-permute-start.57 = (bf16[72,1792]{1,0:T(8,128)(2,1)S(1)}, bf16[72,1792]{1,0:T(8,128)(2,1)S(1)}, u32[]{:S(2)}, u32[]{:S(2)}) collective-permute-start(bf16[72,1792]{1,0:T(8,128)(2,1)S(1)} %get-tuple-element.452), channel_id=1, source_target_pairs={{0,24},{1,25},{2,26},{3,27},{4,28},{5,29},{6,30},{7,31},{8,0},{9,1... | collective-permute-start | bytes 774152 | tf_op jit(solution)/shard_map/ppermute | solution.py:1196
  737.4 3.1 collective-permute-start.53
  759.0 3.8 collective-permute-start.58
  (39 other events, 320.1 us)
Sparse Core Ops, SparseCore 0:
  64.6 151.7 all-gather.1
